TPU v7x, 32 devices: a whole 2x2x4 slice. The times are simulated.
32 devices in a mesh: rows: 32 (over z, y, x, core), users: 1.
Axes of the slice: x: 2, y: 2, z: 4, core: 2. Of those that a mesh axis runs over, the one named last changes fastest.
Arguments:
- old_basis: bfloat16 [12288, 4096], P('rows', 'users'), may hold values from -24 to 24
- new_atoms: bfloat16 [12288, 128], P('rows'), may hold values from -300 to 300
- user_residuals: bfloat16 [12288, 128], P('rows', 'users'), may hold values from -850 to 850
Outputs:
- new_block: bfloat16 [12288, 128], P('rows')
- updated_residuals: bfloat16 [12288, 128], P('rows', 'users')
All inputs are finite; a program needn't handle non-finite values.
Results may differ from a plain program's by a relative error of at most 0.019.
Values may be sent and summed in bfloat16 or wider, within the bound.
No kernel may reach another device: no remote copies, remote signals or barrier semaphores. Data moves between devices by JAX's collectives and lax.ppermute only.
A program may use at most 64 MiB of HBM per device.

v0:
```python
import jax
import jax.numpy as jnp
from jax import lax
from jax.sharding import PartitionSpec as P


def coefficient_sum(partial_coef, m_total):
    summed = lax.psum(partial_coef, "rows")
    return (summed / m_total).astype(jnp.bfloat16)


def rows_product(left_rows, right_rows):
    return jnp.einsum("rk,rb->kb", left_rows, right_rows, preferred_element_type=jnp.float32)


def finish_block(remainder_low, gram_total, coupling_total, user_residuals, m_total):
    gram_matrix = gram_total / m_total
    factor_lower = jnp.linalg.cholesky(gram_matrix)
    identity = jnp.eye(gram_matrix.shape[0], dtype=jnp.float32)
    inverse = jax.scipy.linalg.solve_triangular(factor_lower, identity, lower=True)
    new_block = jnp.dot(
        remainder_low.astype(jnp.float32), inverse.T, precision=lax.Precision.HIGHEST
    ).astype(jnp.bfloat16)
    weights_low = jnp.dot(
        inverse, coupling_total / m_total, precision=lax.Precision.HIGHEST
    ).astype(jnp.bfloat16)
    updated = user_residuals.astype(jnp.float32) - jnp.dot(
        new_block, weights_low, preferred_element_type=jnp.float32
    )
    return (new_block, updated.astype(jnp.bfloat16))


def local(old_basis, new_atoms, user_residuals):
    local_rows = old_basis.shape[0]
    m_total = float(local_rows * lax.axis_size("rows"))
    remainder = new_atoms.astype(jnp.float32)
    remainder_low = new_atoms
    for sweep_index in range(2):
        coef_low = coefficient_sum(rows_product(old_basis, remainder_low), m_total)
        local_image = jnp.dot(old_basis, coef_low, preferred_element_type=jnp.float32)
        projected = lax.psum(local_image, "users")
        remainder = remainder - projected
        remainder_low = remainder.astype(jnp.bfloat16)
    gram_total, coupling_total = lax.psum(
        (rows_product(remainder_low, remainder_low), rows_product(remainder_low, user_residuals)),
        "rows",
    )
    return finish_block(remainder_low, gram_total, coupling_total, user_residuals, m_total)


def solution(mesh):
    in_specs = (P("rows", "users"), P("rows", None), P("rows", "users"))
    out_specs = (P("rows", None), P("rows", "users"))
    return jax.shard_map(local, mesh=mesh, in_specs=in_specs, out_specs=out_specs, check_vma=False)
```

profile of v0, /device:TPU:0, one launch (start us, length us, event | category | flops | bytes accessed | tf_op | source)
XLA Modules:
  0.0 450.5 jit_solution(1842009063590101689)
XLA Ops:
  7.2 0.0 copy-start
  7.2 0.0 all-reduce.5.cloned.1.call-start
  7.2 1.8 copy-done
  9.1 3.2 fusion.16
  12.3 0.0 copy-start.1
  12.3 0.0 all-reduce.5.cloned.1.call-update
  12.3 0.0 all-reduce.7.cloned.1.call-start
  12.4 0.8 copy-done.1
  13.2 0.1 copy.5
  13.3 136.5 %all-reduce.5.cloned.1.call-done = f32[4096,128]{1,0:T(8,128)} async-done(((f32[4096,128]{1,0:T(8,128)}), f32[4096,128]{1,0:T(8,128)}) %all-reduce.5.cloned.1.call-update) | async-done | bytes 2097168 | tf_op jit(solution)/shard_map/psum | solution.py:8
  149.9 2.7 fusion.1
  152.5 2.6 convolution_bitcast_fusion
  155.2 0.0 all-reduce.7.cloned.1.call-update
  155.2 0.0 copy-start.2
  155.2 0.0 all-reduce.9.cloned.1.call-start
  155.2 133.5 %all-reduce.7.cloned.1.call-done = f32[4096,128]{1,0:T(8,128)} async-done(((f32[4096,128]{1,0:T(8,128)}), f32[4096,128]{1,0:T(8,128)}) %all-reduce.7.cloned.1.call-update) | async-done | bytes 2097168 | tf_op jit(solution)/shard_map/psum | solution.py:8
  288.8 2.7 fusion.2
  291.4 0.8 fusion.17
  292.2 0.0 copy-done.2
  292.2 0.9 fusion.18
  293.1 0.0 all-reduce.9.cloned.1.call-update
  293.1 123.7 %all-reduce.9.cloned.1.call-done = (f32[128,128]{0,1:T(8,128)}, f32[128,128]{0,1:T(8,128)}) async-done(((f32[128,128]{0,1:T(8,128)}, f32[128,128]{0,1:T(8,128)}), (f32[128,128]{0,1:T(8,128)}, f32[128,128]{0,1:T(8,128)})) %all-reduce.9.cloned.1.call-update) | async-done | bytes 131088 | tf_op jit(solution)/shard_map/psum | solution.py:44
  416.8 0.8 broadcast_multiply_fusion
  417.6 0.1 copy.7
  417.7 0.9 fusion.10
  418.6 11.7 %cholesky.17 = f32[128,128]{1,0:T(8,128)S(1)} custom-call(f32[128,128]{1,0:T(8,128)S(1)} %fusion.10), custom_call_target="Cholesky" | custom-call | tf_op jit(solution)/shard_map/jit(cholesky)/cholesky | solution.py:18
  430.3 0.6 compare_reduce_fusion
  431.0 0.7 fusion.7
  431.6 9.8 %custom-call.7 = f32[1,128,128]{1,2,0:T(8,128)S(1)} custom-call(f32[1,128,128]{2,1,0:T(8,128)S(1)} %fusion.7), custom_call_target="InvertDiagBlocksLowerTriangular" | custom-call | tf_op jit(solution)/shard_map/jit(_solve_triangular)/triangular_solve | solution.py:20
  441.4 0.2 fusion.8
  441.7 0.3 convolution_convert_fusion
  442.0 0.0 copy-start.3
  442.0 1.1 convolution_convert_fusion.1
  443.2 0.8 fusion.3
  444.0 0.0 copy-done.3
  (1 shorter events, 0.0 us)
Async XLA Ops:
  7.2 1.9 copy-start
  7.2 142.7 %all-reduce.5.cloned.1.call-start = ((), (), s32[]{:S(2)}) async-start(), calls=%async_computation | async-start | bytes 4194304 | tf_op jit(solution)/shard_map/psum | solution.py:8
  12.3 0.9 copy-start.1
  12.3 276.4 %all-reduce.7.cloned.1.call-start = ((), (), s32[]{:S(2)}) async-start(), calls=%async_computation.1 | async-start | bytes 4194304 | tf_op jit(solution)/shard_map/psum | solution.py:8
  155.2 137.1 %copy-start.2 = (bf16[384,128]{1,0:T(8,128)(2,1)S(1)}, bf16[384,128]{1,0:T(8,128)(2,1)}, u32[]{:S(2)}) copy-start(bf16[384,128]{1,0:T(8,128)(2,1)} %param.5) | copy-start | bytes 294916
  155.2 261.6 %all-reduce.9.cloned.1.call-start = ((), (), s32[]{:S(2)}) async-start(), calls=%async_computation.2 | async-start | bytes 262144 | tf_op jit(solution)/shard_map/psum | solution.py:44
  442.0 2.0 copy-start.3
Sparse Core Ops, SparseCore 0:
  13.3 136.4 all-reduce.4
  156.1 132.6 all-reduce.6
  295.0 121.6 all-reduce.8
where the time goes:
time: 451 us
  waiting for transfers between devices  394 us (87%)
  other arithmetic  24.6 us (5%)
  matrix products  15.4 us (3%)
  between operations  13.8 us (3%)
    psum x2, waiting for transfers between devices, coefficient_sum(): summed = lax.psum(partial_coef, 'rows')  270 us
    psum x1, waiting for transfers between devices, local(): lax.psum((rows_product(remainder_low, remainder_low), rows_product(remain...  124 us
    another operation x3, other arithmetic, finish_block(): factor_lower = jnp.linalg.cholesky(gram_matrix)  12.4 us
    another operation x2, other arithmetic, finish_block(): jax.scipy.linalg.solve_triangular(factor_lower, identity, lower=True)  10.5 us
  transfers between devices with their start and end apart: 3, of which 3 were waited for; matrix products, arithmetic and copies ran while one was open for 0% of the time, Pallas kernels for 0%

commit v1 on v0

v1 whole, which is shorter than its diff:
```python
import functools

import jax
import jax.numpy as jnp
from jax import lax
from jax.experimental import pallas as pl
from jax.experimental.pallas import tpu as pltpu
from jax.sharding import PartitionSpec as P

BF16, F32 = jnp.bfloat16, jnp.float32
VMEM = pl.BlockSpec(memory_space=pltpu.VMEM)
SMEM = pl.BlockSpec(memory_space=pltpu.SMEM)
QUARTERS = 4
NT = (((1,), (1,)), ((), ()))
TN = (((0,), (0,)), ((), ()))


def params():
    return pltpu.CompilerParams(vmem_limit_bytes=32 * 2**20)


def swap(value, bit_of_core):
    size = lax.axis_size("rows")
    pairs = [(i, i ^ (1 << bit_of_core[i & 1])) for i in range(size)]
    return lax.ppermute(value, "rows", pairs)


def coef_kernel(places, offset_ref, basis_ref, rem_ref, *out_refs):
    width = out_refs[0].shape[2]
    turned = rem_ref[...].T
    for out_ref, first in zip(out_refs, places):
        for q in range(QUARTERS):
            start = pl.multiple_of(offset_ref[first + q], width)
            product = jnp.dot(turned, basis_ref[:, pl.ds(start, width)], preferred_element_type=F32)
            out_ref[q] = product.astype(out_ref.dtype)


def coef_call(offsets, basis, rem_low, places, width, dtype):
    block = rem_low.shape[1]
    shape = jax.ShapeDtypeStruct((QUARTERS, block, width), dtype)
    flops = 2 * basis.shape[0] * block * width * QUARTERS * len(places)
    return pl.pallas_call(
        functools.partial(coef_kernel, places),
        in_specs=[SMEM, VMEM, VMEM],
        out_specs=[VMEM] * len(places),
        out_shape=[shape] * len(places),
        compiler_params=params(),
        cost_estimate=pl.CostEstimate(flops=flops, bytes_accessed=0, transcendentals=0),
    )(offsets, basis, rem_low)


def project(places, offset_ref, basis_ref, coef_refs, total):
    for coef_ref, first in zip(coef_refs, places):
        width = coef_ref.shape[2]
        for q in range(QUARTERS):
            start = pl.multiple_of(offset_ref[first + q], width)
            total = total - lax.dot_general(
                basis_ref[:, pl.ds(start, width)], coef_ref[q], NT, preferred_element_type=F32
            )
    return total


def image_kernel(places, offset_ref, basis_ref, rem_ref, *refs):
    coef_refs, out_refs = refs[: len(places)], refs[len(places) :]
    total = project(places, offset_ref, basis_ref, coef_refs, rem_ref[...].astype(F32))
    out_refs[0][...] = total
    if len(out_refs) > 1:
        out_refs[1][...] = total.astype(BF16)


def image_call(offsets, basis, rem, coefs, places, low):
    shapes = [jax.ShapeDtypeStruct(rem.shape, F32)]
    if low:
        shapes.append(jax.ShapeDtypeStruct(rem.shape, BF16))
    flops = 2 * rem.size * coefs[0].shape[2] * QUARTERS * len(places)
    return pl.pallas_call(
        functools.partial(image_kernel, places),
        in_specs=[SMEM] + [VMEM] * (2 + len(coefs)),
        out_specs=[VMEM] * len(shapes),
        out_shape=shapes,
        compiler_params=params(),
        cost_estimate=pl.CostEstimate(flops=flops, bytes_accessed=0, transcendentals=0),
    )(offsets, basis, rem, *coefs)


def block_offsets(width, chains):
    me = lax.axis_index("rows")
    core, low, high = me & 1, (me >> 1) & 1, (me >> 2) & 1
    order = jnp.arange(QUARTERS, dtype=jnp.int32)
    turns = jnp.stack([2 * low + high, 2 * high + low])
    lists = []
    for half in (core, 1 - core):
        turn = jnp.where(half == 0, turns[0], turns[1])
        for chain in range(chains):
            lists.append((chain * 2 + half) * QUARTERS + (order ^ turn))
    return jnp.concatenate(lists).astype(jnp.int32) * width


def summed_coefs(own, other, m_total):
    bits = (lax.axis_size("rows") - 1).bit_length()
    first, second = (1, 2), (2, 1)
    chains = range(len(own))
    got = [swap(v, (0, 0)) for v in other]
    own = [own[i] + got[i] for i in chains]
    got = [swap(v[2:].astype(BF16), first) for v in own]
    own = [own[i][:2] + got[i] for i in chains]
    got = [swap(v[1:].astype(BF16), second) for v in own]
    own = [own[i][:1] + got[i] for i in chains]
    for bit in range(3, bits):
        got = [swap(v.astype(BF16), (bit, bit)) for v in own]
        own = [own[i] + got[i] for i in chains]
    own = [(v / m_total).astype(BF16) for v in own]
    got = [swap(v, second) for v in own]
    own = [jnp.concatenate([own[i], got[i]]) for i in chains]
    got = [swap(v, first) for v in own]
    own = [jnp.concatenate([own[i], got[i]]) for i in chains]
    return own, [swap(v, (0, 0)) for v in own]


def sweep(offsets, basis, rem, rem_low, width, chains, m_total):
    mine = tuple(QUARTERS * i for i in range(chains))
    others = tuple(QUARTERS * (chains + i) for i in range(chains))
    other = coef_call(offsets, basis, rem_low, others, width, BF16)
    own = coef_call(offsets, basis, rem_low, mine, width, F32)
    own, other = summed_coefs(own, other, m_total)
    for i in range(chains):
        (rem,) = image_call(offsets, basis, rem, own[i : i + 1], mine[i : i + 1], False)
    return image_call(offsets, basis, rem, other, others, True)


def plain_sweep(basis, rem, rem_low, m_total):
    partial_coef = jnp.einsum("rk,rb->kb", basis, rem_low, preferred_element_type=F32)
    coef_low = (lax.psum(partial_coef, "rows") / m_total).astype(BF16)
    image = jnp.dot(basis, coef_low, preferred_element_type=F32)
    rem = rem - lax.psum(image, "users")
    return rem, rem.astype(BF16)


def small_sums(gram_part, coupling_part):
    bits = (lax.axis_size("rows") - 1).bit_length()
    core = lax.axis_index("rows") & 1
    own = jnp.where(core == 0, gram_part, coupling_part)
    own = own + swap(jnp.where(core == 0, coupling_part, gram_part), (0, 0))
    for pair in [(1, 2), (2, 1)] + [(bit, bit) for bit in range(3, bits)]:
        own = own + swap(own, pair)
    got = swap(own, (0, 0))
    return jnp.where(core == 0, own, got), jnp.where(core == 0, got, own)


def finish_block(remainder_low, gram_total, coupling_total, user_residuals, m_total):
    gram_matrix = gram_total / m_total
    factor_lower = jnp.linalg.cholesky(gram_matrix)
    identity = jnp.eye(gram_matrix.shape[0], dtype=F32)
    inverse = jax.scipy.linalg.solve_triangular(factor_lower, identity, lower=True)
    new_block = jnp.dot(
        remainder_low.astype(F32), inverse.T, precision=lax.Precision.HIGHEST
    ).astype(BF16)
    weights_low = jnp.dot(
        inverse, coupling_total / m_total, precision=lax.Precision.HIGHEST
    ).astype(BF16)
    updated = user_residuals.astype(F32) - jnp.dot(
        new_block, weights_low, preferred_element_type=F32
    )
    return (new_block, updated.astype(BF16))


def local(old_basis, new_atoms, user_residuals):
    rows, atoms = old_basis.shape
    size = lax.axis_size("rows")
    users = lax.axis_size("users")
    m_total = float(rows * size)
    power = size >= 8 and size & (size - 1) == 0
    chains = 2 if atoms % (2 * 2 * QUARTERS * 128) == 0 else 1
    width = atoms // (chains * 2 * QUARTERS)
    paired = power and atoms % (chains * 2 * QUARTERS * 128) == 0 and rows % 128 == 0

    rem, rem_low = new_atoms.astype(F32), new_atoms
    offsets = block_offsets(width, chains) if paired else None
    for _ in range(2):
        if not paired:
            rem, rem_low = plain_sweep(old_basis, rem, rem_low, m_total)
        elif users == 1:
            rem, rem_low = sweep(offsets, old_basis, rem, rem_low, width, chains, m_total)
        else:
            image, _ = sweep(offsets, old_basis, jnp.zeros_like(rem), rem_low, width, chains, m_total)
            rem = rem + lax.psum(image, "users")
            rem_low = rem.astype(BF16)
    gram_part = lax.dot_general(rem_low, rem_low, TN, preferred_element_type=F32)
    coupling_part = lax.dot_general(rem_low, user_residuals, TN, preferred_element_type=F32)
    if power and gram_part.shape == coupling_part.shape:
        gram_total, coupling_total = small_sums(gram_part, coupling_part)
    else:
        gram_total, coupling_total = lax.psum((gram_part, coupling_part), "rows")
    return finish_block(rem_low, gram_total, coupling_total, user_residuals, m_total)


def solution(mesh):
    in_specs = (P("rows", "users"), P("rows", None), P("rows", "users"))
    out_specs = (P("rows", None), P("rows", "users"))
    return jax.shard_map(local, mesh=mesh, in_specs=in_specs, out_specs=out_specs, check_vma=False)
```

time: 451 us -> 128 us (0.28)
  waiting for transfers between devices: 394 us -> 41.7 us
  starting transfers between devices: 0.12 us -> 45.2 us
  matrix products: 15.4 us -> 2.04 us
  between operations: 13.8 us -> 1.12 us
  Pallas kernels: 0 us -> 10.6 us
    psum x3 -> x0, waiting for transfers between devices: 394 us -> none  [the longest x2 270 us: coefficient_sum(): summed = lax.psum(partial_coef, 'rows')]
    ppermute x0 -> x38, starting transfers between devices: none -> 45.2 us  [swap(): return lax.ppermute(value, 'rows', pairs)]
    ppermute x0 -> x38, waiting for transfers between devices: none -> 41.7 us  [swap(): return lax.ppermute(value, 'rows', pairs)]
    dot_general x8 -> x4, matrix products: 14 us -> 1.52 us  [the longest x1 0.81 us: finish_block(): jnp.dot(new_block, weights_low, preferred_element_type=F32)]
    pallas_call x0 -> x10, Pallas kernels: none -> 10.6 us  [the longest x6 6.56 us: image_call(): pl.pallas_call(functools.partial(image_kernel, places), in_specs=[SMEM] +...]
  transfers between devices with their start and end apart: 3 -> 38, of which waited for: 3 -> 26; matrix products, arithmetic and copies ran while one was open for 0% -> 1% of each run, Pallas kernels for 0% -> 4%
where the time goes in v1:
time: 128 us
  starting transfers between devices  45.2 us (35%)
  waiting for transfers between devices  41.7 us (33%)
  other arithmetic  23.9 us (19%)
  Pallas kernels  10.6 us (8%)
  local copies, waits for them, and re-layouts  2.99 us (2%)
  matrix products  2.04 us (2%)
    ppermute x38, starting transfers between devices, swap(): return lax.ppermute(value, 'rows', pairs)  45.2 us
    ppermute x38, waiting for transfers between devices, swap(): return lax.ppermute(value, 'rows', pairs)  41.7 us
    another operation x3, other arithmetic, finish_block(): factor_lower = jnp.linalg.cholesky(gram_matrix)  12.5 us
    another operation x2, other arithmetic, finish_block(): jax.scipy.linalg.solve_triangular(factor_lower, identity, lower=True)  10.5 us
    pallas_call x6, Pallas kernels, image_call(): pl.pallas_call(functools.partial(image_kernel, places), in_specs=[SMEM] +...  6.56 us
    pallas_call x4, Pallas kernels, coef_call(): pl.pallas_call(functools.partial(coef_kernel, places), in_specs=[SMEM, VM...  4.04 us
    unnamed x8, local copies, waits for them, and re-layouts  2.8 us
  transfers between devices with their start and end apart: 38, of which 26 were waited for; matrix products, arithmetic and copies ran while one was open for 1% of the time, Pallas kernels for 4%

profile of v1, /device:TPU:0, one launch (start us, length us, event | category | flops | bytes accessed | tf_op | source)
XLA Modules:
  0.0 127.6 jit_solution(15056474267922095577)
XLA Ops:
  0.8 1.9 %copy-done = bf16[384,4096]{1,0:T(8,128)(2,1)S(1)} copy-done((bf16[384,4096]{1,0:T(8,128)(2,1)S(1)}, bf16[384,4096]{1,0:T(8,128)(2,1)}, u32[]{:S(2)}) %copy-start) | copy-done | bytes 3145752
  2.7 0.9 copy-done.1
  3.5 1.0 shard_map.51
  5.2 1.0 shard_map.50
  6.3 2.9 %collective-permute-start.8 = (bf16[2,128,256]{2,1,0:T(8,128)(2,1)S(1)}, bf16[2,128,256]{2,1,0:T(8,128)(2,1)S(1)}, u32[]{:S(2)}, u32[]{:S(2)}) collective-permute-start(bf16[2,128,256]{2,1,0:T(8,128)(2,1)S(1)} %slice.142), channel_id=1, source_target_pairs={{0,2},{1,5},{2,0},{3,7},{4,6},{5,1},{6,4},{7,3},{8,10},{9,13},{10,... | collective-permute-start | bytes 393224 | tf_op jit(solution)/shard_map/ppermute | solution.py:25
  9.6 2.6 %collective-permute-done.8 = bf16[2,128,256]{2,1,0:T(8,128)(2,1)S(1)} collective-permute-done((bf16[2,128,256]{2,1,0:T(8,128)(2,1)S(1)}, bf16[2,128,256]{2,1,0:T(8,128)(2,1)S(1)}, u32[]{:S(2)}, u32[]{:S(2)}) %collective-permute-start.8) | collective-permute-done | bytes 131104 | tf_op jit(solution)/shard_map/ppermute | solution.py:25
  12.3 2.1 %collective-permute-start.9 = (bf16[1,128,256]{2,1,0:T(8,128)(2,1)S(1)}, bf16[1,128,256]{2,1,0:T(8,128)(2,1)S(1)}, u32[]{:S(2)}, u32[]{:S(2)}) collective-permute-start(bf16[1,128,256]{2,1,0:T(8,128)(2,1)S(1)} %slice.146), channel_id=1, source_target_pairs={{0,4},{1,3},{2,6},{3,1},{4,0},{5,7},{6,2},{7,5},{8,12},{9,11},{10,... | collective-permute-start | bytes 196616 | tf_op jit(solution)/shard_map/ppermute | solution.py:25
  14.4 1.6 %collective-permute-start.2 = (bf16[1,128,256]{2,1,0:T(8,128)(2,1)S(1)}, bf16[1,128,256]{2,1,0:T(8,128)(2,1)S(1)}, u32[]{:S(2)}, u32[]{:S(2)}) collective-permute-start(bf16[1,128,256]{2,1,0:T(8,128)(2,1)S(1)} %slice.147), channel_id=1, source_target_pairs={{0,4},{1,3},{2,6},{3,1},{4,0},{5,7},{6,2},{7,5},{8,12},{9,11},{10,... | collective-permute-start | bytes 196616 | tf_op jit(solution)/shard_map/ppermute | solution.py:25
  16.0 0.6 collective-permute-done.9
  16.6 2.1 %collective-permute-start.10 = (bf16[1,128,256]{2,1,0:T(8,128)(2,1)S(1)}, bf16[1,128,256]{2,1,0:T(8,128)(2,1)S(1)}, u32[]{:S(2)}, u32[]{:S(2)}) collective-permute-start(bf16[1,128,256]{2,1,0:T(8,128)(2,1)S(1)} %fusion.12), channel_id=1, source_target_pairs={{0,8},{1,9},{2,10},{3,11},{4,12},{5,13},{6,14},{7,15},{8,0},{9,1},... | collective-permute-start | bytes 196616 | tf_op jit(solution)/shard_map/ppermute | solution.py:25
  18.8 1.6 %collective-permute-start.3 = (bf16[1,128,256]{2,1,0:T(8,128)(2,1)S(1)}, bf16[1,128,256]{2,1,0:T(8,128)(2,1)S(1)}, u32[]{:S(2)}, u32[]{:S(2)}) collective-permute-start(bf16[1,128,256]{2,1,0:T(8,128)(2,1)S(1)} %fusion.11), channel_id=1, source_target_pairs={{0,8},{1,9},{2,10},{3,11},{4,12},{5,13},{6,14},{7,15},{8,0},{9,1},... | collective-permute-start | bytes 196616 | tf_op jit(solution)/shard_map/ppermute | solution.py:25
  20.4 0.6 collective-permute-done.10
  21.0 3.3 %collective-permute-start.11 = (bf16[1,128,256]{2,1,0:T(8,128)(2,1)S(1)}, bf16[1,128,256]{2,1,0:T(8,128)(2,1)S(1)}, u32[]{:S(2)}, u32[]{:S(2)}) collective-permute-start(bf16[1,128,256]{2,1,0:T(8,128)(2,1)S(1)} %fusion.2), channel_id=1, source_target_pairs={{0,16},{1,17},{2,18},{3,19},{4,20},{5,21},{6,22},{7,23},{8,24},{9,... | collective-permute-start | bytes 196616 | tf_op jit(solution)/shard_map/ppermute | solution.py:25
  24.4 1.4 %collective-permute-start.4 = (bf16[1,128,256]{2,1,0:T(8,128)(2,1)S(1)}, bf16[1,128,256]{2,1,0:T(8,128)(2,1)S(1)}, u32[]{:S(2)}, u32[]{:S(2)}) collective-permute-start(bf16[1,128,256]{2,1,0:T(8,128)(2,1)S(1)} %fusion.1), channel_id=1, source_target_pairs={{0,16},{1,17},{2,18},{3,19},{4,20},{5,21},{6,22},{7,23},{8,24},{9,... | collective-permute-start | bytes 196616 | tf_op jit(solution)/shard_map/ppermute | solution.py:25
  25.8 2.0 %collective-permute-done.11 = bf16[1,128,256]{2,1,0:T(8,128)(2,1)S(1)} collective-permute-done((bf16[1,128,256]{2,1,0:T(8,128)(2,1)S(1)}, bf16[1,128,256]{2,1,0:T(8,128)(2,1)S(1)}, u32[]{:S(2)}, u32[]{:S(2)}) %collective-permute-start.11) | collective-permute-done | bytes 65568 | tf_op jit(solution)/shard_map/ppermute | solution.py:25
  27.9 1.6 %collective-permute-start.12 = (bf16[1,128,256]{2,1,0:T(8,128)(2,1)S(1)}, bf16[1,128,256]{2,1,0:T(8,128)(2,1)S(1)}, u32[]{:S(2)}, u32[]{:S(2)}) collective-permute-start(bf16[1,128,256]{2,1,0:T(8,128)(2,1)S(1)} %multiply_convert_fusion.2), channel_id=1, source_target_pairs={{0,4},{1,3},{2,6},{3,1},{4,0},{5,7},{6,2},{7,5},{8,12},{9,11},{10,... | collective-permute-start | bytes 196616 | tf_op jit(solution)/shard_map/ppermute | solution.py:25
  29.7 1.6 %collective-permute-start.5 = (bf16[1,128,256]{2,1,0:T(8,128)(2,1)S(1)}, bf16[1,128,256]{2,1,0:T(8,128)(2,1)S(1)}, u32[]{:S(2)}, u32[]{:S(2)}) collective-permute-start(bf16[1,128,256]{2,1,0:T(8,128)(2,1)S(1)} %multiply_convert_fusion.3), channel_id=1, source_target_pairs={{0,4},{1,3},{2,6},{3,1},{4,0},{5,7},{6,2},{7,5},{8,12},{9,11},{10,... | collective-permute-start | bytes 196616 | tf_op jit(solution)/shard_map/ppermute | solution.py:25
  31.2 1.6 %collective-permute-done.12 = bf16[1,128,256]{2,1,0:T(8,128)(2,1)S(1)} collective-permute-done((bf16[1,128,256]{2,1,0:T(8,128)(2,1)S(1)}, bf16[1,128,256]{2,1,0:T(8,128)(2,1)S(1)}, u32[]{:S(2)}, u32[]{:S(2)}) %collective-permute-start.12) | collective-permute-done | bytes 65568 | tf_op jit(solution)/shard_map/ppermute | solution.py:25
  32.8 0.6 collective-permute-start.13
  34.0 1.5 %collective-permute-start.6 = (bf16[2,128,256]{2,1,0:T(8,128)(2,1)S(1)}, bf16[2,128,256]{2,1,0:T(8,128)(2,1)S(1)}, u32[]{:S(2)}, u32[]{:S(2)}) collective-permute-start(bf16[2,128,256]{2,1,0:T(8,128)(2,1)S(1)} %pad_maximum_fusion.4), channel_id=1, source_target_pairs={{0,2},{1,5},{2,0},{3,7},{4,6},{5,1},{6,4},{7,3},{8,10},{9,13},{10,... | collective-permute-start | bytes 393224 | tf_op jit(solution)/shard_map/ppermute | solution.py:25
  35.5 2.3 %collective-permute-done.13 = bf16[2,128,256]{2,1,0:T(8,128)(2,1)S(1)} collective-permute-done((bf16[2,128,256]{2,1,0:T(8,128)(2,1)S(1)}, bf16[2,128,256]{2,1,0:T(8,128)(2,1)S(1)}, u32[]{:S(2)}, u32[]{:S(2)}) %collective-permute-start.13) | collective-permute-done | bytes 131104 | tf_op jit(solution)/shard_map/ppermute | solution.py:25
  38.0 1.3 %collective-permute-done.6 = bf16[2,128,256]{2,1,0:T(8,128)(2,1)S(1)} collective-permute-done((bf16[2,128,256]{2,1,0:T(8,128)(2,1)S(1)}, bf16[2,128,256]{2,1,0:T(8,128)(2,1)S(1)}, u32[]{:S(2)}, u32[]{:S(2)}) %collective-permute-start.6) | collective-permute-done | bytes 131104 | tf_op jit(solution)/shard_map/ppermute | solution.py:25
  39.4 0.9 shard_map.52.rem_ref
  40.3 0.9 shard_map.53.rem_ref
  41.3 1.1 shard_map.54
  42.4 1.0 shard_map.56
  44.0 1.0 shard_map.55
  45.2 1.3 %collective-permute-start.24 = (bf16[2,128,256]{2,1,0:T(8,128)(2,1)S(1)}, bf16[2,128,256]{2,1,0:T(8,128)(2,1)S(1)}, u32[]{:S(2)}, u32[]{:S(2)}) collective-permute-start(bf16[2,128,256]{2,1,0:T(8,128)(2,1)S(1)} %slice.140), channel_id=1, source_target_pairs={{0,2},{1,5},{2,0},{3,7},{4,6},{5,1},{6,4},{7,3},{8,10},{9,13},{10,... | collective-permute-start | bytes 393224 | tf_op jit(solution)/shard_map/ppermute | solution.py:25
  46.6 0.9 collective-permute-start.17
  47.5 2.8 %collective-permute-done.24 = bf16[2,128,256]{2,1,0:T(8,128)(2,1)S(1)} collective-permute-done((bf16[2,128,256]{2,1,0:T(8,128)(2,1)S(1)}, bf16[2,128,256]{2,1,0:T(8,128)(2,1)S(1)}, u32[]{:S(2)}, u32[]{:S(2)}) %collective-permute-start.24) | collective-permute-done | bytes 131104 | tf_op jit(solution)/shard_map/ppermute | solution.py:25
  50.3 1.6 %collective-permute-start.25 = (bf16[1,128,256]{2,1,0:T(8,128)(2,1)S(1)}, bf16[1,128,256]{2,1,0:T(8,128)(2,1)S(1)}, u32[]{:S(2)}, u32[]{:S(2)}) collective-permute-start(bf16[1,128,256]{2,1,0:T(8,128)(2,1)S(1)} %slice.144), channel_id=1, source_target_pairs={{0,4},{1,3},{2,6},{3,1},{4,0},{5,7},{6,2},{7,5},{8,12},{9,11},{10,... | collective-permute-start | bytes 196616 | tf_op jit(solution)/shard_map/ppermute | solution.py:25
  51.9 1.5 %collective-permute-start.18 = (bf16[1,128,256]{2,1,0:T(8,128)(2,1)S(1)}, bf16[1,128,256]{2,1,0:T(8,128)(2,1)S(1)}, u32[]{:S(2)}, u32[]{:S(2)}) collective-permute-start(bf16[1,128,256]{2,1,0:T(8,128)(2,1)S(1)} %slice.145), channel_id=1, source_target_pairs={{0,4},{1,3},{2,6},{3,1},{4,0},{5,7},{6,2},{7,5},{8,12},{9,11},{10,... | collective-permute-start | bytes 196616 | tf_op jit(solution)/shard_map/ppermute | solution.py:25
  53.4 1.2 collective-permute-done.25
  54.6 1.2 collective-permute-start.26
  56.3 1.2 collective-permute-start.19
  57.5 1.5 %collective-permute-done.26 = bf16[1,128,256]{2,1,0:T(8,128)(2,1)S(1)} collective-permute-done((bf16[1,128,256]{2,1,0:T(8,128)(2,1)S(1)}, bf16[1,128,256]{2,1,0:T(8,128)(2,1)S(1)}, u32[]{:S(2)}, u32[]{:S(2)}) %collective-permute-start.26) | collective-permute-done | bytes 65568 | tf_op jit(solution)/shard_map/ppermute | solution.py:25
  59.0 2.2 %collective-permute-start.27 = (bf16[1,128,256]{2,1,0:T(8,128)(2,1)S(1)}, bf16[1,128,256]{2,1,0:T(8,128)(2,1)S(1)}, u32[]{:S(2)}, u32[]{:S(2)}) collective-permute-start(bf16[1,128,256]{2,1,0:T(8,128)(2,1)S(1)} %fusion.4), channel_id=1, source_target_pairs={{0,16},{1,17},{2,18},{3,19},{4,20},{5,21},{6,22},{7,23},{8,24},{9,... | collective-permute-start | bytes 196616 | tf_op jit(solution)/shard_map/ppermute | solution.py:25
  61.3 1.9 %collective-permute-start.20 = (bf16[1,128,256]{2,1,0:T(8,128)(2,1)S(1)}, bf16[1,128,256]{2,1,0:T(8,128)(2,1)S(1)}, u32[]{:S(2)}, u32[]{:S(2)}) collective-permute-start(bf16[1,128,256]{2,1,0:T(8,128)(2,1)S(1)} %fusion.3), channel_id=1, source_target_pairs={{0,16},{1,17},{2,18},{3,19},{4,20},{5,21},{6,22},{7,23},{8,24},{9,... | collective-permute-start | bytes 196616 | tf_op jit(solution)/shard_map/ppermute | solution.py:25
  63.2 2.2 %collective-permute-done.27 = bf16[1,128,256]{2,1,0:T(8,128)(2,1)S(1)} collective-permute-done((bf16[1,128,256]{2,1,0:T(8,128)(2,1)S(1)}, bf16[1,128,256]{2,1,0:T(8,128)(2,1)S(1)}, u32[]{:S(2)}, u32[]{:S(2)}) %collective-permute-start.27) | collective-permute-done | bytes 65568 | tf_op jit(solution)/shard_map/ppermute | solution.py:25
  65.4 1.4 %collective-permute-start.28 = (bf16[1,128,256]{2,1,0:T(8,128)(2,1)S(1)}, bf16[1,128,256]{2,1,0:T(8,128)(2,1)S(1)}, u32[]{:S(2)}, u32[]{:S(2)}) collective-permute-start(bf16[1,128,256]{2,1,0:T(8,128)(2,1)S(1)} %multiply_convert_fusion), channel_id=1, source_target_pairs={{0,4},{1,3},{2,6},{3,1},{4,0},{5,7},{6,2},{7,5},{8,12},{9,11},{10,... | collective-permute-start | bytes 196616 | tf_op jit(solution)/shard_map/ppermute | solution.py:25
  66.8 1.4 %collective-permute-start.21 = (bf16[1,128,256]{2,1,0:T(8,128)(2,1)S(1)}, bf16[1,128,256]{2,1,0:T(8,128)(2,1)S(1)}, u32[]{:S(2)}, u32[]{:S(2)}) collective-permute-start(bf16[1,128,256]{2,1,0:T(8,128)(2,1)S(1)} %multiply_convert_fusion.1), channel_id=1, source_target_pairs={{0,4},{1,3},{2,6},{3,1},{4,0},{5,7},{6,2},{7,5},{8,12},{9,11},{10,... | collective-permute-start | bytes 196616 | tf_op jit(solution)/shard_map/ppermute | solution.py:25
  68.3 2.2 %collective-permute-done.28 = bf16[1,128,256]{2,1,0:T(8,128)(2,1)S(1)} collective-permute-done((bf16[1,128,256]{2,1,0:T(8,128)(2,1)S(1)}, bf16[1,128,256]{2,1,0:T(8,128)(2,1)S(1)}, u32[]{:S(2)}, u32[]{:S(2)}) %collective-permute-start.28) | collective-permute-done | bytes 65568 | tf_op jit(solution)/shard_map/ppermute | solution.py:25
  70.4 1.3 %collective-permute-start.29 = (bf16[2,128,256]{2,1,0:T(8,128)(2,1)S(1)}, bf16[2,128,256]{2,1,0:T(8,128)(2,1)S(1)}, u32[]{:S(2)}, u32[]{:S(2)}) collective-permute-start(bf16[2,128,256]{2,1,0:T(8,128)(2,1)S(1)} %pad_maximum_fusion.7), channel_id=1, source_target_pairs={{0,2},{1,5},{2,0},{3,7},{4,6},{5,1},{6,4},{7,3},{8,10},{9,13},{10,... | collective-permute-start | bytes 393224 | tf_op jit(solution)/shard_map/ppermute | solution.py:25
  71.8 1.0 collective-permute-start.22
  72.7 2.8 %collective-permute-done.29 = bf16[2,128,256]{2,1,0:T(8,128)(2,1)S(1)} collective-permute-done((bf16[2,128,256]{2,1,0:T(8,128)(2,1)S(1)}, bf16[2,128,256]{2,1,0:T(8,128)(2,1)S(1)}, u32[]{:S(2)}, u32[]{:S(2)}) %collective-permute-start.29) | collective-permute-done | bytes 131104 | tf_op jit(solution)/shard_map/ppermute | solution.py:25
  75.6 1.3 %collective-permute-done.22 = bf16[2,128,256]{2,1,0:T(8,128)(2,1)S(1)} collective-permute-done((bf16[2,128,256]{2,1,0:T(8,128)(2,1)S(1)}, bf16[2,128,256]{2,1,0:T(8,128)(2,1)S(1)}, u32[]{:S(2)}, u32[]{:S(2)}) %collective-permute-start.22) | collective-permute-done | bytes 131104 | tf_op jit(solution)/shard_map/ppermute | solution.py:25
  77.0 0.9 shard_map.57.rem_ref
  77.9 0.9 shard_map.58.rem_ref
  78.9 1.8 %shard_map.59 = (f32[384,128]{1,0:T(8,128)}, bf16[384,128]{1,0:T(8,128)(2,1)S(1)}) custom-call(s32[16]{0:T(128)S(1)} %add_multiply_fusion.offset_ref, bf16[384,4096]{1,0:T(8,128)(2,1)S(1)} %copy-done, f32[384,128]{1,0:T(8,128)S(1)} %shard_map.58.rem_ref, bf16[4,128,256]{2,1,0:T(8,128)(2,1)S(1)} %collective-permute-done.30.refs_0_, ...), custom_call_target="tpu_custom_call" | custom-call | flops 201326592 | tf_op jit(solution)/shard_map/pallas_call | solution.py:76
  81.7 0.9 collective-permute-done.32
  82.6 1.3 %collective-permute-start.33 = (f32[128,128]{0,1:T(8,128)S(1)}, f32[128,128]{0,1:T(8,128)S(1)}, u32[]{:S(2)}, u32[]{:S(2)}) collective-permute-start(f32[128,128]{0,1:T(8,128)S(1)} %select_add_fusion), channel_id=1, source_target_pairs={{0,2},{1,5},{2,0},{3,7},{4,6},{5,1},{6,4},{7,3},{8,10},{9,13},{10,... | collective-permute-start | bytes 196616 | tf_op jit(solution)/shard_map/ppermute | solution.py:25
  83.9 3.0 %collective-permute-done.33 = f32[128,128]{0,1:T(8,128)S(1)} collective-permute-done((f32[128,128]{0,1:T(8,128)S(1)}, f32[128,128]{0,1:T(8,128)S(1)}, u32[]{:S(2)}, u32[]{:S(2)}) %collective-permute-start.33) | collective-permute-done | bytes 65568 | tf_op jit(solution)/shard_map/ppermute | solution.py:25
  86.9 1.3 %collective-permute-start.34 = (f32[128,128]{0,1:T(8,128)S(1)}, f32[128,128]{0,1:T(8,128)S(1)}, u32[]{:S(2)}, u32[]{:S(2)}) collective-permute-start(f32[128,128]{0,1:T(8,128)S(1)} %add.157), channel_id=1, source_target_pairs={{0,4},{1,3},{2,6},{3,1},{4,0},{5,7},{6,2},{7,5},{8,12},{9,11},{10,... | collective-permute-start | bytes 196616 | tf_op jit(solution)/shard_map/ppermute | solution.py:25
  88.3 3.0 %collective-permute-done.34 = f32[128,128]{0,1:T(8,128)S(1)} collective-permute-done((f32[128,128]{0,1:T(8,128)S(1)}, f32[128,128]{0,1:T(8,128)S(1)}, u32[]{:S(2)}, u32[]{:S(2)}) %collective-permute-start.34) | collective-permute-done | bytes 65568 | tf_op jit(solution)/shard_map/ppermute | solution.py:25
  91.3 1.0 collective-permute-start.35
  92.3 3.3 %collective-permute-done.35 = f32[128,128]{0,1:T(8,128)S(1)} collective-permute-done((f32[128,128]{0,1:T(8,128)S(1)}, f32[128,128]{0,1:T(8,128)S(1)}, u32[]{:S(2)}, u32[]{:S(2)}) %collective-permute-start.35) | collective-permute-done | bytes 65568 | tf_op jit(solution)/shard_map/ppermute | solution.py:25
  95.6 1.9 %collective-permute-start.36 = (f32[128,128]{0,1:T(8,128)S(1)}, f32[128,128]{0,1:T(8,128)S(1)}, u32[]{:S(2)}, u32[]{:S(2)}) collective-permute-start(f32[128,128]{0,1:T(8,128)S(1)} %add.159), channel_id=1, source_target_pairs={{0,16},{1,17},{2,18},{3,19},{4,20},{5,21},{6,22},{7,23},{8,24},{9,... | collective-permute-start | bytes 196616 | tf_op jit(solution)/shard_map/ppermute | solution.py:25
  97.6 4.0 %collective-permute-done.36 = f32[128,128]{0,1:T(8,128)S(1)} collective-permute-done((f32[128,128]{0,1:T(8,128)S(1)}, f32[128,128]{0,1:T(8,128)S(1)}, u32[]{:S(2)}, u32[]{:S(2)}) %collective-permute-start.36) | collective-permute-done | bytes 65568 | tf_op jit(solution)/shard_map/ppermute | solution.py:25
  101.7 1.2 collective-permute-done.37
  103.0 11.7 %cholesky.17 = f32[128,128]{1,0:T(8,128)S(1)} custom-call(f32[128,128]{1,0:T(8,128)S(1)} %fusion.8), custom_call_target="Cholesky" | custom-call | tf_op jit(solution)/shard_map/jit(cholesky)/cholesky | solution.py:152
  114.8 0.8 compare_reduce_fusion
  115.5 0.7 fusion.5
  116.2 9.8 %custom-call.7 = f32[1,128,128]{1,2,0:T(8,128)S(1)} custom-call(f32[1,128,128]{2,1,0:T(8,128)S(1)} %fusion.5), custom_call_target="InvertDiagBlocksLowerTriangular" | custom-call | tf_op jit(solution)/shard_map/jit(_solve_triangular)/triangular_solve | solution.py:154
  126.8 0.8 fusion
  (89 shorter events, 6.2 us)
Async XLA Ops:
  0.8 1.9 %copy-start = (bf16[384,4096]{1,0:T(8,128)(2,1)S(1)}, bf16[384,4096]{1,0:T(8,128)(2,1)}, u32[]{:S(2)}) copy-start(bf16[384,4096]{1,0:T(8,128)(2,1)} %basis_ref.19) | copy-start | bytes 9437188
  2.6 0.9 copy-start.1
  4.6 1.7 %collective-permute-start.7 = (bf16[4,128,256]{2,1,0:T(8,128)(2,1)S(1)}, bf16[4,128,256]{2,1,0:T(8,128)(2,1)S(1)}, u32[]{:S(2)}, u32[]{:S(2)}) collective-permute-start(bf16[4,128,256]{2,1,0:T(8,128)(2,1)S(1)} %get-tuple-element.16), channel_id=1, source_target_pairs={{0,1},{1,0},{2,3},{3,2},{4,5},{5,4},{6,7},{7,6},{8,9},{9,8},{10,11... | collective-permute-start | bytes 786440 | tf_op jit(solution)/shard_map/ppermute | solution.py:25
  5.1 4.2 %collective-permute-start = (bf16[4,128,256]{2,1,0:T(8,128)(2,1)S(1)}, bf16[4,128,256]{2,1,0:T(8,128)(2,1)S(1)}, u32[]{:S(2)}, u32[]{:S(2)}) collective-permute-start(bf16[4,128,256]{2,1,0:T(8,128)(2,1)S(1)} %get-tuple-element.14), channel_id=1, source_target_pairs={{0,1},{1,0},{2,3},{3,2},{4,5},{5,4},{6,7},{7,6},{8,9},{9,8},{10,11... | collective-permute-start | bytes 786440 | tf_op jit(solution)/shard_map/ppermute | solution.py:25
  6.3 5.9 %collective-permute-start.8 = (bf16[2,128,256]{2,1,0:T(8,128)(2,1)S(1)}, bf16[2,128,256]{2,1,0:T(8,128)(2,1)S(1)}, u32[]{:S(2)}, u32[]{:S(2)}) collective-permute-start(bf16[2,128,256]{2,1,0:T(8,128)(2,1)S(1)} %slice.142), channel_id=1, source_target_pairs={{0,2},{1,5},{2,0},{3,7},{4,6},{5,1},{6,4},{7,3},{8,10},{9,13},{10,... | collective-permute-start | bytes 393224 | tf_op jit(solution)/shard_map/ppermute | solution.py:25
  9.4 5.0 %collective-permute-start.1 = (bf16[2,128,256]{2,1,0:T(8,128)(2,1)S(1)}, bf16[2,128,256]{2,1,0:T(8,128)(2,1)S(1)}, u32[]{:S(2)}, u32[]{:S(2)}) collective-permute-start(bf16[2,128,256]{2,1,0:T(8,128)(2,1)S(1)} %slice.143), channel_id=1, source_target_pairs={{0,2},{1,5},{2,0},{3,7},{4,6},{5,1},{6,4},{7,3},{8,10},{9,13},{10,... | collective-permute-start | bytes 393224 | tf_op jit(solution)/shard_map/ppermute | solution.py:25
  12.3 4.3 %collective-permute-start.9 = (bf16[1,128,256]{2,1,0:T(8,128)(2,1)S(1)}, bf16[1,128,256]{2,1,0:T(8,128)(2,1)S(1)}, u32[]{:S(2)}, u32[]{:S(2)}) collective-permute-start(bf16[1,128,256]{2,1,0:T(8,128)(2,1)S(1)} %slice.146), channel_id=1, source_target_pairs={{0,4},{1,3},{2,6},{3,1},{4,0},{5,7},{6,2},{7,5},{8,12},{9,11},{10,... | collective-permute-start | bytes 196616 | tf_op jit(solution)/shard_map/ppermute | solution.py:25
  14.4 4.3 %collective-permute-start.2 = (bf16[1,128,256]{2,1,0:T(8,128)(2,1)S(1)}, bf16[1,128,256]{2,1,0:T(8,128)(2,1)S(1)}, u32[]{:S(2)}, u32[]{:S(2)}) collective-permute-start(bf16[1,128,256]{2,1,0:T(8,128)(2,1)S(1)} %slice.147), channel_id=1, source_target_pairs={{0,4},{1,3},{2,6},{3,1},{4,0},{5,7},{6,2},{7,5},{8,12},{9,11},{10,... | collective-permute-start | bytes 196616 | tf_op jit(solution)/shard_map/ppermute | solution.py:25
  16.6 4.4 %collective-permute-start.10 = (bf16[1,128,256]{2,1,0:T(8,128)(2,1)S(1)}, bf16[1,128,256]{2,1,0:T(8,128)(2,1)S(1)}, u32[]{:S(2)}, u32[]{:S(2)}) collective-permute-start(bf16[1,128,256]{2,1,0:T(8,128)(2,1)S(1)} %fusion.12), channel_id=1, source_target_pairs={{0,8},{1,9},{2,10},{3,11},{4,12},{5,13},{6,14},{7,15},{8,0},{9,1},... | collective-permute-start | bytes 196616 | tf_op jit(solution)/shard_map/ppermute | solution.py:25
  18.8 5.6 %collective-permute-start.3 = (bf16[1,128,256]{2,1,0:T(8,128)(2,1)S(1)}, bf16[1,128,256]{2,1,0:T(8,128)(2,1)S(1)}, u32[]{:S(2)}, u32[]{:S(2)}) collective-permute-start(bf16[1,128,256]{2,1,0:T(8,128)(2,1)S(1)} %fusion.11), channel_id=1, source_target_pairs={{0,8},{1,9},{2,10},{3,11},{4,12},{5,13},{6,14},{7,15},{8,0},{9,1},... | collective-permute-start | bytes 196616 | tf_op jit(solution)/shard_map/ppermute | solution.py:25
  21.0 6.8 %collective-permute-start.11 = (bf16[1,128,256]{2,1,0:T(8,128)(2,1)S(1)}, bf16[1,128,256]{2,1,0:T(8,128)(2,1)S(1)}, u32[]{:S(2)}, u32[]{:S(2)}) collective-permute-start(bf16[1,128,256]{2,1,0:T(8,128)(2,1)S(1)} %fusion.2), channel_id=1, source_target_pairs={{0,16},{1,17},{2,18},{3,19},{4,20},{5,21},{6,22},{7,23},{8,24},{9,... | collective-permute-start | bytes 196616 | tf_op jit(solution)/shard_map/ppermute | solution.py:25
  24.4 5.2 %collective-permute-start.4 = (bf16[1,128,256]{2,1,0:T(8,128)(2,1)S(1)}, bf16[1,128,256]{2,1,0:T(8,128)(2,1)S(1)}, u32[]{:S(2)}, u32[]{:S(2)}) collective-permute-start(bf16[1,128,256]{2,1,0:T(8,128)(2,1)S(1)} %fusion.1), channel_id=1, source_target_pairs={{0,16},{1,17},{2,18},{3,19},{4,20},{5,21},{6,22},{7,23},{8,24},{9,... | collective-permute-start | bytes 196616 | tf_op jit(solution)/shard_map/ppermute | solution.py:25
  27.9 4.9 %collective-permute-start.12 = (bf16[1,128,256]{2,1,0:T(8,128)(2,1)S(1)}, bf16[1,128,256]{2,1,0:T(8,128)(2,1)S(1)}, u32[]{:S(2)}, u32[]{:S(2)}) collective-permute-start(bf16[1,128,256]{2,1,0:T(8,128)(2,1)S(1)} %multiply_convert_fusion.2), channel_id=1, source_target_pairs={{0,4},{1,3},{2,6},{3,1},{4,0},{5,7},{6,2},{7,5},{8,12},{9,11},{10,... | collective-permute-start | bytes 196616 | tf_op jit(solution)/shard_map/ppermute | solution.py:25
  29.7 4.3 %collective-permute-start.5 = (bf16[1,128,256]{2,1,0:T(8,128)(2,1)S(1)}, bf16[1,128,256]{2,1,0:T(8,128)(2,1)S(1)}, u32[]{:S(2)}, u32[]{:S(2)}) collective-permute-start(bf16[1,128,256]{2,1,0:T(8,128)(2,1)S(1)} %multiply_convert_fusion.3), channel_id=1, source_target_pairs={{0,4},{1,3},{2,6},{3,1},{4,0},{5,7},{6,2},{7,5},{8,12},{9,11},{10,... | collective-permute-start | bytes 196616 | tf_op jit(solution)/shard_map/ppermute | solution.py:25
  32.8 5.0 %collective-permute-start.13 = (bf16[2,128,256]{2,1,0:T(8,128)(2,1)S(1)}, bf16[2,128,256]{2,1,0:T(8,128)(2,1)S(1)}, u32[]{:S(2)}, u32[]{:S(2)}) collective-permute-start(bf16[2,128,256]{2,1,0:T(8,128)(2,1)S(1)} %pad_maximum_fusion.5), channel_id=1, source_target_pairs={{0,2},{1,5},{2,0},{3,7},{4,6},{5,1},{6,4},{7,3},{8,10},{9,13},{10,... | collective-permute-start | bytes 393224 | tf_op jit(solution)/shard_map/ppermute | solution.py:25
  34.0 5.3 %collective-permute-start.6 = (bf16[2,128,256]{2,1,0:T(8,128)(2,1)S(1)}, bf16[2,128,256]{2,1,0:T(8,128)(2,1)S(1)}, u32[]{:S(2)}, u32[]{:S(2)}) collective-permute-start(bf16[2,128,256]{2,1,0:T(8,128)(2,1)S(1)} %pad_maximum_fusion.4), channel_id=1, source_target_pairs={{0,2},{1,5},{2,0},{3,7},{4,6},{5,1},{6,4},{7,3},{8,10},{9,13},{10,... | collective-permute-start | bytes 393224 | tf_op jit(solution)/shard_map/ppermute | solution.py:25
  37.9 3.3 %collective-permute-start.15 = (bf16[4,128,256]{2,1,0:T(8,128)(2,1)S(1)}, bf16[4,128,256]{2,1,0:T(8,128)(2,1)S(1)}, u32[]{:S(2)}, u32[]{:S(2)}) collective-permute-start(bf16[4,128,256]{2,1,0:T(8,128)(2,1)S(1)} %pad_maximum_fusion.1.refs_0_), channel_id=1, source_target_pairs={{0,1},{1,0},{2,3},{3,2},{4,5},{5,4},{6,7},{7,6},{8,9},{9,8},{10,11... | collective-permute-start | bytes 786440 | tf_op jit(solution)/shard_map/ppermute | solution.py:25
  39.3 2.0 %collective-permute-start.14 = (bf16[4,128,256]{2,1,0:T(8,128)(2,1)S(1)}, bf16[4,128,256]{2,1,0:T(8,128)(2,1)S(1)}, u32[]{:S(2)}, u32[]{:S(2)}) collective-permute-start(bf16[4,128,256]{2,1,0:T(8,128)(2,1)S(1)} %pad_maximum_fusion.refs_0_), channel_id=1, source_target_pairs={{0,1},{1,0},{2,3},{3,2},{4,5},{5,4},{6,7},{7,6},{8,9},{9,8},{10,11... | collective-permute-start | bytes 786440 | tf_op jit(solution)/shard_map/ppermute | solution.py:25
  43.4 1.7 %collective-permute-start.23 = (bf16[4,128,256]{2,1,0:T(8,128)(2,1)S(1)}, bf16[4,128,256]{2,1,0:T(8,128)(2,1)S(1)}, u32[]{:S(2)}, u32[]{:S(2)}) collective-permute-start(bf16[4,128,256]{2,1,0:T(8,128)(2,1)S(1)} %get-tuple-element.22), channel_id=1, source_target_pairs={{0,1},{1,0},{2,3},{3,2},{4,5},{5,4},{6,7},{7,6},{8,9},{9,8},{10,11... | collective-permute-start | bytes 786440 | tf_op jit(solution)/shard_map/ppermute | solution.py:25
  44.0 2.6 %collective-permute-start.16 = (bf16[4,128,256]{2,1,0:T(8,128)(2,1)S(1)}, bf16[4,128,256]{2,1,0:T(8,128)(2,1)S(1)}, u32[]{:S(2)}, u32[]{:S(2)}) collective-permute-start(bf16[4,128,256]{2,1,0:T(8,128)(2,1)S(1)} %get-tuple-element.20), channel_id=1, source_target_pairs={{0,1},{1,0},{2,3},{3,2},{4,5},{5,4},{6,7},{7,6},{8,9},{9,8},{10,11... | collective-permute-start | bytes 786440 | tf_op jit(solution)/shard_map/ppermute | solution.py:25
  45.2 5.0 %collective-permute-start.24 = (bf16[2,128,256]{2,1,0:T(8,128)(2,1)S(1)}, bf16[2,128,256]{2,1,0:T(8,128)(2,1)S(1)}, u32[]{:S(2)}, u32[]{:S(2)}) collective-permute-start(bf16[2,128,256]{2,1,0:T(8,128)(2,1)S(1)} %slice.140), channel_id=1, source_target_pairs={{0,2},{1,5},{2,0},{3,7},{4,6},{5,1},{6,4},{7,3},{8,10},{9,13},{10,... | collective-permute-start | bytes 393224 | tf_op jit(solution)/shard_map/ppermute | solution.py:25
  46.6 5.3 %collective-permute-start.17 = (bf16[2,128,256]{2,1,0:T(8,128)(2,1)S(1)}, bf16[2,128,256]{2,1,0:T(8,128)(2,1)S(1)}, u32[]{:S(2)}, u32[]{:S(2)}) collective-permute-start(bf16[2,128,256]{2,1,0:T(8,128)(2,1)S(1)} %slice.141), channel_id=1, source_target_pairs={{0,2},{1,5},{2,0},{3,7},{4,6},{5,1},{6,4},{7,3},{8,10},{9,13},{10,... | collective-permute-start | bytes 393224 | tf_op jit(solution)/shard_map/ppermute | solution.py:25
  50.3 4.3 %collective-permute-start.25 = (bf16[1,128,256]{2,1,0:T(8,128)(2,1)S(1)}, bf16[1,128,256]{2,1,0:T(8,128)(2,1)S(1)}, u32[]{:S(2)}, u32[]{:S(2)}) collective-permute-start(bf16[1,128,256]{2,1,0:T(8,128)(2,1)S(1)} %slice.144), channel_id=1, source_target_pairs={{0,4},{1,3},{2,6},{3,1},{4,0},{5,7},{6,2},{7,5},{8,12},{9,11},{10,... | collective-permute-start | bytes 196616 | tf_op jit(solution)/shard_map/ppermute | solution.py:25
  51.9 4.3 %collective-permute-start.18 = (bf16[1,128,256]{2,1,0:T(8,128)(2,1)S(1)}, bf16[1,128,256]{2,1,0:T(8,128)(2,1)S(1)}, u32[]{:S(2)}, u32[]{:S(2)}) collective-permute-start(bf16[1,128,256]{2,1,0:T(8,128)(2,1)S(1)} %slice.145), channel_id=1, source_target_pairs={{0,4},{1,3},{2,6},{3,1},{4,0},{5,7},{6,2},{7,5},{8,12},{9,11},{10,... | collective-permute-start | bytes 196616 | tf_op jit(solution)/shard_map/ppermute | solution.py:25
  54.6 4.3 %collective-permute-start.26 = (bf16[1,128,256]{2,1,0:T(8,128)(2,1)S(1)}, bf16[1,128,256]{2,1,0:T(8,128)(2,1)S(1)}, u32[]{:S(2)}, u32[]{:S(2)}) collective-permute-start(bf16[1,128,256]{2,1,0:T(8,128)(2,1)S(1)} %fusion.14), channel_id=1, source_target_pairs={{0,8},{1,9},{2,10},{3,11},{4,12},{5,13},{6,14},{7,15},{8,0},{9,1},... | collective-permute-start | bytes 196616 | tf_op jit(solution)/shard_map/ppermute | solution.py:25
  56.3 5.0 %collective-permute-start.19 = (bf16[1,128,256]{2,1,0:T(8,128)(2,1)S(1)}, bf16[1,128,256]{2,1,0:T(8,128)(2,1)S(1)}, u32[]{:S(2)}, u32[]{:S(2)}) collective-permute-start(bf16[1,128,256]{2,1,0:T(8,128)(2,1)S(1)} %fusion.13), channel_id=1, source_target_pairs={{0,8},{1,9},{2,10},{3,11},{4,12},{5,13},{6,14},{7,15},{8,0},{9,1},... | collective-permute-start | bytes 196616 | tf_op jit(solution)/shard_map/ppermute | solution.py:25
  59.0 6.3 %collective-permute-start.27 = (bf16[1,128,256]{2,1,0:T(8,128)(2,1)S(1)}, bf16[1,128,256]{2,1,0:T(8,128)(2,1)S(1)}, u32[]{:S(2)}, u32[]{:S(2)}) collective-permute-start(bf16[1,128,256]{2,1,0:T(8,128)(2,1)S(1)} %fusion.4), channel_id=1, source_target_pairs={{0,16},{1,17},{2,18},{3,19},{4,20},{5,21},{6,22},{7,23},{8,24},{9,... | collective-permute-start | bytes 196616 | tf_op jit(solution)/shard_map/ppermute | solution.py:25
  61.3 5.5 %collective-permute-start.20 = (bf16[1,128,256]{2,1,0:T(8,128)(2,1)S(1)}, bf16[1,128,256]{2,1,0:T(8,128)(2,1)S(1)}, u32[]{:S(2)}, u32[]{:S(2)}) collective-permute-start(bf16[1,128,256]{2,1,0:T(8,128)(2,1)S(1)} %fusion.3), channel_id=1, source_target_pairs={{0,16},{1,17},{2,18},{3,19},{4,20},{5,21},{6,22},{7,23},{8,24},{9,... | collective-permute-start | bytes 196616 | tf_op jit(solution)/shard_map/ppermute | solution.py:25
  65.4 5.0 %collective-permute-start.28 = (bf16[1,128,256]{2,1,0:T(8,128)(2,1)S(1)}, bf16[1,128,256]{2,1,0:T(8,128)(2,1)S(1)}, u32[]{:S(2)}, u32[]{:S(2)}) collective-permute-start(bf16[1,128,256]{2,1,0:T(8,128)(2,1)S(1)} %multiply_convert_fusion), channel_id=1, source_target_pairs={{0,4},{1,3},{2,6},{3,1},{4,0},{5,7},{6,2},{7,5},{8,12},{9,11},{10,... | collective-permute-start | bytes 196616 | tf_op jit(solution)/shard_map/ppermute | solution.py:25
  66.8 4.9 %collective-permute-start.21 = (bf16[1,128,256]{2,1,0:T(8,128)(2,1)S(1)}, bf16[1,128,256]{2,1,0:T(8,128)(2,1)S(1)}, u32[]{:S(2)}, u32[]{:S(2)}) collective-permute-start(bf16[1,128,256]{2,1,0:T(8,128)(2,1)S(1)} %multiply_convert_fusion.1), channel_id=1, source_target_pairs={{0,4},{1,3},{2,6},{3,1},{4,0},{5,7},{6,2},{7,5},{8,12},{9,11},{10,... | collective-permute-start | bytes 196616 | tf_op jit(solution)/shard_map/ppermute | solution.py:25
  70.4 5.0 %collective-permute-start.29 = (bf16[2,128,256]{2,1,0:T(8,128)(2,1)S(1)}, bf16[2,128,256]{2,1,0:T(8,128)(2,1)S(1)}, u32[]{:S(2)}, u32[]{:S(2)}) collective-permute-start(bf16[2,128,256]{2,1,0:T(8,128)(2,1)S(1)} %pad_maximum_fusion.7), channel_id=1, source_target_pairs={{0,2},{1,5},{2,0},{3,7},{4,6},{5,1},{6,4},{7,3},{8,10},{9,13},{10,... | collective-permute-start | bytes 393224 | tf_op jit(solution)/shard_map/ppermute | solution.py:25
  71.8 5.1 %collective-permute-start.22 = (bf16[2,128,256]{2,1,0:T(8,128)(2,1)S(1)}, bf16[2,128,256]{2,1,0:T(8,128)(2,1)S(1)}, u32[]{:S(2)}, u32[]{:S(2)}) collective-permute-start(bf16[2,128,256]{2,1,0:T(8,128)(2,1)S(1)} %pad_maximum_fusion.6), channel_id=1, source_target_pairs={{0,2},{1,5},{2,0},{3,7},{4,6},{5,1},{6,4},{7,3},{8,10},{9,13},{10,... | collective-permute-start | bytes 393224 | tf_op jit(solution)/shard_map/ppermute | solution.py:25
  75.5 3.3 %collective-permute-start.31 = (bf16[4,128,256]{2,1,0:T(8,128)(2,1)S(1)}, bf16[4,128,256]{2,1,0:T(8,128)(2,1)S(1)}, u32[]{:S(2)}, u32[]{:S(2)}) collective-permute-start(bf16[4,128,256]{2,1,0:T(8,128)(2,1)S(1)} %pad_maximum_fusion.3.refs_0_), channel_id=1, source_target_pairs={{0,1},{1,0},{2,3},{3,2},{4,5},{5,4},{6,7},{7,6},{8,9},{9,8},{10,11... | collective-permute-start | bytes 786440 | tf_op jit(solution)/shard_map/ppermute | solution.py:25
  76.9 1.9 %collective-permute-start.30 = (bf16[4,128,256]{2,1,0:T(8,128)(2,1)S(1)}, bf16[4,128,256]{2,1,0:T(8,128)(2,1)S(1)}, u32[]{:S(2)}, u32[]{:S(2)}) collective-permute-start(bf16[4,128,256]{2,1,0:T(8,128)(2,1)S(1)} %pad_maximum_fusion.2.refs_0_), channel_id=1, source_target_pairs={{0,1},{1,0},{2,3},{3,2},{4,5},{5,4},{6,7},{7,6},{8,9},{9,8},{10,11... | collective-permute-start | bytes 786440 | tf_op jit(solution)/shard_map/ppermute | solution.py:25
  77.9 3.0 %copy-start.2 = (bf16[384,128]{1,0:T(8,128)(2,1)S(1)}, bf16[384,128]{1,0:T(8,128)(2,1)}, u32[]{:S(2)}) copy-start(bf16[384,128]{1,0:T(8,128)(2,1)} %param.5) | copy-start | bytes 294916
  81.1 1.5 %collective-permute-start.32 = (f32[128,128]{0,1:T(8,128)S(1)}, f32[128,128]{0,1:T(8,128)S(1)}, u32[]{:S(2)}, u32[]{:S(2)}) collective-permute-start(f32[128,128]{0,1:T(8,128)S(1)} %get-tuple-element.24), channel_id=1, source_target_pairs={{0,1},{1,0},{2,3},{3,2},{4,5},{5,4},{6,7},{7,6},{8,9},{9,8},{10,11... | collective-permute-start | bytes 196616 | tf_op jit(solution)/shard_map/ppermute | solution.py:25
  82.6 4.3 %collective-permute-start.33 = (f32[128,128]{0,1:T(8,128)S(1)}, f32[128,128]{0,1:T(8,128)S(1)}, u32[]{:S(2)}, u32[]{:S(2)}) collective-permute-start(f32[128,128]{0,1:T(8,128)S(1)} %select_add_fusion), channel_id=1, source_target_pairs={{0,2},{1,5},{2,0},{3,7},{4,6},{5,1},{6,4},{7,3},{8,10},{9,13},{10,... | collective-permute-start | bytes 196616 | tf_op jit(solution)/shard_map/ppermute | solution.py:25
  86.9 4.3 %collective-permute-start.34 = (f32[128,128]{0,1:T(8,128)S(1)}, f32[128,128]{0,1:T(8,128)S(1)}, u32[]{:S(2)}, u32[]{:S(2)}) collective-permute-start(f32[128,128]{0,1:T(8,128)S(1)} %add.157), channel_id=1, source_target_pairs={{0,4},{1,3},{2,6},{3,1},{4,0},{5,7},{6,2},{7,5},{8,12},{9,11},{10,... | collective-permute-start | bytes 196616 | tf_op jit(solution)/shard_map/ppermute | solution.py:25
  91.3 4.3 %collective-permute-start.35 = (f32[128,128]{0,1:T(8,128)S(1)}, f32[128,128]{0,1:T(8,128)S(1)}, u32[]{:S(2)}, u32[]{:S(2)}) collective-permute-start(f32[128,128]{0,1:T(8,128)S(1)} %add.158), channel_id=1, source_target_pairs={{0,8},{1,9},{2,10},{3,11},{4,12},{5,13},{6,14},{7,15},{8,0},{9,1},... | collective-permute-start | bytes 196616 | tf_op jit(solution)/shard_map/ppermute | solution.py:25
  95.6 5.9 %collective-permute-start.36 = (f32[128,128]{0,1:T(8,128)S(1)}, f32[128,128]{0,1:T(8,128)S(1)}, u32[]{:S(2)}, u32[]{:S(2)}) collective-permute-start(f32[128,128]{0,1:T(8,128)S(1)} %add.159), channel_id=1, source_target_pairs={{0,16},{1,17},{2,18},{3,19},{4,20},{5,21},{6,22},{7,23},{8,24},{9,... | collective-permute-start | bytes 196616 | tf_op jit(solution)/shard_map/ppermute | solution.py:25
  101.6 1.3 %collective-permute-start.37 = (f32[128,128]{0,1:T(8,128)S(1)}, f32[128,128]{0,1:T(8,128)S(1)}, u32[]{:S(2)}, u32[]{:S(2)}) collective-permute-start(f32[128,128]{0,1:T(8,128)S(1)} %add.160), channel_id=1, source_target_pairs={{0,1},{1,0},{2,3},{3,2},{4,5},{5,4},{6,7},{7,6},{8,9},{9,8},{10,11... | collective-permute-start | bytes 196616 | tf_op jit(solution)/shard_map/ppermute | solution.py:25
  126.5 1.1 copy-start.3

commit v2 on v0

v2 whole, which is shorter than its diff:
```python
import functools

import jax
import jax.numpy as jnp
from jax import lax
from jax.experimental import pallas as pl
from jax.experimental.pallas import tpu as pltpu
from jax.sharding import PartitionSpec as P

BF16, F32 = jnp.bfloat16, jnp.float32
VMEM = pl.BlockSpec(memory_space=pltpu.VMEM)
HBM = pl.BlockSpec(memory_space=pltpu.HBM)
QUARTERS = 4
NT = (((1,), (1,)), ((), ()))


def swap(value, bit_of_core):
    size = lax.axis_size("rows")
    pairs = [(i, i ^ (1 << bit_of_core[i & 1])) for i in range(size)]
    return lax.ppermute(value, "rows", pairs)


def call(kernel, shapes, flops, *operands, in_specs=None, scratch=()):
    return pl.pallas_call(
        kernel,
        in_specs=in_specs or [VMEM] * len(operands),
        out_specs=[VMEM] * len(shapes),
        out_shape=[jax.ShapeDtypeStruct(*shape) for shape in shapes],
        scratch_shapes=scratch,
        compiler_params=pltpu.CompilerParams(vmem_limit_bytes=32 * 2**20),
        cost_estimate=pl.CostEstimate(flops=flops, bytes_accessed=0, transcendentals=0),
    )(*operands)


def turns(half):
    me = lax.axis_index("rows")
    low, high = (me >> 1) & 1, (me >> 2) & 1
    return jnp.where(half == 0, 2 * low + high, 2 * high + low)


def halves():
    core = lax.axis_index("rows") & 1
    return core, 1 - core


def products(chain, swapped, rem, basis_ref, out_ref):
    width = out_ref.shape[2]
    quarter = basis_ref.shape[1] // QUARTERS
    turn = turns(halves()[swapped])
    for place in range(QUARTERS):
        start = pl.multiple_of((turn ^ place) * quarter + chain * width, width)
        product = jnp.dot(rem, basis_ref[:, pl.ds(start, width)], preferred_element_type=F32)
        out_ref[place] = product.astype(out_ref.dtype)


def load_kernel(chains, swapped, basis_ref, rows_ref, *refs):
    if not swapped:
        rem_ref, *refs = refs
    product_refs, (half_ref, kept_ref, *turned_refs, sems) = refs[:chains], refs[chains:]
    columns = half_ref.shape[1]
    start = pl.multiple_of(halves()[swapped] * columns, columns)
    copy = pltpu.make_async_copy(basis_ref.at[:, pl.ds(start, columns)], half_ref, sems.at[0])
    copy.start()
    rows_copy = pltpu.make_async_copy(rows_ref, kept_ref, sems.at[1])
    rows_copy.start()
    rows_copy.wait()
    if swapped:
        rem = kept_ref[...].T
        turned_refs[0][...] = rem
    else:
        rem = rem_ref[...]
    copy.wait()
    for chain, out_ref in enumerate(product_refs):
        products(chain, swapped, rem, half_ref, out_ref)


def load_call(swapped, basis, rows, rem, chains):
    height, atoms = basis.shape
    block = rem.shape[1] if swapped else rem.shape[0]
    width = atoms // (2 * QUARTERS * chains)
    shapes = [((QUARTERS, block, width), BF16 if swapped else F32)] * chains
    shapes += [((height, atoms // 2), BF16), (rows.shape, BF16)]
    if swapped:
        shapes.append(((block, height), BF16))
    basis, rows = (pltpu.with_memory_space_constraint(v, pltpu.HBM) for v in (basis, rows))
    kernel = functools.partial(load_kernel, chains, swapped)
    operands = [basis, rows] if swapped else [basis, rows, rem]
    specs = [HBM, HBM, VMEM][: len(operands)]
    scratch = [pltpu.SemaphoreType.DMA((2,))]
    return call(kernel, shapes, basis.size * block, *operands, in_specs=specs, scratch=scratch)


def coef_kernel(chain, swapped, basis_ref, rem_ref, out_ref):
    products(chain, swapped, rem_ref[...], basis_ref, out_ref)


def coef_call(swapped, basis, rem_low, chain, chains):
    block = rem_low.shape[0]
    width = basis.shape[1] // (QUARTERS * chains)
    kernel = functools.partial(coef_kernel, chain, swapped)
    shape = ((QUARTERS, block, width), BF16 if swapped else F32)
    return call(kernel, [shape], 2 * basis.size * block // chains, basis, rem_low)[0]


def image_kernel(chain, swapped, first, basis_ref, rem_ref, coef_ref, *out_refs):
    total = rem_ref[...].astype(F32)
    count, _, width = coef_ref.shape
    quarter = basis_ref.shape[1] // QUARTERS
    turn = turns(halves()[swapped])
    for i in range(count):
        start = pl.multiple_of((turn ^ (first + i)) * quarter + chain * width, width)
        columns = basis_ref[:, pl.ds(start, width)]
        total = total - lax.dot_general(coef_ref[i], columns, NT, preferred_element_type=F32)
    for out_ref in out_refs:
        out_ref[...] = total.astype(out_ref.dtype)


def image_call(chain, swapped, basis, rem, coef, first, dtypes):
    shapes = [(rem.shape, dtype) for dtype in dtypes]
    flops = 2 * rem.size * coef.shape[0] * coef.shape[2]
    return call(functools.partial(image_kernel, chain, swapped, first), shapes, flops, basis, rem, coef)


def sweep(own_half, other_half, rem, own, other, m_total, dtypes):
    bits = (lax.axis_size("rows") - 1).bit_length()
    chains = range(len(own))
    got = [swap(v, (0, 0)) for v in other]
    own = [own[i] + got[i] for i in chains]
    got = [swap(v[2:].astype(BF16), (1, 2)) for v in own]
    own = [own[i][:2] + got[i] for i in chains]
    got = [swap(v[1:].astype(BF16), (2, 1)) for v in own]
    own = [own[i][:1] + got[i] for i in chains]
    for bit in range(3, bits):
        got = [swap(v.astype(BF16), (bit, bit)) for v in own]
        own = [own[i] + got[i] for i in chains]
    own = [(v / m_total).astype(BF16) for v in own]
    got = [swap(v, (2, 1)) for v in own]
    near = [jnp.concatenate([own[i], got[i]]) for i in chains]
    far = [swap(v, (1, 2)) for v in near]
    other = [swap(jnp.concatenate([near[i], far[i]]), (0, 0)) for i in chains]
    for first, parts in ((0, near), (2, far)):
        for i in chains:
            (rem,) = image_call(i, False, own_half, rem, parts[i], first, [F32])
    for i in chains[:-1]:
        (rem,) = image_call(i, True, other_half, rem, other[i], 0, [F32])
    return image_call(chains[-1], True, other_half, rem, other[-1], 0, dtypes)


def plain_sweep(basis, rem, rem_low, m_total):
    coef = jnp.einsum("br,rk->bk", rem_low, basis, preferred_element_type=F32)
    coef_low = (lax.psum(coef, "rows") / m_total).astype(BF16)
    image = lax.dot_general(coef_low, basis, NT, preferred_element_type=F32)
    rem = rem - lax.psum(image, "users")
    return rem, rem.astype(BF16)


def small_kernel(turned_ref, user_ref, own_ref, other_ref, rem_ref):
    turned = turned_ref[...]
    rem = turned.T
    gram = jnp.dot(turned, rem, preferred_element_type=F32)
    coupling = jnp.dot(turned, user_ref[...], preferred_element_type=F32)
    first = (lax.axis_index("rows") & 1) == 0
    own_ref[...] = jnp.where(first, gram, coupling)
    other_ref[...] = jnp.where(first, coupling, gram)
    rem_ref[...] = rem


def small_parts(turned_low, user_residuals):
    square = ((user_residuals.shape[1],) * 2, F32)
    return call(small_kernel, [square, square, (user_residuals.shape, BF16)], 0, turned_low, user_residuals)


def small_sums(own, other):
    bits = (lax.axis_size("rows") - 1).bit_length()
    own = own + swap(other, (0, 0))
    for pair in [(1, 2), (2, 1)] + [(bit, bit) for bit in range(3, bits)]:
        own = own + swap(own, pair)
    return own, swap(own, (0, 0))


def inverse_factor(gram):
    size = gram.shape[0]
    lane = lax.broadcasted_iota(jnp.int32, (8, size), 1)
    row = lax.broadcasted_iota(jnp.int32, (8, size), 0)
    panels = [gram[8 * i : 8 * i + 8] for i in range(size // 8)]
    result = []

    def across(value, index):
        return jnp.broadcast_to(value[:, index : index + 1], (8, size))

    def down(value, index):
        return jnp.broadcast_to(value[index : index + 1], (8, size))

    for k, panel in enumerate(panels):
        inside = (lane >= 8 * k) & (lane < 8 * k + 8)
        columns = [across(panel, 8 * k + c) for c in range(8)]
        full = jnp.where(inside, (lane == row + 8 * k).astype(F32), panel)
        lower, pivots = full, columns[0]
        for s in range(8):
            pivot, line = down(columns[s], s), down(full, s)
            if s:
                lower, pivots = jnp.where(row == s, line, lower), jnp.where(row == s, pivot, pivots)
            factor = jnp.where(row == s, 0.0, columns[s] * (1.0 / pivot))
            for c in range(s + 1, 8):
                columns[c] = columns[c] - factor * down(columns[c], s)
            full = full - factor * line
        full = full * (1.0 / pivots)
        result.append(jnp.where(lane <= row + 8 * k, lower * lax.rsqrt(pivots), 0.0))
        for i in range(k + 1, size // 8):
            value = jnp.where(inside, 0.0, panels[i])
            for c in range(8):
                value = value - across(panels[i], 8 * k + c) * down(full, c)
            panels[i] = value
    return jnp.concatenate(result)


def thirds(value):
    high = value.astype(BF16)
    rest = value - high.astype(F32)
    middle = rest.astype(BF16)
    return high, middle, (rest - middle.astype(F32)).astype(BF16)


def finish_kernel(m_total, own_ref, other_ref, rem_ref, user_ref, block_ref, updated_ref):
    first = (lax.axis_index("rows") & 1) == 0
    own, other = own_ref[...], other_ref[...]
    inverse = inverse_factor(jnp.where(first, own, other) * (1.0 / m_total))
    rem = rem_ref[...]
    parts = [lax.dot_general(rem, part, NT, preferred_element_type=F32) for part in thirds(inverse)]
    block = (parts[2] + parts[1] + parts[0]).astype(BF16)
    coupling = jnp.where(first, other, own) * (1.0 / m_total)
    weights = jnp.dot(inverse, coupling, precision=lax.Precision.HIGHEST, preferred_element_type=F32)
    block_ref[...] = block
    image = jnp.dot(block, weights.astype(BF16), preferred_element_type=F32)
    updated_ref[...] = (user_ref[...].astype(F32) - image).astype(BF16)


def finish(own, other, rem_low, user_residuals, m_total):
    shapes = [(v.shape, BF16) for v in (rem_low, user_residuals)]
    return tuple(call(functools.partial(finish_kernel, m_total), shapes, 0, own, other, rem_low, user_residuals))


def plain_finish(remainder_low, gram_total, coupling_total, user_residuals, m_total):
    factor_lower = jnp.linalg.cholesky(gram_total / m_total)
    identity = jnp.eye(factor_lower.shape[0], dtype=F32)
    inverse = jax.scipy.linalg.solve_triangular(factor_lower, identity, lower=True)
    new_block = jnp.dot(remainder_low.astype(F32), inverse.T, precision=lax.Precision.HIGHEST).astype(BF16)
    weights = jnp.dot(inverse, coupling_total / m_total, precision=lax.Precision.HIGHEST).astype(BF16)
    updated = user_residuals.astype(F32) - jnp.dot(new_block, weights, preferred_element_type=F32)
    return (new_block, updated.astype(BF16))


def plain_local(old_basis, new_atoms, user_residuals):
    m_total = float(old_basis.shape[0] * lax.axis_size("rows"))
    rem, rem_low = new_atoms.T.astype(F32), new_atoms.T
    for _ in range(2):
        rem, rem_low = plain_sweep(old_basis, rem, rem_low, m_total)
    gram = lax.dot_general(rem_low, rem_low, NT, preferred_element_type=F32)
    coupling = jnp.dot(rem_low, user_residuals, preferred_element_type=F32)
    gram, coupling = lax.psum((gram, coupling), "rows")
    return plain_finish(rem_low.T, gram, coupling, user_residuals, m_total)


def local(old_basis, new_atoms, user_residuals):
    rows, atoms = old_basis.shape
    block = new_atoms.shape[1]
    size = lax.axis_size("rows")
    users = lax.axis_size("users")
    m_total = float(rows * size)
    chains = 2 if atoms % (2 * 2 * QUARTERS * 128) == 0 else 1
    power = size >= 8 and size & (size - 1) == 0
    tiled = rows % 128 == 0 and atoms % (chains * 2 * QUARTERS * 128) == 0
    if not power or not tiled or block != 128 or user_residuals.shape[1] != block:
        return plain_local(old_basis, new_atoms, user_residuals)

    *other, other_half, _, rem_low = load_call(True, old_basis, new_atoms, new_atoms, chains)
    *own, own_half, user_rows = load_call(False, old_basis, user_residuals, rem_low, chains)
    rem = rem_low
    for last in (False, True):
        if last:
            other = [coef_call(True, other_half, rem_low, i, chains) for i in range(chains)]
            own = [coef_call(False, own_half, rem_low, i, chains) for i in range(chains)]
        dtypes = [BF16] if last and users == 1 else [F32, BF16]
        start = rem if users == 1 else jnp.zeros(rem.shape, F32)
        *new, rem_low = sweep(own_half, other_half, start, own, other, m_total, dtypes)
        if users == 1:
            rem = new[0] if new else rem
        else:
            rem = rem.astype(F32) + lax.psum(new[0], "users")
            rem_low = rem.astype(BF16)
    own, other, rem_low = small_parts(rem_low, user_rows)
    own, other = small_sums(own, other)
    return finish(own, other, rem_low, user_rows, m_total)


def solution(mesh):
    in_specs = (P("rows", "users"), P("rows", None), P("rows", "users"))
    out_specs = (P("rows", None), P("rows", "users"))
    return jax.shard_map(local, mesh=mesh, in_specs=in_specs, out_specs=out_specs, check_vma=False)
```

time: 451 us -> 104 us (0.23)
  waiting for transfers between devices: 394 us -> 40.3 us
  starting transfers between devices: 0.12 us -> 47 us
  other arithmetic: 24.6 us -> 0.83 us
  matrix products: 15.4 us -> 0 us
  Pallas kernels: 0 us -> 14.9 us
  between operations: 13.8 us -> 1.07 us
    psum x3 -> x0, waiting for transfers between devices: 394 us -> none  [the longest x2 270 us: coefficient_sum(): summed = lax.psum(partial_coef, 'rows')]
    ppermute x0 -> x38, starting transfers between devices: none -> 47 us  [swap(): return lax.ppermute(value, 'rows', pairs)]
    ppermute x0 -> x38, waiting for transfers between devices: none -> 40.3 us  [swap(): return lax.ppermute(value, 'rows', pairs)]
    another operation x5 -> x0, other arithmetic: 22.9 us -> none  [the longest x3 12.4 us: finish_block(): factor_lower = jnp.linalg.cholesky(gram_matrix)]
    dot_general x9 -> x0, matrix products: 15.1 us -> none  [the longest x4 7.55 us: rows_product(): jnp.einsum('rk,rb->kb', left_rows, right_rows, preferred_element_type=jnp...]
    pallas_call x0 -> x20, Pallas kernels: none -> 14.9 us  [call(): pl.pallas_call(kernel, in_specs=in_specs or [VMEM] * len(operands), out_s...]
  transfers between devices with their start and end apart: 3 -> 38, of which waited for: 3 -> 24; matrix products, arithmetic and copies ran while one was open for 0% -> 1% of each run, Pallas kernels for 0% -> 5%
where the time goes in v2:
time: 104 us
  starting transfers between devices  47 us (45%)
  waiting for transfers between devices  40.3 us (39%)
  Pallas kernels  14.9 us (14%)
  between operations  1.07 us (1%)
    ppermute x38, starting transfers between devices, swap(): return lax.ppermute(value, 'rows', pairs)  47 us
    ppermute x38, waiting for transfers between devices, swap(): return lax.ppermute(value, 'rows', pairs)  40.3 us
    pallas_call x20, Pallas kernels, call(): pl.pallas_call(kernel, in_specs=in_specs or [VMEM] * len(operands), out_s...  14.9 us
  transfers between devices with their start and end apart: 38, of which 24 were waited for; matrix products, arithmetic and copies ran while one was open for 1% of the time, Pallas kernels for 5%

profile of v2, /device:TPU:0, one launch (start us, length us, event | category | flops | bytes accessed | tf_op | source)
XLA Modules:
  0.0 104.2 jit_solution(5823794184822466741)
XLA Ops:
  0.6 2.2 %shard_map.50 = (bf16[4,128,256]{2,1,0:T(8,128)(2,1)S(1)}, bf16[4,128,256]{2,1,0:T(8,128)(2,1)S(1)}, bf16[384,2048]{1,0:T(8,128)(2,1)S(1)}, bf16[384,128]{1,0:T(8,128)(2,1)}, bf16[128,384]{1,0:T(8,128)(2,1)S(1)}) custom-call(bf16[384,4096]{1,0:T(8,128)(2,1)} %basis_ref.3, bf16[384,128]{1,0:T(8,128)(2,1)} %rows_ref.2), custom_call_target="tpu_custom_call" | custom-call | flops 201326592 | tf_op jit(solution)/shard_map/pallas_call | solution.py:24
  2.8 0.5 collective-permute-start
  3.4 1.9 %shard_map.51 = (f32[4,128,256]{2,1,0:T(8,128)S(1)}, f32[4,128,256]{2,1,0:T(8,128)S(1)}, bf16[384,2048]{1,0:T(8,128)(2,1)S(1)}, bf16[384,128]{1,0:T(8,128)(2,1)S(1)}) custom-call(bf16[384,4096]{1,0:T(8,128)(2,1)} %basis_ref.3, bf16[384,128]{1,0:T(8,128)(2,1)} %rows_ref.3, bf16[128,384]{1,0:T(8,128)(2,1)S(1)} %get-tuple-element.16.refs_0_.rem_ref), custom_call_target="tpu_custom_call" | custom-call | flops 201326592 | tf_op jit(solution)/shard_map/pallas_call | solution.py:24
  5.4 3.0 %collective-permute-start.1 = (bf16[2,128,256]{2,1,0:T(8,128)(2,1)S(1)}, bf16[2,128,256]{2,1,0:T(8,128)(2,1)S(1)}, u32[]{:S(2)}, u32[]{:S(2)}) collective-permute-start(bf16[2,128,256]{2,1,0:T(8,128)(2,1)S(1)} %slice.131), channel_id=1, source_target_pairs={{0,2},{1,5},{2,0},{3,7},{4,6},{5,1},{6,4},{7,3},{8,10},{9,13},{10,... | collective-permute-start | bytes 393224 | tf_op jit(solution)/shard_map/ppermute | solution.py:20
  8.6 2.8 %collective-permute-done.1 = bf16[2,128,256]{2,1,0:T(8,128)(2,1)S(1)} collective-permute-done((bf16[2,128,256]{2,1,0:T(8,128)(2,1)S(1)}, bf16[2,128,256]{2,1,0:T(8,128)(2,1)S(1)}, u32[]{:S(2)}, u32[]{:S(2)}) %collective-permute-start.1) | collective-permute-done | bytes 131104 | tf_op jit(solution)/shard_map/ppermute | solution.py:20
  11.4 2.1 %collective-permute-start.2 = (bf16[1,128,256]{2,1,0:T(8,128)(2,1)S(1)}, bf16[1,128,256]{2,1,0:T(8,128)(2,1)S(1)}, u32[]{:S(2)}, u32[]{:S(2)}) collective-permute-start(bf16[1,128,256]{2,1,0:T(8,128)(2,1)S(1)} %slice.135), channel_id=1, source_target_pairs={{0,4},{1,3},{2,6},{3,1},{4,0},{5,7},{6,2},{7,5},{8,12},{9,11},{10,... | collective-permute-start | bytes 196616 | tf_op jit(solution)/shard_map/ppermute | solution.py:20
  13.6 1.6 %collective-permute-start.8 = (bf16[1,128,256]{2,1,0:T(8,128)(2,1)S(1)}, bf16[1,128,256]{2,1,0:T(8,128)(2,1)S(1)}, u32[]{:S(2)}, u32[]{:S(2)}) collective-permute-start(bf16[1,128,256]{2,1,0:T(8,128)(2,1)S(1)} %slice.134), channel_id=1, source_target_pairs={{0,4},{1,3},{2,6},{3,1},{4,0},{5,7},{6,2},{7,5},{8,12},{9,11},{10,... | collective-permute-start | bytes 196616 | tf_op jit(solution)/shard_map/ppermute | solution.py:20
  15.2 0.6 collective-permute-done.2
  15.8 2.1 %collective-permute-start.3 = (bf16[1,128,256]{2,1,0:T(8,128)(2,1)S(1)}, bf16[1,128,256]{2,1,0:T(8,128)(2,1)S(1)}, u32[]{:S(2)}, u32[]{:S(2)}) collective-permute-start(bf16[1,128,256]{2,1,0:T(8,128)(2,1)S(1)} %fusion.4), channel_id=1, source_target_pairs={{0,8},{1,9},{2,10},{3,11},{4,12},{5,13},{6,14},{7,15},{8,0},{9,1},... | collective-permute-start | bytes 196616 | tf_op jit(solution)/shard_map/ppermute | solution.py:20
  17.9 1.6 %collective-permute-start.9 = (bf16[1,128,256]{2,1,0:T(8,128)(2,1)S(1)}, bf16[1,128,256]{2,1,0:T(8,128)(2,1)S(1)}, u32[]{:S(2)}, u32[]{:S(2)}) collective-permute-start(bf16[1,128,256]{2,1,0:T(8,128)(2,1)S(1)} %fusion.5), channel_id=1, source_target_pairs={{0,8},{1,9},{2,10},{3,11},{4,12},{5,13},{6,14},{7,15},{8,0},{9,1},... | collective-permute-start | bytes 196616 | tf_op jit(solution)/shard_map/ppermute | solution.py:20
  19.6 0.6 collective-permute-done.3
  20.2 3.4 %collective-permute-start.4 = (bf16[1,128,256]{2,1,0:T(8,128)(2,1)S(1)}, bf16[1,128,256]{2,1,0:T(8,128)(2,1)S(1)}, u32[]{:S(2)}, u32[]{:S(2)}) collective-permute-start(bf16[1,128,256]{2,1,0:T(8,128)(2,1)S(1)} %fusion), channel_id=1, source_target_pairs={{0,16},{1,17},{2,18},{3,19},{4,20},{5,21},{6,22},{7,23},{8,24},{9,... | collective-permute-start | bytes 196616 | tf_op jit(solution)/shard_map/ppermute | solution.py:20
  23.6 1.4 %collective-permute-start.10 = (bf16[1,128,256]{2,1,0:T(8,128)(2,1)S(1)}, bf16[1,128,256]{2,1,0:T(8,128)(2,1)S(1)}, u32[]{:S(2)}, u32[]{:S(2)}) collective-permute-start(bf16[1,128,256]{2,1,0:T(8,128)(2,1)S(1)} %fusion.1), channel_id=1, source_target_pairs={{0,16},{1,17},{2,18},{3,19},{4,20},{5,21},{6,22},{7,23},{8,24},{9,... | collective-permute-start | bytes 196616 | tf_op jit(solution)/shard_map/ppermute | solution.py:20
  24.9 1.3 %collective-permute-done.4 = bf16[1,128,256]{2,1,0:T(8,128)(2,1)S(1)} collective-permute-done((bf16[1,128,256]{2,1,0:T(8,128)(2,1)S(1)}, bf16[1,128,256]{2,1,0:T(8,128)(2,1)S(1)}, u32[]{:S(2)}, u32[]{:S(2)}) %collective-permute-start.4) | collective-permute-done | bytes 65568 | tf_op jit(solution)/shard_map/ppermute | solution.py:20
  26.3 1.6 %collective-permute-start.5 = (bf16[1,128,256]{2,1,0:T(8,128)(2,1)S(1)}, bf16[1,128,256]{2,1,0:T(8,128)(2,1)S(1)}, u32[]{:S(2)}, u32[]{:S(2)}) collective-permute-start(bf16[1,128,256]{2,1,0:T(8,128)(2,1)S(1)} %multiply_convert_fusion.3), channel_id=1, source_target_pairs={{0,4},{1,3},{2,6},{3,1},{4,0},{5,7},{6,2},{7,5},{8,12},{9,11},{10,... | collective-permute-start | bytes 196616 | tf_op jit(solution)/shard_map/ppermute | solution.py:20
  27.9 1.0 collective-permute-done.10
  28.9 1.6 %collective-permute-start.11 = (bf16[1,128,256]{2,1,0:T(8,128)(2,1)S(1)}, bf16[1,128,256]{2,1,0:T(8,128)(2,1)S(1)}, u32[]{:S(2)}, u32[]{:S(2)}) collective-permute-start(bf16[1,128,256]{2,1,0:T(8,128)(2,1)S(1)} %multiply_convert_fusion.2), channel_id=1, source_target_pairs={{0,4},{1,3},{2,6},{3,1},{4,0},{5,7},{6,2},{7,5},{8,12},{9,11},{10,... | collective-permute-start | bytes 196616 | tf_op jit(solution)/shard_map/ppermute | solution.py:20
  30.5 0.5 collective-permute-done.5
  31.0 1.6 %collective-permute-start.12 = (bf16[2,128,256]{2,1,0:T(8,128)(2,1)S(1)}, bf16[2,128,256]{2,1,0:T(8,128)(2,1)S(1)}, u32[]{:S(2)}, u32[]{:S(2)}) collective-permute-start(bf16[2,128,256]{2,1,0:T(8,128)(2,1)S(1)} %pad_maximum_fusion.4.coef_ref), channel_id=1, source_target_pairs={{0,2},{1,5},{2,0},{3,7},{4,6},{5,1},{6,4},{7,3},{8,10},{9,13},{10,... | collective-permute-start | bytes 393224 | tf_op jit(solution)/shard_map/ppermute | solution.py:20
  32.6 0.6 collective-permute-done.11
  33.2 1.6 %collective-permute-start.13 = (bf16[2,128,256]{2,1,0:T(8,128)(2,1)S(1)}, bf16[2,128,256]{2,1,0:T(8,128)(2,1)S(1)}, u32[]{:S(2)}, u32[]{:S(2)}) collective-permute-start(bf16[2,128,256]{2,1,0:T(8,128)(2,1)S(1)} %pad_maximum_fusion.5.coef_ref), channel_id=1, source_target_pairs={{0,2},{1,5},{2,0},{3,7},{4,6},{5,1},{6,4},{7,3},{8,10},{9,13},{10,... | collective-permute-start | bytes 393224 | tf_op jit(solution)/shard_map/ppermute | solution.py:20
  34.8 1.3 %collective-permute-done.12.coef_ref = bf16[2,128,256]{2,1,0:T(8,128)(2,1)S(1)} collective-permute-done((bf16[2,128,256]{2,1,0:T(8,128)(2,1)S(1)}, bf16[2,128,256]{2,1,0:T(8,128)(2,1)S(1)}, u32[]{:S(2)}, u32[]{:S(2)}) %collective-permute-start.12) | collective-permute-done | bytes 131104 | tf_op jit(solution)/shard_map/ppermute | solution.py:20
  36.1 2.1 %collective-permute-done.13.coef_ref = bf16[2,128,256]{2,1,0:T(8,128)(2,1)S(1)} collective-permute-done((bf16[2,128,256]{2,1,0:T(8,128)(2,1)S(1)}, bf16[2,128,256]{2,1,0:T(8,128)(2,1)S(1)}, u32[]{:S(2)}, u32[]{:S(2)}) %collective-permute-start.13) | collective-permute-done | bytes 131104 | tf_op jit(solution)/shard_map/ppermute | solution.py:20
  39.5 0.4 shard_map.56.rem_ref
  39.9 0.4 shard_map.57
  40.2 0.3 shard_map.59
  40.6 0.5 collective-permute-start.16
  41.1 0.3 shard_map.62
  41.5 0.3 shard_map.61
  41.8 0.3 shard_map.58
  42.4 1.6 %collective-permute-start.17 = (bf16[2,128,256]{2,1,0:T(8,128)(2,1)S(1)}, bf16[2,128,256]{2,1,0:T(8,128)(2,1)S(1)}, u32[]{:S(2)}, u32[]{:S(2)}) collective-permute-start(bf16[2,128,256]{2,1,0:T(8,128)(2,1)S(1)} %slice.129), channel_id=1, source_target_pairs={{0,2},{1,5},{2,0},{3,7},{4,6},{5,1},{6,4},{7,3},{8,10},{9,13},{10,... | collective-permute-start | bytes 393224 | tf_op jit(solution)/shard_map/ppermute | solution.py:20
  44.0 0.7 collective-permute-start.23
  44.7 2.7 %collective-permute-done.17 = bf16[2,128,256]{2,1,0:T(8,128)(2,1)S(1)} collective-permute-done((bf16[2,128,256]{2,1,0:T(8,128)(2,1)S(1)}, bf16[2,128,256]{2,1,0:T(8,128)(2,1)S(1)}, u32[]{:S(2)}, u32[]{:S(2)}) %collective-permute-start.17) | collective-permute-done | bytes 131104 | tf_op jit(solution)/shard_map/ppermute | solution.py:20
  47.4 1.6 %collective-permute-start.18 = (bf16[1,128,256]{2,1,0:T(8,128)(2,1)S(1)}, bf16[1,128,256]{2,1,0:T(8,128)(2,1)S(1)}, u32[]{:S(2)}, u32[]{:S(2)}) collective-permute-start(bf16[1,128,256]{2,1,0:T(8,128)(2,1)S(1)} %slice.133), channel_id=1, source_target_pairs={{0,4},{1,3},{2,6},{3,1},{4,0},{5,7},{6,2},{7,5},{8,12},{9,11},{10,... | collective-permute-start | bytes 196616 | tf_op jit(solution)/shard_map/ppermute | solution.py:20
  49.1 1.7 %collective-permute-start.24 = (bf16[1,128,256]{2,1,0:T(8,128)(2,1)S(1)}, bf16[1,128,256]{2,1,0:T(8,128)(2,1)S(1)}, u32[]{:S(2)}, u32[]{:S(2)}) collective-permute-start(bf16[1,128,256]{2,1,0:T(8,128)(2,1)S(1)} %slice.132), channel_id=1, source_target_pairs={{0,4},{1,3},{2,6},{3,1},{4,0},{5,7},{6,2},{7,5},{8,12},{9,11},{10,... | collective-permute-start | bytes 196616 | tf_op jit(solution)/shard_map/ppermute | solution.py:20
  50.7 1.0 collective-permute-done.18
  51.8 1.4 %collective-permute-start.19 = (bf16[1,128,256]{2,1,0:T(8,128)(2,1)S(1)}, bf16[1,128,256]{2,1,0:T(8,128)(2,1)S(1)}, u32[]{:S(2)}, u32[]{:S(2)}) collective-permute-start(bf16[1,128,256]{2,1,0:T(8,128)(2,1)S(1)} %fusion.6), channel_id=1, source_target_pairs={{0,8},{1,9},{2,10},{3,11},{4,12},{5,13},{6,14},{7,15},{8,0},{9,1},... | collective-permute-start | bytes 196616 | tf_op jit(solution)/shard_map/ppermute | solution.py:20
  53.2 0.3 collective-permute-done.24
  53.4 1.4 %collective-permute-start.25 = (bf16[1,128,256]{2,1,0:T(8,128)(2,1)S(1)}, bf16[1,128,256]{2,1,0:T(8,128)(2,1)S(1)}, u32[]{:S(2)}, u32[]{:S(2)}) collective-permute-start(bf16[1,128,256]{2,1,0:T(8,128)(2,1)S(1)} %fusion.7), channel_id=1, source_target_pairs={{0,8},{1,9},{2,10},{3,11},{4,12},{5,13},{6,14},{7,15},{8,0},{9,1},... | collective-permute-start | bytes 196616 | tf_op jit(solution)/shard_map/ppermute | solution.py:20
  54.8 1.3 %collective-permute-done.19 = bf16[1,128,256]{2,1,0:T(8,128)(2,1)S(1)} collective-permute-done((bf16[1,128,256]{2,1,0:T(8,128)(2,1)S(1)}, bf16[1,128,256]{2,1,0:T(8,128)(2,1)S(1)}, u32[]{:S(2)}, u32[]{:S(2)}) %collective-permute-start.19) | collective-permute-done | bytes 65568 | tf_op jit(solution)/shard_map/ppermute | solution.py:20
  56.2 2.5 %collective-permute-start.20 = (bf16[1,128,256]{2,1,0:T(8,128)(2,1)S(1)}, bf16[1,128,256]{2,1,0:T(8,128)(2,1)S(1)}, u32[]{:S(2)}, u32[]{:S(2)}) collective-permute-start(bf16[1,128,256]{2,1,0:T(8,128)(2,1)S(1)} %fusion.2), channel_id=1, source_target_pairs={{0,16},{1,17},{2,18},{3,19},{4,20},{5,21},{6,22},{7,23},{8,24},{9,... | collective-permute-start | bytes 196616 | tf_op jit(solution)/shard_map/ppermute | solution.py:20
  58.7 1.9 %collective-permute-start.26 = (bf16[1,128,256]{2,1,0:T(8,128)(2,1)S(1)}, bf16[1,128,256]{2,1,0:T(8,128)(2,1)S(1)}, u32[]{:S(2)}, u32[]{:S(2)}) collective-permute-start(bf16[1,128,256]{2,1,0:T(8,128)(2,1)S(1)} %fusion.3), channel_id=1, source_target_pairs={{0,16},{1,17},{2,18},{3,19},{4,20},{5,21},{6,22},{7,23},{8,24},{9,... | collective-permute-start | bytes 196616 | tf_op jit(solution)/shard_map/ppermute | solution.py:20
  60.5 2.3 %collective-permute-done.20 = bf16[1,128,256]{2,1,0:T(8,128)(2,1)S(1)} collective-permute-done((bf16[1,128,256]{2,1,0:T(8,128)(2,1)S(1)}, bf16[1,128,256]{2,1,0:T(8,128)(2,1)S(1)}, u32[]{:S(2)}, u32[]{:S(2)}) %collective-permute-start.20) | collective-permute-done | bytes 65568 | tf_op jit(solution)/shard_map/ppermute | solution.py:20
  62.8 1.5 %collective-permute-start.21 = (bf16[1,128,256]{2,1,0:T(8,128)(2,1)S(1)}, bf16[1,128,256]{2,1,0:T(8,128)(2,1)S(1)}, u32[]{:S(2)}, u32[]{:S(2)}) collective-permute-start(bf16[1,128,256]{2,1,0:T(8,128)(2,1)S(1)} %multiply_convert_fusion.1), channel_id=1, source_target_pairs={{0,4},{1,3},{2,6},{3,1},{4,0},{5,7},{6,2},{7,5},{8,12},{9,11},{10,... | collective-permute-start | bytes 196616 | tf_op jit(solution)/shard_map/ppermute | solution.py:20
  64.4 1.1 %collective-permute-start.27 = (bf16[1,128,256]{2,1,0:T(8,128)(2,1)S(1)}, bf16[1,128,256]{2,1,0:T(8,128)(2,1)S(1)}, u32[]{:S(2)}, u32[]{:S(2)}) collective-permute-start(bf16[1,128,256]{2,1,0:T(8,128)(2,1)S(1)} %multiply_convert_fusion), channel_id=1, source_target_pairs={{0,4},{1,3},{2,6},{3,1},{4,0},{5,7},{6,2},{7,5},{8,12},{9,11},{10,... | collective-permute-start | bytes 196616 | tf_op jit(solution)/shard_map/ppermute | solution.py:20
  65.5 2.3 %collective-permute-done.21 = bf16[1,128,256]{2,1,0:T(8,128)(2,1)S(1)} collective-permute-done((bf16[1,128,256]{2,1,0:T(8,128)(2,1)S(1)}, bf16[1,128,256]{2,1,0:T(8,128)(2,1)S(1)}, u32[]{:S(2)}, u32[]{:S(2)}) %collective-permute-start.21) | collective-permute-done | bytes 65568 | tf_op jit(solution)/shard_map/ppermute | solution.py:20
  67.8 1.6 %collective-permute-start.28 = (bf16[2,128,256]{2,1,0:T(8,128)(2,1)S(1)}, bf16[2,128,256]{2,1,0:T(8,128)(2,1)S(1)}, u32[]{:S(2)}, u32[]{:S(2)}) collective-permute-start(bf16[2,128,256]{2,1,0:T(8,128)(2,1)S(1)} %pad_maximum_fusion.6.coef_ref), channel_id=1, source_target_pairs={{0,2},{1,5},{2,0},{3,7},{4,6},{5,1},{6,4},{7,3},{8,10},{9,13},{10,... | collective-permute-start | bytes 393224 | tf_op jit(solution)/shard_map/ppermute | solution.py:20
  69.4 1.1 %collective-permute-start.29 = (bf16[2,128,256]{2,1,0:T(8,128)(2,1)S(1)}, bf16[2,128,256]{2,1,0:T(8,128)(2,1)S(1)}, u32[]{:S(2)}, u32[]{:S(2)}) collective-permute-start(bf16[2,128,256]{2,1,0:T(8,128)(2,1)S(1)} %pad_maximum_fusion.7.coef_ref), channel_id=1, source_target_pairs={{0,2},{1,5},{2,0},{3,7},{4,6},{5,1},{6,4},{7,3},{8,10},{9,13},{10,... | collective-permute-start | bytes 393224 | tf_op jit(solution)/shard_map/ppermute | solution.py:20
  70.5 2.4 %collective-permute-done.28.coef_ref = bf16[2,128,256]{2,1,0:T(8,128)(2,1)S(1)} collective-permute-done((bf16[2,128,256]{2,1,0:T(8,128)(2,1)S(1)}, bf16[2,128,256]{2,1,0:T(8,128)(2,1)S(1)}, u32[]{:S(2)}, u32[]{:S(2)}) %collective-permute-start.28) | collective-permute-done | bytes 131104 | tf_op jit(solution)/shard_map/ppermute | solution.py:20
  72.9 1.5 %collective-permute-done.29.coef_ref = bf16[2,128,256]{2,1,0:T(8,128)(2,1)S(1)} collective-permute-done((bf16[2,128,256]{2,1,0:T(8,128)(2,1)S(1)}, bf16[2,128,256]{2,1,0:T(8,128)(2,1)S(1)}, u32[]{:S(2)}, u32[]{:S(2)}) %collective-permute-start.29) | collective-permute-done | bytes 131104 | tf_op jit(solution)/shard_map/ppermute | solution.py:20
  75.6 0.4 shard_map.66.rem_ref
  76.0 0.4 shard_map.67.turned_ref
  76.7 0.5 collective-permute-start.32
  77.2 0.9 collective-permute-done.32
  78.1 1.4 %collective-permute-start.33 = (f32[128,128]{1,0:T(8,128)S(1)}, f32[128,128]{1,0:T(8,128)S(1)}, u32[]{:S(2)}, u32[]{:S(2)}) collective-permute-start(f32[128,128]{1,0:T(8,128)S(1)} %add.95), channel_id=1, source_target_pairs={{0,2},{1,5},{2,0},{3,7},{4,6},{5,1},{6,4},{7,3},{8,10},{9,13},{10,... | collective-permute-start | bytes 196616 | tf_op jit(solution)/shard_map/ppermute | solution.py:20
  79.5 2.9 %collective-permute-done.33 = f32[128,128]{1,0:T(8,128)S(1)} collective-permute-done((f32[128,128]{1,0:T(8,128)S(1)}, f32[128,128]{1,0:T(8,128)S(1)}, u32[]{:S(2)}, u32[]{:S(2)}) %collective-permute-start.33) | collective-permute-done | bytes 65568 | tf_op jit(solution)/shard_map/ppermute | solution.py:20
  82.5 1.4 %collective-permute-start.34 = (f32[128,128]{1,0:T(8,128)S(1)}, f32[128,128]{1,0:T(8,128)S(1)}, u32[]{:S(2)}, u32[]{:S(2)}) collective-permute-start(f32[128,128]{1,0:T(8,128)S(1)} %add.96), channel_id=1, source_target_pairs={{0,4},{1,3},{2,6},{3,1},{4,0},{5,7},{6,2},{7,5},{8,12},{9,11},{10,... | collective-permute-start | bytes 196616 | tf_op jit(solution)/shard_map/ppermute | solution.py:20
  83.9 2.9 %collective-permute-done.34 = f32[128,128]{1,0:T(8,128)S(1)} collective-permute-done((f32[128,128]{1,0:T(8,128)S(1)}, f32[128,128]{1,0:T(8,128)S(1)}, u32[]{:S(2)}, u32[]{:S(2)}) %collective-permute-start.34) | collective-permute-done | bytes 65568 | tf_op jit(solution)/shard_map/ppermute | solution.py:20
  86.8 0.8 collective-permute-start.35
  87.7 3.5 %collective-permute-done.35 = f32[128,128]{1,0:T(8,128)S(1)} collective-permute-done((f32[128,128]{1,0:T(8,128)S(1)}, f32[128,128]{1,0:T(8,128)S(1)}, u32[]{:S(2)}, u32[]{:S(2)}) %collective-permute-start.35) | collective-permute-done | bytes 65568 | tf_op jit(solution)/shard_map/ppermute | solution.py:20
  91.2 1.9 %collective-permute-start.36 = (f32[128,128]{1,0:T(8,128)S(1)}, f32[128,128]{1,0:T(8,128)S(1)}, u32[]{:S(2)}, u32[]{:S(2)}) collective-permute-start(f32[128,128]{1,0:T(8,128)S(1)} %add.98), channel_id=1, source_target_pairs={{0,16},{1,17},{2,18},{3,19},{4,20},{5,21},{6,22},{7,23},{8,24},{9,... | collective-permute-start | bytes 196616 | tf_op jit(solution)/shard_map/ppermute | solution.py:20
  93.0 4.1 %collective-permute-done.36 = f32[128,128]{1,0:T(8,128)S(1)} collective-permute-done((f32[128,128]{1,0:T(8,128)S(1)}, f32[128,128]{1,0:T(8,128)S(1)}, u32[]{:S(2)}, u32[]{:S(2)}) %collective-permute-start.36) | collective-permute-done | bytes 65568 | tf_op jit(solution)/shard_map/ppermute | solution.py:20
  97.2 1.2 %collective-permute-done.37.other_ref = f32[128,128]{1,0:T(8,128)S(1)} collective-permute-done((f32[128,128]{1,0:T(8,128)S(1)}, f32[128,128]{1,0:T(8,128)S(1)}, u32[]{:S(2)}, u32[]{:S(2)}) %collective-permute-start.37) | collective-permute-done | bytes 65568 | tf_op jit(solution)/shard_map/ppermute | solution.py:20
  98.4 5.7 %shard_map.69 = (bf16[384,128]{1,0:T(8,128)(2,1)}, bf16[384,128]{1,0:T(8,128)(2,1)}) custom-call(f32[128,128]{1,0:T(8,128)S(1)} %add.99.own_ref, f32[128,128]{1,0:T(8,128)S(1)} %collective-permute-done.37.other_ref, bf16[384,128]{1,0:T(8,128)(2,1)S(1)} %get-tuple-element.27.rem_ref, bf16[384,128]{1,0:T(8,128)(2,1)S(1)} %get-tuple-element.24.user_ref), custom_call_target="tpu_custom_call" | custom-call | tf_op jit(solution)/shard_map/pallas_call | solution.py:24
  (73 shorter events, 4.2 us)
Async XLA Ops:
  2.8 2.5 %collective-permute-start = (bf16[4,128,256]{2,1,0:T(8,128)(2,1)S(1)}, bf16[4,128,256]{2,1,0:T(8,128)(2,1)S(1)}, u32[]{:S(2)}, u32[]{:S(2)}) collective-permute-start(bf16[4,128,256]{2,1,0:T(8,128)(2,1)S(1)} %get-tuple-element.19), channel_id=1, source_target_pairs={{0,1},{1,0},{2,3},{3,2},{4,5},{5,4},{6,7},{7,6},{8,9},{9,8},{10,11... | collective-permute-start | bytes 786440 | tf_op jit(solution)/shard_map/ppermute | solution.py:20
  3.4 5.0 %collective-permute-start.6 = (bf16[4,128,256]{2,1,0:T(8,128)(2,1)S(1)}, bf16[4,128,256]{2,1,0:T(8,128)(2,1)S(1)}, u32[]{:S(2)}, u32[]{:S(2)}) collective-permute-start(bf16[4,128,256]{2,1,0:T(8,128)(2,1)S(1)} %get-tuple-element.21), channel_id=1, source_target_pairs={{0,1},{1,0},{2,3},{3,2},{4,5},{5,4},{6,7},{7,6},{8,9},{9,8},{10,11... | collective-permute-start | bytes 786440 | tf_op jit(solution)/shard_map/ppermute | solution.py:20
  5.4 5.9 %collective-permute-start.1 = (bf16[2,128,256]{2,1,0:T(8,128)(2,1)S(1)}, bf16[2,128,256]{2,1,0:T(8,128)(2,1)S(1)}, u32[]{:S(2)}, u32[]{:S(2)}) collective-permute-start(bf16[2,128,256]{2,1,0:T(8,128)(2,1)S(1)} %slice.131), channel_id=1, source_target_pairs={{0,2},{1,5},{2,0},{3,7},{4,6},{5,1},{6,4},{7,3},{8,10},{9,13},{10,... | collective-permute-start | bytes 393224 | tf_op jit(solution)/shard_map/ppermute | solution.py:20
  8.5 5.0 %collective-permute-start.7 = (bf16[2,128,256]{2,1,0:T(8,128)(2,1)S(1)}, bf16[2,128,256]{2,1,0:T(8,128)(2,1)S(1)}, u32[]{:S(2)}, u32[]{:S(2)}) collective-permute-start(bf16[2,128,256]{2,1,0:T(8,128)(2,1)S(1)} %slice.130), channel_id=1, source_target_pairs={{0,2},{1,5},{2,0},{3,7},{4,6},{5,1},{6,4},{7,3},{8,10},{9,13},{10,... | collective-permute-start | bytes 393224 | tf_op jit(solution)/shard_map/ppermute | solution.py:20
  11.4 4.4 %collective-permute-start.2 = (bf16[1,128,256]{2,1,0:T(8,128)(2,1)S(1)}, bf16[1,128,256]{2,1,0:T(8,128)(2,1)S(1)}, u32[]{:S(2)}, u32[]{:S(2)}) collective-permute-start(bf16[1,128,256]{2,1,0:T(8,128)(2,1)S(1)} %slice.135), channel_id=1, source_target_pairs={{0,4},{1,3},{2,6},{3,1},{4,0},{5,7},{6,2},{7,5},{8,12},{9,11},{10,... | collective-permute-start | bytes 196616 | tf_op jit(solution)/shard_map/ppermute | solution.py:20
  13.6 4.4 %collective-permute-start.8 = (bf16[1,128,256]{2,1,0:T(8,128)(2,1)S(1)}, bf16[1,128,256]{2,1,0:T(8,128)(2,1)S(1)}, u32[]{:S(2)}, u32[]{:S(2)}) collective-permute-start(bf16[1,128,256]{2,1,0:T(8,128)(2,1)S(1)} %slice.134), channel_id=1, source_target_pairs={{0,4},{1,3},{2,6},{3,1},{4,0},{5,7},{6,2},{7,5},{8,12},{9,11},{10,... | collective-permute-start | bytes 196616 | tf_op jit(solution)/shard_map/ppermute | solution.py:20
  15.8 4.4 %collective-permute-start.3 = (bf16[1,128,256]{2,1,0:T(8,128)(2,1)S(1)}, bf16[1,128,256]{2,1,0:T(8,128)(2,1)S(1)}, u32[]{:S(2)}, u32[]{:S(2)}) collective-permute-start(bf16[1,128,256]{2,1,0:T(8,128)(2,1)S(1)} %fusion.4), channel_id=1, source_target_pairs={{0,8},{1,9},{2,10},{3,11},{4,12},{5,13},{6,14},{7,15},{8,0},{9,1},... | collective-permute-start | bytes 196616 | tf_op jit(solution)/shard_map/ppermute | solution.py:20
  17.9 5.6 %collective-permute-start.9 = (bf16[1,128,256]{2,1,0:T(8,128)(2,1)S(1)}, bf16[1,128,256]{2,1,0:T(8,128)(2,1)S(1)}, u32[]{:S(2)}, u32[]{:S(2)}) collective-permute-start(bf16[1,128,256]{2,1,0:T(8,128)(2,1)S(1)} %fusion.5), channel_id=1, source_target_pairs={{0,8},{1,9},{2,10},{3,11},{4,12},{5,13},{6,14},{7,15},{8,0},{9,1},... | collective-permute-start | bytes 196616 | tf_op jit(solution)/shard_map/ppermute | solution.py:20
  20.2 6.0 %collective-permute-start.4 = (bf16[1,128,256]{2,1,0:T(8,128)(2,1)S(1)}, bf16[1,128,256]{2,1,0:T(8,128)(2,1)S(1)}, u32[]{:S(2)}, u32[]{:S(2)}) collective-permute-start(bf16[1,128,256]{2,1,0:T(8,128)(2,1)S(1)} %fusion), channel_id=1, source_target_pairs={{0,16},{1,17},{2,18},{3,19},{4,20},{5,21},{6,22},{7,23},{8,24},{9,... | collective-permute-start | bytes 196616 | tf_op jit(solution)/shard_map/ppermute | solution.py:20
  23.6 5.2 %collective-permute-start.10 = (bf16[1,128,256]{2,1,0:T(8,128)(2,1)S(1)}, bf16[1,128,256]{2,1,0:T(8,128)(2,1)S(1)}, u32[]{:S(2)}, u32[]{:S(2)}) collective-permute-start(bf16[1,128,256]{2,1,0:T(8,128)(2,1)S(1)} %fusion.1), channel_id=1, source_target_pairs={{0,16},{1,17},{2,18},{3,19},{4,20},{5,21},{6,22},{7,23},{8,24},{9,... | collective-permute-start | bytes 196616 | tf_op jit(solution)/shard_map/ppermute | solution.py:20
  26.3 4.7 %collective-permute-start.5 = (bf16[1,128,256]{2,1,0:T(8,128)(2,1)S(1)}, bf16[1,128,256]{2,1,0:T(8,128)(2,1)S(1)}, u32[]{:S(2)}, u32[]{:S(2)}) collective-permute-start(bf16[1,128,256]{2,1,0:T(8,128)(2,1)S(1)} %multiply_convert_fusion.3), channel_id=1, source_target_pairs={{0,4},{1,3},{2,6},{3,1},{4,0},{5,7},{6,2},{7,5},{8,12},{9,11},{10,... | collective-permute-start | bytes 196616 | tf_op jit(solution)/shard_map/ppermute | solution.py:20
  28.9 4.3 %collective-permute-start.11 = (bf16[1,128,256]{2,1,0:T(8,128)(2,1)S(1)}, bf16[1,128,256]{2,1,0:T(8,128)(2,1)S(1)}, u32[]{:S(2)}, u32[]{:S(2)}) collective-permute-start(bf16[1,128,256]{2,1,0:T(8,128)(2,1)S(1)} %multiply_convert_fusion.2), channel_id=1, source_target_pairs={{0,4},{1,3},{2,6},{3,1},{4,0},{5,7},{6,2},{7,5},{8,12},{9,11},{10,... | collective-permute-start | bytes 196616 | tf_op jit(solution)/shard_map/ppermute | solution.py:20
  31.0 5.0 %collective-permute-start.12 = (bf16[2,128,256]{2,1,0:T(8,128)(2,1)S(1)}, bf16[2,128,256]{2,1,0:T(8,128)(2,1)S(1)}, u32[]{:S(2)}, u32[]{:S(2)}) collective-permute-start(bf16[2,128,256]{2,1,0:T(8,128)(2,1)S(1)} %pad_maximum_fusion.4.coef_ref), channel_id=1, source_target_pairs={{0,2},{1,5},{2,0},{3,7},{4,6},{5,1},{6,4},{7,3},{8,10},{9,13},{10,... | collective-permute-start | bytes 393224 | tf_op jit(solution)/shard_map/ppermute | solution.py:20
  33.2 5.0 %collective-permute-start.13 = (bf16[2,128,256]{2,1,0:T(8,128)(2,1)S(1)}, bf16[2,128,256]{2,1,0:T(8,128)(2,1)S(1)}, u32[]{:S(2)}, u32[]{:S(2)}) collective-permute-start(bf16[2,128,256]{2,1,0:T(8,128)(2,1)S(1)} %pad_maximum_fusion.5.coef_ref), channel_id=1, source_target_pairs={{0,2},{1,5},{2,0},{3,7},{4,6},{5,1},{6,4},{7,3},{8,10},{9,13},{10,... | collective-permute-start | bytes 393224 | tf_op jit(solution)/shard_map/ppermute | solution.py:20
  36.1 3.4 %collective-permute-start.14 = (bf16[4,128,256]{2,1,0:T(8,128)(2,1)S(1)}, bf16[4,128,256]{2,1,0:T(8,128)(2,1)S(1)}, u32[]{:S(2)}, u32[]{:S(2)}) collective-permute-start(bf16[4,128,256]{2,1,0:T(8,128)(2,1)S(1)} %pad_maximum_fusion), channel_id=1, source_target_pairs={{0,1},{1,0},{2,3},{3,2},{4,5},{5,4},{6,7},{7,6},{8,9},{9,8},{10,11... | collective-permute-start | bytes 786440 | tf_op jit(solution)/shard_map/ppermute | solution.py:20
  38.3 1.6 %collective-permute-start.15 = (bf16[4,128,256]{2,1,0:T(8,128)(2,1)S(1)}, bf16[4,128,256]{2,1,0:T(8,128)(2,1)S(1)}, u32[]{:S(2)}, u32[]{:S(2)}) collective-permute-start(bf16[4,128,256]{2,1,0:T(8,128)(2,1)S(1)} %pad_maximum_fusion.1), channel_id=1, source_target_pairs={{0,1},{1,0},{2,3},{3,2},{4,5},{5,4},{6,7},{7,6},{8,9},{9,8},{10,11... | collective-permute-start | bytes 786440 | tf_op jit(solution)/shard_map/ppermute | solution.py:20
  40.6 1.7 %collective-permute-start.16 = (bf16[4,128,256]{2,1,0:T(8,128)(2,1)S(1)}, bf16[4,128,256]{2,1,0:T(8,128)(2,1)S(1)}, u32[]{:S(2)}, u32[]{:S(2)}) collective-permute-start(bf16[4,128,256]{2,1,0:T(8,128)(2,1)S(1)} %shard_map.59), channel_id=1, source_target_pairs={{0,1},{1,0},{2,3},{3,2},{4,5},{5,4},{6,7},{7,6},{8,9},{9,8},{10,11... | collective-permute-start | bytes 786440 | tf_op jit(solution)/shard_map/ppermute | solution.py:20
  41.4 2.5 %collective-permute-start.22 = (bf16[4,128,256]{2,1,0:T(8,128)(2,1)S(1)}, bf16[4,128,256]{2,1,0:T(8,128)(2,1)S(1)}, u32[]{:S(2)}, u32[]{:S(2)}) collective-permute-start(bf16[4,128,256]{2,1,0:T(8,128)(2,1)S(1)} %shard_map.62), channel_id=1, source_target_pairs={{0,1},{1,0},{2,3},{3,2},{4,5},{5,4},{6,7},{7,6},{8,9},{9,8},{10,11... | collective-permute-start | bytes 786440 | tf_op jit(solution)/shard_map/ppermute | solution.py:20
  42.4 5.0 %collective-permute-start.17 = (bf16[2,128,256]{2,1,0:T(8,128)(2,1)S(1)}, bf16[2,128,256]{2,1,0:T(8,128)(2,1)S(1)}, u32[]{:S(2)}, u32[]{:S(2)}) collective-permute-start(bf16[2,128,256]{2,1,0:T(8,128)(2,1)S(1)} %slice.129), channel_id=1, source_target_pairs={{0,2},{1,5},{2,0},{3,7},{4,6},{5,1},{6,4},{7,3},{8,10},{9,13},{10,... | collective-permute-start | bytes 393224 | tf_op jit(solution)/shard_map/ppermute | solution.py:20
  44.0 5.0 %collective-permute-start.23 = (bf16[2,128,256]{2,1,0:T(8,128)(2,1)S(1)}, bf16[2,128,256]{2,1,0:T(8,128)(2,1)S(1)}, u32[]{:S(2)}, u32[]{:S(2)}) collective-permute-start(bf16[2,128,256]{2,1,0:T(8,128)(2,1)S(1)} %slice.128), channel_id=1, source_target_pairs={{0,2},{1,5},{2,0},{3,7},{4,6},{5,1},{6,4},{7,3},{8,10},{9,13},{10,... | collective-permute-start | bytes 393224 | tf_op jit(solution)/shard_map/ppermute | solution.py:20
  47.4 4.3 %collective-permute-start.18 = (bf16[1,128,256]{2,1,0:T(8,128)(2,1)S(1)}, bf16[1,128,256]{2,1,0:T(8,128)(2,1)S(1)}, u32[]{:S(2)}, u32[]{:S(2)}) collective-permute-start(bf16[1,128,256]{2,1,0:T(8,128)(2,1)S(1)} %slice.133), channel_id=1, source_target_pairs={{0,4},{1,3},{2,6},{3,1},{4,0},{5,7},{6,2},{7,5},{8,12},{9,11},{10,... | collective-permute-start | bytes 196616 | tf_op jit(solution)/shard_map/ppermute | solution.py:20
  49.1 4.3 %collective-permute-start.24 = (bf16[1,128,256]{2,1,0:T(8,128)(2,1)S(1)}, bf16[1,128,256]{2,1,0:T(8,128)(2,1)S(1)}, u32[]{:S(2)}, u32[]{:S(2)}) collective-permute-start(bf16[1,128,256]{2,1,0:T(8,128)(2,1)S(1)} %slice.132), channel_id=1, source_target_pairs={{0,4},{1,3},{2,6},{3,1},{4,0},{5,7},{6,2},{7,5},{8,12},{9,11},{10,... | collective-permute-start | bytes 196616 | tf_op jit(solution)/shard_map/ppermute | solution.py:20
  51.8 4.3 %collective-permute-start.19 = (bf16[1,128,256]{2,1,0:T(8,128)(2,1)S(1)}, bf16[1,128,256]{2,1,0:T(8,128)(2,1)S(1)}, u32[]{:S(2)}, u32[]{:S(2)}) collective-permute-start(bf16[1,128,256]{2,1,0:T(8,128)(2,1)S(1)} %fusion.6), channel_id=1, source_target_pairs={{0,8},{1,9},{2,10},{3,11},{4,12},{5,13},{6,14},{7,15},{8,0},{9,1},... | collective-permute-start | bytes 196616 | tf_op jit(solution)/shard_map/ppermute | solution.py:20
  53.4 5.2 %collective-permute-start.25 = (bf16[1,128,256]{2,1,0:T(8,128)(2,1)S(1)}, bf16[1,128,256]{2,1,0:T(8,128)(2,1)S(1)}, u32[]{:S(2)}, u32[]{:S(2)}) collective-permute-start(bf16[1,128,256]{2,1,0:T(8,128)(2,1)S(1)} %fusion.7), channel_id=1, source_target_pairs={{0,8},{1,9},{2,10},{3,11},{4,12},{5,13},{6,14},{7,15},{8,0},{9,1},... | collective-permute-start | bytes 196616 | tf_op jit(solution)/shard_map/ppermute | solution.py:20
  56.2 6.6 %collective-permute-start.20 = (bf16[1,128,256]{2,1,0:T(8,128)(2,1)S(1)}, bf16[1,128,256]{2,1,0:T(8,128)(2,1)S(1)}, u32[]{:S(2)}, u32[]{:S(2)}) collective-permute-start(bf16[1,128,256]{2,1,0:T(8,128)(2,1)S(1)} %fusion.2), channel_id=1, source_target_pairs={{0,16},{1,17},{2,18},{3,19},{4,20},{5,21},{6,22},{7,23},{8,24},{9,... | collective-permute-start | bytes 196616 | tf_op jit(solution)/shard_map/ppermute | solution.py:20
  58.7 5.7 %collective-permute-start.26 = (bf16[1,128,256]{2,1,0:T(8,128)(2,1)S(1)}, bf16[1,128,256]{2,1,0:T(8,128)(2,1)S(1)}, u32[]{:S(2)}, u32[]{:S(2)}) collective-permute-start(bf16[1,128,256]{2,1,0:T(8,128)(2,1)S(1)} %fusion.3), channel_id=1, source_target_pairs={{0,16},{1,17},{2,18},{3,19},{4,20},{5,21},{6,22},{7,23},{8,24},{9,... | collective-permute-start | bytes 196616 | tf_op jit(solution)/shard_map/ppermute | solution.py:20
  62.8 4.9 %collective-permute-start.21 = (bf16[1,128,256]{2,1,0:T(8,128)(2,1)S(1)}, bf16[1,128,256]{2,1,0:T(8,128)(2,1)S(1)}, u32[]{:S(2)}, u32[]{:S(2)}) collective-permute-start(bf16[1,128,256]{2,1,0:T(8,128)(2,1)S(1)} %multiply_convert_fusion.1), channel_id=1, source_target_pairs={{0,4},{1,3},{2,6},{3,1},{4,0},{5,7},{6,2},{7,5},{8,12},{9,11},{10,... | collective-permute-start | bytes 196616 | tf_op jit(solution)/shard_map/ppermute | solution.py:20
  64.4 5.0 %collective-permute-start.27 = (bf16[1,128,256]{2,1,0:T(8,128)(2,1)S(1)}, bf16[1,128,256]{2,1,0:T(8,128)(2,1)S(1)}, u32[]{:S(2)}, u32[]{:S(2)}) collective-permute-start(bf16[1,128,256]{2,1,0:T(8,128)(2,1)S(1)} %multiply_convert_fusion), channel_id=1, source_target_pairs={{0,4},{1,3},{2,6},{3,1},{4,0},{5,7},{6,2},{7,5},{8,12},{9,11},{10,... | collective-permute-start | bytes 196616 | tf_op jit(solution)/shard_map/ppermute | solution.py:20
  67.8 5.0 %collective-permute-start.28 = (bf16[2,128,256]{2,1,0:T(8,128)(2,1)S(1)}, bf16[2,128,256]{2,1,0:T(8,128)(2,1)S(1)}, u32[]{:S(2)}, u32[]{:S(2)}) collective-permute-start(bf16[2,128,256]{2,1,0:T(8,128)(2,1)S(1)} %pad_maximum_fusion.6.coef_ref), channel_id=1, source_target_pairs={{0,2},{1,5},{2,0},{3,7},{4,6},{5,1},{6,4},{7,3},{8,10},{9,13},{10,... | collective-permute-start | bytes 393224 | tf_op jit(solution)/shard_map/ppermute | solution.py:20
  69.4 5.0 %collective-permute-start.29 = (bf16[2,128,256]{2,1,0:T(8,128)(2,1)S(1)}, bf16[2,128,256]{2,1,0:T(8,128)(2,1)S(1)}, u32[]{:S(2)}, u32[]{:S(2)}) collective-permute-start(bf16[2,128,256]{2,1,0:T(8,128)(2,1)S(1)} %pad_maximum_fusion.7.coef_ref), channel_id=1, source_target_pairs={{0,2},{1,5},{2,0},{3,7},{4,6},{5,1},{6,4},{7,3},{8,10},{9,13},{10,... | collective-permute-start | bytes 393224 | tf_op jit(solution)/shard_map/ppermute | solution.py:20
  72.8 2.8 %collective-permute-start.30 = (bf16[4,128,256]{2,1,0:T(8,128)(2,1)S(1)}, bf16[4,128,256]{2,1,0:T(8,128)(2,1)S(1)}, u32[]{:S(2)}, u32[]{:S(2)}) collective-permute-start(bf16[4,128,256]{2,1,0:T(8,128)(2,1)S(1)} %pad_maximum_fusion.2), channel_id=1, source_target_pairs={{0,1},{1,0},{2,3},{3,2},{4,5},{5,4},{6,7},{7,6},{8,9},{9,8},{10,11... | collective-permute-start | bytes 786440 | tf_op jit(solution)/shard_map/ppermute | solution.py:20
  74.4 1.6 %collective-permute-start.31 = (bf16[4,128,256]{2,1,0:T(8,128)(2,1)S(1)}, bf16[4,128,256]{2,1,0:T(8,128)(2,1)S(1)}, u32[]{:S(2)}, u32[]{:S(2)}) collective-permute-start(bf16[4,128,256]{2,1,0:T(8,128)(2,1)S(1)} %pad_maximum_fusion.3), channel_id=1, source_target_pairs={{0,1},{1,0},{2,3},{3,2},{4,5},{5,4},{6,7},{7,6},{8,9},{9,8},{10,11... | collective-permute-start | bytes 786440 | tf_op jit(solution)/shard_map/ppermute | solution.py:20
  76.7 1.4 %collective-permute-start.32 = (f32[128,128]{1,0:T(8,128)S(1)}, f32[128,128]{1,0:T(8,128)S(1)}, u32[]{:S(2)}, u32[]{:S(2)}) collective-permute-start(f32[128,128]{1,0:T(8,128)S(1)} %get-tuple-element.26), channel_id=1, source_target_pairs={{0,1},{1,0},{2,3},{3,2},{4,5},{5,4},{6,7},{7,6},{8,9},{9,8},{10,11... | collective-permute-start | bytes 196616 | tf_op jit(solution)/shard_map/ppermute | solution.py:20
  78.1 4.3 %collective-permute-start.33 = (f32[128,128]{1,0:T(8,128)S(1)}, f32[128,128]{1,0:T(8,128)S(1)}, u32[]{:S(2)}, u32[]{:S(2)}) collective-permute-start(f32[128,128]{1,0:T(8,128)S(1)} %add.95), channel_id=1, source_target_pairs={{0,2},{1,5},{2,0},{3,7},{4,6},{5,1},{6,4},{7,3},{8,10},{9,13},{10,... | collective-permute-start | bytes 196616 | tf_op jit(solution)/shard_map/ppermute | solution.py:20
  82.5 4.3 %collective-permute-start.34 = (f32[128,128]{1,0:T(8,128)S(1)}, f32[128,128]{1,0:T(8,128)S(1)}, u32[]{:S(2)}, u32[]{:S(2)}) collective-permute-start(f32[128,128]{1,0:T(8,128)S(1)} %add.96), channel_id=1, source_target_pairs={{0,4},{1,3},{2,6},{3,1},{4,0},{5,7},{6,2},{7,5},{8,12},{9,11},{10,... | collective-permute-start | bytes 196616 | tf_op jit(solution)/shard_map/ppermute | solution.py:20
  86.8 4.3 %collective-permute-start.35 = (f32[128,128]{1,0:T(8,128)S(1)}, f32[128,128]{1,0:T(8,128)S(1)}, u32[]{:S(2)}, u32[]{:S(2)}) collective-permute-start(f32[128,128]{1,0:T(8,128)S(1)} %add.97), channel_id=1, source_target_pairs={{0,8},{1,9},{2,10},{3,11},{4,12},{5,13},{6,14},{7,15},{8,0},{9,1},... | collective-permute-start | bytes 196616 | tf_op jit(solution)/shard_map/ppermute | solution.py:20
  91.2 5.9 %collective-permute-start.36 = (f32[128,128]{1,0:T(8,128)S(1)}, f32[128,128]{1,0:T(8,128)S(1)}, u32[]{:S(2)}, u32[]{:S(2)}) collective-permute-start(f32[128,128]{1,0:T(8,128)S(1)} %add.98), channel_id=1, source_target_pairs={{0,16},{1,17},{2,18},{3,19},{4,20},{5,21},{6,22},{7,23},{8,24},{9,... | collective-permute-start | bytes 196616 | tf_op jit(solution)/shard_map/ppermute | solution.py:20
  97.1 1.3 %collective-permute-start.37 = (f32[128,128]{1,0:T(8,128)S(1)}, f32[128,128]{1,0:T(8,128)S(1)}, u32[]{:S(2)}, u32[]{:S(2)}) collective-permute-start(f32[128,128]{1,0:T(8,128)S(1)} %add.99.own_ref), channel_id=1, source_target_pairs={{0,1},{1,0},{2,3},{3,2},{4,5},{5,4},{6,7},{7,6},{8,9},{9,8},{10,11... | collective-permute-start | bytes 196616 | tf_op jit(solution)/shard_map/ppermute | solution.py:20

commit v3 on v2

v3 whole, which is shorter than its diff:
```python
import functools

import jax
import jax.numpy as jnp
from jax import lax
from jax.experimental import pallas as pl
from jax.experimental.pallas import tpu as pltpu
from jax.sharding import PartitionSpec as P

BF16, F32 = jnp.bfloat16, jnp.float32
VMEM = pl.BlockSpec(memory_space=pltpu.VMEM)
HBM = pl.BlockSpec(memory_space=pltpu.HBM)
QUARTERS = 4
NT = (((1,), (1,)), ((), ()))


CORE = (1, 1)
SHARE = ((2, 4), (4, 2))


def summed_bits():
    bits = [1 << bit for bit in range(3, (lax.axis_size("rows") - 1).bit_length())]
    pairs = []
    while bits:
        first, second = bits[0], bits[min(1, len(bits) - 1)]
        pairs += [(first, second), (second, first)][: len(bits)]
        bits = bits[2:]
    return pairs


def place_masks(place):
    return tuple((place >> 1) * high + (place & 1) * low for high, low in SHARE)


def swap(value, masks):
    size = lax.axis_size("rows")
    return lax.ppermute(value, "rows", [(i, i ^ masks[i & 1]) for i in range(size)])


def call(kernel, shapes, flops, *operands, in_specs=None, scratch=()):
    return pl.pallas_call(
        kernel,
        in_specs=in_specs or [VMEM] * len(operands),
        out_specs=[VMEM] * len(shapes),
        out_shape=[jax.ShapeDtypeStruct(*shape) for shape in shapes],
        scratch_shapes=scratch,
        compiler_params=pltpu.CompilerParams(vmem_limit_bytes=32 * 2**20),
        cost_estimate=pl.CostEstimate(flops=flops, bytes_accessed=0, transcendentals=0),
    )(*operands)


def turns(half):
    me = lax.axis_index("rows")
    turn = [2 * jnp.where(me & high, 1, 0) + jnp.where(me & low, 1, 0) for high, low in SHARE]
    return jnp.where(half == 0, turn[0], turn[1])


def halves():
    core = lax.axis_index("rows") & 1
    return core, 1 - core


def products(swapped, places, rem, basis_ref, out_refs):
    quarter = basis_ref.shape[1] // QUARTERS
    turn = turns(halves()[swapped])
    for place, out_ref in zip(places, out_refs):
        start = pl.multiple_of((turn ^ place) * quarter, quarter)
        product = jnp.dot(rem, basis_ref[:, pl.ds(start, quarter)], preferred_element_type=F32)
        out_ref[...] = product.astype(out_ref.dtype)


def load_kernel(swapped, basis_ref, rows_ref, *refs):
    if not swapped:
        rem_ref, *refs = refs
    product_refs, (half_ref, kept_ref, *turned_refs, sems) = refs[:QUARTERS], refs[QUARTERS:]
    columns = half_ref.shape[1]
    start = pl.multiple_of(halves()[swapped] * columns, columns)
    copy = pltpu.make_async_copy(basis_ref.at[:, pl.ds(start, columns)], half_ref, sems.at[0])
    copy.start()
    rows_copy = pltpu.make_async_copy(rows_ref, kept_ref, sems.at[1])
    rows_copy.start()
    rows_copy.wait()
    if swapped:
        rem = kept_ref[...].T
        turned_refs[0][...] = rem
    else:
        rem = rem_ref[...]
    copy.wait()
    products(swapped, range(QUARTERS), rem, half_ref, product_refs)


def load_call(swapped, basis, rows, rem):
    height, atoms = basis.shape
    block = rem.shape[1] if swapped else rem.shape[0]
    shapes = [((block, atoms // (2 * QUARTERS)), BF16 if swapped else F32)] * QUARTERS
    shapes += [((height, atoms // 2), BF16), (rows.shape, BF16)]
    if swapped:
        shapes.append(((block, height), BF16))
    basis, rows = (pltpu.with_memory_space_constraint(v, pltpu.HBM) for v in (basis, rows))
    kernel = functools.partial(load_kernel, swapped)
    operands = [basis, rows] if swapped else [basis, rows, rem]
    specs = [HBM, HBM, VMEM][: len(operands)]
    scratch = [pltpu.SemaphoreType.DMA((2,))]
    return call(kernel, shapes, basis.size * block, *operands, in_specs=specs, scratch=scratch)


def coef_kernel(swapped, places, basis_ref, rem_ref, *out_refs):
    products(swapped, places, rem_ref[...], basis_ref, out_refs)


def coef_call(swapped, places, basis, rem_low):
    block = rem_low.shape[0]
    quarter = basis.shape[1] // QUARTERS
    shapes = [((block, quarter), BF16 if swapped else F32)] * len(places)
    flops = 2 * rem_low.size * quarter * len(places)
    return call(functools.partial(coef_kernel, swapped, places), shapes, flops, basis, rem_low)


def image_kernel(swapped, places, basis_ref, rem_ref, *refs):
    coef_refs, out_refs = refs[: len(places)], refs[len(places) :]
    total = rem_ref[...].astype(F32)
    quarter = basis_ref.shape[1] // QUARTERS
    turn = turns(halves()[swapped])
    for place, coef_ref in zip(places, coef_refs):
        start = pl.multiple_of((turn ^ place) * quarter, quarter)
        columns = basis_ref[:, pl.ds(start, quarter)]
        total = total - lax.dot_general(coef_ref[...], columns, NT, preferred_element_type=F32)
    for out_ref in out_refs:
        out_ref[...] = total.astype(out_ref.dtype)


def image_call(swapped, places, basis, rem, coefs, dtypes):
    shapes = [(rem.shape, dtype) for dtype in dtypes]
    flops = 2 * rem.size * coefs[0].shape[1] * len(places)
    return call(functools.partial(image_kernel, swapped, places), shapes, flops, basis, rem, *coefs)


def sweep(own_half, other_half, rem, own, other, m_total, dtypes):
    got = {place: swap(other[place], CORE) for place in (3, 2, 1, 0)}
    sent = {place: swap((own[place] + got[place]).astype(BF16), place_masks(place)) for place in (3, 2, 1)}
    total = own[0] + got[0] + sent[3] + sent[2] + sent[1]
    for masks in summed_bits():
        total = total + swap(total.astype(BF16), masks)
    coef = {0: (total / m_total).astype(BF16)}
    for place in (3, 2, 1):
        coef[place] = swap(coef[0], place_masks(place))
    other = {place: swap(coef[place], CORE) for place in (0, 3, 2, 1)}
    (rem,) = image_call(False, (0, 3), own_half, rem, [coef[0], coef[3]], [F32])
    (rem,) = image_call(True, (0, 3), other_half, rem, [other[0], other[3]], [F32])
    (rem,) = image_call(False, (2, 1), own_half, rem, [coef[2], coef[1]], [F32])
    return image_call(True, (2, 1), other_half, rem, [other[2], other[1]], dtypes)


def plain_sweep(basis, rem, rem_low, m_total):
    coef = jnp.einsum("br,rk->bk", rem_low, basis, preferred_element_type=F32)
    coef_low = (lax.psum(coef, "rows") / m_total).astype(BF16)
    image = lax.dot_general(coef_low, basis, NT, preferred_element_type=F32)
    rem = rem - lax.psum(image, "users")
    return rem, rem.astype(BF16)


def small_kernel(turned_ref, user_ref, own_ref, other_ref, rem_ref):
    turned = turned_ref[...]
    rem = turned.T
    gram = jnp.dot(turned, rem, preferred_element_type=F32)
    coupling = jnp.dot(turned, user_ref[...], preferred_element_type=F32)
    first = (lax.axis_index("rows") & 1) == 0
    own_ref[...] = jnp.where(first, gram, coupling)
    other_ref[...] = jnp.where(first, coupling, gram)
    rem_ref[...] = rem


def small_parts(turned_low, user_residuals):
    square = ((user_residuals.shape[1],) * 2, F32)
    return call(small_kernel, [square, square, (user_residuals.shape, BF16)], 0, turned_low, user_residuals)


def small_sums(own, other):
    own = own + swap(other, CORE)
    own = own + sum(swap(own, place_masks(place)) for place in (3, 2, 1))
    for masks in summed_bits():
        own = own + swap(own, masks)
    return own, swap(own, CORE)


def inverse_factor(gram):
    size = gram.shape[0]
    group = 32
    lane = lax.broadcasted_iota(jnp.int32, (8, size), 1)
    row = lax.broadcasted_iota(jnp.int32, (8, size), 0)
    panels = [gram[i : i + 8] for i in range(0, size, 8)]
    result = []

    def across(value, index):
        return jnp.broadcast_to(value[:, index : index + 1], (8, size))

    def down(value, index):
        return jnp.broadcast_to(value[index : index + 1], (8, size))

    for top in range(0, size, group):
        end = min(top + group, size)
        scaled = []
        for first in range(top, end, 8):
            panel = panels[first // 8]
            inside = (lane >= first) & (lane < first + 8)
            columns = [across(panel, first + c) for c in range(8)]
            full = jnp.where(inside, (lane == row + first).astype(F32), panel)
            lower, pivots = full, columns[0]
            for s in range(8):
                pivot, line = down(columns[s], s), down(full, s)
                if s:
                    lower, pivots = jnp.where(row == s, line, lower), jnp.where(row == s, pivot, pivots)
                factor = jnp.where(row == s, 0.0, columns[s] * (1.0 / pivot))
                for c in range(s + 1, 8):
                    columns[c] = columns[c] - factor * down(columns[c], s)
                full = full - factor * line
            full = full * (1.0 / pivots)
            lower = lower * lax.rsqrt(pivots)
            scaled.append(jnp.where((lane > row + first) & (lane < end), 0.0, lower))
            for later in range(first + 8, end, 8):
                value = panels[later // 8]
                total = jnp.where(inside, 0.0, value)
                for c in range(8):
                    total = total - across(value, first + c) * down(full, c)
                panels[later // 8] = total
        result += [jnp.where(lane < end, value, 0.0) for value in scaled]
        if end < size:
            rows = jnp.concatenate(scaled)
            update = jnp.dot(
                rows.T[end:], rows, precision=lax.Precision.HIGHEST, preferred_element_type=F32
            )
            inside = (lane >= top) & (lane < end)
            for first in range(end, size, 8):
                value = jnp.where(inside, 0.0, panels[first // 8])
                panels[first // 8] = value - update[first - end : first - end + 8]
    return jnp.concatenate(result)


def thirds(value):
    high = value.astype(BF16)
    rest = value - high.astype(F32)
    middle = rest.astype(BF16)
    return high, middle, (rest - middle.astype(F32)).astype(BF16)


def finish_kernel(m_total, own_ref, other_ref, rem_ref, user_ref, block_ref, updated_ref):
    first = (lax.axis_index("rows") & 1) == 0
    own, other = own_ref[...], other_ref[...]
    inverse = inverse_factor(jnp.where(first, own, other) * (1.0 / m_total))
    rem = rem_ref[...]
    parts = [lax.dot_general(rem, part, NT, preferred_element_type=F32) for part in thirds(inverse)]
    block = (parts[2] + parts[1] + parts[0]).astype(BF16)
    coupling = jnp.where(first, other, own) * (1.0 / m_total)
    weights = jnp.dot(inverse, coupling, precision=lax.Precision.HIGHEST, preferred_element_type=F32)
    block_ref[...] = block
    image = jnp.dot(block, weights.astype(BF16), preferred_element_type=F32)
    updated_ref[...] = (user_ref[...].astype(F32) - image).astype(BF16)


def finish(own, other, rem_low, user_residuals, m_total):
    shapes = [(v.shape, BF16) for v in (rem_low, user_residuals)]
    return tuple(call(functools.partial(finish_kernel, m_total), shapes, 0, own, other, rem_low, user_residuals))


def plain_finish(remainder_low, gram_total, coupling_total, user_residuals, m_total):
    factor_lower = jnp.linalg.cholesky(gram_total / m_total)
    identity = jnp.eye(factor_lower.shape[0], dtype=F32)
    inverse = jax.scipy.linalg.solve_triangular(factor_lower, identity, lower=True)
    new_block = jnp.dot(remainder_low.astype(F32), inverse.T, precision=lax.Precision.HIGHEST).astype(BF16)
    weights = jnp.dot(inverse, coupling_total / m_total, precision=lax.Precision.HIGHEST).astype(BF16)
    updated = user_residuals.astype(F32) - jnp.dot(new_block, weights, preferred_element_type=F32)
    return (new_block, updated.astype(BF16))


def plain_local(old_basis, new_atoms, user_residuals):
    m_total = float(old_basis.shape[0] * lax.axis_size("rows"))
    rem, rem_low = new_atoms.T.astype(F32), new_atoms.T
    for _ in range(2):
        rem, rem_low = plain_sweep(old_basis, rem, rem_low, m_total)
    gram = lax.dot_general(rem_low, rem_low, NT, preferred_element_type=F32)
    coupling = jnp.dot(rem_low, user_residuals, preferred_element_type=F32)
    gram, coupling = lax.psum((gram, coupling), "rows")
    return plain_finish(rem_low.T, gram, coupling, user_residuals, m_total)


def local(old_basis, new_atoms, user_residuals):
    rows, atoms = old_basis.shape
    block = new_atoms.shape[1]
    size = lax.axis_size("rows")
    users = lax.axis_size("users")
    m_total = float(rows * size)
    power = size >= 16 and size & (size - 1) == 0
    tiled = rows % 128 == 0 and atoms % (2 * QUARTERS * 128) == 0
    if not power or not tiled or block != 128 or user_residuals.shape[1] != block:
        return plain_local(old_basis, new_atoms, user_residuals)

    *other, other_half, _, rem_low = load_call(True, old_basis, new_atoms, new_atoms)
    *own, own_half, user_rows = load_call(False, old_basis, user_residuals, rem_low)
    rem = rem_low
    for last in (False, True):
        if last:
            last_place = coef_call(True, (3,), other_half, rem_low)
            other = coef_call(True, (0, 1, 2), other_half, rem_low) + last_place
            own = coef_call(False, (0, 1, 2, 3), own_half, rem_low)
        dtypes = [BF16] if last and users == 1 else [F32, BF16]
        start = rem if users == 1 else jnp.zeros(rem.shape, F32)
        *new, rem_low = sweep(own_half, other_half, start, own, other, m_total, dtypes)
        if users == 1:
            rem = new[0] if new else rem
        else:
            rem = rem.astype(F32) + lax.psum(new[0], "users")
            rem_low = rem.astype(BF16)
    own, other, rem_low = small_parts(rem_low, user_rows)
    own, other = small_sums(own, other)
    return finish(own, other, rem_low, user_rows, m_total)


def solution(mesh):
    in_specs = (P("rows", "users"), P("rows", None), P("rows", "users"))
    out_specs = (P("rows", None), P("rows", "users"))
    return jax.shard_map(local, mesh=mesh, in_specs=in_specs, out_specs=out_specs, check_vma=False)
```

time: 104 us -> 98.2 us (0.944)
  starting transfers between devices: 47 us -> 33.8 us
  waiting for transfers between devices: 40.3 us -> 48.9 us
  Pallas kernels: 14.9 us -> 13.8 us
    ppermute x38 -> x39, starting transfers between devices: 47 us -> 33.8 us  [swap(): lax.ppermute(value, 'rows', [(i, i ^ masks[i & 1]) for i in range(size)])]
    ppermute x38 -> x39, waiting for transfers between devices: 40.3 us -> 48.9 us  [swap(): lax.ppermute(value, 'rows', [(i, i ^ masks[i & 1]) for i in range(size)])]
    pallas_call x20 -> x15, Pallas kernels: 14.9 us -> 13.8 us  [call(): pl.pallas_call(kernel, in_specs=in_specs or [VMEM] * len(operands), out_s...]
  transfers between devices with their start and end apart: 38 -> 39, of which waited for: 24 -> 23; matrix products, arithmetic and copies ran while one was open for 1% -> 0% of each run, Pallas kernels for 5% -> 5%
where the time goes in v3:
time: 98.2 us; the launch traced here: 98 us
  waiting for transfers between devices  48.9 us (50%)
  starting transfers between devices  33.8 us (34%)
  Pallas kernels  13.8 us (14%)
    ppermute x39, waiting for transfers between devices, swap(): lax.ppermute(value, 'rows', [(i, i ^ masks[i & 1]) for i in range(size)])  48.9 us
    ppermute x39, starting transfers between devices, swap(): lax.ppermute(value, 'rows', [(i, i ^ masks[i & 1]) for i in range(size)])  33.8 us
    pallas_call x15, Pallas kernels, call(): pl.pallas_call(kernel, in_specs=in_specs or [VMEM] * len(operands), out_s...  13.8 us
  transfers between devices with their start and end apart: 39, of which 23 were waited for; matrix products, arithmetic and copies ran while one was open for 0% of the time, Pallas kernels for 5%

profile of v3, /device:TPU:0, one launch (start us, length us, event | category | flops | bytes accessed | tf_op | source)
XLA Modules:
  0.0 98.0 jit_solution(1815060442095424980)
XLA Ops:
  0.6 2.4 %shard_map.50 = (bf16[128,512]{1,0:T(8,128)(2,1)S(1)}, bf16[128,512]{1,0:T(8,128)(2,1)S(1)}, bf16[128,512]{1,0:T(8,128)(2,1)S(1)}, bf16[128,512]{1,0:T(8,128)(2,...) custom-call(bf16[384,4096]{1,0:T(8,128)(2,1)} %basis_ref.3, ...), custom_call_target="tpu_custom_call" | custom-call | flops 201326592 | tf_op jit(solution)/shard_map/pallas_call | solution.py:41
  3.0 0.5 collective-permute-start.1
  3.6 0.4 collective-permute-start.5
  4.1 1.9 %shard_map.51 = (f32[128,512]{1,0:T(8,128)S(1)}, f32[128,512]{1,0:T(8,128)S(1)}, f32[128,512]{1,0:T(8,128)S(1)}, f32[128,512]{1,0:T(8,128)S(1)}, bf16[384,2048]{...) custom-call(bf16[384,4096]{1,0:T(8,128)(2,1)} %basis_ref.3, bf16[384,128]{1,0:T(8,128)(2,1)} %rows_ref.3, ...), custom_call_target="tpu_custom_call" | custom-call | flops 201326592 | tf_op jit(solution)/shard_map/pallas_call | solution.py:41
  6.0 3.9 %collective-permute-start.2 = (bf16[128,512]{1,0:T(8,128)(2,1)S(1)}, bf16[128,512]{1,0:T(8,128)(2,1)S(1)}, u32[]{:S(2)}, u32[]{:S(2)}) collective-permute-start(bf16[128,512]{1,0:T(8,128)(2,1)S(1)} %add_convert_fusion.5), channel_id=1, source_target_pairs={{0,6},{1,7},{2,4},{3,5},{4,2},{5,3},{6,0},{7,1},{8,14},{9,15},{10,... | collective-permute-start | bytes 393224 | tf_op jit(solution)/shard_map/ppermute | solution.py:37
  10.0 0.6 collective-permute-start.4
  10.6 0.1 collective-permute-start.6
  10.8 3.1 %collective-permute-done.2 = bf16[128,512]{1,0:T(8,128)(2,1)S(1)} collective-permute-done((bf16[128,512]{1,0:T(8,128)(2,1)S(1)}, bf16[128,512]{1,0:T(8,128)(2,1)S(1)}, u32[]{:S(2)}, u32[]{:S(2)}) %collective-permute-start.2) | collective-permute-done | bytes 131104 | tf_op jit(solution)/shard_map/ppermute | solution.py:37
  13.9 2.9 %collective-permute-done.4 = bf16[128,512]{1,0:T(8,128)(2,1)S(1)} collective-permute-done((bf16[128,512]{1,0:T(8,128)(2,1)S(1)}, bf16[128,512]{1,0:T(8,128)(2,1)S(1)}, u32[]{:S(2)}, u32[]{:S(2)}) %collective-permute-start.4) | collective-permute-done | bytes 131104 | tf_op jit(solution)/shard_map/ppermute | solution.py:37
  16.9 1.6 %collective-permute-start.7 = (bf16[128,512]{1,0:T(8,128)(2,1)S(1)}, bf16[128,512]{1,0:T(8,128)(2,1)S(1)}, u32[]{:S(2)}, u32[]{:S(2)}) collective-permute-start(bf16[128,512]{1,0:T(8,128)(2,1)S(1)} %get-tuple-element.52), channel_id=1, source_target_pairs={{0,8},{1,17},{2,10},{3,19},{4,12},{5,21},{6,14},{7,23},{8,0},{9,25... | collective-permute-start | bytes 393224 | tf_op jit(solution)/shard_map/ppermute | solution.py:37
  18.5 4.0 %collective-permute-done.7 = bf16[128,512]{1,0:T(8,128)(2,1)S(1)} collective-permute-done((bf16[128,512]{1,0:T(8,128)(2,1)S(1)}, bf16[128,512]{1,0:T(8,128)(2,1)S(1)}, u32[]{:S(2)}, u32[]{:S(2)}) %collective-permute-start.7) | collective-permute-done | bytes 131104 | tf_op jit(solution)/shard_map/ppermute | solution.py:37
  22.6 2.4 %collective-permute-start.8 = (bf16[128,512]{1,0:T(8,128)(2,1)S(1)}, bf16[128,512]{1,0:T(8,128)(2,1)S(1)}, u32[]{:S(2)}, u32[]{:S(2)}) collective-permute-start(bf16[128,512]{1,0:T(8,128)(2,1)S(1)} %fusion), channel_id=1, source_target_pairs={{0,16},{1,9},{2,18},{3,11},{4,20},{5,13},{6,22},{7,15},{8,24},{9,1... | collective-permute-start | bytes 393224 | tf_op jit(solution)/shard_map/ppermute | solution.py:37
  25.0 3.6 %collective-permute-done.8 = bf16[128,512]{1,0:T(8,128)(2,1)S(1)} collective-permute-done((bf16[128,512]{1,0:T(8,128)(2,1)S(1)}, bf16[128,512]{1,0:T(8,128)(2,1)S(1)}, u32[]{:S(2)}, u32[]{:S(2)}) %collective-permute-start.8) | collective-permute-done | bytes 131104 | tf_op jit(solution)/shard_map/ppermute | solution.py:37
  28.6 1.6 %collective-permute-start.9 = (bf16[128,512]{1,0:T(8,128)(2,1)S(1)}, bf16[128,512]{1,0:T(8,128)(2,1)S(1)}, u32[]{:S(2)}, u32[]{:S(2)}) collective-permute-start(bf16[128,512]{1,0:T(8,128)(2,1)S(1)} %multiply_convert_fusion.1.refs_0_), channel_id=1, source_target_pairs={{0,6},{1,7},{2,4},{3,5},{4,2},{5,3},{6,0},{7,1},{8,14},{9,15},{10,... | collective-permute-start | bytes 393224 | tf_op jit(solution)/shard_map/ppermute | solution.py:37
  30.1 2.5 %collective-permute-start.12 = (bf16[128,512]{1,0:T(8,128)(2,1)S(1)}, bf16[128,512]{1,0:T(8,128)(2,1)S(1)}, u32[]{:S(2)}, u32[]{:S(2)}) collective-permute-start(bf16[128,512]{1,0:T(8,128)(2,1)S(1)} %multiply_convert_fusion.1.refs_0_), channel_id=1, source_target_pairs={{0,2},{1,5},{2,0},{3,7},{4,6},{5,1},{6,4},{7,3},{8,10},{9,13},{10,... | collective-permute-start | bytes 393224 | tf_op jit(solution)/shard_map/ppermute | solution.py:37
  32.7 1.9 %collective-permute-done.9.refs_1_ = bf16[128,512]{1,0:T(8,128)(2,1)S(1)} collective-permute-done((bf16[128,512]{1,0:T(8,128)(2,1)S(1)}, bf16[128,512]{1,0:T(8,128)(2,1)S(1)}, u32[]{:S(2)}, u32[]{:S(2)}) %collective-permute-start.9) | collective-permute-done | bytes 131104 | tf_op jit(solution)/shard_map/ppermute | solution.py:37
  34.6 2.4 %collective-permute-done.12.refs_0_ = bf16[128,512]{1,0:T(8,128)(2,1)S(1)} collective-permute-done((bf16[128,512]{1,0:T(8,128)(2,1)S(1)}, bf16[128,512]{1,0:T(8,128)(2,1)S(1)}, u32[]{:S(2)}, u32[]{:S(2)}) %collective-permute-start.12) | collective-permute-done | bytes 131104 | tf_op jit(solution)/shard_map/ppermute | solution.py:37
  37.0 0.6 collective-permute-done.13.refs_1_
  37.6 0.4 shard_map.52.rem_ref
  38.0 0.4 shard_map.53.rem_ref
  38.4 0.4 shard_map.54.rem_ref
  38.9 0.1 collective-permute-done.15.refs_1_
  39.0 0.4 shard_map.55
  39.4 0.2 shard_map.58
  39.6 0.5 collective-permute-start.17
  40.1 0.4 shard_map.57
  40.5 0.2 collective-permute-start.19
  40.6 0.4 collective-permute-start.21
  41.0 0.1 collective-permute-start.16
  41.2 0.4 shard_map.56
  41.6 0.6 collective-permute-start.18
  42.3 1.8 %collective-permute-start.20 = (bf16[128,512]{1,0:T(8,128)(2,1)S(1)}, bf16[128,512]{1,0:T(8,128)(2,1)S(1)}, u32[]{:S(2)}, u32[]{:S(2)}) collective-permute-start(bf16[128,512]{1,0:T(8,128)(2,1)S(1)} %add_convert_fusion.1), channel_id=1, source_target_pairs={{0,2},{1,5},{2,0},{3,7},{4,6},{5,1},{6,4},{7,3},{8,10},{9,13},{10,... | collective-permute-start | bytes 393224 | tf_op jit(solution)/shard_map/ppermute | solution.py:37
  44.1 1.3 %collective-permute-start.22 = (bf16[128,512]{1,0:T(8,128)(2,1)S(1)}, bf16[128,512]{1,0:T(8,128)(2,1)S(1)}, u32[]{:S(2)}, u32[]{:S(2)}) collective-permute-start(bf16[128,512]{1,0:T(8,128)(2,1)S(1)} %add_convert_fusion), channel_id=1, source_target_pairs={{0,4},{1,3},{2,6},{3,1},{4,0},{5,7},{6,2},{7,5},{8,12},{9,11},{10,... | collective-permute-start | bytes 393224 | tf_op jit(solution)/shard_map/ppermute | solution.py:37
  45.4 3.6 %collective-permute-done.18 = bf16[128,512]{1,0:T(8,128)(2,1)S(1)} collective-permute-done((bf16[128,512]{1,0:T(8,128)(2,1)S(1)}, bf16[128,512]{1,0:T(8,128)(2,1)S(1)}, u32[]{:S(2)}, u32[]{:S(2)}) %collective-permute-start.18) | collective-permute-done | bytes 131104 | tf_op jit(solution)/shard_map/ppermute | solution.py:37
  49.0 1.7 %collective-permute-done.20 = bf16[128,512]{1,0:T(8,128)(2,1)S(1)} collective-permute-done((bf16[128,512]{1,0:T(8,128)(2,1)S(1)}, bf16[128,512]{1,0:T(8,128)(2,1)S(1)}, u32[]{:S(2)}, u32[]{:S(2)}) %collective-permute-start.20) | collective-permute-done | bytes 131104 | tf_op jit(solution)/shard_map/ppermute | solution.py:37
  50.8 1.8 %collective-permute-start.23 = (bf16[128,512]{1,0:T(8,128)(2,1)S(1)}, bf16[128,512]{1,0:T(8,128)(2,1)S(1)}, u32[]{:S(2)}, u32[]{:S(2)}) collective-permute-start(bf16[128,512]{1,0:T(8,128)(2,1)S(1)} %get-tuple-element.50), channel_id=1, source_target_pairs={{0,8},{1,17},{2,10},{3,19},{4,12},{5,21},{6,14},{7,23},{8,0},{9,25... | collective-permute-start | bytes 393224 | tf_op jit(solution)/shard_map/ppermute | solution.py:37
  52.6 4.5 %collective-permute-done.23 = bf16[128,512]{1,0:T(8,128)(2,1)S(1)} collective-permute-done((bf16[128,512]{1,0:T(8,128)(2,1)S(1)}, bf16[128,512]{1,0:T(8,128)(2,1)S(1)}, u32[]{:S(2)}, u32[]{:S(2)}) %collective-permute-start.23) | collective-permute-done | bytes 131104 | tf_op jit(solution)/shard_map/ppermute | solution.py:37
  57.1 2.3 %collective-permute-start.24 = (bf16[128,512]{1,0:T(8,128)(2,1)S(1)}, bf16[128,512]{1,0:T(8,128)(2,1)S(1)}, u32[]{:S(2)}, u32[]{:S(2)}) collective-permute-start(bf16[128,512]{1,0:T(8,128)(2,1)S(1)} %fusion.1), channel_id=1, source_target_pairs={{0,16},{1,9},{2,18},{3,11},{4,20},{5,13},{6,22},{7,15},{8,24},{9,1... | collective-permute-start | bytes 393224 | tf_op jit(solution)/shard_map/ppermute | solution.py:37
  59.5 3.8 %collective-permute-done.24 = bf16[128,512]{1,0:T(8,128)(2,1)S(1)} collective-permute-done((bf16[128,512]{1,0:T(8,128)(2,1)S(1)}, bf16[128,512]{1,0:T(8,128)(2,1)S(1)}, u32[]{:S(2)}, u32[]{:S(2)}) %collective-permute-start.24) | collective-permute-done | bytes 131104 | tf_op jit(solution)/shard_map/ppermute | solution.py:37
  63.3 0.8 collective-permute-start.25
  64.1 2.8 %collective-permute-start.28 = (bf16[128,512]{1,0:T(8,128)(2,1)S(1)}, bf16[128,512]{1,0:T(8,128)(2,1)S(1)}, u32[]{:S(2)}, u32[]{:S(2)}) collective-permute-start(bf16[128,512]{1,0:T(8,128)(2,1)S(1)} %multiply_convert_fusion.refs_0_), channel_id=1, source_target_pairs={{0,2},{1,5},{2,0},{3,7},{4,6},{5,1},{6,4},{7,3},{8,10},{9,13},{10,... | collective-permute-start | bytes 393224 | tf_op jit(solution)/shard_map/ppermute | solution.py:37
  66.9 2.3 %collective-permute-done.25.refs_1_ = bf16[128,512]{1,0:T(8,128)(2,1)S(1)} collective-permute-done((bf16[128,512]{1,0:T(8,128)(2,1)S(1)}, bf16[128,512]{1,0:T(8,128)(2,1)S(1)}, u32[]{:S(2)}, u32[]{:S(2)}) %collective-permute-start.25) | collective-permute-done | bytes 131104 | tf_op jit(solution)/shard_map/ppermute | solution.py:37
  69.2 2.0 %collective-permute-done.28.refs_0_ = bf16[128,512]{1,0:T(8,128)(2,1)S(1)} collective-permute-done((bf16[128,512]{1,0:T(8,128)(2,1)S(1)}, bf16[128,512]{1,0:T(8,128)(2,1)S(1)}, u32[]{:S(2)}, u32[]{:S(2)}) %collective-permute-start.28) | collective-permute-done | bytes 131104 | tf_op jit(solution)/shard_map/ppermute | solution.py:37
  71.2 0.6 collective-permute-done.29.refs_1_
  71.9 0.4 shard_map.59.rem_ref
  72.3 0.4 shard_map.60.rem_ref
  72.7 0.4 shard_map.61.rem_ref
  73.1 0.1 collective-permute-done.31.refs_1_
  73.2 0.4 shard_map.62.turned_ref
  73.6 0.3 shard_map.63
  73.9 0.5 collective-permute-start.32
  74.3 0.9 collective-permute-done.32
  75.3 0.1 collective-permute-start.33
  75.4 2.2 %collective-permute-start.34 = (f32[128,128]{1,0:T(8,128)S(1)}, f32[128,128]{1,0:T(8,128)S(1)}, u32[]{:S(2)}, u32[]{:S(2)}) collective-permute-start(f32[128,128]{1,0:T(8,128)S(1)} %add.90), channel_id=1, source_target_pairs={{0,2},{1,5},{2,0},{3,7},{4,6},{5,1},{6,4},{7,3},{8,10},{9,13},{10,... | collective-permute-start | bytes 196616 | tf_op jit(solution)/shard_map/ppermute | solution.py:37
  77.6 1.2 %collective-permute-start.35 = (f32[128,128]{1,0:T(8,128)S(1)}, f32[128,128]{1,0:T(8,128)S(1)}, u32[]{:S(2)}, u32[]{:S(2)}) collective-permute-start(f32[128,128]{1,0:T(8,128)S(1)} %add.90), channel_id=1, source_target_pairs={{0,4},{1,3},{2,6},{3,1},{4,0},{5,7},{6,2},{7,5},{8,12},{9,11},{10,... | collective-permute-start | bytes 196616 | tf_op jit(solution)/shard_map/ppermute | solution.py:37
  78.8 2.3 %collective-permute-done.33 = f32[128,128]{1,0:T(8,128)S(1)} collective-permute-done((f32[128,128]{1,0:T(8,128)S(1)}, f32[128,128]{1,0:T(8,128)S(1)}, u32[]{:S(2)}, u32[]{:S(2)}) %collective-permute-start.33) | collective-permute-done | bytes 65568 | tf_op jit(solution)/shard_map/ppermute | solution.py:37
  81.1 0.2 collective-permute-done.34
  81.3 0.5 collective-permute-done.35
  81.9 1.1 %collective-permute-start.36 = (f32[128,128]{1,0:T(8,128)S(1)}, f32[128,128]{1,0:T(8,128)S(1)}, u32[]{:S(2)}, u32[]{:S(2)}) collective-permute-start(f32[128,128]{1,0:T(8,128)S(1)} %add_add_fusion), channel_id=1, source_target_pairs={{0,8},{1,17},{2,10},{3,19},{4,12},{5,21},{6,14},{7,23},{8,0},{9,25... | collective-permute-start | bytes 196616 | tf_op jit(solution)/shard_map/ppermute | solution.py:37
  83.0 3.3 %collective-permute-done.36 = f32[128,128]{1,0:T(8,128)S(1)} collective-permute-done((f32[128,128]{1,0:T(8,128)S(1)}, f32[128,128]{1,0:T(8,128)S(1)}, u32[]{:S(2)}, u32[]{:S(2)}) %collective-permute-start.36) | collective-permute-done | bytes 65568 | tf_op jit(solution)/shard_map/ppermute | solution.py:37
  86.3 2.1 %collective-permute-start.37 = (f32[128,128]{1,0:T(8,128)S(1)}, f32[128,128]{1,0:T(8,128)S(1)}, u32[]{:S(2)}, u32[]{:S(2)}) collective-permute-start(f32[128,128]{1,0:T(8,128)S(1)} %add.94), channel_id=1, source_target_pairs={{0,16},{1,9},{2,18},{3,11},{4,20},{5,13},{6,22},{7,15},{8,24},{9,1... | collective-permute-start | bytes 196616 | tf_op jit(solution)/shard_map/ppermute | solution.py:37
  88.4 3.1 %collective-permute-done.37 = f32[128,128]{1,0:T(8,128)S(1)} collective-permute-done((f32[128,128]{1,0:T(8,128)S(1)}, f32[128,128]{1,0:T(8,128)S(1)}, u32[]{:S(2)}, u32[]{:S(2)}) %collective-permute-start.37) | collective-permute-done | bytes 65568 | tf_op jit(solution)/shard_map/ppermute | solution.py:37
  91.6 1.2 %collective-permute-done.38.other_ref = f32[128,128]{1,0:T(8,128)S(1)} collective-permute-done((f32[128,128]{1,0:T(8,128)S(1)}, f32[128,128]{1,0:T(8,128)S(1)}, u32[]{:S(2)}, u32[]{:S(2)}) %collective-permute-start.38) | collective-permute-done | bytes 65568 | tf_op jit(solution)/shard_map/ppermute | solution.py:37
  92.8 5.2 %shard_map.64 = (bf16[384,128]{1,0:T(8,128)(2,1)}, bf16[384,128]{1,0:T(8,128)(2,1)}) custom-call(f32[128,128]{1,0:T(8,128)S(1)} %add.95.own_ref, f32[128,128]{1,0:T(8,128)S(1)} %collective-permute-done.38.other_ref, bf16[384,128]{1,0:T(8,128)(2,1)S(1)} %get-tuple-element.49.rem_ref, bf16[384,128]{1,0:T(8,128)(2,1)S(1)} %get-tuple-element.46.user_ref), custom_call_target="tpu_custom_call" | custom-call | tf_op jit(solution)/shard_map/pallas_call | solution.py:41
  (45 shorter events, 0.8 us)
Async XLA Ops:
  3.0 3.0 %collective-permute-start.1 = (bf16[128,512]{1,0:T(8,128)(2,1)S(1)}, bf16[128,512]{1,0:T(8,128)(2,1)S(1)}, u32[]{:S(2)}, u32[]{:S(2)}) collective-permute-start(bf16[128,512]{1,0:T(8,128)(2,1)S(1)} %get-tuple-element.32), channel_id=1, source_target_pairs={{0,1},{1,0},{2,3},{3,2},{4,5},{5,4},{6,7},{7,6},{8,9},{9,8},{10,11... | collective-permute-start | bytes 393224 | tf_op jit(solution)/shard_map/ppermute | solution.py:37
  3.5 6.5 %collective-permute-start.3 = (bf16[128,512]{1,0:T(8,128)(2,1)S(1)}, bf16[128,512]{1,0:T(8,128)(2,1)S(1)}, u32[]{:S(2)}, u32[]{:S(2)}) collective-permute-start(bf16[128,512]{1,0:T(8,128)(2,1)S(1)} %get-tuple-element.34), channel_id=1, source_target_pairs={{0,1},{1,0},{2,3},{3,2},{4,5},{5,4},{6,7},{7,6},{8,9},{9,8},{10,11... | collective-permute-start | bytes 393224 | tf_op jit(solution)/shard_map/ppermute | solution.py:37
  3.6 7.0 %collective-permute-start.5 = (bf16[128,512]{1,0:T(8,128)(2,1)S(1)}, bf16[128,512]{1,0:T(8,128)(2,1)S(1)}, u32[]{:S(2)}, u32[]{:S(2)}) collective-permute-start(bf16[128,512]{1,0:T(8,128)(2,1)S(1)} %get-tuple-element.36), channel_id=1, source_target_pairs={{0,1},{1,0},{2,3},{3,2},{4,5},{5,4},{6,7},{7,6},{8,9},{9,8},{10,11... | collective-permute-start | bytes 393224 | tf_op jit(solution)/shard_map/ppermute | solution.py:37
  4.0 6.7 %collective-permute-start = (bf16[128,512]{1,0:T(8,128)(2,1)S(1)}, bf16[128,512]{1,0:T(8,128)(2,1)S(1)}, u32[]{:S(2)}, u32[]{:S(2)}) collective-permute-start(bf16[128,512]{1,0:T(8,128)(2,1)S(1)} %get-tuple-element.30), channel_id=1, source_target_pairs={{0,1},{1,0},{2,3},{3,2},{4,5},{5,4},{6,7},{7,6},{8,9},{9,8},{10,11... | collective-permute-start | bytes 393224 | tf_op jit(solution)/shard_map/ppermute | solution.py:37
  6.0 7.8 %collective-permute-start.2 = (bf16[128,512]{1,0:T(8,128)(2,1)S(1)}, bf16[128,512]{1,0:T(8,128)(2,1)S(1)}, u32[]{:S(2)}, u32[]{:S(2)}) collective-permute-start(bf16[128,512]{1,0:T(8,128)(2,1)S(1)} %add_convert_fusion.5), channel_id=1, source_target_pairs={{0,6},{1,7},{2,4},{3,5},{4,2},{5,3},{6,0},{7,1},{8,14},{9,15},{10,... | collective-permute-start | bytes 393224 | tf_op jit(solution)/shard_map/ppermute | solution.py:37
  10.0 6.8 %collective-permute-start.4 = (bf16[128,512]{1,0:T(8,128)(2,1)S(1)}, bf16[128,512]{1,0:T(8,128)(2,1)S(1)}, u32[]{:S(2)}, u32[]{:S(2)}) collective-permute-start(bf16[128,512]{1,0:T(8,128)(2,1)S(1)} %add_convert_fusion.4), channel_id=1, source_target_pairs={{0,2},{1,5},{2,0},{3,7},{4,6},{5,1},{6,4},{7,3},{8,10},{9,13},{10,... | collective-permute-start | bytes 393224 | tf_op jit(solution)/shard_map/ppermute | solution.py:37
  10.6 6.2 %collective-permute-start.6 = (bf16[128,512]{1,0:T(8,128)(2,1)S(1)}, bf16[128,512]{1,0:T(8,128)(2,1)S(1)}, u32[]{:S(2)}, u32[]{:S(2)}) collective-permute-start(bf16[128,512]{1,0:T(8,128)(2,1)S(1)} %add_convert_fusion.3), channel_id=1, source_target_pairs={{0,4},{1,3},{2,6},{3,1},{4,0},{5,7},{6,2},{7,5},{8,12},{9,11},{10,... | collective-permute-start | bytes 393224 | tf_op jit(solution)/shard_map/ppermute | solution.py:37
  16.9 5.7 %collective-permute-start.7 = (bf16[128,512]{1,0:T(8,128)(2,1)S(1)}, bf16[128,512]{1,0:T(8,128)(2,1)S(1)}, u32[]{:S(2)}, u32[]{:S(2)}) collective-permute-start(bf16[128,512]{1,0:T(8,128)(2,1)S(1)} %get-tuple-element.52), channel_id=1, source_target_pairs={{0,8},{1,17},{2,10},{3,19},{4,12},{5,21},{6,14},{7,23},{8,0},{9,25... | collective-permute-start | bytes 393224 | tf_op jit(solution)/shard_map/ppermute | solution.py:37
  22.6 5.9 %collective-permute-start.8 = (bf16[128,512]{1,0:T(8,128)(2,1)S(1)}, bf16[128,512]{1,0:T(8,128)(2,1)S(1)}, u32[]{:S(2)}, u32[]{:S(2)}) collective-permute-start(bf16[128,512]{1,0:T(8,128)(2,1)S(1)} %fusion), channel_id=1, source_target_pairs={{0,16},{1,9},{2,18},{3,11},{4,20},{5,13},{6,22},{7,15},{8,24},{9,1... | collective-permute-start | bytes 393224 | tf_op jit(solution)/shard_map/ppermute | solution.py:37
  28.6 6.0 %collective-permute-start.9 = (bf16[128,512]{1,0:T(8,128)(2,1)S(1)}, bf16[128,512]{1,0:T(8,128)(2,1)S(1)}, u32[]{:S(2)}, u32[]{:S(2)}) collective-permute-start(bf16[128,512]{1,0:T(8,128)(2,1)S(1)} %multiply_convert_fusion.1.refs_0_), channel_id=1, source_target_pairs={{0,6},{1,7},{2,4},{3,5},{4,2},{5,3},{6,0},{7,1},{8,14},{9,15},{10,... | collective-permute-start | bytes 393224 | tf_op jit(solution)/shard_map/ppermute | solution.py:37
  30.1 6.9 %collective-permute-start.12 = (bf16[128,512]{1,0:T(8,128)(2,1)S(1)}, bf16[128,512]{1,0:T(8,128)(2,1)S(1)}, u32[]{:S(2)}, u32[]{:S(2)}) collective-permute-start(bf16[128,512]{1,0:T(8,128)(2,1)S(1)} %multiply_convert_fusion.1.refs_0_), channel_id=1, source_target_pairs={{0,2},{1,5},{2,0},{3,7},{4,6},{5,1},{6,4},{7,3},{8,10},{9,13},{10,... | collective-permute-start | bytes 393224 | tf_op jit(solution)/shard_map/ppermute | solution.py:37
  32.7 5.0 %collective-permute-start.13 = (bf16[128,512]{1,0:T(8,128)(2,1)S(1)}, bf16[128,512]{1,0:T(8,128)(2,1)S(1)}, u32[]{:S(2)}, u32[]{:S(2)}) collective-permute-start(bf16[128,512]{1,0:T(8,128)(2,1)S(1)} %multiply_convert_fusion.1.refs_0_), channel_id=1, source_target_pairs={{0,4},{1,3},{2,6},{3,1},{4,0},{5,7},{6,2},{7,5},{8,12},{9,11},{10,... | collective-permute-start | bytes 393224 | tf_op jit(solution)/shard_map/ppermute | solution.py:37
  32.7 5.4 %collective-permute-start.10 = (bf16[128,512]{1,0:T(8,128)(2,1)S(1)}, bf16[128,512]{1,0:T(8,128)(2,1)S(1)}, u32[]{:S(2)}, u32[]{:S(2)}) collective-permute-start(bf16[128,512]{1,0:T(8,128)(2,1)S(1)} %multiply_convert_fusion.1.refs_0_), channel_id=1, source_target_pairs={{0,1},{1,0},{2,3},{3,2},{4,5},{5,4},{6,7},{7,6},{8,9},{9,8},{10,11... | collective-permute-start | bytes 393224 | tf_op jit(solution)/shard_map/ppermute | solution.py:37
  34.6 3.4 %collective-permute-start.11 = (bf16[128,512]{1,0:T(8,128)(2,1)S(1)}, bf16[128,512]{1,0:T(8,128)(2,1)S(1)}, u32[]{:S(2)}, u32[]{:S(2)}) collective-permute-start(bf16[128,512]{1,0:T(8,128)(2,1)S(1)} %collective-permute-done.9.refs_1_), channel_id=1, source_target_pairs={{0,1},{1,0},{2,3},{3,2},{4,5},{5,4},{6,7},{7,6},{8,9},{9,8},{10,11... | collective-permute-start | bytes 393224 | tf_op jit(solution)/shard_map/ppermute | solution.py:37
  37.0 1.8 %collective-permute-start.14 = (bf16[128,512]{1,0:T(8,128)(2,1)S(1)}, bf16[128,512]{1,0:T(8,128)(2,1)S(1)}, u32[]{:S(2)}, u32[]{:S(2)}) collective-permute-start(bf16[128,512]{1,0:T(8,128)(2,1)S(1)} %collective-permute-done.12.refs_0_), channel_id=1, source_target_pairs={{0,1},{1,0},{2,3},{3,2},{4,5},{5,4},{6,7},{7,6},{8,9},{9,8},{10,11... | collective-permute-start | bytes 393224 | tf_op jit(solution)/shard_map/ppermute | solution.py:37
  37.6 1.3 %collective-permute-start.15 = (bf16[128,512]{1,0:T(8,128)(2,1)S(1)}, bf16[128,512]{1,0:T(8,128)(2,1)S(1)}, u32[]{:S(2)}, u32[]{:S(2)}) collective-permute-start(bf16[128,512]{1,0:T(8,128)(2,1)S(1)} %collective-permute-done.13.refs_1_), channel_id=1, source_target_pairs={{0,1},{1,0},{2,3},{3,2},{4,5},{5,4},{6,7},{7,6},{8,9},{9,8},{10,11... | collective-permute-start | bytes 393224 | tf_op jit(solution)/shard_map/ppermute | solution.py:37
  39.6 2.0 %collective-permute-start.17 = (bf16[128,512]{1,0:T(8,128)(2,1)S(1)}, bf16[128,512]{1,0:T(8,128)(2,1)S(1)}, u32[]{:S(2)}, u32[]{:S(2)}) collective-permute-start(bf16[128,512]{1,0:T(8,128)(2,1)S(1)} %shard_map.58), channel_id=1, source_target_pairs={{0,1},{1,0},{2,3},{3,2},{4,5},{5,4},{6,7},{7,6},{8,9},{9,8},{10,11... | collective-permute-start | bytes 393224 | tf_op jit(solution)/shard_map/ppermute | solution.py:37
  40.5 1.8 %collective-permute-start.19 = (bf16[128,512]{1,0:T(8,128)(2,1)S(1)}, bf16[128,512]{1,0:T(8,128)(2,1)S(1)}, u32[]{:S(2)}, u32[]{:S(2)}) collective-permute-start(bf16[128,512]{1,0:T(8,128)(2,1)S(1)} %get-tuple-element.43), channel_id=1, source_target_pairs={{0,1},{1,0},{2,3},{3,2},{4,5},{5,4},{6,7},{7,6},{8,9},{9,8},{10,11... | collective-permute-start | bytes 393224 | tf_op jit(solution)/shard_map/ppermute | solution.py:37
  40.6 3.5 %collective-permute-start.21 = (bf16[128,512]{1,0:T(8,128)(2,1)S(1)}, bf16[128,512]{1,0:T(8,128)(2,1)S(1)}, u32[]{:S(2)}, u32[]{:S(2)}) collective-permute-start(bf16[128,512]{1,0:T(8,128)(2,1)S(1)} %get-tuple-element.45), channel_id=1, source_target_pairs={{0,1},{1,0},{2,3},{3,2},{4,5},{5,4},{6,7},{7,6},{8,9},{9,8},{10,11... | collective-permute-start | bytes 393224 | tf_op jit(solution)/shard_map/ppermute | solution.py:37
  41.0 4.4 %collective-permute-start.16 = (bf16[128,512]{1,0:T(8,128)(2,1)S(1)}, bf16[128,512]{1,0:T(8,128)(2,1)S(1)}, u32[]{:S(2)}, u32[]{:S(2)}) collective-permute-start(bf16[128,512]{1,0:T(8,128)(2,1)S(1)} %get-tuple-element.40), channel_id=1, source_target_pairs={{0,1},{1,0},{2,3},{3,2},{4,5},{5,4},{6,7},{7,6},{8,9},{9,8},{10,11... | collective-permute-start | bytes 393224 | tf_op jit(solution)/shard_map/ppermute | solution.py:37
  41.6 7.3 %collective-permute-start.18 = (bf16[128,512]{1,0:T(8,128)(2,1)S(1)}, bf16[128,512]{1,0:T(8,128)(2,1)S(1)}, u32[]{:S(2)}, u32[]{:S(2)}) collective-permute-start(bf16[128,512]{1,0:T(8,128)(2,1)S(1)} %add_convert_fusion.2), channel_id=1, source_target_pairs={{0,6},{1,7},{2,4},{3,5},{4,2},{5,3},{6,0},{7,1},{8,14},{9,15},{10,... | collective-permute-start | bytes 393224 | tf_op jit(solution)/shard_map/ppermute | solution.py:37
  42.3 8.4 %collective-permute-start.20 = (bf16[128,512]{1,0:T(8,128)(2,1)S(1)}, bf16[128,512]{1,0:T(8,128)(2,1)S(1)}, u32[]{:S(2)}, u32[]{:S(2)}) collective-permute-start(bf16[128,512]{1,0:T(8,128)(2,1)S(1)} %add_convert_fusion.1), channel_id=1, source_target_pairs={{0,2},{1,5},{2,0},{3,7},{4,6},{5,1},{6,4},{7,3},{8,10},{9,13},{10,... | collective-permute-start | bytes 393224 | tf_op jit(solution)/shard_map/ppermute | solution.py:37
  44.1 6.5 %collective-permute-start.22 = (bf16[128,512]{1,0:T(8,128)(2,1)S(1)}, bf16[128,512]{1,0:T(8,128)(2,1)S(1)}, u32[]{:S(2)}, u32[]{:S(2)}) collective-permute-start(bf16[128,512]{1,0:T(8,128)(2,1)S(1)} %add_convert_fusion), channel_id=1, source_target_pairs={{0,4},{1,3},{2,6},{3,1},{4,0},{5,7},{6,2},{7,5},{8,12},{9,11},{10,... | collective-permute-start | bytes 393224 | tf_op jit(solution)/shard_map/ppermute | solution.py:37
  50.8 6.3 %collective-permute-start.23 = (bf16[128,512]{1,0:T(8,128)(2,1)S(1)}, bf16[128,512]{1,0:T(8,128)(2,1)S(1)}, u32[]{:S(2)}, u32[]{:S(2)}) collective-permute-start(bf16[128,512]{1,0:T(8,128)(2,1)S(1)} %get-tuple-element.50), channel_id=1, source_target_pairs={{0,8},{1,17},{2,10},{3,19},{4,12},{5,21},{6,14},{7,23},{8,0},{9,25... | collective-permute-start | bytes 393224 | tf_op jit(solution)/shard_map/ppermute | solution.py:37
  57.1 6.1 %collective-permute-start.24 = (bf16[128,512]{1,0:T(8,128)(2,1)S(1)}, bf16[128,512]{1,0:T(8,128)(2,1)S(1)}, u32[]{:S(2)}, u32[]{:S(2)}) collective-permute-start(bf16[128,512]{1,0:T(8,128)(2,1)S(1)} %fusion.1), channel_id=1, source_target_pairs={{0,16},{1,9},{2,18},{3,11},{4,20},{5,13},{6,22},{7,15},{8,24},{9,1... | collective-permute-start | bytes 393224 | tf_op jit(solution)/shard_map/ppermute | solution.py:37
  63.3 5.9 %collective-permute-start.25 = (bf16[128,512]{1,0:T(8,128)(2,1)S(1)}, bf16[128,512]{1,0:T(8,128)(2,1)S(1)}, u32[]{:S(2)}, u32[]{:S(2)}) collective-permute-start(bf16[128,512]{1,0:T(8,128)(2,1)S(1)} %multiply_convert_fusion.refs_0_), channel_id=1, source_target_pairs={{0,6},{1,7},{2,4},{3,5},{4,2},{5,3},{6,0},{7,1},{8,14},{9,15},{10,... | collective-permute-start | bytes 393224 | tf_op jit(solution)/shard_map/ppermute | solution.py:37
  64.1 7.1 %collective-permute-start.28 = (bf16[128,512]{1,0:T(8,128)(2,1)S(1)}, bf16[128,512]{1,0:T(8,128)(2,1)S(1)}, u32[]{:S(2)}, u32[]{:S(2)}) collective-permute-start(bf16[128,512]{1,0:T(8,128)(2,1)S(1)} %multiply_convert_fusion.refs_0_), channel_id=1, source_target_pairs={{0,2},{1,5},{2,0},{3,7},{4,6},{5,1},{6,4},{7,3},{8,10},{9,13},{10,... | collective-permute-start | bytes 393224 | tf_op jit(solution)/shard_map/ppermute | solution.py:37
  66.9 5.0 %collective-permute-start.29 = (bf16[128,512]{1,0:T(8,128)(2,1)S(1)}, bf16[128,512]{1,0:T(8,128)(2,1)S(1)}, u32[]{:S(2)}, u32[]{:S(2)}) collective-permute-start(bf16[128,512]{1,0:T(8,128)(2,1)S(1)} %multiply_convert_fusion.refs_0_), channel_id=1, source_target_pairs={{0,4},{1,3},{2,6},{3,1},{4,0},{5,7},{6,2},{7,5},{8,12},{9,11},{10,... | collective-permute-start | bytes 393224 | tf_op jit(solution)/shard_map/ppermute | solution.py:37
  66.9 5.4 %collective-permute-start.26 = (bf16[128,512]{1,0:T(8,128)(2,1)S(1)}, bf16[128,512]{1,0:T(8,128)(2,1)S(1)}, u32[]{:S(2)}, u32[]{:S(2)}) collective-permute-start(bf16[128,512]{1,0:T(8,128)(2,1)S(1)} %multiply_convert_fusion.refs_0_), channel_id=1, source_target_pairs={{0,1},{1,0},{2,3},{3,2},{4,5},{5,4},{6,7},{7,6},{8,9},{9,8},{10,11... | collective-permute-start | bytes 393224 | tf_op jit(solution)/shard_map/ppermute | solution.py:37
  69.2 3.0 %collective-permute-start.27 = (bf16[128,512]{1,0:T(8,128)(2,1)S(1)}, bf16[128,512]{1,0:T(8,128)(2,1)S(1)}, u32[]{:S(2)}, u32[]{:S(2)}) collective-permute-start(bf16[128,512]{1,0:T(8,128)(2,1)S(1)} %collective-permute-done.25.refs_1_), channel_id=1, source_target_pairs={{0,1},{1,0},{2,3},{3,2},{4,5},{5,4},{6,7},{7,6},{8,9},{9,8},{10,11... | collective-permute-start | bytes 393224 | tf_op jit(solution)/shard_map/ppermute | solution.py:37
  71.2 1.8 %collective-permute-start.30 = (bf16[128,512]{1,0:T(8,128)(2,1)S(1)}, bf16[128,512]{1,0:T(8,128)(2,1)S(1)}, u32[]{:S(2)}, u32[]{:S(2)}) collective-permute-start(bf16[128,512]{1,0:T(8,128)(2,1)S(1)} %collective-permute-done.28.refs_0_), channel_id=1, source_target_pairs={{0,1},{1,0},{2,3},{3,2},{4,5},{5,4},{6,7},{7,6},{8,9},{9,8},{10,11... | collective-permute-start | bytes 393224 | tf_op jit(solution)/shard_map/ppermute | solution.py:37
  71.9 1.3 %collective-permute-start.31 = (bf16[128,512]{1,0:T(8,128)(2,1)S(1)}, bf16[128,512]{1,0:T(8,128)(2,1)S(1)}, u32[]{:S(2)}, u32[]{:S(2)}) collective-permute-start(bf16[128,512]{1,0:T(8,128)(2,1)S(1)} %collective-permute-done.29.refs_1_), channel_id=1, source_target_pairs={{0,1},{1,0},{2,3},{3,2},{4,5},{5,4},{6,7},{7,6},{8,9},{9,8},{10,11... | collective-permute-start | bytes 393224 | tf_op jit(solution)/shard_map/ppermute | solution.py:37
  73.9 1.4 %collective-permute-start.32 = (f32[128,128]{1,0:T(8,128)S(1)}, f32[128,128]{1,0:T(8,128)S(1)}, u32[]{:S(2)}, u32[]{:S(2)}) collective-permute-start(f32[128,128]{1,0:T(8,128)S(1)} %get-tuple-element.48), channel_id=1, source_target_pairs={{0,1},{1,0},{2,3},{3,2},{4,5},{5,4},{6,7},{7,6},{8,9},{9,8},{10,11... | collective-permute-start | bytes 196616 | tf_op jit(solution)/shard_map/ppermute | solution.py:37
  75.3 5.9 %collective-permute-start.33 = (f32[128,128]{1,0:T(8,128)S(1)}, f32[128,128]{1,0:T(8,128)S(1)}, u32[]{:S(2)}, u32[]{:S(2)}) collective-permute-start(f32[128,128]{1,0:T(8,128)S(1)} %add.90), channel_id=1, source_target_pairs={{0,6},{1,7},{2,4},{3,5},{4,2},{5,3},{6,0},{7,1},{8,14},{9,15},{10,... | collective-permute-start | bytes 196616 | tf_op jit(solution)/shard_map/ppermute | solution.py:37
  75.4 6.0 %collective-permute-start.34 = (f32[128,128]{1,0:T(8,128)S(1)}, f32[128,128]{1,0:T(8,128)S(1)}, u32[]{:S(2)}, u32[]{:S(2)}) collective-permute-start(f32[128,128]{1,0:T(8,128)S(1)} %add.90), channel_id=1, source_target_pairs={{0,2},{1,5},{2,0},{3,7},{4,6},{5,1},{6,4},{7,3},{8,10},{9,13},{10,... | collective-permute-start | bytes 196616 | tf_op jit(solution)/shard_map/ppermute | solution.py:37
  77.6 4.3 %collective-permute-start.35 = (f32[128,128]{1,0:T(8,128)S(1)}, f32[128,128]{1,0:T(8,128)S(1)}, u32[]{:S(2)}, u32[]{:S(2)}) collective-permute-start(f32[128,128]{1,0:T(8,128)S(1)} %add.90), channel_id=1, source_target_pairs={{0,4},{1,3},{2,6},{3,1},{4,0},{5,7},{6,2},{7,5},{8,12},{9,11},{10,... | collective-permute-start | bytes 196616 | tf_op jit(solution)/shard_map/ppermute | solution.py:37
  81.9 4.3 %collective-permute-start.36 = (f32[128,128]{1,0:T(8,128)S(1)}, f32[128,128]{1,0:T(8,128)S(1)}, u32[]{:S(2)}, u32[]{:S(2)}) collective-permute-start(f32[128,128]{1,0:T(8,128)S(1)} %add_add_fusion), channel_id=1, source_target_pairs={{0,8},{1,17},{2,10},{3,19},{4,12},{5,21},{6,14},{7,23},{8,0},{9,25... | collective-permute-start | bytes 196616 | tf_op jit(solution)/shard_map/ppermute | solution.py:37
  86.3 5.2 %collective-permute-start.37 = (f32[128,128]{1,0:T(8,128)S(1)}, f32[128,128]{1,0:T(8,128)S(1)}, u32[]{:S(2)}, u32[]{:S(2)}) collective-permute-start(f32[128,128]{1,0:T(8,128)S(1)} %add.94), channel_id=1, source_target_pairs={{0,16},{1,9},{2,18},{3,11},{4,20},{5,13},{6,22},{7,15},{8,24},{9,1... | collective-permute-start | bytes 196616 | tf_op jit(solution)/shard_map/ppermute | solution.py:37
  91.5 1.3 %collective-permute-start.38 = (f32[128,128]{1,0:T(8,128)S(1)}, f32[128,128]{1,0:T(8,128)S(1)}, u32[]{:S(2)}, u32[]{:S(2)}) collective-permute-start(f32[128,128]{1,0:T(8,128)S(1)} %add.95.own_ref), channel_id=1, source_target_pairs={{0,1},{1,0},{2,3},{3,2},{4,5},{5,4},{6,7},{7,6},{8,9},{9,8},{10,11... | collective-permute-start | bytes 196616 | tf_op jit(solution)/shard_map/ppermute | solution.py:37

commit v4 on v3

--- a/solution.py
+++ b/solution.py
@@ -69,39 +69,51 @@
         out_ref[...] = product.astype(out_ref.dtype)
 
 
-def load_kernel(swapped, basis_ref, rows_ref, *refs):
-    if not swapped:
-        rem_ref, *refs = refs
-    product_refs, (half_ref, kept_ref, *turned_refs, sems) = refs[:QUARTERS], refs[QUARTERS:]
-    columns = half_ref.shape[1]
-    start = pl.multiple_of(halves()[swapped] * columns, columns)
-    copy = pltpu.make_async_copy(basis_ref.at[:, pl.ds(start, columns)], half_ref, sems.at[0])
-    copy.start()
-    rows_copy = pltpu.make_async_copy(rows_ref, kept_ref, sems.at[1])
-    rows_copy.start()
-    rows_copy.wait()
-    if swapped:
-        rem = kept_ref[...].T
-        turned_refs[0][...] = rem
-    else:
-        rem = rem_ref[...]
-    copy.wait()
-    products(swapped, range(QUARTERS), rem, half_ref, product_refs)
-
-
-def load_call(swapped, basis, rows, rem):
-    height, atoms = basis.shape
-    block = rem.shape[1] if swapped else rem.shape[0]
-    shapes = [((block, atoms // (2 * QUARTERS)), BF16 if swapped else F32)] * QUARTERS
-    shapes += [((height, atoms // 2), BF16), (rows.shape, BF16)]
-    if swapped:
-        shapes.append(((block, height), BF16))
-    basis, rows = (pltpu.with_memory_space_constraint(v, pltpu.HBM) for v in (basis, rows))
-    kernel = functools.partial(load_kernel, swapped)
-    operands = [basis, rows] if swapped else [basis, rows, rem]
-    specs = [HBM, HBM, VMEM][: len(operands)]
-    scratch = [pltpu.SemaphoreType.DMA((2,))]
-    return call(kernel, shapes, basis.size * block, *operands, in_specs=specs, scratch=scratch)
+def load_kernel(basis_ref, atoms_ref, user_ref, *refs):
+    other_refs, own_refs, refs = refs[:QUARTERS], refs[QUARTERS : 2 * QUARTERS], refs[2 * QUARTERS :]
+    other_half_ref, own_half_ref, user_rows_ref, turned_ref, rows_ref, sems = refs
+    own, other = halves()
+
+    def half_copy(half, half_ref, sem):
+        columns = half_ref.shape[1]
+        start = pl.multiple_of(half * columns, columns)
+        return pltpu.make_async_copy(basis_ref.at[:, pl.ds(start, columns)], half_ref, sem)
+
+    copies = [
+        pltpu.make_async_copy(atoms_ref, rows_ref, sems.at[0]),
+        half_copy(other, other_half_ref, sems.at[1]),
+        half_copy(own, own_half_ref, sems.at[2]),
+        pltpu.make_async_copy(user_ref, user_rows_ref, sems.at[3]),
+    ]
+    for copy in copies:
+        copy.start()
+    copies[0].wait()
+    rem = rows_ref[...].T
+    turned_ref[...] = rem
+    copies[1].wait()
+    products(1, range(QUARTERS), rem, other_half_ref, other_refs)
+    copies[2].wait()
+    products(0, range(QUARTERS), rem, own_half_ref, own_refs)
+    copies[3].wait()
+
+
+def first_products(basis, atoms, user_residuals):
+    rows, count = basis.shape
+    block = atoms.shape[1]
+    product = (block, count // (2 * QUARTERS))
+    half = ((rows, count // 2), BF16)
+    shapes = [(product, BF16)] * QUARTERS + [(product, F32)] * QUARTERS
+    shapes += [half, half, (user_residuals.shape, BF16), ((block, rows), BF16)]
+    arrays = [pltpu.with_memory_space_constraint(v, pltpu.HBM) for v in (basis, atoms, user_residuals)]
+    results = call(
+        load_kernel,
+        shapes,
+        2 * atoms.size * count,
+        *arrays,
+        in_specs=[HBM] * 3,
+        scratch=[pltpu.VMEM(atoms.shape, BF16), pltpu.SemaphoreType.DMA((4,))],
+    )
+    return results[:QUARTERS], results[QUARTERS : 2 * QUARTERS], *results[2 * QUARTERS :]
 
 
 def coef_kernel(swapped, places, basis_ref, rem_ref, *out_refs):
@@ -294,8 +306,7 @@
     if not power or not tiled or block != 128 or user_residuals.shape[1] != block:
         return plain_local(old_basis, new_atoms, user_residuals)
 
-    *other, other_half, _, rem_low = load_call(True, old_basis, new_atoms, new_atoms)
-    *own, own_half, user_rows = load_call(False, old_basis, user_residuals, rem_low)
+    other, own, other_half, own_half, user_rows, rem_low = first_products(old_basis, new_atoms, user_residuals)
     rem = rem_low
     for last in (False, True):
         if last:

time: 98.2 us -> 96.7 us (0.985)
  Pallas kernels: 13.8 us -> 12 us
    pallas_call x15 -> x14, Pallas kernels: 13.8 us -> 12 us  [call(): pl.pallas_call(kernel, in_specs=in_specs or [VMEM] * len(operands), out_s...]
  transfers between devices with their start and end apart: 39 -> 39, of which waited for: 23 -> 24; matrix products, arithmetic and copies ran while one was open for 0% -> 0% of each run, Pallas kernels for 5% -> 3%
where the time goes in v4:
time: 96.7 us; the launch traced here: 96.6 us
  waiting for transfers between devices  49.7 us (51%)
  starting transfers between devices  33.5 us (35%)
  Pallas kernels  12 us (12%)
    ppermute x39, waiting for transfers between devices, swap(): lax.ppermute(value, 'rows', [(i, i ^ masks[i & 1]) for i in range(size)])  49.7 us
    ppermute x39, starting transfers between devices, swap(): lax.ppermute(value, 'rows', [(i, i ^ masks[i & 1]) for i in range(size)])  33.5 us
    pallas_call x14, Pallas kernels, call(): pl.pallas_call(kernel, in_specs=in_specs or [VMEM] * len(operands), out_s...  12 us
  transfers between devices with their start and end apart: 39, of which 24 were waited for; matrix products, arithmetic and copies ran while one was open for 0% of the time, Pallas kernels for 3%

profile of v4, /device:TPU:0, one launch (start us, length us, event | category | flops | bytes accessed | tf_op | source)
XLA Modules:
  0.0 96.6 jit_solution(561760563398513229)
XLA Ops:
  0.6 2.4 %shard_map.50 = (bf16[128,512]{1,0:T(8,128)(2,1)S(1)}, bf16[128,512]{1,0:T(8,128)(2,1)S(1)}, bf16[128,512]{1,0:T(8,128)(2,1)S(1)}, bf16[128,512]{1,0:T(8,128)(2,...) custom-call(bf16[384,4096]{1,0:T(8,128)(2,1)} %basis_ref.1, ...), custom_call_target="tpu_custom_call" | custom-call | flops 402653184 | tf_op jit(solution)/shard_map/pallas_call | solution.py:41
  3.1 0.5 collective-permute-start.1
  3.7 0.4 collective-permute-start.5
  4.2 0.4 collective-permute-done.1
  4.6 3.9 %collective-permute-start.2 = (bf16[128,512]{1,0:T(8,128)(2,1)S(1)}, bf16[128,512]{1,0:T(8,128)(2,1)S(1)}, u32[]{:S(2)}, u32[]{:S(2)}) collective-permute-start(bf16[128,512]{1,0:T(8,128)(2,1)S(1)} %add_convert_fusion.5), channel_id=1, source_target_pairs={{0,6},{1,7},{2,4},{3,5},{4,2},{5,3},{6,0},{7,1},{8,14},{9,15},{10,... | collective-permute-start | bytes 393224 | tf_op jit(solution)/shard_map/ppermute | solution.py:37
  8.5 0.6 collective-permute-start.4
  9.1 0.2 collective-permute-start.6
  9.3 3.1 %collective-permute-done.2 = bf16[128,512]{1,0:T(8,128)(2,1)S(1)} collective-permute-done((bf16[128,512]{1,0:T(8,128)(2,1)S(1)}, bf16[128,512]{1,0:T(8,128)(2,1)S(1)}, u32[]{:S(2)}, u32[]{:S(2)}) %collective-permute-start.2) | collective-permute-done | bytes 131104 | tf_op jit(solution)/shard_map/ppermute | solution.py:37
  12.4 3.0 %collective-permute-done.4 = bf16[128,512]{1,0:T(8,128)(2,1)S(1)} collective-permute-done((bf16[128,512]{1,0:T(8,128)(2,1)S(1)}, bf16[128,512]{1,0:T(8,128)(2,1)S(1)}, u32[]{:S(2)}, u32[]{:S(2)}) %collective-permute-start.4) | collective-permute-done | bytes 131104 | tf_op jit(solution)/shard_map/ppermute | solution.py:37
  15.5 1.6 %collective-permute-start.7 = (bf16[128,512]{1,0:T(8,128)(2,1)S(1)}, bf16[128,512]{1,0:T(8,128)(2,1)S(1)}, u32[]{:S(2)}, u32[]{:S(2)}) collective-permute-start(bf16[128,512]{1,0:T(8,128)(2,1)S(1)} %get-tuple-element.52), channel_id=1, source_target_pairs={{0,8},{1,17},{2,10},{3,19},{4,12},{5,21},{6,14},{7,23},{8,0},{9,25... | collective-permute-start | bytes 393224 | tf_op jit(solution)/shard_map/ppermute | solution.py:37
  17.1 4.2 %collective-permute-done.7 = bf16[128,512]{1,0:T(8,128)(2,1)S(1)} collective-permute-done((bf16[128,512]{1,0:T(8,128)(2,1)S(1)}, bf16[128,512]{1,0:T(8,128)(2,1)S(1)}, u32[]{:S(2)}, u32[]{:S(2)}) %collective-permute-start.7) | collective-permute-done | bytes 131104 | tf_op jit(solution)/shard_map/ppermute | solution.py:37
  21.3 2.3 %collective-permute-start.8 = (bf16[128,512]{1,0:T(8,128)(2,1)S(1)}, bf16[128,512]{1,0:T(8,128)(2,1)S(1)}, u32[]{:S(2)}, u32[]{:S(2)}) collective-permute-start(bf16[128,512]{1,0:T(8,128)(2,1)S(1)} %fusion), channel_id=1, source_target_pairs={{0,16},{1,9},{2,18},{3,11},{4,20},{5,13},{6,22},{7,15},{8,24},{9,1... | collective-permute-start | bytes 393224 | tf_op jit(solution)/shard_map/ppermute | solution.py:37
  23.6 3.6 %collective-permute-done.8 = bf16[128,512]{1,0:T(8,128)(2,1)S(1)} collective-permute-done((bf16[128,512]{1,0:T(8,128)(2,1)S(1)}, bf16[128,512]{1,0:T(8,128)(2,1)S(1)}, u32[]{:S(2)}, u32[]{:S(2)}) %collective-permute-start.8) | collective-permute-done | bytes 131104 | tf_op jit(solution)/shard_map/ppermute | solution.py:37
  27.3 1.6 %collective-permute-start.9 = (bf16[128,512]{1,0:T(8,128)(2,1)S(1)}, bf16[128,512]{1,0:T(8,128)(2,1)S(1)}, u32[]{:S(2)}, u32[]{:S(2)}) collective-permute-start(bf16[128,512]{1,0:T(8,128)(2,1)S(1)} %multiply_convert_fusion.1.refs_0_), channel_id=1, source_target_pairs={{0,6},{1,7},{2,4},{3,5},{4,2},{5,3},{6,0},{7,1},{8,14},{9,15},{10,... | collective-permute-start | bytes 393224 | tf_op jit(solution)/shard_map/ppermute | solution.py:37
  28.8 2.4 %collective-permute-start.12 = (bf16[128,512]{1,0:T(8,128)(2,1)S(1)}, bf16[128,512]{1,0:T(8,128)(2,1)S(1)}, u32[]{:S(2)}, u32[]{:S(2)}) collective-permute-start(bf16[128,512]{1,0:T(8,128)(2,1)S(1)} %multiply_convert_fusion.1.refs_0_), channel_id=1, source_target_pairs={{0,2},{1,5},{2,0},{3,7},{4,6},{5,1},{6,4},{7,3},{8,10},{9,13},{10,... | collective-permute-start | bytes 393224 | tf_op jit(solution)/shard_map/ppermute | solution.py:37
  31.2 2.0 %collective-permute-done.9.refs_1_ = bf16[128,512]{1,0:T(8,128)(2,1)S(1)} collective-permute-done((bf16[128,512]{1,0:T(8,128)(2,1)S(1)}, bf16[128,512]{1,0:T(8,128)(2,1)S(1)}, u32[]{:S(2)}, u32[]{:S(2)}) %collective-permute-start.9) | collective-permute-done | bytes 131104 | tf_op jit(solution)/shard_map/ppermute | solution.py:37
  33.2 2.4 %collective-permute-done.12.refs_0_ = bf16[128,512]{1,0:T(8,128)(2,1)S(1)} collective-permute-done((bf16[128,512]{1,0:T(8,128)(2,1)S(1)}, bf16[128,512]{1,0:T(8,128)(2,1)S(1)}, u32[]{:S(2)}, u32[]{:S(2)}) %collective-permute-start.12) | collective-permute-done | bytes 131104 | tf_op jit(solution)/shard_map/ppermute | solution.py:37
  35.6 0.6 collective-permute-done.13.refs_1_
  36.2 0.4 shard_map.51.rem_ref
  36.6 0.4 shard_map.52.rem_ref
  37.0 0.4 shard_map.53.rem_ref
  37.4 0.1 collective-permute-done.15.refs_1_
  37.6 0.4 shard_map.54
  37.9 0.2 shard_map.57
  38.2 0.5 collective-permute-start.17
  38.7 0.4 shard_map.56
  39.0 0.2 collective-permute-start.19
  39.2 0.4 collective-permute-start.21
  39.6 0.1 collective-permute-start.16
  39.7 0.4 shard_map.55
  40.2 0.5 collective-permute-start.18
  40.8 1.9 %collective-permute-start.20 = (bf16[128,512]{1,0:T(8,128)(2,1)S(1)}, bf16[128,512]{1,0:T(8,128)(2,1)S(1)}, u32[]{:S(2)}, u32[]{:S(2)}) collective-permute-start(bf16[128,512]{1,0:T(8,128)(2,1)S(1)} %add_convert_fusion.1), channel_id=1, source_target_pairs={{0,2},{1,5},{2,0},{3,7},{4,6},{5,1},{6,4},{7,3},{8,10},{9,13},{10,... | collective-permute-start | bytes 393224 | tf_op jit(solution)/shard_map/ppermute | solution.py:37
  42.7 1.3 %collective-permute-start.22 = (bf16[128,512]{1,0:T(8,128)(2,1)S(1)}, bf16[128,512]{1,0:T(8,128)(2,1)S(1)}, u32[]{:S(2)}, u32[]{:S(2)}) collective-permute-start(bf16[128,512]{1,0:T(8,128)(2,1)S(1)} %add_convert_fusion), channel_id=1, source_target_pairs={{0,4},{1,3},{2,6},{3,1},{4,0},{5,7},{6,2},{7,5},{8,12},{9,11},{10,... | collective-permute-start | bytes 393224 | tf_op jit(solution)/shard_map/ppermute | solution.py:37
  44.0 3.6 %collective-permute-done.18 = bf16[128,512]{1,0:T(8,128)(2,1)S(1)} collective-permute-done((bf16[128,512]{1,0:T(8,128)(2,1)S(1)}, bf16[128,512]{1,0:T(8,128)(2,1)S(1)}, u32[]{:S(2)}, u32[]{:S(2)}) %collective-permute-start.18) | collective-permute-done | bytes 131104 | tf_op jit(solution)/shard_map/ppermute | solution.py:37
  47.5 1.7 %collective-permute-done.20 = bf16[128,512]{1,0:T(8,128)(2,1)S(1)} collective-permute-done((bf16[128,512]{1,0:T(8,128)(2,1)S(1)}, bf16[128,512]{1,0:T(8,128)(2,1)S(1)}, u32[]{:S(2)}, u32[]{:S(2)}) %collective-permute-start.20) | collective-permute-done | bytes 131104 | tf_op jit(solution)/shard_map/ppermute | solution.py:37
  49.3 1.8 %collective-permute-start.23 = (bf16[128,512]{1,0:T(8,128)(2,1)S(1)}, bf16[128,512]{1,0:T(8,128)(2,1)S(1)}, u32[]{:S(2)}, u32[]{:S(2)}) collective-permute-start(bf16[128,512]{1,0:T(8,128)(2,1)S(1)} %get-tuple-element.50), channel_id=1, source_target_pairs={{0,8},{1,17},{2,10},{3,19},{4,12},{5,21},{6,14},{7,23},{8,0},{9,25... | collective-permute-start | bytes 393224 | tf_op jit(solution)/shard_map/ppermute | solution.py:37
  51.2 4.6 %collective-permute-done.23 = bf16[128,512]{1,0:T(8,128)(2,1)S(1)} collective-permute-done((bf16[128,512]{1,0:T(8,128)(2,1)S(1)}, bf16[128,512]{1,0:T(8,128)(2,1)S(1)}, u32[]{:S(2)}, u32[]{:S(2)}) %collective-permute-start.23) | collective-permute-done | bytes 131104 | tf_op jit(solution)/shard_map/ppermute | solution.py:37
  55.8 2.3 %collective-permute-start.24 = (bf16[128,512]{1,0:T(8,128)(2,1)S(1)}, bf16[128,512]{1,0:T(8,128)(2,1)S(1)}, u32[]{:S(2)}, u32[]{:S(2)}) collective-permute-start(bf16[128,512]{1,0:T(8,128)(2,1)S(1)} %fusion.1), channel_id=1, source_target_pairs={{0,16},{1,9},{2,18},{3,11},{4,20},{5,13},{6,22},{7,15},{8,24},{9,1... | collective-permute-start | bytes 393224 | tf_op jit(solution)/shard_map/ppermute | solution.py:37
  58.0 3.8 %collective-permute-done.24 = bf16[128,512]{1,0:T(8,128)(2,1)S(1)} collective-permute-done((bf16[128,512]{1,0:T(8,128)(2,1)S(1)}, bf16[128,512]{1,0:T(8,128)(2,1)S(1)}, u32[]{:S(2)}, u32[]{:S(2)}) %collective-permute-start.24) | collective-permute-done | bytes 131104 | tf_op jit(solution)/shard_map/ppermute | solution.py:37
  61.9 0.8 collective-permute-start.25
  62.7 2.8 %collective-permute-start.28 = (bf16[128,512]{1,0:T(8,128)(2,1)S(1)}, bf16[128,512]{1,0:T(8,128)(2,1)S(1)}, u32[]{:S(2)}, u32[]{:S(2)}) collective-permute-start(bf16[128,512]{1,0:T(8,128)(2,1)S(1)} %multiply_convert_fusion.refs_0_), channel_id=1, source_target_pairs={{0,2},{1,5},{2,0},{3,7},{4,6},{5,1},{6,4},{7,3},{8,10},{9,13},{10,... | collective-permute-start | bytes 393224 | tf_op jit(solution)/shard_map/ppermute | solution.py:37
  65.5 2.4 %collective-permute-done.25.refs_1_ = bf16[128,512]{1,0:T(8,128)(2,1)S(1)} collective-permute-done((bf16[128,512]{1,0:T(8,128)(2,1)S(1)}, bf16[128,512]{1,0:T(8,128)(2,1)S(1)}, u32[]{:S(2)}, u32[]{:S(2)}) %collective-permute-start.25) | collective-permute-done | bytes 131104 | tf_op jit(solution)/shard_map/ppermute | solution.py:37
  67.9 1.9 %collective-permute-done.28.refs_0_ = bf16[128,512]{1,0:T(8,128)(2,1)S(1)} collective-permute-done((bf16[128,512]{1,0:T(8,128)(2,1)S(1)}, bf16[128,512]{1,0:T(8,128)(2,1)S(1)}, u32[]{:S(2)}, u32[]{:S(2)}) %collective-permute-start.28) | collective-permute-done | bytes 131104 | tf_op jit(solution)/shard_map/ppermute | solution.py:37
  69.8 0.6 collective-permute-done.29.refs_1_
  70.5 0.4 shard_map.58.rem_ref
  70.9 0.4 shard_map.59.rem_ref
  71.3 0.4 shard_map.60.rem_ref
  71.7 0.1 collective-permute-done.31.refs_1_
  71.8 0.4 shard_map.61.turned_ref
  72.2 0.3 shard_map.62
  72.4 0.5 collective-permute-start.32
  72.9 0.9 collective-permute-done.32
  73.8 0.1 collective-permute-start.33
  74.0 2.2 %collective-permute-start.34 = (f32[128,128]{1,0:T(8,128)S(1)}, f32[128,128]{1,0:T(8,128)S(1)}, u32[]{:S(2)}, u32[]{:S(2)}) collective-permute-start(f32[128,128]{1,0:T(8,128)S(1)} %add.90), channel_id=1, source_target_pairs={{0,2},{1,5},{2,0},{3,7},{4,6},{5,1},{6,4},{7,3},{8,10},{9,13},{10,... | collective-permute-start | bytes 196616 | tf_op jit(solution)/shard_map/ppermute | solution.py:37
  76.2 1.2 %collective-permute-start.35 = (f32[128,128]{1,0:T(8,128)S(1)}, f32[128,128]{1,0:T(8,128)S(1)}, u32[]{:S(2)}, u32[]{:S(2)}) collective-permute-start(f32[128,128]{1,0:T(8,128)S(1)} %add.90), channel_id=1, source_target_pairs={{0,4},{1,3},{2,6},{3,1},{4,0},{5,7},{6,2},{7,5},{8,12},{9,11},{10,... | collective-permute-start | bytes 196616 | tf_op jit(solution)/shard_map/ppermute | solution.py:37
  77.4 2.3 %collective-permute-done.33 = f32[128,128]{1,0:T(8,128)S(1)} collective-permute-done((f32[128,128]{1,0:T(8,128)S(1)}, f32[128,128]{1,0:T(8,128)S(1)}, u32[]{:S(2)}, u32[]{:S(2)}) %collective-permute-start.33) | collective-permute-done | bytes 65568 | tf_op jit(solution)/shard_map/ppermute | solution.py:37
  79.7 0.2 collective-permute-done.34
  79.9 0.5 collective-permute-done.35
  80.5 1.1 %collective-permute-start.36 = (f32[128,128]{1,0:T(8,128)S(1)}, f32[128,128]{1,0:T(8,128)S(1)}, u32[]{:S(2)}, u32[]{:S(2)}) collective-permute-start(f32[128,128]{1,0:T(8,128)S(1)} %add_add_fusion), channel_id=1, source_target_pairs={{0,8},{1,17},{2,10},{3,19},{4,12},{5,21},{6,14},{7,23},{8,0},{9,25... | collective-permute-start | bytes 196616 | tf_op jit(solution)/shard_map/ppermute | solution.py:37
  81.6 3.2 %collective-permute-done.36 = f32[128,128]{1,0:T(8,128)S(1)} collective-permute-done((f32[128,128]{1,0:T(8,128)S(1)}, f32[128,128]{1,0:T(8,128)S(1)}, u32[]{:S(2)}, u32[]{:S(2)}) %collective-permute-start.36) | collective-permute-done | bytes 65568 | tf_op jit(solution)/shard_map/ppermute | solution.py:37
  84.8 2.1 %collective-permute-start.37 = (f32[128,128]{1,0:T(8,128)S(1)}, f32[128,128]{1,0:T(8,128)S(1)}, u32[]{:S(2)}, u32[]{:S(2)}) collective-permute-start(f32[128,128]{1,0:T(8,128)S(1)} %add.94), channel_id=1, source_target_pairs={{0,16},{1,9},{2,18},{3,11},{4,20},{5,13},{6,22},{7,15},{8,24},{9,1... | collective-permute-start | bytes 196616 | tf_op jit(solution)/shard_map/ppermute | solution.py:37
  86.9 3.1 %collective-permute-done.37 = f32[128,128]{1,0:T(8,128)S(1)} collective-permute-done((f32[128,128]{1,0:T(8,128)S(1)}, f32[128,128]{1,0:T(8,128)S(1)}, u32[]{:S(2)}, u32[]{:S(2)}) %collective-permute-start.37) | collective-permute-done | bytes 65568 | tf_op jit(solution)/shard_map/ppermute | solution.py:37
  90.2 1.2 %collective-permute-done.38.other_ref = f32[128,128]{1,0:T(8,128)S(1)} collective-permute-done((f32[128,128]{1,0:T(8,128)S(1)}, f32[128,128]{1,0:T(8,128)S(1)}, u32[]{:S(2)}, u32[]{:S(2)}) %collective-permute-start.38) | collective-permute-done | bytes 65568 | tf_op jit(solution)/shard_map/ppermute | solution.py:37
  91.4 5.2 %shard_map.63 = (bf16[384,128]{1,0:T(8,128)(2,1)}, bf16[384,128]{1,0:T(8,128)(2,1)}) custom-call(f32[128,128]{1,0:T(8,128)S(1)} %add.95.own_ref, f32[128,128]{1,0:T(8,128)S(1)} %collective-permute-done.38.other_ref, bf16[384,128]{1,0:T(8,128)(2,1)S(1)} %get-tuple-element.49.rem_ref, bf16[384,128]{1,0:T(8,128)(2,1)S(1)} %get-tuple-element.46.user_ref), custom_call_target="tpu_custom_call" | custom-call | tf_op jit(solution)/shard_map/pallas_call | solution.py:41
  (44 shorter events, 0.8 us)
Async XLA Ops:
  3.1 1.5 %collective-permute-start.1 = (bf16[128,512]{1,0:T(8,128)(2,1)S(1)}, bf16[128,512]{1,0:T(8,128)(2,1)S(1)}, u32[]{:S(2)}, u32[]{:S(2)}) collective-permute-start(bf16[128,512]{1,0:T(8,128)(2,1)S(1)} %get-tuple-element.32), channel_id=1, source_target_pairs={{0,1},{1,0},{2,3},{3,2},{4,5},{5,4},{6,7},{7,6},{8,9},{9,8},{10,11... | collective-permute-start | bytes 393224 | tf_op jit(solution)/shard_map/ppermute | solution.py:37
  3.6 4.9 %collective-permute-start.3 = (bf16[128,512]{1,0:T(8,128)(2,1)S(1)}, bf16[128,512]{1,0:T(8,128)(2,1)S(1)}, u32[]{:S(2)}, u32[]{:S(2)}) collective-permute-start(bf16[128,512]{1,0:T(8,128)(2,1)S(1)} %get-tuple-element.34), channel_id=1, source_target_pairs={{0,1},{1,0},{2,3},{3,2},{4,5},{5,4},{6,7},{7,6},{8,9},{9,8},{10,11... | collective-permute-start | bytes 393224 | tf_op jit(solution)/shard_map/ppermute | solution.py:37
  3.7 5.5 %collective-permute-start.5 = (bf16[128,512]{1,0:T(8,128)(2,1)S(1)}, bf16[128,512]{1,0:T(8,128)(2,1)S(1)}, u32[]{:S(2)}, u32[]{:S(2)}) collective-permute-start(bf16[128,512]{1,0:T(8,128)(2,1)S(1)} %get-tuple-element.36), channel_id=1, source_target_pairs={{0,1},{1,0},{2,3},{3,2},{4,5},{5,4},{6,7},{7,6},{8,9},{9,8},{10,11... | collective-permute-start | bytes 393224 | tf_op jit(solution)/shard_map/ppermute | solution.py:37
  4.1 5.2 %collective-permute-start = (bf16[128,512]{1,0:T(8,128)(2,1)S(1)}, bf16[128,512]{1,0:T(8,128)(2,1)S(1)}, u32[]{:S(2)}, u32[]{:S(2)}) collective-permute-start(bf16[128,512]{1,0:T(8,128)(2,1)S(1)} %get-tuple-element.30), channel_id=1, source_target_pairs={{0,1},{1,0},{2,3},{3,2},{4,5},{5,4},{6,7},{7,6},{8,9},{9,8},{10,11... | collective-permute-start | bytes 393224 | tf_op jit(solution)/shard_map/ppermute | solution.py:37
  4.6 7.8 %collective-permute-start.2 = (bf16[128,512]{1,0:T(8,128)(2,1)S(1)}, bf16[128,512]{1,0:T(8,128)(2,1)S(1)}, u32[]{:S(2)}, u32[]{:S(2)}) collective-permute-start(bf16[128,512]{1,0:T(8,128)(2,1)S(1)} %add_convert_fusion.5), channel_id=1, source_target_pairs={{0,6},{1,7},{2,4},{3,5},{4,2},{5,3},{6,0},{7,1},{8,14},{9,15},{10,... | collective-permute-start | bytes 393224 | tf_op jit(solution)/shard_map/ppermute | solution.py:37
  8.5 6.9 %collective-permute-start.4 = (bf16[128,512]{1,0:T(8,128)(2,1)S(1)}, bf16[128,512]{1,0:T(8,128)(2,1)S(1)}, u32[]{:S(2)}, u32[]{:S(2)}) collective-permute-start(bf16[128,512]{1,0:T(8,128)(2,1)S(1)} %add_convert_fusion.4), channel_id=1, source_target_pairs={{0,2},{1,5},{2,0},{3,7},{4,6},{5,1},{6,4},{7,3},{8,10},{9,13},{10,... | collective-permute-start | bytes 393224 | tf_op jit(solution)/shard_map/ppermute | solution.py:37
  9.1 6.2 %collective-permute-start.6 = (bf16[128,512]{1,0:T(8,128)(2,1)S(1)}, bf16[128,512]{1,0:T(8,128)(2,1)S(1)}, u32[]{:S(2)}, u32[]{:S(2)}) collective-permute-start(bf16[128,512]{1,0:T(8,128)(2,1)S(1)} %add_convert_fusion.3), channel_id=1, source_target_pairs={{0,4},{1,3},{2,6},{3,1},{4,0},{5,7},{6,2},{7,5},{8,12},{9,11},{10,... | collective-permute-start | bytes 393224 | tf_op jit(solution)/shard_map/ppermute | solution.py:37
  15.5 5.8 %collective-permute-start.7 = (bf16[128,512]{1,0:T(8,128)(2,1)S(1)}, bf16[128,512]{1,0:T(8,128)(2,1)S(1)}, u32[]{:S(2)}, u32[]{:S(2)}) collective-permute-start(bf16[128,512]{1,0:T(8,128)(2,1)S(1)} %get-tuple-element.52), channel_id=1, source_target_pairs={{0,8},{1,17},{2,10},{3,19},{4,12},{5,21},{6,14},{7,23},{8,0},{9,25... | collective-permute-start | bytes 393224 | tf_op jit(solution)/shard_map/ppermute | solution.py:37
  21.3 5.9 %collective-permute-start.8 = (bf16[128,512]{1,0:T(8,128)(2,1)S(1)}, bf16[128,512]{1,0:T(8,128)(2,1)S(1)}, u32[]{:S(2)}, u32[]{:S(2)}) collective-permute-start(bf16[128,512]{1,0:T(8,128)(2,1)S(1)} %fusion), channel_id=1, source_target_pairs={{0,16},{1,9},{2,18},{3,11},{4,20},{5,13},{6,22},{7,15},{8,24},{9,1... | collective-permute-start | bytes 393224 | tf_op jit(solution)/shard_map/ppermute | solution.py:37
  27.3 5.9 %collective-permute-start.9 = (bf16[128,512]{1,0:T(8,128)(2,1)S(1)}, bf16[128,512]{1,0:T(8,128)(2,1)S(1)}, u32[]{:S(2)}, u32[]{:S(2)}) collective-permute-start(bf16[128,512]{1,0:T(8,128)(2,1)S(1)} %multiply_convert_fusion.1.refs_0_), channel_id=1, source_target_pairs={{0,6},{1,7},{2,4},{3,5},{4,2},{5,3},{6,0},{7,1},{8,14},{9,15},{10,... | collective-permute-start | bytes 393224 | tf_op jit(solution)/shard_map/ppermute | solution.py:37
  28.8 6.7 %collective-permute-start.12 = (bf16[128,512]{1,0:T(8,128)(2,1)S(1)}, bf16[128,512]{1,0:T(8,128)(2,1)S(1)}, u32[]{:S(2)}, u32[]{:S(2)}) collective-permute-start(bf16[128,512]{1,0:T(8,128)(2,1)S(1)} %multiply_convert_fusion.1.refs_0_), channel_id=1, source_target_pairs={{0,2},{1,5},{2,0},{3,7},{4,6},{5,1},{6,4},{7,3},{8,10},{9,13},{10,... | collective-permute-start | bytes 393224 | tf_op jit(solution)/shard_map/ppermute | solution.py:37
  31.2 5.0 %collective-permute-start.13 = (bf16[128,512]{1,0:T(8,128)(2,1)S(1)}, bf16[128,512]{1,0:T(8,128)(2,1)S(1)}, u32[]{:S(2)}, u32[]{:S(2)}) collective-permute-start(bf16[128,512]{1,0:T(8,128)(2,1)S(1)} %multiply_convert_fusion.1.refs_0_), channel_id=1, source_target_pairs={{0,4},{1,3},{2,6},{3,1},{4,0},{5,7},{6,2},{7,5},{8,12},{9,11},{10,... | collective-permute-start | bytes 393224 | tf_op jit(solution)/shard_map/ppermute | solution.py:37
  31.2 5.4 %collective-permute-start.10 = (bf16[128,512]{1,0:T(8,128)(2,1)S(1)}, bf16[128,512]{1,0:T(8,128)(2,1)S(1)}, u32[]{:S(2)}, u32[]{:S(2)}) collective-permute-start(bf16[128,512]{1,0:T(8,128)(2,1)S(1)} %multiply_convert_fusion.1.refs_0_), channel_id=1, source_target_pairs={{0,1},{1,0},{2,3},{3,2},{4,5},{5,4},{6,7},{7,6},{8,9},{9,8},{10,11... | collective-permute-start | bytes 393224 | tf_op jit(solution)/shard_map/ppermute | solution.py:37
  33.2 3.4 %collective-permute-start.11 = (bf16[128,512]{1,0:T(8,128)(2,1)S(1)}, bf16[128,512]{1,0:T(8,128)(2,1)S(1)}, u32[]{:S(2)}, u32[]{:S(2)}) collective-permute-start(bf16[128,512]{1,0:T(8,128)(2,1)S(1)} %collective-permute-done.9.refs_1_), channel_id=1, source_target_pairs={{0,1},{1,0},{2,3},{3,2},{4,5},{5,4},{6,7},{7,6},{8,9},{9,8},{10,11... | collective-permute-start | bytes 393224 | tf_op jit(solution)/shard_map/ppermute | solution.py:37
  35.6 1.8 %collective-permute-start.14 = (bf16[128,512]{1,0:T(8,128)(2,1)S(1)}, bf16[128,512]{1,0:T(8,128)(2,1)S(1)}, u32[]{:S(2)}, u32[]{:S(2)}) collective-permute-start(bf16[128,512]{1,0:T(8,128)(2,1)S(1)} %collective-permute-done.12.refs_0_), channel_id=1, source_target_pairs={{0,1},{1,0},{2,3},{3,2},{4,5},{5,4},{6,7},{7,6},{8,9},{9,8},{10,11... | collective-permute-start | bytes 393224 | tf_op jit(solution)/shard_map/ppermute | solution.py:37
  36.2 1.3 %collective-permute-start.15 = (bf16[128,512]{1,0:T(8,128)(2,1)S(1)}, bf16[128,512]{1,0:T(8,128)(2,1)S(1)}, u32[]{:S(2)}, u32[]{:S(2)}) collective-permute-start(bf16[128,512]{1,0:T(8,128)(2,1)S(1)} %collective-permute-done.13.refs_1_), channel_id=1, source_target_pairs={{0,1},{1,0},{2,3},{3,2},{4,5},{5,4},{6,7},{7,6},{8,9},{9,8},{10,11... | collective-permute-start | bytes 393224 | tf_op jit(solution)/shard_map/ppermute | solution.py:37
  38.2 2.0 %collective-permute-start.17 = (bf16[128,512]{1,0:T(8,128)(2,1)S(1)}, bf16[128,512]{1,0:T(8,128)(2,1)S(1)}, u32[]{:S(2)}, u32[]{:S(2)}) collective-permute-start(bf16[128,512]{1,0:T(8,128)(2,1)S(1)} %shard_map.57), channel_id=1, source_target_pairs={{0,1},{1,0},{2,3},{3,2},{4,5},{5,4},{6,7},{7,6},{8,9},{9,8},{10,11... | collective-permute-start | bytes 393224 | tf_op jit(solution)/shard_map/ppermute | solution.py:37
  39.0 1.7 %collective-permute-start.19 = (bf16[128,512]{1,0:T(8,128)(2,1)S(1)}, bf16[128,512]{1,0:T(8,128)(2,1)S(1)}, u32[]{:S(2)}, u32[]{:S(2)}) collective-permute-start(bf16[128,512]{1,0:T(8,128)(2,1)S(1)} %get-tuple-element.43), channel_id=1, source_target_pairs={{0,1},{1,0},{2,3},{3,2},{4,5},{5,4},{6,7},{7,6},{8,9},{9,8},{10,11... | collective-permute-start | bytes 393224 | tf_op jit(solution)/shard_map/ppermute | solution.py:37
  39.2 3.5 %collective-permute-start.21 = (bf16[128,512]{1,0:T(8,128)(2,1)S(1)}, bf16[128,512]{1,0:T(8,128)(2,1)S(1)}, u32[]{:S(2)}, u32[]{:S(2)}) collective-permute-start(bf16[128,512]{1,0:T(8,128)(2,1)S(1)} %get-tuple-element.45), channel_id=1, source_target_pairs={{0,1},{1,0},{2,3},{3,2},{4,5},{5,4},{6,7},{7,6},{8,9},{9,8},{10,11... | collective-permute-start | bytes 393224 | tf_op jit(solution)/shard_map/ppermute | solution.py:37
  39.6 4.4 %collective-permute-start.16 = (bf16[128,512]{1,0:T(8,128)(2,1)S(1)}, bf16[128,512]{1,0:T(8,128)(2,1)S(1)}, u32[]{:S(2)}, u32[]{:S(2)}) collective-permute-start(bf16[128,512]{1,0:T(8,128)(2,1)S(1)} %get-tuple-element.40), channel_id=1, source_target_pairs={{0,1},{1,0},{2,3},{3,2},{4,5},{5,4},{6,7},{7,6},{8,9},{9,8},{10,11... | collective-permute-start | bytes 393224 | tf_op jit(solution)/shard_map/ppermute | solution.py:37
  40.2 7.3 %collective-permute-start.18 = (bf16[128,512]{1,0:T(8,128)(2,1)S(1)}, bf16[128,512]{1,0:T(8,128)(2,1)S(1)}, u32[]{:S(2)}, u32[]{:S(2)}) collective-permute-start(bf16[128,512]{1,0:T(8,128)(2,1)S(1)} %add_convert_fusion.2), channel_id=1, source_target_pairs={{0,6},{1,7},{2,4},{3,5},{4,2},{5,3},{6,0},{7,1},{8,14},{9,15},{10,... | collective-permute-start | bytes 393224 | tf_op jit(solution)/shard_map/ppermute | solution.py:37
  40.8 8.5 %collective-permute-start.20 = (bf16[128,512]{1,0:T(8,128)(2,1)S(1)}, bf16[128,512]{1,0:T(8,128)(2,1)S(1)}, u32[]{:S(2)}, u32[]{:S(2)}) collective-permute-start(bf16[128,512]{1,0:T(8,128)(2,1)S(1)} %add_convert_fusion.1), channel_id=1, source_target_pairs={{0,2},{1,5},{2,0},{3,7},{4,6},{5,1},{6,4},{7,3},{8,10},{9,13},{10,... | collective-permute-start | bytes 393224 | tf_op jit(solution)/shard_map/ppermute | solution.py:37
  42.7 6.5 %collective-permute-start.22 = (bf16[128,512]{1,0:T(8,128)(2,1)S(1)}, bf16[128,512]{1,0:T(8,128)(2,1)S(1)}, u32[]{:S(2)}, u32[]{:S(2)}) collective-permute-start(bf16[128,512]{1,0:T(8,128)(2,1)S(1)} %add_convert_fusion), channel_id=1, source_target_pairs={{0,4},{1,3},{2,6},{3,1},{4,0},{5,7},{6,2},{7,5},{8,12},{9,11},{10,... | collective-permute-start | bytes 393224 | tf_op jit(solution)/shard_map/ppermute | solution.py:37
  49.3 6.4 %collective-permute-start.23 = (bf16[128,512]{1,0:T(8,128)(2,1)S(1)}, bf16[128,512]{1,0:T(8,128)(2,1)S(1)}, u32[]{:S(2)}, u32[]{:S(2)}) collective-permute-start(bf16[128,512]{1,0:T(8,128)(2,1)S(1)} %get-tuple-element.50), channel_id=1, source_target_pairs={{0,8},{1,17},{2,10},{3,19},{4,12},{5,21},{6,14},{7,23},{8,0},{9,25... | collective-permute-start | bytes 393224 | tf_op jit(solution)/shard_map/ppermute | solution.py:37
  55.8 6.1 %collective-permute-start.24 = (bf16[128,512]{1,0:T(8,128)(2,1)S(1)}, bf16[128,512]{1,0:T(8,128)(2,1)S(1)}, u32[]{:S(2)}, u32[]{:S(2)}) collective-permute-start(bf16[128,512]{1,0:T(8,128)(2,1)S(1)} %fusion.1), channel_id=1, source_target_pairs={{0,16},{1,9},{2,18},{3,11},{4,20},{5,13},{6,22},{7,15},{8,24},{9,1... | collective-permute-start | bytes 393224 | tf_op jit(solution)/shard_map/ppermute | solution.py:37
  61.9 5.9 %collective-permute-start.25 = (bf16[128,512]{1,0:T(8,128)(2,1)S(1)}, bf16[128,512]{1,0:T(8,128)(2,1)S(1)}, u32[]{:S(2)}, u32[]{:S(2)}) collective-permute-start(bf16[128,512]{1,0:T(8,128)(2,1)S(1)} %multiply_convert_fusion.refs_0_), channel_id=1, source_target_pairs={{0,6},{1,7},{2,4},{3,5},{4,2},{5,3},{6,0},{7,1},{8,14},{9,15},{10,... | collective-permute-start | bytes 393224 | tf_op jit(solution)/shard_map/ppermute | solution.py:37
  62.7 7.1 %collective-permute-start.28 = (bf16[128,512]{1,0:T(8,128)(2,1)S(1)}, bf16[128,512]{1,0:T(8,128)(2,1)S(1)}, u32[]{:S(2)}, u32[]{:S(2)}) collective-permute-start(bf16[128,512]{1,0:T(8,128)(2,1)S(1)} %multiply_convert_fusion.refs_0_), channel_id=1, source_target_pairs={{0,2},{1,5},{2,0},{3,7},{4,6},{5,1},{6,4},{7,3},{8,10},{9,13},{10,... | collective-permute-start | bytes 393224 | tf_op jit(solution)/shard_map/ppermute | solution.py:37
  65.5 5.0 %collective-permute-start.29 = (bf16[128,512]{1,0:T(8,128)(2,1)S(1)}, bf16[128,512]{1,0:T(8,128)(2,1)S(1)}, u32[]{:S(2)}, u32[]{:S(2)}) collective-permute-start(bf16[128,512]{1,0:T(8,128)(2,1)S(1)} %multiply_convert_fusion.refs_0_), channel_id=1, source_target_pairs={{0,4},{1,3},{2,6},{3,1},{4,0},{5,7},{6,2},{7,5},{8,12},{9,11},{10,... | collective-permute-start | bytes 393224 | tf_op jit(solution)/shard_map/ppermute | solution.py:37
  65.5 5.3 %collective-permute-start.26 = (bf16[128,512]{1,0:T(8,128)(2,1)S(1)}, bf16[128,512]{1,0:T(8,128)(2,1)S(1)}, u32[]{:S(2)}, u32[]{:S(2)}) collective-permute-start(bf16[128,512]{1,0:T(8,128)(2,1)S(1)} %multiply_convert_fusion.refs_0_), channel_id=1, source_target_pairs={{0,1},{1,0},{2,3},{3,2},{4,5},{5,4},{6,7},{7,6},{8,9},{9,8},{10,11... | collective-permute-start | bytes 393224 | tf_op jit(solution)/shard_map/ppermute | solution.py:37
  67.9 3.0 %collective-permute-start.27 = (bf16[128,512]{1,0:T(8,128)(2,1)S(1)}, bf16[128,512]{1,0:T(8,128)(2,1)S(1)}, u32[]{:S(2)}, u32[]{:S(2)}) collective-permute-start(bf16[128,512]{1,0:T(8,128)(2,1)S(1)} %collective-permute-done.25.refs_1_), channel_id=1, source_target_pairs={{0,1},{1,0},{2,3},{3,2},{4,5},{5,4},{6,7},{7,6},{8,9},{9,8},{10,11... | collective-permute-start | bytes 393224 | tf_op jit(solution)/shard_map/ppermute | solution.py:37
  69.8 1.8 %collective-permute-start.30 = (bf16[128,512]{1,0:T(8,128)(2,1)S(1)}, bf16[128,512]{1,0:T(8,128)(2,1)S(1)}, u32[]{:S(2)}, u32[]{:S(2)}) collective-permute-start(bf16[128,512]{1,0:T(8,128)(2,1)S(1)} %collective-permute-done.28.refs_0_), channel_id=1, source_target_pairs={{0,1},{1,0},{2,3},{3,2},{4,5},{5,4},{6,7},{7,6},{8,9},{9,8},{10,11... | collective-permute-start | bytes 393224 | tf_op jit(solution)/shard_map/ppermute | solution.py:37
  70.4 1.3 %collective-permute-start.31 = (bf16[128,512]{1,0:T(8,128)(2,1)S(1)}, bf16[128,512]{1,0:T(8,128)(2,1)S(1)}, u32[]{:S(2)}, u32[]{:S(2)}) collective-permute-start(bf16[128,512]{1,0:T(8,128)(2,1)S(1)} %collective-permute-done.29.refs_1_), channel_id=1, source_target_pairs={{0,1},{1,0},{2,3},{3,2},{4,5},{5,4},{6,7},{7,6},{8,9},{9,8},{10,11... | collective-permute-start | bytes 393224 | tf_op jit(solution)/shard_map/ppermute | solution.py:37
  72.4 1.4 %collective-permute-start.32 = (f32[128,128]{1,0:T(8,128)S(1)}, f32[128,128]{1,0:T(8,128)S(1)}, u32[]{:S(2)}, u32[]{:S(2)}) collective-permute-start(f32[128,128]{1,0:T(8,128)S(1)} %get-tuple-element.48), channel_id=1, source_target_pairs={{0,1},{1,0},{2,3},{3,2},{4,5},{5,4},{6,7},{7,6},{8,9},{9,8},{10,11... | collective-permute-start | bytes 196616 | tf_op jit(solution)/shard_map/ppermute | solution.py:37
  73.8 5.9 %collective-permute-start.33 = (f32[128,128]{1,0:T(8,128)S(1)}, f32[128,128]{1,0:T(8,128)S(1)}, u32[]{:S(2)}, u32[]{:S(2)}) collective-permute-start(f32[128,128]{1,0:T(8,128)S(1)} %add.90), channel_id=1, source_target_pairs={{0,6},{1,7},{2,4},{3,5},{4,2},{5,3},{6,0},{7,1},{8,14},{9,15},{10,... | collective-permute-start | bytes 196616 | tf_op jit(solution)/shard_map/ppermute | solution.py:37
  74.0 6.0 %collective-permute-start.34 = (f32[128,128]{1,0:T(8,128)S(1)}, f32[128,128]{1,0:T(8,128)S(1)}, u32[]{:S(2)}, u32[]{:S(2)}) collective-permute-start(f32[128,128]{1,0:T(8,128)S(1)} %add.90), channel_id=1, source_target_pairs={{0,2},{1,5},{2,0},{3,7},{4,6},{5,1},{6,4},{7,3},{8,10},{9,13},{10,... | collective-permute-start | bytes 196616 | tf_op jit(solution)/shard_map/ppermute | solution.py:37
  76.2 4.3 %collective-permute-start.35 = (f32[128,128]{1,0:T(8,128)S(1)}, f32[128,128]{1,0:T(8,128)S(1)}, u32[]{:S(2)}, u32[]{:S(2)}) collective-permute-start(f32[128,128]{1,0:T(8,128)S(1)} %add.90), channel_id=1, source_target_pairs={{0,4},{1,3},{2,6},{3,1},{4,0},{5,7},{6,2},{7,5},{8,12},{9,11},{10,... | collective-permute-start | bytes 196616 | tf_op jit(solution)/shard_map/ppermute | solution.py:37
  80.5 4.3 %collective-permute-start.36 = (f32[128,128]{1,0:T(8,128)S(1)}, f32[128,128]{1,0:T(8,128)S(1)}, u32[]{:S(2)}, u32[]{:S(2)}) collective-permute-start(f32[128,128]{1,0:T(8,128)S(1)} %add_add_fusion), channel_id=1, source_target_pairs={{0,8},{1,17},{2,10},{3,19},{4,12},{5,21},{6,14},{7,23},{8,0},{9,25... | collective-permute-start | bytes 196616 | tf_op jit(solution)/shard_map/ppermute | solution.py:37
  84.8 5.2 %collective-permute-start.37 = (f32[128,128]{1,0:T(8,128)S(1)}, f32[128,128]{1,0:T(8,128)S(1)}, u32[]{:S(2)}, u32[]{:S(2)}) collective-permute-start(f32[128,128]{1,0:T(8,128)S(1)} %add.94), channel_id=1, source_target_pairs={{0,16},{1,9},{2,18},{3,11},{4,20},{5,13},{6,22},{7,15},{8,24},{9,1... | collective-permute-start | bytes 196616 | tf_op jit(solution)/shard_map/ppermute | solution.py:37
  90.1 1.3 %collective-permute-start.38 = (f32[128,128]{1,0:T(8,128)S(1)}, f32[128,128]{1,0:T(8,128)S(1)}, u32[]{:S(2)}, u32[]{:S(2)}) collective-permute-start(f32[128,128]{1,0:T(8,128)S(1)} %add.95.own_ref), channel_id=1, source_target_pairs={{0,1},{1,0},{2,3},{3,2},{4,5},{5,4},{6,7},{7,6},{8,9},{9,8},{10,11... | collective-permute-start | bytes 196616 | tf_op jit(solution)/shard_map/ppermute | solution.py:37

commit v5 on v4

--- a/solution.py
+++ b/solution.py
@@ -15,17 +15,25 @@
 
 
 CORE = (1, 1)
-SHARE = ((2, 4), (4, 2))
-
-
-def summed_bits():
-    bits = [1 << bit for bit in range(3, (lax.axis_size("rows") - 1).bit_length())]
-    pairs = []
+SHARE = ((2, 4), (8, 2))
+
+
+def later_bits(first):
+    return [1 << bit for bit in range(first, (lax.axis_size("rows") - 1).bit_length())]
+
+
+def quarter_masks():
+    return [(8, 16), (16, 4)] + [(bit, bit) for bit in later_bits(5)]
+
+
+def small_masks():
+    bits = later_bits(3)
+    groups = [[(6, 6), (2, 4), (4, 2)]]
     while bits:
-        first, second = bits[0], bits[min(1, len(bits) - 1)]
-        pairs += [(first, second), (second, first)][: len(bits)]
+        low, high = bits[0], sum(bits[1:2])
+        groups.append([(mask, mask) for mask in ((high, high | low, low) if high else (low,))])
         bits = bits[2:]
-    return pairs
+    return groups
 
 
 def place_masks(place):
@@ -151,7 +159,7 @@
     got = {place: swap(other[place], CORE) for place in (3, 2, 1, 0)}
     sent = {place: swap((own[place] + got[place]).astype(BF16), place_masks(place)) for place in (3, 2, 1)}
     total = own[0] + got[0] + sent[3] + sent[2] + sent[1]
-    for masks in summed_bits():
+    for masks in quarter_masks():
         total = total + swap(total.astype(BF16), masks)
     coef = {0: (total / m_total).astype(BF16)}
     for place in (3, 2, 1):
@@ -189,9 +197,8 @@
 
 def small_sums(own, other):
     own = own + swap(other, CORE)
-    own = own + sum(swap(own, place_masks(place)) for place in (3, 2, 1))
-    for masks in summed_bits():
-        own = own + swap(own, masks)
+    for group in small_masks():
+        own = own + sum(swap(own, masks) for masks in group)
     return own, swap(own, CORE)
 
 
@@ -301,7 +308,7 @@
     size = lax.axis_size("rows")
     users = lax.axis_size("users")
     m_total = float(rows * size)
-    power = size >= 16 and size & (size - 1) == 0
+    power = size >= 32 and size & (size - 1) == 0
     tiled = rows % 128 == 0 and atoms % (2 * QUARTERS * 128) == 0
     if not power or not tiled or block != 128 or user_residuals.shape[1] != block:
         return plain_local(old_basis, new_atoms, user_residuals)

time: 96.7 us -> 94.8 us (0.980)
  waiting for transfers between devices: 49.7 us -> 44.2 us
  starting transfers between devices: 33.5 us -> 37 us
    ppermute x39 -> x40, waiting for transfers between devices: 49.7 us -> 44.2 us  [swap(): lax.ppermute(value, 'rows', [(i, i ^ masks[i & 1]) for i in range(size)])]
    ppermute x39 -> x40, starting transfers between devices: 33.5 us -> 37 us  [swap(): lax.ppermute(value, 'rows', [(i, i ^ masks[i & 1]) for i in range(size)])]
  transfers between devices with their start and end apart: 39 -> 40, of which waited for: 24 -> 24; matrix products, arithmetic and copies ran while one was open for 0% -> 0% of each run, Pallas kernels for 3% -> 3%
where the time goes in v5:
time: 94.8 us; the launch traced here: 94.7 us
  waiting for transfers between devices  44.2 us (47%)
  starting transfers between devices  37 us (39%)
  Pallas kernels  12 us (13%)
    ppermute x40, waiting for transfers between devices, swap(): lax.ppermute(value, 'rows', [(i, i ^ masks[i & 1]) for i in range(size)])  44.2 us
    ppermute x40, starting transfers between devices, swap(): lax.ppermute(value, 'rows', [(i, i ^ masks[i & 1]) for i in range(size)])  37 us
    pallas_call x14, Pallas kernels, call(): pl.pallas_call(kernel, in_specs=in_specs or [VMEM] * len(operands), out_s...  12 us
  transfers between devices with their start and end apart: 40, of which 24 were waited for; matrix products, arithmetic and copies ran while one was open for 0% of the time, Pallas kernels for 3%

profile of v5, /device:TPU:0, one launch (start us, length us, event | category | flops | bytes accessed | tf_op | source)
XLA Modules:
  0.0 94.7 jit_solution(6986612311307833682)
XLA Ops:
  0.6 2.4 %shard_map.50 = (bf16[128,512]{1,0:T(8,128)(2,1)S(1)}, bf16[128,512]{1,0:T(8,128)(2,1)S(1)}, bf16[128,512]{1,0:T(8,128)(2,1)S(1)}, bf16[128,512]{1,0:T(8,128)(2,...) custom-call(bf16[384,4096]{1,0:T(8,128)(2,1)} %basis_ref.1, ...), custom_call_target="tpu_custom_call" | custom-call | flops 402653184 | tf_op jit(solution)/shard_map/pallas_call | solution.py:49
  3.1 0.5 collective-permute-start.1
  3.7 0.4 collective-permute-start.5
  4.2 0.4 collective-permute-done.1
  4.6 3.9 %collective-permute-start.2 = (bf16[128,512]{1,0:T(8,128)(2,1)S(1)}, bf16[128,512]{1,0:T(8,128)(2,1)S(1)}, u32[]{:S(2)}, u32[]{:S(2)}) collective-permute-start(bf16[128,512]{1,0:T(8,128)(2,1)S(1)} %add_convert_fusion.5), channel_id=1, source_target_pairs={{0,6},{1,11},{2,4},{3,9},{4,2},{5,15},{6,0},{7,13},{8,14},{9,3},{1... | collective-permute-start | bytes 393224 | tf_op jit(solution)/shard_map/ppermute | solution.py:45
  8.5 0.6 collective-permute-start.4
  9.1 0.2 collective-permute-start.6
  9.3 3.9 %collective-permute-done.2 = bf16[128,512]{1,0:T(8,128)(2,1)S(1)} collective-permute-done((bf16[128,512]{1,0:T(8,128)(2,1)S(1)}, bf16[128,512]{1,0:T(8,128)(2,1)S(1)}, u32[]{:S(2)}, u32[]{:S(2)}) %collective-permute-start.2) | collective-permute-done | bytes 131104 | tf_op jit(solution)/shard_map/ppermute | solution.py:45
  13.3 1.9 %collective-permute-done.4 = bf16[128,512]{1,0:T(8,128)(2,1)S(1)} collective-permute-done((bf16[128,512]{1,0:T(8,128)(2,1)S(1)}, bf16[128,512]{1,0:T(8,128)(2,1)S(1)}, u32[]{:S(2)}, u32[]{:S(2)}) %collective-permute-start.4) | collective-permute-done | bytes 131104 | tf_op jit(solution)/shard_map/ppermute | solution.py:45
  15.2 1.8 %collective-permute-start.7 = (bf16[128,512]{1,0:T(8,128)(2,1)S(1)}, bf16[128,512]{1,0:T(8,128)(2,1)S(1)}, u32[]{:S(2)}, u32[]{:S(2)}) collective-permute-start(bf16[128,512]{1,0:T(8,128)(2,1)S(1)} %get-tuple-element.52), channel_id=1, source_target_pairs={{0,8},{1,17},{2,10},{3,19},{4,12},{5,21},{6,14},{7,23},{8,0},{9,25... | collective-permute-start | bytes 393224 | tf_op jit(solution)/shard_map/ppermute | solution.py:45
  17.0 3.4 %collective-permute-done.7 = bf16[128,512]{1,0:T(8,128)(2,1)S(1)} collective-permute-done((bf16[128,512]{1,0:T(8,128)(2,1)S(1)}, bf16[128,512]{1,0:T(8,128)(2,1)S(1)}, u32[]{:S(2)}, u32[]{:S(2)}) %collective-permute-start.7) | collective-permute-done | bytes 131104 | tf_op jit(solution)/shard_map/ppermute | solution.py:45
  20.5 3.0 %collective-permute-start.8 = (bf16[128,512]{1,0:T(8,128)(2,1)S(1)}, bf16[128,512]{1,0:T(8,128)(2,1)S(1)}, u32[]{:S(2)}, u32[]{:S(2)}) collective-permute-start(bf16[128,512]{1,0:T(8,128)(2,1)S(1)} %fusion), channel_id=1, source_target_pairs={{0,16},{1,5},{2,18},{3,7},{4,20},{5,1},{6,22},{7,3},{8,24},{9,13},... | collective-permute-start | bytes 393224 | tf_op jit(solution)/shard_map/ppermute | solution.py:45
  23.5 3.0 %collective-permute-done.8 = bf16[128,512]{1,0:T(8,128)(2,1)S(1)} collective-permute-done((bf16[128,512]{1,0:T(8,128)(2,1)S(1)}, bf16[128,512]{1,0:T(8,128)(2,1)S(1)}, u32[]{:S(2)}, u32[]{:S(2)}) %collective-permute-start.8) | collective-permute-done | bytes 131104 | tf_op jit(solution)/shard_map/ppermute | solution.py:45
  26.5 2.4 %collective-permute-start.9 = (bf16[128,512]{1,0:T(8,128)(2,1)S(1)}, bf16[128,512]{1,0:T(8,128)(2,1)S(1)}, u32[]{:S(2)}, u32[]{:S(2)}) collective-permute-start(bf16[128,512]{1,0:T(8,128)(2,1)S(1)} %multiply_convert_fusion.1.refs_0_), channel_id=1, source_target_pairs={{0,6},{1,11},{2,4},{3,9},{4,2},{5,15},{6,0},{7,13},{8,14},{9,3},{1... | collective-permute-start | bytes 393224 | tf_op jit(solution)/shard_map/ppermute | solution.py:45
  28.9 0.7 collective-permute-start.12
  29.6 0.5 collective-permute-start.13
  30.0 3.3 %collective-permute-done.9.refs_1_ = bf16[128,512]{1,0:T(8,128)(2,1)S(1)} collective-permute-done((bf16[128,512]{1,0:T(8,128)(2,1)S(1)}, bf16[128,512]{1,0:T(8,128)(2,1)S(1)}, u32[]{:S(2)}, u32[]{:S(2)}) %collective-permute-start.9) | collective-permute-done | bytes 131104 | tf_op jit(solution)/shard_map/ppermute | solution.py:45
  33.3 0.6 collective-permute-done.12.refs_0_
  33.9 0.8 collective-permute-done.13.refs_1_
  34.7 0.4 shard_map.51.rem_ref
  35.1 0.4 shard_map.52.rem_ref
  35.5 0.4 shard_map.53.rem_ref
  36.1 0.4 shard_map.54
  36.5 0.2 shard_map.57
  36.7 0.5 collective-permute-start.17
  37.2 0.4 shard_map.56
  37.5 0.2 collective-permute-start.19
  37.7 0.4 collective-permute-start.21
  38.2 0.4 shard_map.55
  38.7 1.7 %collective-permute-start.18 = (bf16[128,512]{1,0:T(8,128)(2,1)S(1)}, bf16[128,512]{1,0:T(8,128)(2,1)S(1)}, u32[]{:S(2)}, u32[]{:S(2)}) collective-permute-start(bf16[128,512]{1,0:T(8,128)(2,1)S(1)} %add_convert_fusion.2), channel_id=1, source_target_pairs={{0,6},{1,11},{2,4},{3,9},{4,2},{5,15},{6,0},{7,13},{8,14},{9,3},{1... | collective-permute-start | bytes 393224 | tf_op jit(solution)/shard_map/ppermute | solution.py:45
  40.5 0.8 collective-permute-start.20
  41.4 1.1 %collective-permute-start.22 = (bf16[128,512]{1,0:T(8,128)(2,1)S(1)}, bf16[128,512]{1,0:T(8,128)(2,1)S(1)}, u32[]{:S(2)}, u32[]{:S(2)}) collective-permute-start(bf16[128,512]{1,0:T(8,128)(2,1)S(1)} %add_convert_fusion), channel_id=1, source_target_pairs={{0,4},{1,3},{2,6},{3,1},{4,0},{5,7},{6,2},{7,5},{8,12},{9,11},{10,... | collective-permute-start | bytes 393224 | tf_op jit(solution)/shard_map/ppermute | solution.py:45
  42.5 4.5 %collective-permute-done.18 = bf16[128,512]{1,0:T(8,128)(2,1)S(1)} collective-permute-done((bf16[128,512]{1,0:T(8,128)(2,1)S(1)}, bf16[128,512]{1,0:T(8,128)(2,1)S(1)}, u32[]{:S(2)}, u32[]{:S(2)}) %collective-permute-start.18) | collective-permute-done | bytes 131104 | tf_op jit(solution)/shard_map/ppermute | solution.py:45
  47.0 1.4 %collective-permute-done.20 = bf16[128,512]{1,0:T(8,128)(2,1)S(1)} collective-permute-done((bf16[128,512]{1,0:T(8,128)(2,1)S(1)}, bf16[128,512]{1,0:T(8,128)(2,1)S(1)}, u32[]{:S(2)}, u32[]{:S(2)}) %collective-permute-start.20) | collective-permute-done | bytes 131104 | tf_op jit(solution)/shard_map/ppermute | solution.py:45
  48.5 2.0 %collective-permute-start.23 = (bf16[128,512]{1,0:T(8,128)(2,1)S(1)}, bf16[128,512]{1,0:T(8,128)(2,1)S(1)}, u32[]{:S(2)}, u32[]{:S(2)}) collective-permute-start(bf16[128,512]{1,0:T(8,128)(2,1)S(1)} %get-tuple-element.50), channel_id=1, source_target_pairs={{0,8},{1,17},{2,10},{3,19},{4,12},{5,21},{6,14},{7,23},{8,0},{9,25... | collective-permute-start | bytes 393224 | tf_op jit(solution)/shard_map/ppermute | solution.py:45
  50.5 4.0 %collective-permute-done.23 = bf16[128,512]{1,0:T(8,128)(2,1)S(1)} collective-permute-done((bf16[128,512]{1,0:T(8,128)(2,1)S(1)}, bf16[128,512]{1,0:T(8,128)(2,1)S(1)}, u32[]{:S(2)}, u32[]{:S(2)}) %collective-permute-start.23) | collective-permute-done | bytes 131104 | tf_op jit(solution)/shard_map/ppermute | solution.py:45
  54.6 2.8 %collective-permute-start.24 = (bf16[128,512]{1,0:T(8,128)(2,1)S(1)}, bf16[128,512]{1,0:T(8,128)(2,1)S(1)}, u32[]{:S(2)}, u32[]{:S(2)}) collective-permute-start(bf16[128,512]{1,0:T(8,128)(2,1)S(1)} %fusion.1), channel_id=1, source_target_pairs={{0,16},{1,5},{2,18},{3,7},{4,20},{5,1},{6,22},{7,3},{8,24},{9,13},... | collective-permute-start | bytes 393224 | tf_op jit(solution)/shard_map/ppermute | solution.py:45
  57.4 3.1 %collective-permute-done.24 = bf16[128,512]{1,0:T(8,128)(2,1)S(1)} collective-permute-done((bf16[128,512]{1,0:T(8,128)(2,1)S(1)}, bf16[128,512]{1,0:T(8,128)(2,1)S(1)}, u32[]{:S(2)}, u32[]{:S(2)}) %collective-permute-start.24) | collective-permute-done | bytes 131104 | tf_op jit(solution)/shard_map/ppermute | solution.py:45
  60.6 1.5 %collective-permute-start.25 = (bf16[128,512]{1,0:T(8,128)(2,1)S(1)}, bf16[128,512]{1,0:T(8,128)(2,1)S(1)}, u32[]{:S(2)}, u32[]{:S(2)}) collective-permute-start(bf16[128,512]{1,0:T(8,128)(2,1)S(1)} %multiply_convert_fusion.refs_0_), channel_id=1, source_target_pairs={{0,6},{1,11},{2,4},{3,9},{4,2},{5,15},{6,0},{7,13},{8,14},{9,3},{1... | collective-permute-start | bytes 393224 | tf_op jit(solution)/shard_map/ppermute | solution.py:45
  62.0 1.2 %collective-permute-start.28 = (bf16[128,512]{1,0:T(8,128)(2,1)S(1)}, bf16[128,512]{1,0:T(8,128)(2,1)S(1)}, u32[]{:S(2)}, u32[]{:S(2)}) collective-permute-start(bf16[128,512]{1,0:T(8,128)(2,1)S(1)} %multiply_convert_fusion.refs_0_), channel_id=1, source_target_pairs={{0,2},{1,9},{2,0},{3,11},{4,6},{5,13},{6,4},{7,15},{8,10},{9,1},{1... | collective-permute-start | bytes 393224 | tf_op jit(solution)/shard_map/ppermute | solution.py:45
  63.2 0.9 collective-permute-start.29
  64.1 2.7 %collective-permute-done.25.refs_1_ = bf16[128,512]{1,0:T(8,128)(2,1)S(1)} collective-permute-done((bf16[128,512]{1,0:T(8,128)(2,1)S(1)}, bf16[128,512]{1,0:T(8,128)(2,1)S(1)}, u32[]{:S(2)}, u32[]{:S(2)}) %collective-permute-start.25) | collective-permute-done | bytes 131104 | tf_op jit(solution)/shard_map/ppermute | solution.py:45
  66.8 0.7 collective-permute-done.28.refs_0_
  67.6 0.6 collective-permute-done.29.refs_1_
  68.2 0.4 shard_map.58.rem_ref
  68.6 0.4 shard_map.59.rem_ref
  69.0 0.4 shard_map.60.rem_ref
  69.6 0.4 shard_map.61.turned_ref
  70.0 0.3 shard_map.62
  70.2 0.5 collective-permute-start.32
  70.7 0.9 collective-permute-done.32
  71.6 1.4 %collective-permute-start.33 = (f32[128,128]{1,0:T(8,128)S(1)}, f32[128,128]{1,0:T(8,128)S(1)}, u32[]{:S(2)}, u32[]{:S(2)}) collective-permute-start(f32[128,128]{1,0:T(8,128)S(1)} %add.93), channel_id=1, source_target_pairs={{0,6},{1,7},{2,4},{3,5},{4,2},{5,3},{6,0},{7,1},{8,14},{9,15},{10,... | collective-permute-start | bytes 196616 | tf_op jit(solution)/shard_map/ppermute | solution.py:45
  73.1 1.0 %collective-permute-start.34 = (f32[128,128]{1,0:T(8,128)S(1)}, f32[128,128]{1,0:T(8,128)S(1)}, u32[]{:S(2)}, u32[]{:S(2)}) collective-permute-start(f32[128,128]{1,0:T(8,128)S(1)} %add.93), channel_id=1, source_target_pairs={{0,2},{1,5},{2,0},{3,7},{4,6},{5,1},{6,4},{7,3},{8,10},{9,13},{10,... | collective-permute-start | bytes 196616 | tf_op jit(solution)/shard_map/ppermute | solution.py:45
  74.1 1.1 %collective-permute-start.35 = (f32[128,128]{1,0:T(8,128)S(1)}, f32[128,128]{1,0:T(8,128)S(1)}, u32[]{:S(2)}, u32[]{:S(2)}) collective-permute-start(f32[128,128]{1,0:T(8,128)S(1)} %add.93), channel_id=1, source_target_pairs={{0,4},{1,3},{2,6},{3,1},{4,0},{5,7},{6,2},{7,5},{8,12},{9,11},{10,... | collective-permute-start | bytes 196616 | tf_op jit(solution)/shard_map/ppermute | solution.py:45
  75.2 1.9 %collective-permute-done.33 = f32[128,128]{1,0:T(8,128)S(1)} collective-permute-done((f32[128,128]{1,0:T(8,128)S(1)}, f32[128,128]{1,0:T(8,128)S(1)}, u32[]{:S(2)}, u32[]{:S(2)}) %collective-permute-start.33) | collective-permute-done | bytes 65568 | tf_op jit(solution)/shard_map/ppermute | solution.py:45
  77.0 0.7 collective-permute-done.34
  77.7 0.6 collective-permute-done.35
  78.4 2.8 %collective-permute-start.36 = (f32[128,128]{1,0:T(8,128)S(1)}, f32[128,128]{1,0:T(8,128)S(1)}, u32[]{:S(2)}, u32[]{:S(2)}) collective-permute-start(f32[128,128]{1,0:T(8,128)S(1)} %add_add_fusion.1), channel_id=1, source_target_pairs={{0,16},{1,17},{2,18},{3,19},{4,20},{5,21},{6,22},{7,23},{8,24},{9,... | collective-permute-start | bytes 196616 | tf_op jit(solution)/shard_map/ppermute | solution.py:45
  81.1 2.4 %collective-permute-start.37 = (f32[128,128]{1,0:T(8,128)S(1)}, f32[128,128]{1,0:T(8,128)S(1)}, u32[]{:S(2)}, u32[]{:S(2)}) collective-permute-start(f32[128,128]{1,0:T(8,128)S(1)} %add_add_fusion.1), channel_id=1, source_target_pairs={{0,24},{1,25},{2,26},{3,27},{4,28},{5,29},{6,30},{7,31},{8,16},{9,... | collective-permute-start | bytes 196616 | tf_op jit(solution)/shard_map/ppermute | solution.py:45
  83.5 0.5 collective-permute-start.38
  84.0 3.9 %collective-permute-done.37 = f32[128,128]{1,0:T(8,128)S(1)} collective-permute-done((f32[128,128]{1,0:T(8,128)S(1)}, f32[128,128]{1,0:T(8,128)S(1)}, u32[]{:S(2)}, u32[]{:S(2)}) %collective-permute-start.37) | collective-permute-done | bytes 65568 | tf_op jit(solution)/shard_map/ppermute | solution.py:45
  87.9 0.3 collective-permute-done.38
  88.3 1.2 %collective-permute-done.39.other_ref = f32[128,128]{1,0:T(8,128)S(1)} collective-permute-done((f32[128,128]{1,0:T(8,128)S(1)}, f32[128,128]{1,0:T(8,128)S(1)}, u32[]{:S(2)}, u32[]{:S(2)}) %collective-permute-start.39) | collective-permute-done | bytes 65568 | tf_op jit(solution)/shard_map/ppermute | solution.py:45
  89.5 5.2 %shard_map.63 = (bf16[384,128]{1,0:T(8,128)(2,1)}, bf16[384,128]{1,0:T(8,128)(2,1)}) custom-call(f32[128,128]{1,0:T(8,128)S(1)} %add_add_fusion.own_ref, f32[128,128]{1,0:T(8,128)S(1)} %collective-permute-done.39.other_ref, bf16[384,128]{1,0:T(8,128)(2,1)S(1)} %get-tuple-element.49.rem_ref, bf16[384,128]{1,0:T(8,128)(2,1)S(1)} %get-tuple-element.46.user_ref), custom_call_target="tpu_custom_call" | custom-call | tf_op jit(solution)/shard_map/pallas_call | solution.py:49
  (45 shorter events, 1.2 us)
Async XLA Ops:
  3.1 1.5 %collective-permute-start.1 = (bf16[128,512]{1,0:T(8,128)(2,1)S(1)}, bf16[128,512]{1,0:T(8,128)(2,1)S(1)}, u32[]{:S(2)}, u32[]{:S(2)}) collective-permute-start(bf16[128,512]{1,0:T(8,128)(2,1)S(1)} %get-tuple-element.32), channel_id=1, source_target_pairs={{0,1},{1,0},{2,3},{3,2},{4,5},{5,4},{6,7},{7,6},{8,9},{9,8},{10,11... | collective-permute-start | bytes 393224 | tf_op jit(solution)/shard_map/ppermute | solution.py:45
  3.6 4.9 %collective-permute-start.3 = (bf16[128,512]{1,0:T(8,128)(2,1)S(1)}, bf16[128,512]{1,0:T(8,128)(2,1)S(1)}, u32[]{:S(2)}, u32[]{:S(2)}) collective-permute-start(bf16[128,512]{1,0:T(8,128)(2,1)S(1)} %get-tuple-element.34), channel_id=1, source_target_pairs={{0,1},{1,0},{2,3},{3,2},{4,5},{5,4},{6,7},{7,6},{8,9},{9,8},{10,11... | collective-permute-start | bytes 393224 | tf_op jit(solution)/shard_map/ppermute | solution.py:45
  3.7 5.5 %collective-permute-start.5 = (bf16[128,512]{1,0:T(8,128)(2,1)S(1)}, bf16[128,512]{1,0:T(8,128)(2,1)S(1)}, u32[]{:S(2)}, u32[]{:S(2)}) collective-permute-start(bf16[128,512]{1,0:T(8,128)(2,1)S(1)} %get-tuple-element.36), channel_id=1, source_target_pairs={{0,1},{1,0},{2,3},{3,2},{4,5},{5,4},{6,7},{7,6},{8,9},{9,8},{10,11... | collective-permute-start | bytes 393224 | tf_op jit(solution)/shard_map/ppermute | solution.py:45
  4.1 5.2 %collective-permute-start = (bf16[128,512]{1,0:T(8,128)(2,1)S(1)}, bf16[128,512]{1,0:T(8,128)(2,1)S(1)}, u32[]{:S(2)}, u32[]{:S(2)}) collective-permute-start(bf16[128,512]{1,0:T(8,128)(2,1)S(1)} %get-tuple-element.30), channel_id=1, source_target_pairs={{0,1},{1,0},{2,3},{3,2},{4,5},{5,4},{6,7},{7,6},{8,9},{9,8},{10,11... | collective-permute-start | bytes 393224 | tf_op jit(solution)/shard_map/ppermute | solution.py:45
  4.6 8.7 %collective-permute-start.2 = (bf16[128,512]{1,0:T(8,128)(2,1)S(1)}, bf16[128,512]{1,0:T(8,128)(2,1)S(1)}, u32[]{:S(2)}, u32[]{:S(2)}) collective-permute-start(bf16[128,512]{1,0:T(8,128)(2,1)S(1)} %add_convert_fusion.5), channel_id=1, source_target_pairs={{0,6},{1,11},{2,4},{3,9},{4,2},{5,15},{6,0},{7,13},{8,14},{9,3},{1... | collective-permute-start | bytes 393224 | tf_op jit(solution)/shard_map/ppermute | solution.py:45
  8.5 6.7 %collective-permute-start.4 = (bf16[128,512]{1,0:T(8,128)(2,1)S(1)}, bf16[128,512]{1,0:T(8,128)(2,1)S(1)}, u32[]{:S(2)}, u32[]{:S(2)}) collective-permute-start(bf16[128,512]{1,0:T(8,128)(2,1)S(1)} %add_convert_fusion.4), channel_id=1, source_target_pairs={{0,2},{1,9},{2,0},{3,11},{4,6},{5,13},{6,4},{7,15},{8,10},{9,1},{1... | collective-permute-start | bytes 393224 | tf_op jit(solution)/shard_map/ppermute | solution.py:45
  9.1 6.0 %collective-permute-start.6 = (bf16[128,512]{1,0:T(8,128)(2,1)S(1)}, bf16[128,512]{1,0:T(8,128)(2,1)S(1)}, u32[]{:S(2)}, u32[]{:S(2)}) collective-permute-start(bf16[128,512]{1,0:T(8,128)(2,1)S(1)} %add_convert_fusion.3), channel_id=1, source_target_pairs={{0,4},{1,3},{2,6},{3,1},{4,0},{5,7},{6,2},{7,5},{8,12},{9,11},{10,... | collective-permute-start | bytes 393224 | tf_op jit(solution)/shard_map/ppermute | solution.py:45
  15.2 5.2 %collective-permute-start.7 = (bf16[128,512]{1,0:T(8,128)(2,1)S(1)}, bf16[128,512]{1,0:T(8,128)(2,1)S(1)}, u32[]{:S(2)}, u32[]{:S(2)}) collective-permute-start(bf16[128,512]{1,0:T(8,128)(2,1)S(1)} %get-tuple-element.52), channel_id=1, source_target_pairs={{0,8},{1,17},{2,10},{3,19},{4,12},{5,21},{6,14},{7,23},{8,0},{9,25... | collective-permute-start | bytes 393224 | tf_op jit(solution)/shard_map/ppermute | solution.py:45
  20.5 5.9 %collective-permute-start.8 = (bf16[128,512]{1,0:T(8,128)(2,1)S(1)}, bf16[128,512]{1,0:T(8,128)(2,1)S(1)}, u32[]{:S(2)}, u32[]{:S(2)}) collective-permute-start(bf16[128,512]{1,0:T(8,128)(2,1)S(1)} %fusion), channel_id=1, source_target_pairs={{0,16},{1,5},{2,18},{3,7},{4,20},{5,1},{6,22},{7,3},{8,24},{9,13},... | collective-permute-start | bytes 393224 | tf_op jit(solution)/shard_map/ppermute | solution.py:45
  26.5 6.9 %collective-permute-start.9 = (bf16[128,512]{1,0:T(8,128)(2,1)S(1)}, bf16[128,512]{1,0:T(8,128)(2,1)S(1)}, u32[]{:S(2)}, u32[]{:S(2)}) collective-permute-start(bf16[128,512]{1,0:T(8,128)(2,1)S(1)} %multiply_convert_fusion.1.refs_0_), channel_id=1, source_target_pairs={{0,6},{1,11},{2,4},{3,9},{4,2},{5,15},{6,0},{7,13},{8,14},{9,3},{1... | collective-permute-start | bytes 393224 | tf_op jit(solution)/shard_map/ppermute | solution.py:45
  28.9 5.1 %collective-permute-start.12 = (bf16[128,512]{1,0:T(8,128)(2,1)S(1)}, bf16[128,512]{1,0:T(8,128)(2,1)S(1)}, u32[]{:S(2)}, u32[]{:S(2)}) collective-permute-start(bf16[128,512]{1,0:T(8,128)(2,1)S(1)} %multiply_convert_fusion.1.refs_0_), channel_id=1, source_target_pairs={{0,2},{1,9},{2,0},{3,11},{4,6},{5,13},{6,4},{7,15},{8,10},{9,1},{1... | collective-permute-start | bytes 393224 | tf_op jit(solution)/shard_map/ppermute | solution.py:45
  29.6 5.1 %collective-permute-start.13 = (bf16[128,512]{1,0:T(8,128)(2,1)S(1)}, bf16[128,512]{1,0:T(8,128)(2,1)S(1)}, u32[]{:S(2)}, u32[]{:S(2)}) collective-permute-start(bf16[128,512]{1,0:T(8,128)(2,1)S(1)} %multiply_convert_fusion.1.refs_0_), channel_id=1, source_target_pairs={{0,4},{1,3},{2,6},{3,1},{4,0},{5,7},{6,2},{7,5},{8,12},{9,11},{10,... | collective-permute-start | bytes 393224 | tf_op jit(solution)/shard_map/ppermute | solution.py:45
  30.0 5.1 %collective-permute-start.10 = (bf16[128,512]{1,0:T(8,128)(2,1)S(1)}, bf16[128,512]{1,0:T(8,128)(2,1)S(1)}, u32[]{:S(2)}, u32[]{:S(2)}) collective-permute-start(bf16[128,512]{1,0:T(8,128)(2,1)S(1)} %multiply_convert_fusion.1.refs_0_), channel_id=1, source_target_pairs={{0,1},{1,0},{2,3},{3,2},{4,5},{5,4},{6,7},{7,6},{8,9},{9,8},{10,11... | collective-permute-start | bytes 393224 | tf_op jit(solution)/shard_map/ppermute | solution.py:45
  33.3 1.8 %collective-permute-start.11 = (bf16[128,512]{1,0:T(8,128)(2,1)S(1)}, bf16[128,512]{1,0:T(8,128)(2,1)S(1)}, u32[]{:S(2)}, u32[]{:S(2)}) collective-permute-start(bf16[128,512]{1,0:T(8,128)(2,1)S(1)} %collective-permute-done.9.refs_1_), channel_id=1, source_target_pairs={{0,1},{1,0},{2,3},{3,2},{4,5},{5,4},{6,7},{7,6},{8,9},{9,8},{10,11... | collective-permute-start | bytes 393224 | tf_op jit(solution)/shard_map/ppermute | solution.py:45
  33.9 2.0 %collective-permute-start.14 = (bf16[128,512]{1,0:T(8,128)(2,1)S(1)}, bf16[128,512]{1,0:T(8,128)(2,1)S(1)}, u32[]{:S(2)}, u32[]{:S(2)}) collective-permute-start(bf16[128,512]{1,0:T(8,128)(2,1)S(1)} %collective-permute-done.12.refs_0_), channel_id=1, source_target_pairs={{0,1},{1,0},{2,3},{3,2},{4,5},{5,4},{6,7},{7,6},{8,9},{9,8},{10,11... | collective-permute-start | bytes 393224 | tf_op jit(solution)/shard_map/ppermute | solution.py:45
  34.7 1.3 %collective-permute-start.15 = (bf16[128,512]{1,0:T(8,128)(2,1)S(1)}, bf16[128,512]{1,0:T(8,128)(2,1)S(1)}, u32[]{:S(2)}, u32[]{:S(2)}) collective-permute-start(bf16[128,512]{1,0:T(8,128)(2,1)S(1)} %collective-permute-done.13.refs_1_), channel_id=1, source_target_pairs={{0,1},{1,0},{2,3},{3,2},{4,5},{5,4},{6,7},{7,6},{8,9},{9,8},{10,11... | collective-permute-start | bytes 393224 | tf_op jit(solution)/shard_map/ppermute | solution.py:45
  36.7 2.0 %collective-permute-start.17 = (bf16[128,512]{1,0:T(8,128)(2,1)S(1)}, bf16[128,512]{1,0:T(8,128)(2,1)S(1)}, u32[]{:S(2)}, u32[]{:S(2)}) collective-permute-start(bf16[128,512]{1,0:T(8,128)(2,1)S(1)} %shard_map.57), channel_id=1, source_target_pairs={{0,1},{1,0},{2,3},{3,2},{4,5},{5,4},{6,7},{7,6},{8,9},{9,8},{10,11... | collective-permute-start | bytes 393224 | tf_op jit(solution)/shard_map/ppermute | solution.py:45
  37.5 2.9 %collective-permute-start.19 = (bf16[128,512]{1,0:T(8,128)(2,1)S(1)}, bf16[128,512]{1,0:T(8,128)(2,1)S(1)}, u32[]{:S(2)}, u32[]{:S(2)}) collective-permute-start(bf16[128,512]{1,0:T(8,128)(2,1)S(1)} %get-tuple-element.43), channel_id=1, source_target_pairs={{0,1},{1,0},{2,3},{3,2},{4,5},{5,4},{6,7},{7,6},{8,9},{9,8},{10,11... | collective-permute-start | bytes 393224 | tf_op jit(solution)/shard_map/ppermute | solution.py:45
  37.7 3.6 %collective-permute-start.21 = (bf16[128,512]{1,0:T(8,128)(2,1)S(1)}, bf16[128,512]{1,0:T(8,128)(2,1)S(1)}, u32[]{:S(2)}, u32[]{:S(2)}) collective-permute-start(bf16[128,512]{1,0:T(8,128)(2,1)S(1)} %get-tuple-element.45), channel_id=1, source_target_pairs={{0,1},{1,0},{2,3},{3,2},{4,5},{5,4},{6,7},{7,6},{8,9},{9,8},{10,11... | collective-permute-start | bytes 393224 | tf_op jit(solution)/shard_map/ppermute | solution.py:45
  38.1 4.4 %collective-permute-start.16 = (bf16[128,512]{1,0:T(8,128)(2,1)S(1)}, bf16[128,512]{1,0:T(8,128)(2,1)S(1)}, u32[]{:S(2)}, u32[]{:S(2)}) collective-permute-start(bf16[128,512]{1,0:T(8,128)(2,1)S(1)} %get-tuple-element.40), channel_id=1, source_target_pairs={{0,1},{1,0},{2,3},{3,2},{4,5},{5,4},{6,7},{7,6},{8,9},{9,8},{10,11... | collective-permute-start | bytes 393224 | tf_op jit(solution)/shard_map/ppermute | solution.py:45
  38.7 8.3 %collective-permute-start.18 = (bf16[128,512]{1,0:T(8,128)(2,1)S(1)}, bf16[128,512]{1,0:T(8,128)(2,1)S(1)}, u32[]{:S(2)}, u32[]{:S(2)}) collective-permute-start(bf16[128,512]{1,0:T(8,128)(2,1)S(1)} %add_convert_fusion.2), channel_id=1, source_target_pairs={{0,6},{1,11},{2,4},{3,9},{4,2},{5,15},{6,0},{7,13},{8,14},{9,3},{1... | collective-permute-start | bytes 393224 | tf_op jit(solution)/shard_map/ppermute | solution.py:45
  40.5 7.9 %collective-permute-start.20 = (bf16[128,512]{1,0:T(8,128)(2,1)S(1)}, bf16[128,512]{1,0:T(8,128)(2,1)S(1)}, u32[]{:S(2)}, u32[]{:S(2)}) collective-permute-start(bf16[128,512]{1,0:T(8,128)(2,1)S(1)} %add_convert_fusion.1), channel_id=1, source_target_pairs={{0,2},{1,9},{2,0},{3,11},{4,6},{5,13},{6,4},{7,15},{8,10},{9,1},{1... | collective-permute-start | bytes 393224 | tf_op jit(solution)/shard_map/ppermute | solution.py:45
  41.4 7.0 %collective-permute-start.22 = (bf16[128,512]{1,0:T(8,128)(2,1)S(1)}, bf16[128,512]{1,0:T(8,128)(2,1)S(1)}, u32[]{:S(2)}, u32[]{:S(2)}) collective-permute-start(bf16[128,512]{1,0:T(8,128)(2,1)S(1)} %add_convert_fusion), channel_id=1, source_target_pairs={{0,4},{1,3},{2,6},{3,1},{4,0},{5,7},{6,2},{7,5},{8,12},{9,11},{10,... | collective-permute-start | bytes 393224 | tf_op jit(solution)/shard_map/ppermute | solution.py:45
  48.5 6.1 %collective-permute-start.23 = (bf16[128,512]{1,0:T(8,128)(2,1)S(1)}, bf16[128,512]{1,0:T(8,128)(2,1)S(1)}, u32[]{:S(2)}, u32[]{:S(2)}) collective-permute-start(bf16[128,512]{1,0:T(8,128)(2,1)S(1)} %get-tuple-element.50), channel_id=1, source_target_pairs={{0,8},{1,17},{2,10},{3,19},{4,12},{5,21},{6,14},{7,23},{8,0},{9,25... | collective-permute-start | bytes 393224 | tf_op jit(solution)/shard_map/ppermute | solution.py:45
  54.6 5.9 %collective-permute-start.24 = (bf16[128,512]{1,0:T(8,128)(2,1)S(1)}, bf16[128,512]{1,0:T(8,128)(2,1)S(1)}, u32[]{:S(2)}, u32[]{:S(2)}) collective-permute-start(bf16[128,512]{1,0:T(8,128)(2,1)S(1)} %fusion.1), channel_id=1, source_target_pairs={{0,16},{1,5},{2,18},{3,7},{4,20},{5,1},{6,22},{7,3},{8,24},{9,13},... | collective-permute-start | bytes 393224 | tf_op jit(solution)/shard_map/ppermute | solution.py:45
  60.6 6.3 %collective-permute-start.25 = (bf16[128,512]{1,0:T(8,128)(2,1)S(1)}, bf16[128,512]{1,0:T(8,128)(2,1)S(1)}, u32[]{:S(2)}, u32[]{:S(2)}) collective-permute-start(bf16[128,512]{1,0:T(8,128)(2,1)S(1)} %multiply_convert_fusion.refs_0_), channel_id=1, source_target_pairs={{0,6},{1,11},{2,4},{3,9},{4,2},{5,15},{6,0},{7,13},{8,14},{9,3},{1... | collective-permute-start | bytes 393224 | tf_op jit(solution)/shard_map/ppermute | solution.py:45
  62.0 5.6 %collective-permute-start.28 = (bf16[128,512]{1,0:T(8,128)(2,1)S(1)}, bf16[128,512]{1,0:T(8,128)(2,1)S(1)}, u32[]{:S(2)}, u32[]{:S(2)}) collective-permute-start(bf16[128,512]{1,0:T(8,128)(2,1)S(1)} %multiply_convert_fusion.refs_0_), channel_id=1, source_target_pairs={{0,2},{1,9},{2,0},{3,11},{4,6},{5,13},{6,4},{7,15},{8,10},{9,1},{1... | collective-permute-start | bytes 393224 | tf_op jit(solution)/shard_map/ppermute | solution.py:45
  63.2 5.0 %collective-permute-start.29 = (bf16[128,512]{1,0:T(8,128)(2,1)S(1)}, bf16[128,512]{1,0:T(8,128)(2,1)S(1)}, u32[]{:S(2)}, u32[]{:S(2)}) collective-permute-start(bf16[128,512]{1,0:T(8,128)(2,1)S(1)} %multiply_convert_fusion.refs_0_), channel_id=1, source_target_pairs={{0,4},{1,3},{2,6},{3,1},{4,0},{5,7},{6,2},{7,5},{8,12},{9,11},{10,... | collective-permute-start | bytes 393224 | tf_op jit(solution)/shard_map/ppermute | solution.py:45
  64.1 4.5 %collective-permute-start.26 = (bf16[128,512]{1,0:T(8,128)(2,1)S(1)}, bf16[128,512]{1,0:T(8,128)(2,1)S(1)}, u32[]{:S(2)}, u32[]{:S(2)}) collective-permute-start(bf16[128,512]{1,0:T(8,128)(2,1)S(1)} %multiply_convert_fusion.refs_0_), channel_id=1, source_target_pairs={{0,1},{1,0},{2,3},{3,2},{4,5},{5,4},{6,7},{7,6},{8,9},{9,8},{10,11... | collective-permute-start | bytes 393224 | tf_op jit(solution)/shard_map/ppermute | solution.py:45
  66.8 1.8 %collective-permute-start.27 = (bf16[128,512]{1,0:T(8,128)(2,1)S(1)}, bf16[128,512]{1,0:T(8,128)(2,1)S(1)}, u32[]{:S(2)}, u32[]{:S(2)}) collective-permute-start(bf16[128,512]{1,0:T(8,128)(2,1)S(1)} %collective-permute-done.25.refs_1_), channel_id=1, source_target_pairs={{0,1},{1,0},{2,3},{3,2},{4,5},{5,4},{6,7},{7,6},{8,9},{9,8},{10,11... | collective-permute-start | bytes 393224 | tf_op jit(solution)/shard_map/ppermute | solution.py:45
  67.6 1.9 %collective-permute-start.30 = (bf16[128,512]{1,0:T(8,128)(2,1)S(1)}, bf16[128,512]{1,0:T(8,128)(2,1)S(1)}, u32[]{:S(2)}, u32[]{:S(2)}) collective-permute-start(bf16[128,512]{1,0:T(8,128)(2,1)S(1)} %collective-permute-done.28.refs_0_), channel_id=1, source_target_pairs={{0,1},{1,0},{2,3},{3,2},{4,5},{5,4},{6,7},{7,6},{8,9},{9,8},{10,11... | collective-permute-start | bytes 393224 | tf_op jit(solution)/shard_map/ppermute | solution.py:45
  68.2 1.3 %collective-permute-start.31 = (bf16[128,512]{1,0:T(8,128)(2,1)S(1)}, bf16[128,512]{1,0:T(8,128)(2,1)S(1)}, u32[]{:S(2)}, u32[]{:S(2)}) collective-permute-start(bf16[128,512]{1,0:T(8,128)(2,1)S(1)} %collective-permute-done.29.refs_1_), channel_id=1, source_target_pairs={{0,1},{1,0},{2,3},{3,2},{4,5},{5,4},{6,7},{7,6},{8,9},{9,8},{10,11... | collective-permute-start | bytes 393224 | tf_op jit(solution)/shard_map/ppermute | solution.py:45
  70.2 1.4 %collective-permute-start.32 = (f32[128,128]{1,0:T(8,128)S(1)}, f32[128,128]{1,0:T(8,128)S(1)}, u32[]{:S(2)}, u32[]{:S(2)}) collective-permute-start(f32[128,128]{1,0:T(8,128)S(1)} %get-tuple-element.48), channel_id=1, source_target_pairs={{0,1},{1,0},{2,3},{3,2},{4,5},{5,4},{6,7},{7,6},{8,9},{9,8},{10,11... | collective-permute-start | bytes 196616 | tf_op jit(solution)/shard_map/ppermute | solution.py:45
  71.6 5.4 %collective-permute-start.33 = (f32[128,128]{1,0:T(8,128)S(1)}, f32[128,128]{1,0:T(8,128)S(1)}, u32[]{:S(2)}, u32[]{:S(2)}) collective-permute-start(f32[128,128]{1,0:T(8,128)S(1)} %add.93), channel_id=1, source_target_pairs={{0,6},{1,7},{2,4},{3,5},{4,2},{5,3},{6,0},{7,1},{8,14},{9,15},{10,... | collective-permute-start | bytes 196616 | tf_op jit(solution)/shard_map/ppermute | solution.py:45
  73.1 4.7 %collective-permute-start.34 = (f32[128,128]{1,0:T(8,128)S(1)}, f32[128,128]{1,0:T(8,128)S(1)}, u32[]{:S(2)}, u32[]{:S(2)}) collective-permute-start(f32[128,128]{1,0:T(8,128)S(1)} %add.93), channel_id=1, source_target_pairs={{0,2},{1,5},{2,0},{3,7},{4,6},{5,1},{6,4},{7,3},{8,10},{9,13},{10,... | collective-permute-start | bytes 196616 | tf_op jit(solution)/shard_map/ppermute | solution.py:45
  74.1 4.3 %collective-permute-start.35 = (f32[128,128]{1,0:T(8,128)S(1)}, f32[128,128]{1,0:T(8,128)S(1)}, u32[]{:S(2)}, u32[]{:S(2)}) collective-permute-start(f32[128,128]{1,0:T(8,128)S(1)} %add.93), channel_id=1, source_target_pairs={{0,4},{1,3},{2,6},{3,1},{4,0},{5,7},{6,2},{7,5},{8,12},{9,11},{10,... | collective-permute-start | bytes 196616 | tf_op jit(solution)/shard_map/ppermute | solution.py:45
  78.4 5.7 %collective-permute-start.36 = (f32[128,128]{1,0:T(8,128)S(1)}, f32[128,128]{1,0:T(8,128)S(1)}, u32[]{:S(2)}, u32[]{:S(2)}) collective-permute-start(f32[128,128]{1,0:T(8,128)S(1)} %add_add_fusion.1), channel_id=1, source_target_pairs={{0,16},{1,17},{2,18},{3,19},{4,20},{5,21},{6,22},{7,23},{8,24},{9,... | collective-permute-start | bytes 196616 | tf_op jit(solution)/shard_map/ppermute | solution.py:45
  81.1 6.7 %collective-permute-start.37 = (f32[128,128]{1,0:T(8,128)S(1)}, f32[128,128]{1,0:T(8,128)S(1)}, u32[]{:S(2)}, u32[]{:S(2)}) collective-permute-start(f32[128,128]{1,0:T(8,128)S(1)} %add_add_fusion.1), channel_id=1, source_target_pairs={{0,24},{1,25},{2,26},{3,27},{4,28},{5,29},{6,30},{7,31},{8,16},{9,... | collective-permute-start | bytes 196616 | tf_op jit(solution)/shard_map/ppermute | solution.py:45
  83.5 4.7 %collective-permute-start.38 = (f32[128,128]{1,0:T(8,128)S(1)}, f32[128,128]{1,0:T(8,128)S(1)}, u32[]{:S(2)}, u32[]{:S(2)}) collective-permute-start(f32[128,128]{1,0:T(8,128)S(1)} %add_add_fusion.1), channel_id=1, source_target_pairs={{0,8},{1,9},{2,10},{3,11},{4,12},{5,13},{6,14},{7,15},{8,0},{9,1},... | collective-permute-start | bytes 196616 | tf_op jit(solution)/shard_map/ppermute | solution.py:45
  88.2 1.3 %collective-permute-start.39 = (f32[128,128]{1,0:T(8,128)S(1)}, f32[128,128]{1,0:T(8,128)S(1)}, u32[]{:S(2)}, u32[]{:S(2)}) collective-permute-start(f32[128,128]{1,0:T(8,128)S(1)} %add_add_fusion.own_ref), channel_id=1, source_target_pairs={{0,1},{1,0},{2,3},{3,2},{4,5},{5,4},{6,7},{7,6},{8,9},{9,8},{10,11... | collective-permute-start | bytes 196616 | tf_op jit(solution)/shard_map/ppermute | solution.py:45

commit v6 on v5

--- a/solution.py
+++ b/solution.py
@@ -78,7 +78,7 @@
 
 
 def load_kernel(basis_ref, atoms_ref, user_ref, *refs):
-    other_refs, own_refs, refs = refs[:QUARTERS], refs[QUARTERS : 2 * QUARTERS], refs[2 * QUARTERS :]
+    other_refs, refs = refs[:QUARTERS], refs[QUARTERS:]
     other_half_ref, own_half_ref, user_rows_ref, turned_ref, rows_ref, sems = refs
     own, other = halves()
 
@@ -100,9 +100,8 @@
     turned_ref[...] = rem
     copies[1].wait()
     products(1, range(QUARTERS), rem, other_half_ref, other_refs)
-    copies[2].wait()
-    products(0, range(QUARTERS), rem, own_half_ref, own_refs)
-    copies[3].wait()
+    for copy in copies[2:]:
+        copy.wait()
 
 
 def first_products(basis, atoms, user_residuals):
@@ -110,18 +109,18 @@
     block = atoms.shape[1]
     product = (block, count // (2 * QUARTERS))
     half = ((rows, count // 2), BF16)
-    shapes = [(product, BF16)] * QUARTERS + [(product, F32)] * QUARTERS
+    shapes = [(product, BF16)] * QUARTERS
     shapes += [half, half, (user_residuals.shape, BF16), ((block, rows), BF16)]
     arrays = [pltpu.with_memory_space_constraint(v, pltpu.HBM) for v in (basis, atoms, user_residuals)]
     results = call(
         load_kernel,
         shapes,
-        2 * atoms.size * count,
+        atoms.size * count,
         *arrays,
         in_specs=[HBM] * 3,
         scratch=[pltpu.VMEM(atoms.shape, BF16), pltpu.SemaphoreType.DMA((4,))],
     )
-    return results[:QUARTERS], results[QUARTERS : 2 * QUARTERS], *results[2 * QUARTERS :]
+    return results[:QUARTERS], *results[QUARTERS:]
 
 
 def coef_kernel(swapped, places, basis_ref, rem_ref, *out_refs):
@@ -313,13 +312,13 @@
     if not power or not tiled or block != 128 or user_residuals.shape[1] != block:
         return plain_local(old_basis, new_atoms, user_residuals)
 
-    other, own, other_half, own_half, user_rows, rem_low = first_products(old_basis, new_atoms, user_residuals)
+    other, other_half, own_half, user_rows, rem_low = first_products(old_basis, new_atoms, user_residuals)
     rem = rem_low
     for last in (False, True):
         if last:
             last_place = coef_call(True, (3,), other_half, rem_low)
             other = coef_call(True, (0, 1, 2), other_half, rem_low) + last_place
-            own = coef_call(False, (0, 1, 2, 3), own_half, rem_low)
+        own = coef_call(False, (0, 1, 2, 3), own_half, rem_low)
         dtypes = [BF16] if last and users == 1 else [F32, BF16]
         start = rem if users == 1 else jnp.zeros(rem.shape, F32)
         *new, rem_low = sweep(own_half, other_half, start, own, other, m_total, dtypes)

time: 94.8 us -> 94.6 us (level)
    pallas_call x14 -> x15, Pallas kernels: 12 us -> 12 us  [call(): pl.pallas_call(kernel, in_specs=in_specs or [VMEM] * len(operands), out_s...]
  transfers between devices with their start and end apart: 40 -> 40, of which waited for: 24 -> 23; matrix products, arithmetic and copies ran while one was open for 0% -> 0% of each run, Pallas kernels for 3% -> 4%
where the time goes in v6:
time: 94.6 us; the launch traced here: 94.4 us
  waiting for transfers between devices  43.8 us (46%)
  starting transfers between devices  37.2 us (39%)
  Pallas kernels  12 us (13%)
    ppermute x40, waiting for transfers between devices, swap(): lax.ppermute(value, 'rows', [(i, i ^ masks[i & 1]) for i in range(size)])  43.8 us
    ppermute x40, starting transfers between devices, swap(): lax.ppermute(value, 'rows', [(i, i ^ masks[i & 1]) for i in range(size)])  37.2 us
    pallas_call x15, Pallas kernels, call(): pl.pallas_call(kernel, in_specs=in_specs or [VMEM] * len(operands), out_s...  12 us
  transfers between devices with their start and end apart: 40, of which 23 were waited for; matrix products, arithmetic and copies ran while one was open for 0% of the time, Pallas kernels for 4%

profile of v6, /device:TPU:0, one launch (start us, length us, event | category | flops | bytes accessed | tf_op | source)
XLA Modules:
  0.0 94.4 jit_solution(16219111506077314482)
XLA Ops:
  0.6 2.0 %shard_map.50 = (bf16[128,512]{1,0:T(8,128)(2,1)S(1)}, bf16[128,512]{1,0:T(8,128)(2,1)S(1)}, bf16[128,512]{1,0:T(8,128)(2,1)S(1)}, bf16[128,512]{1,0:T(8,128)(2,...) custom-call(bf16[384,4096]{1,0:T(8,128)(2,1)} %basis_ref.1, ...), custom_call_target="tpu_custom_call" | custom-call | flops 201326592 | tf_op jit(solution)/shard_map/pallas_call | solution.py:49
  2.6 0.5 collective-permute-start.1
  3.2 0.4 collective-permute-start.5
  3.7 0.5 shard_map.51
  4.2 3.9 %collective-permute-start.2 = (bf16[128,512]{1,0:T(8,128)(2,1)S(1)}, bf16[128,512]{1,0:T(8,128)(2,1)S(1)}, u32[]{:S(2)}, u32[]{:S(2)}) collective-permute-start(bf16[128,512]{1,0:T(8,128)(2,1)S(1)} %add_convert_fusion.5), channel_id=1, source_target_pairs={{0,6},{1,11},{2,4},{3,9},{4,2},{5,15},{6,0},{7,13},{8,14},{9,3},{1... | collective-permute-start | bytes 393224 | tf_op jit(solution)/shard_map/ppermute | solution.py:45
  8.2 0.6 collective-permute-start.4
  8.9 4.1 %collective-permute-done.2 = bf16[128,512]{1,0:T(8,128)(2,1)S(1)} collective-permute-done((bf16[128,512]{1,0:T(8,128)(2,1)S(1)}, bf16[128,512]{1,0:T(8,128)(2,1)S(1)}, u32[]{:S(2)}, u32[]{:S(2)}) %collective-permute-start.2) | collective-permute-done | bytes 131104 | tf_op jit(solution)/shard_map/ppermute | solution.py:45
  13.0 1.7 %collective-permute-done.4 = bf16[128,512]{1,0:T(8,128)(2,1)S(1)} collective-permute-done((bf16[128,512]{1,0:T(8,128)(2,1)S(1)}, bf16[128,512]{1,0:T(8,128)(2,1)S(1)}, u32[]{:S(2)}, u32[]{:S(2)}) %collective-permute-start.4) | collective-permute-done | bytes 131104 | tf_op jit(solution)/shard_map/ppermute | solution.py:45
  14.8 1.8 %collective-permute-start.7 = (bf16[128,512]{1,0:T(8,128)(2,1)S(1)}, bf16[128,512]{1,0:T(8,128)(2,1)S(1)}, u32[]{:S(2)}, u32[]{:S(2)}) collective-permute-start(bf16[128,512]{1,0:T(8,128)(2,1)S(1)} %get-tuple-element.52), channel_id=1, source_target_pairs={{0,8},{1,17},{2,10},{3,19},{4,12},{5,21},{6,14},{7,23},{8,0},{9,25... | collective-permute-start | bytes 393224 | tf_op jit(solution)/shard_map/ppermute | solution.py:45
  16.6 3.4 %collective-permute-done.7 = bf16[128,512]{1,0:T(8,128)(2,1)S(1)} collective-permute-done((bf16[128,512]{1,0:T(8,128)(2,1)S(1)}, bf16[128,512]{1,0:T(8,128)(2,1)S(1)}, u32[]{:S(2)}, u32[]{:S(2)}) %collective-permute-start.7) | collective-permute-done | bytes 131104 | tf_op jit(solution)/shard_map/ppermute | solution.py:45
  20.1 3.0 %collective-permute-start.8 = (bf16[128,512]{1,0:T(8,128)(2,1)S(1)}, bf16[128,512]{1,0:T(8,128)(2,1)S(1)}, u32[]{:S(2)}, u32[]{:S(2)}) collective-permute-start(bf16[128,512]{1,0:T(8,128)(2,1)S(1)} %fusion), channel_id=1, source_target_pairs={{0,16},{1,5},{2,18},{3,7},{4,20},{5,1},{6,22},{7,3},{8,24},{9,13},... | collective-permute-start | bytes 393224 | tf_op jit(solution)/shard_map/ppermute | solution.py:45
  23.1 2.9 %collective-permute-done.8 = bf16[128,512]{1,0:T(8,128)(2,1)S(1)} collective-permute-done((bf16[128,512]{1,0:T(8,128)(2,1)S(1)}, bf16[128,512]{1,0:T(8,128)(2,1)S(1)}, u32[]{:S(2)}, u32[]{:S(2)}) %collective-permute-start.8) | collective-permute-done | bytes 131104 | tf_op jit(solution)/shard_map/ppermute | solution.py:45
  26.1 2.5 %collective-permute-start.9 = (bf16[128,512]{1,0:T(8,128)(2,1)S(1)}, bf16[128,512]{1,0:T(8,128)(2,1)S(1)}, u32[]{:S(2)}, u32[]{:S(2)}) collective-permute-start(bf16[128,512]{1,0:T(8,128)(2,1)S(1)} %multiply_convert_fusion.1.refs_0_), channel_id=1, source_target_pairs={{0,6},{1,11},{2,4},{3,9},{4,2},{5,15},{6,0},{7,13},{8,14},{9,3},{1... | collective-permute-start | bytes 393224 | tf_op jit(solution)/shard_map/ppermute | solution.py:45
  28.6 0.6 collective-permute-start.12
  29.1 0.5 collective-permute-start.13
  29.7 3.3 %collective-permute-done.9.refs_1_ = bf16[128,512]{1,0:T(8,128)(2,1)S(1)} collective-permute-done((bf16[128,512]{1,0:T(8,128)(2,1)S(1)}, bf16[128,512]{1,0:T(8,128)(2,1)S(1)}, u32[]{:S(2)}, u32[]{:S(2)}) %collective-permute-start.9) | collective-permute-done | bytes 131104 | tf_op jit(solution)/shard_map/ppermute | solution.py:45
  32.9 0.6 collective-permute-done.12.refs_0_
  33.5 0.8 collective-permute-done.13.refs_1_
  34.3 0.4 shard_map.52.rem_ref
  34.7 0.4 shard_map.53.rem_ref
  35.1 0.4 shard_map.54.rem_ref
  35.6 0.1 collective-permute-done.15.refs_1_
  35.7 0.4 shard_map.55
  36.1 0.2 shard_map.58
  36.3 0.5 collective-permute-start.17
  36.8 0.4 shard_map.57
  37.2 0.2 collective-permute-start.19
  37.4 0.4 collective-permute-start.21
  37.9 0.4 shard_map.56
  38.3 1.8 %collective-permute-start.18 = (bf16[128,512]{1,0:T(8,128)(2,1)S(1)}, bf16[128,512]{1,0:T(8,128)(2,1)S(1)}, u32[]{:S(2)}, u32[]{:S(2)}) collective-permute-start(bf16[128,512]{1,0:T(8,128)(2,1)S(1)} %add_convert_fusion.2), channel_id=1, source_target_pairs={{0,6},{1,11},{2,4},{3,9},{4,2},{5,15},{6,0},{7,13},{8,14},{9,3},{1... | collective-permute-start | bytes 393224 | tf_op jit(solution)/shard_map/ppermute | solution.py:45
  40.2 0.7 collective-permute-start.20
  41.0 1.1 %collective-permute-start.22 = (bf16[128,512]{1,0:T(8,128)(2,1)S(1)}, bf16[128,512]{1,0:T(8,128)(2,1)S(1)}, u32[]{:S(2)}, u32[]{:S(2)}) collective-permute-start(bf16[128,512]{1,0:T(8,128)(2,1)S(1)} %add_convert_fusion), channel_id=1, source_target_pairs={{0,4},{1,3},{2,6},{3,1},{4,0},{5,7},{6,2},{7,5},{8,12},{9,11},{10,... | collective-permute-start | bytes 393224 | tf_op jit(solution)/shard_map/ppermute | solution.py:45
  42.1 4.4 %collective-permute-done.18 = bf16[128,512]{1,0:T(8,128)(2,1)S(1)} collective-permute-done((bf16[128,512]{1,0:T(8,128)(2,1)S(1)}, bf16[128,512]{1,0:T(8,128)(2,1)S(1)}, u32[]{:S(2)}, u32[]{:S(2)}) %collective-permute-start.18) | collective-permute-done | bytes 131104 | tf_op jit(solution)/shard_map/ppermute | solution.py:45
  46.5 1.5 %collective-permute-done.20 = bf16[128,512]{1,0:T(8,128)(2,1)S(1)} collective-permute-done((bf16[128,512]{1,0:T(8,128)(2,1)S(1)}, bf16[128,512]{1,0:T(8,128)(2,1)S(1)}, u32[]{:S(2)}, u32[]{:S(2)}) %collective-permute-start.20) | collective-permute-done | bytes 131104 | tf_op jit(solution)/shard_map/ppermute | solution.py:45
  48.1 2.1 %collective-permute-start.23 = (bf16[128,512]{1,0:T(8,128)(2,1)S(1)}, bf16[128,512]{1,0:T(8,128)(2,1)S(1)}, u32[]{:S(2)}, u32[]{:S(2)}) collective-permute-start(bf16[128,512]{1,0:T(8,128)(2,1)S(1)} %get-tuple-element.50), channel_id=1, source_target_pairs={{0,8},{1,17},{2,10},{3,19},{4,12},{5,21},{6,14},{7,23},{8,0},{9,25... | collective-permute-start | bytes 393224 | tf_op jit(solution)/shard_map/ppermute | solution.py:45
  50.2 4.0 %collective-permute-done.23 = bf16[128,512]{1,0:T(8,128)(2,1)S(1)} collective-permute-done((bf16[128,512]{1,0:T(8,128)(2,1)S(1)}, bf16[128,512]{1,0:T(8,128)(2,1)S(1)}, u32[]{:S(2)}, u32[]{:S(2)}) %collective-permute-start.23) | collective-permute-done | bytes 131104 | tf_op jit(solution)/shard_map/ppermute | solution.py:45
  54.3 2.8 %collective-permute-start.24 = (bf16[128,512]{1,0:T(8,128)(2,1)S(1)}, bf16[128,512]{1,0:T(8,128)(2,1)S(1)}, u32[]{:S(2)}, u32[]{:S(2)}) collective-permute-start(bf16[128,512]{1,0:T(8,128)(2,1)S(1)} %fusion.1), channel_id=1, source_target_pairs={{0,16},{1,5},{2,18},{3,7},{4,20},{5,1},{6,22},{7,3},{8,24},{9,13},... | collective-permute-start | bytes 393224 | tf_op jit(solution)/shard_map/ppermute | solution.py:45
  57.1 3.2 %collective-permute-done.24 = bf16[128,512]{1,0:T(8,128)(2,1)S(1)} collective-permute-done((bf16[128,512]{1,0:T(8,128)(2,1)S(1)}, bf16[128,512]{1,0:T(8,128)(2,1)S(1)}, u32[]{:S(2)}, u32[]{:S(2)}) %collective-permute-start.24) | collective-permute-done | bytes 131104 | tf_op jit(solution)/shard_map/ppermute | solution.py:45
  60.3 1.4 %collective-permute-start.25 = (bf16[128,512]{1,0:T(8,128)(2,1)S(1)}, bf16[128,512]{1,0:T(8,128)(2,1)S(1)}, u32[]{:S(2)}, u32[]{:S(2)}) collective-permute-start(bf16[128,512]{1,0:T(8,128)(2,1)S(1)} %multiply_convert_fusion.refs_0_), channel_id=1, source_target_pairs={{0,6},{1,11},{2,4},{3,9},{4,2},{5,15},{6,0},{7,13},{8,14},{9,3},{1... | collective-permute-start | bytes 393224 | tf_op jit(solution)/shard_map/ppermute | solution.py:45
  61.6 1.3 %collective-permute-start.28 = (bf16[128,512]{1,0:T(8,128)(2,1)S(1)}, bf16[128,512]{1,0:T(8,128)(2,1)S(1)}, u32[]{:S(2)}, u32[]{:S(2)}) collective-permute-start(bf16[128,512]{1,0:T(8,128)(2,1)S(1)} %multiply_convert_fusion.refs_0_), channel_id=1, source_target_pairs={{0,2},{1,9},{2,0},{3,11},{4,6},{5,13},{6,4},{7,15},{8,10},{9,1},{1... | collective-permute-start | bytes 393224 | tf_op jit(solution)/shard_map/ppermute | solution.py:45
  62.9 0.9 collective-permute-start.29
  63.8 2.7 %collective-permute-done.25.refs_1_ = bf16[128,512]{1,0:T(8,128)(2,1)S(1)} collective-permute-done((bf16[128,512]{1,0:T(8,128)(2,1)S(1)}, bf16[128,512]{1,0:T(8,128)(2,1)S(1)}, u32[]{:S(2)}, u32[]{:S(2)}) %collective-permute-start.25) | collective-permute-done | bytes 131104 | tf_op jit(solution)/shard_map/ppermute | solution.py:45
  66.5 0.8 collective-permute-done.28.refs_0_
  67.3 0.6 collective-permute-done.29.refs_1_
  67.9 0.4 shard_map.59.rem_ref
  68.3 0.4 shard_map.60.rem_ref
  68.7 0.4 shard_map.61.rem_ref
  69.3 0.4 shard_map.62.turned_ref
  69.7 0.3 shard_map.63
  69.9 0.5 collective-permute-start.32
  70.4 0.9 collective-permute-done.32
  71.3 1.5 %collective-permute-start.33 = (f32[128,128]{1,0:T(8,128)S(1)}, f32[128,128]{1,0:T(8,128)S(1)}, u32[]{:S(2)}, u32[]{:S(2)}) collective-permute-start(f32[128,128]{1,0:T(8,128)S(1)} %add.93), channel_id=1, source_target_pairs={{0,6},{1,7},{2,4},{3,5},{4,2},{5,3},{6,0},{7,1},{8,14},{9,15},{10,... | collective-permute-start | bytes 196616 | tf_op jit(solution)/shard_map/ppermute | solution.py:45
  72.8 1.0 %collective-permute-start.34 = (f32[128,128]{1,0:T(8,128)S(1)}, f32[128,128]{1,0:T(8,128)S(1)}, u32[]{:S(2)}, u32[]{:S(2)}) collective-permute-start(f32[128,128]{1,0:T(8,128)S(1)} %add.93), channel_id=1, source_target_pairs={{0,2},{1,5},{2,0},{3,7},{4,6},{5,1},{6,4},{7,3},{8,10},{9,13},{10,... | collective-permute-start | bytes 196616 | tf_op jit(solution)/shard_map/ppermute | solution.py:45
  73.8 1.1 %collective-permute-start.35 = (f32[128,128]{1,0:T(8,128)S(1)}, f32[128,128]{1,0:T(8,128)S(1)}, u32[]{:S(2)}, u32[]{:S(2)}) collective-permute-start(f32[128,128]{1,0:T(8,128)S(1)} %add.93), channel_id=1, source_target_pairs={{0,4},{1,3},{2,6},{3,1},{4,0},{5,7},{6,2},{7,5},{8,12},{9,11},{10,... | collective-permute-start | bytes 196616 | tf_op jit(solution)/shard_map/ppermute | solution.py:45
  74.9 1.9 %collective-permute-done.33 = f32[128,128]{1,0:T(8,128)S(1)} collective-permute-done((f32[128,128]{1,0:T(8,128)S(1)}, f32[128,128]{1,0:T(8,128)S(1)}, u32[]{:S(2)}, u32[]{:S(2)}) %collective-permute-start.33) | collective-permute-done | bytes 65568 | tf_op jit(solution)/shard_map/ppermute | solution.py:45
  76.7 0.7 collective-permute-done.34
  77.5 0.6 collective-permute-done.35
  78.1 2.8 %collective-permute-start.36 = (f32[128,128]{1,0:T(8,128)S(1)}, f32[128,128]{1,0:T(8,128)S(1)}, u32[]{:S(2)}, u32[]{:S(2)}) collective-permute-start(f32[128,128]{1,0:T(8,128)S(1)} %add_add_fusion.1), channel_id=1, source_target_pairs={{0,16},{1,17},{2,18},{3,19},{4,20},{5,21},{6,22},{7,23},{8,24},{9,... | collective-permute-start | bytes 196616 | tf_op jit(solution)/shard_map/ppermute | solution.py:45
  80.8 2.4 %collective-permute-start.37 = (f32[128,128]{1,0:T(8,128)S(1)}, f32[128,128]{1,0:T(8,128)S(1)}, u32[]{:S(2)}, u32[]{:S(2)}) collective-permute-start(f32[128,128]{1,0:T(8,128)S(1)} %add_add_fusion.1), channel_id=1, source_target_pairs={{0,24},{1,25},{2,26},{3,27},{4,28},{5,29},{6,30},{7,31},{8,16},{9,... | collective-permute-start | bytes 196616 | tf_op jit(solution)/shard_map/ppermute | solution.py:45
  83.2 0.5 collective-permute-start.38
  83.7 3.9 %collective-permute-done.37 = f32[128,128]{1,0:T(8,128)S(1)} collective-permute-done((f32[128,128]{1,0:T(8,128)S(1)}, f32[128,128]{1,0:T(8,128)S(1)}, u32[]{:S(2)}, u32[]{:S(2)}) %collective-permute-start.37) | collective-permute-done | bytes 65568 | tf_op jit(solution)/shard_map/ppermute | solution.py:45
  87.6 0.3 collective-permute-done.38
  88.0 1.2 %collective-permute-done.39.other_ref = f32[128,128]{1,0:T(8,128)S(1)} collective-permute-done((f32[128,128]{1,0:T(8,128)S(1)}, f32[128,128]{1,0:T(8,128)S(1)}, u32[]{:S(2)}, u32[]{:S(2)}) %collective-permute-start.39) | collective-permute-done | bytes 65568 | tf_op jit(solution)/shard_map/ppermute | solution.py:45
  89.2 5.2 %shard_map.64 = (bf16[384,128]{1,0:T(8,128)(2,1)}, bf16[384,128]{1,0:T(8,128)(2,1)}) custom-call(f32[128,128]{1,0:T(8,128)S(1)} %add_add_fusion.own_ref, f32[128,128]{1,0:T(8,128)S(1)} %collective-permute-done.39.other_ref, bf16[384,128]{1,0:T(8,128)(2,1)S(1)} %get-tuple-element.49.rem_ref, bf16[384,128]{1,0:T(8,128)(2,1)S(1)} %get-tuple-element.46.user_ref), custom_call_target="tpu_custom_call" | custom-call | tf_op jit(solution)/shard_map/pallas_call | solution.py:49
  (46 shorter events, 1.2 us)
Async XLA Ops:
  2.6 1.6 %collective-permute-start.1 = (bf16[128,512]{1,0:T(8,128)(2,1)S(1)}, bf16[128,512]{1,0:T(8,128)(2,1)S(1)}, u32[]{:S(2)}, u32[]{:S(2)}) collective-permute-start(bf16[128,512]{1,0:T(8,128)(2,1)S(1)} %get-tuple-element.32), channel_id=1, source_target_pairs={{0,1},{1,0},{2,3},{3,2},{4,5},{5,4},{6,7},{7,6},{8,9},{9,8},{10,11... | collective-permute-start | bytes 393224 | tf_op jit(solution)/shard_map/ppermute | solution.py:45
  3.1 5.0 %collective-permute-start.3 = (bf16[128,512]{1,0:T(8,128)(2,1)S(1)}, bf16[128,512]{1,0:T(8,128)(2,1)S(1)}, u32[]{:S(2)}, u32[]{:S(2)}) collective-permute-start(bf16[128,512]{1,0:T(8,128)(2,1)S(1)} %get-tuple-element.34), channel_id=1, source_target_pairs={{0,1},{1,0},{2,3},{3,2},{4,5},{5,4},{6,7},{7,6},{8,9},{9,8},{10,11... | collective-permute-start | bytes 393224 | tf_op jit(solution)/shard_map/ppermute | solution.py:45
  3.2 5.6 %collective-permute-start.5 = (bf16[128,512]{1,0:T(8,128)(2,1)S(1)}, bf16[128,512]{1,0:T(8,128)(2,1)S(1)}, u32[]{:S(2)}, u32[]{:S(2)}) collective-permute-start(bf16[128,512]{1,0:T(8,128)(2,1)S(1)} %get-tuple-element.36), channel_id=1, source_target_pairs={{0,1},{1,0},{2,3},{3,2},{4,5},{5,4},{6,7},{7,6},{8,9},{9,8},{10,11... | collective-permute-start | bytes 393224 | tf_op jit(solution)/shard_map/ppermute | solution.py:45
  3.6 5.3 %collective-permute-start = (bf16[128,512]{1,0:T(8,128)(2,1)S(1)}, bf16[128,512]{1,0:T(8,128)(2,1)S(1)}, u32[]{:S(2)}, u32[]{:S(2)}) collective-permute-start(bf16[128,512]{1,0:T(8,128)(2,1)S(1)} %get-tuple-element.30), channel_id=1, source_target_pairs={{0,1},{1,0},{2,3},{3,2},{4,5},{5,4},{6,7},{7,6},{8,9},{9,8},{10,11... | collective-permute-start | bytes 393224 | tf_op jit(solution)/shard_map/ppermute | solution.py:45
  4.2 8.8 %collective-permute-start.2 = (bf16[128,512]{1,0:T(8,128)(2,1)S(1)}, bf16[128,512]{1,0:T(8,128)(2,1)S(1)}, u32[]{:S(2)}, u32[]{:S(2)}) collective-permute-start(bf16[128,512]{1,0:T(8,128)(2,1)S(1)} %add_convert_fusion.5), channel_id=1, source_target_pairs={{0,6},{1,11},{2,4},{3,9},{4,2},{5,15},{6,0},{7,13},{8,14},{9,3},{1... | collective-permute-start | bytes 393224 | tf_op jit(solution)/shard_map/ppermute | solution.py:45
  8.2 6.6 %collective-permute-start.4 = (bf16[128,512]{1,0:T(8,128)(2,1)S(1)}, bf16[128,512]{1,0:T(8,128)(2,1)S(1)}, u32[]{:S(2)}, u32[]{:S(2)}) collective-permute-start(bf16[128,512]{1,0:T(8,128)(2,1)S(1)} %add_convert_fusion.4), channel_id=1, source_target_pairs={{0,2},{1,9},{2,0},{3,11},{4,6},{5,13},{6,4},{7,15},{8,10},{9,1},{1... | collective-permute-start | bytes 393224 | tf_op jit(solution)/shard_map/ppermute | solution.py:45
  8.8 5.9 %collective-permute-start.6 = (bf16[128,512]{1,0:T(8,128)(2,1)S(1)}, bf16[128,512]{1,0:T(8,128)(2,1)S(1)}, u32[]{:S(2)}, u32[]{:S(2)}) collective-permute-start(bf16[128,512]{1,0:T(8,128)(2,1)S(1)} %add_convert_fusion.3), channel_id=1, source_target_pairs={{0,4},{1,3},{2,6},{3,1},{4,0},{5,7},{6,2},{7,5},{8,12},{9,11},{10,... | collective-permute-start | bytes 393224 | tf_op jit(solution)/shard_map/ppermute | solution.py:45
  14.8 5.2 %collective-permute-start.7 = (bf16[128,512]{1,0:T(8,128)(2,1)S(1)}, bf16[128,512]{1,0:T(8,128)(2,1)S(1)}, u32[]{:S(2)}, u32[]{:S(2)}) collective-permute-start(bf16[128,512]{1,0:T(8,128)(2,1)S(1)} %get-tuple-element.52), channel_id=1, source_target_pairs={{0,8},{1,17},{2,10},{3,19},{4,12},{5,21},{6,14},{7,23},{8,0},{9,25... | collective-permute-start | bytes 393224 | tf_op jit(solution)/shard_map/ppermute | solution.py:45
  20.1 6.0 %collective-permute-start.8 = (bf16[128,512]{1,0:T(8,128)(2,1)S(1)}, bf16[128,512]{1,0:T(8,128)(2,1)S(1)}, u32[]{:S(2)}, u32[]{:S(2)}) collective-permute-start(bf16[128,512]{1,0:T(8,128)(2,1)S(1)} %fusion), channel_id=1, source_target_pairs={{0,16},{1,5},{2,18},{3,7},{4,20},{5,1},{6,22},{7,3},{8,24},{9,13},... | collective-permute-start | bytes 393224 | tf_op jit(solution)/shard_map/ppermute | solution.py:45
  26.1 6.8 %collective-permute-start.9 = (bf16[128,512]{1,0:T(8,128)(2,1)S(1)}, bf16[128,512]{1,0:T(8,128)(2,1)S(1)}, u32[]{:S(2)}, u32[]{:S(2)}) collective-permute-start(bf16[128,512]{1,0:T(8,128)(2,1)S(1)} %multiply_convert_fusion.1.refs_0_), channel_id=1, source_target_pairs={{0,6},{1,11},{2,4},{3,9},{4,2},{5,15},{6,0},{7,13},{8,14},{9,3},{1... | collective-permute-start | bytes 393224 | tf_op jit(solution)/shard_map/ppermute | solution.py:45
  28.6 5.0 %collective-permute-start.12 = (bf16[128,512]{1,0:T(8,128)(2,1)S(1)}, bf16[128,512]{1,0:T(8,128)(2,1)S(1)}, u32[]{:S(2)}, u32[]{:S(2)}) collective-permute-start(bf16[128,512]{1,0:T(8,128)(2,1)S(1)} %multiply_convert_fusion.1.refs_0_), channel_id=1, source_target_pairs={{0,2},{1,9},{2,0},{3,11},{4,6},{5,13},{6,4},{7,15},{8,10},{9,1},{1... | collective-permute-start | bytes 393224 | tf_op jit(solution)/shard_map/ppermute | solution.py:45
  29.1 5.2 %collective-permute-start.13 = (bf16[128,512]{1,0:T(8,128)(2,1)S(1)}, bf16[128,512]{1,0:T(8,128)(2,1)S(1)}, u32[]{:S(2)}, u32[]{:S(2)}) collective-permute-start(bf16[128,512]{1,0:T(8,128)(2,1)S(1)} %multiply_convert_fusion.1.refs_0_), channel_id=1, source_target_pairs={{0,4},{1,3},{2,6},{3,1},{4,0},{5,7},{6,2},{7,5},{8,12},{9,11},{10,... | collective-permute-start | bytes 393224 | tf_op jit(solution)/shard_map/ppermute | solution.py:45
  29.7 5.1 %collective-permute-start.10 = (bf16[128,512]{1,0:T(8,128)(2,1)S(1)}, bf16[128,512]{1,0:T(8,128)(2,1)S(1)}, u32[]{:S(2)}, u32[]{:S(2)}) collective-permute-start(bf16[128,512]{1,0:T(8,128)(2,1)S(1)} %multiply_convert_fusion.1.refs_0_), channel_id=1, source_target_pairs={{0,1},{1,0},{2,3},{3,2},{4,5},{5,4},{6,7},{7,6},{8,9},{9,8},{10,11... | collective-permute-start | bytes 393224 | tf_op jit(solution)/shard_map/ppermute | solution.py:45
  32.9 1.8 %collective-permute-start.11 = (bf16[128,512]{1,0:T(8,128)(2,1)S(1)}, bf16[128,512]{1,0:T(8,128)(2,1)S(1)}, u32[]{:S(2)}, u32[]{:S(2)}) collective-permute-start(bf16[128,512]{1,0:T(8,128)(2,1)S(1)} %collective-permute-done.9.refs_1_), channel_id=1, source_target_pairs={{0,1},{1,0},{2,3},{3,2},{4,5},{5,4},{6,7},{7,6},{8,9},{9,8},{10,11... | collective-permute-start | bytes 393224 | tf_op jit(solution)/shard_map/ppermute | solution.py:45
  33.5 2.0 %collective-permute-start.14 = (bf16[128,512]{1,0:T(8,128)(2,1)S(1)}, bf16[128,512]{1,0:T(8,128)(2,1)S(1)}, u32[]{:S(2)}, u32[]{:S(2)}) collective-permute-start(bf16[128,512]{1,0:T(8,128)(2,1)S(1)} %collective-permute-done.12.refs_0_), channel_id=1, source_target_pairs={{0,1},{1,0},{2,3},{3,2},{4,5},{5,4},{6,7},{7,6},{8,9},{9,8},{10,11... | collective-permute-start | bytes 393224 | tf_op jit(solution)/shard_map/ppermute | solution.py:45
  34.3 1.3 %collective-permute-start.15 = (bf16[128,512]{1,0:T(8,128)(2,1)S(1)}, bf16[128,512]{1,0:T(8,128)(2,1)S(1)}, u32[]{:S(2)}, u32[]{:S(2)}) collective-permute-start(bf16[128,512]{1,0:T(8,128)(2,1)S(1)} %collective-permute-done.13.refs_1_), channel_id=1, source_target_pairs={{0,1},{1,0},{2,3},{3,2},{4,5},{5,4},{6,7},{7,6},{8,9},{9,8},{10,11... | collective-permute-start | bytes 393224 | tf_op jit(solution)/shard_map/ppermute | solution.py:45
  36.3 2.0 %collective-permute-start.17 = (bf16[128,512]{1,0:T(8,128)(2,1)S(1)}, bf16[128,512]{1,0:T(8,128)(2,1)S(1)}, u32[]{:S(2)}, u32[]{:S(2)}) collective-permute-start(bf16[128,512]{1,0:T(8,128)(2,1)S(1)} %shard_map.58), channel_id=1, source_target_pairs={{0,1},{1,0},{2,3},{3,2},{4,5},{5,4},{6,7},{7,6},{8,9},{9,8},{10,11... | collective-permute-start | bytes 393224 | tf_op jit(solution)/shard_map/ppermute | solution.py:45
  37.2 3.0 %collective-permute-start.19 = (bf16[128,512]{1,0:T(8,128)(2,1)S(1)}, bf16[128,512]{1,0:T(8,128)(2,1)S(1)}, u32[]{:S(2)}, u32[]{:S(2)}) collective-permute-start(bf16[128,512]{1,0:T(8,128)(2,1)S(1)} %get-tuple-element.43), channel_id=1, source_target_pairs={{0,1},{1,0},{2,3},{3,2},{4,5},{5,4},{6,7},{7,6},{8,9},{9,8},{10,11... | collective-permute-start | bytes 393224 | tf_op jit(solution)/shard_map/ppermute | solution.py:45
  37.4 3.6 %collective-permute-start.21 = (bf16[128,512]{1,0:T(8,128)(2,1)S(1)}, bf16[128,512]{1,0:T(8,128)(2,1)S(1)}, u32[]{:S(2)}, u32[]{:S(2)}) collective-permute-start(bf16[128,512]{1,0:T(8,128)(2,1)S(1)} %get-tuple-element.45), channel_id=1, source_target_pairs={{0,1},{1,0},{2,3},{3,2},{4,5},{5,4},{6,7},{7,6},{8,9},{9,8},{10,11... | collective-permute-start | bytes 393224 | tf_op jit(solution)/shard_map/ppermute | solution.py:45
  37.7 4.4 %collective-permute-start.16 = (bf16[128,512]{1,0:T(8,128)(2,1)S(1)}, bf16[128,512]{1,0:T(8,128)(2,1)S(1)}, u32[]{:S(2)}, u32[]{:S(2)}) collective-permute-start(bf16[128,512]{1,0:T(8,128)(2,1)S(1)} %get-tuple-element.40), channel_id=1, source_target_pairs={{0,1},{1,0},{2,3},{3,2},{4,5},{5,4},{6,7},{7,6},{8,9},{9,8},{10,11... | collective-permute-start | bytes 393224 | tf_op jit(solution)/shard_map/ppermute | solution.py:45
  38.3 8.2 %collective-permute-start.18 = (bf16[128,512]{1,0:T(8,128)(2,1)S(1)}, bf16[128,512]{1,0:T(8,128)(2,1)S(1)}, u32[]{:S(2)}, u32[]{:S(2)}) collective-permute-start(bf16[128,512]{1,0:T(8,128)(2,1)S(1)} %add_convert_fusion.2), channel_id=1, source_target_pairs={{0,6},{1,11},{2,4},{3,9},{4,2},{5,15},{6,0},{7,13},{8,14},{9,3},{1... | collective-permute-start | bytes 393224 | tf_op jit(solution)/shard_map/ppermute | solution.py:45
  40.2 7.8 %collective-permute-start.20 = (bf16[128,512]{1,0:T(8,128)(2,1)S(1)}, bf16[128,512]{1,0:T(8,128)(2,1)S(1)}, u32[]{:S(2)}, u32[]{:S(2)}) collective-permute-start(bf16[128,512]{1,0:T(8,128)(2,1)S(1)} %add_convert_fusion.1), channel_id=1, source_target_pairs={{0,2},{1,9},{2,0},{3,11},{4,6},{5,13},{6,4},{7,15},{8,10},{9,1},{1... | collective-permute-start | bytes 393224 | tf_op jit(solution)/shard_map/ppermute | solution.py:45
  41.0 7.0 %collective-permute-start.22 = (bf16[128,512]{1,0:T(8,128)(2,1)S(1)}, bf16[128,512]{1,0:T(8,128)(2,1)S(1)}, u32[]{:S(2)}, u32[]{:S(2)}) collective-permute-start(bf16[128,512]{1,0:T(8,128)(2,1)S(1)} %add_convert_fusion), channel_id=1, source_target_pairs={{0,4},{1,3},{2,6},{3,1},{4,0},{5,7},{6,2},{7,5},{8,12},{9,11},{10,... | collective-permute-start | bytes 393224 | tf_op jit(solution)/shard_map/ppermute | solution.py:45
  48.1 6.2 %collective-permute-start.23 = (bf16[128,512]{1,0:T(8,128)(2,1)S(1)}, bf16[128,512]{1,0:T(8,128)(2,1)S(1)}, u32[]{:S(2)}, u32[]{:S(2)}) collective-permute-start(bf16[128,512]{1,0:T(8,128)(2,1)S(1)} %get-tuple-element.50), channel_id=1, source_target_pairs={{0,8},{1,17},{2,10},{3,19},{4,12},{5,21},{6,14},{7,23},{8,0},{9,25... | collective-permute-start | bytes 393224 | tf_op jit(solution)/shard_map/ppermute | solution.py:45
  54.3 5.9 %collective-permute-start.24 = (bf16[128,512]{1,0:T(8,128)(2,1)S(1)}, bf16[128,512]{1,0:T(8,128)(2,1)S(1)}, u32[]{:S(2)}, u32[]{:S(2)}) collective-permute-start(bf16[128,512]{1,0:T(8,128)(2,1)S(1)} %fusion.1), channel_id=1, source_target_pairs={{0,16},{1,5},{2,18},{3,7},{4,20},{5,1},{6,22},{7,3},{8,24},{9,13},... | collective-permute-start | bytes 393224 | tf_op jit(solution)/shard_map/ppermute | solution.py:45
  60.3 6.2 %collective-permute-start.25 = (bf16[128,512]{1,0:T(8,128)(2,1)S(1)}, bf16[128,512]{1,0:T(8,128)(2,1)S(1)}, u32[]{:S(2)}, u32[]{:S(2)}) collective-permute-start(bf16[128,512]{1,0:T(8,128)(2,1)S(1)} %multiply_convert_fusion.refs_0_), channel_id=1, source_target_pairs={{0,6},{1,11},{2,4},{3,9},{4,2},{5,15},{6,0},{7,13},{8,14},{9,3},{1... | collective-permute-start | bytes 393224 | tf_op jit(solution)/shard_map/ppermute | solution.py:45
  61.6 5.6 %collective-permute-start.28 = (bf16[128,512]{1,0:T(8,128)(2,1)S(1)}, bf16[128,512]{1,0:T(8,128)(2,1)S(1)}, u32[]{:S(2)}, u32[]{:S(2)}) collective-permute-start(bf16[128,512]{1,0:T(8,128)(2,1)S(1)} %multiply_convert_fusion.refs_0_), channel_id=1, source_target_pairs={{0,2},{1,9},{2,0},{3,11},{4,6},{5,13},{6,4},{7,15},{8,10},{9,1},{1... | collective-permute-start | bytes 393224 | tf_op jit(solution)/shard_map/ppermute | solution.py:45
  62.9 5.0 %collective-permute-start.29 = (bf16[128,512]{1,0:T(8,128)(2,1)S(1)}, bf16[128,512]{1,0:T(8,128)(2,1)S(1)}, u32[]{:S(2)}, u32[]{:S(2)}) collective-permute-start(bf16[128,512]{1,0:T(8,128)(2,1)S(1)} %multiply_convert_fusion.refs_0_), channel_id=1, source_target_pairs={{0,4},{1,3},{2,6},{3,1},{4,0},{5,7},{6,2},{7,5},{8,12},{9,11},{10,... | collective-permute-start | bytes 393224 | tf_op jit(solution)/shard_map/ppermute | solution.py:45
  63.8 4.5 %collective-permute-start.26 = (bf16[128,512]{1,0:T(8,128)(2,1)S(1)}, bf16[128,512]{1,0:T(8,128)(2,1)S(1)}, u32[]{:S(2)}, u32[]{:S(2)}) collective-permute-start(bf16[128,512]{1,0:T(8,128)(2,1)S(1)} %multiply_convert_fusion.refs_0_), channel_id=1, source_target_pairs={{0,1},{1,0},{2,3},{3,2},{4,5},{5,4},{6,7},{7,6},{8,9},{9,8},{10,11... | collective-permute-start | bytes 393224 | tf_op jit(solution)/shard_map/ppermute | solution.py:45
  66.5 1.8 %collective-permute-start.27 = (bf16[128,512]{1,0:T(8,128)(2,1)S(1)}, bf16[128,512]{1,0:T(8,128)(2,1)S(1)}, u32[]{:S(2)}, u32[]{:S(2)}) collective-permute-start(bf16[128,512]{1,0:T(8,128)(2,1)S(1)} %collective-permute-done.25.refs_1_), channel_id=1, source_target_pairs={{0,1},{1,0},{2,3},{3,2},{4,5},{5,4},{6,7},{7,6},{8,9},{9,8},{10,11... | collective-permute-start | bytes 393224 | tf_op jit(solution)/shard_map/ppermute | solution.py:45
  67.3 1.9 %collective-permute-start.30 = (bf16[128,512]{1,0:T(8,128)(2,1)S(1)}, bf16[128,512]{1,0:T(8,128)(2,1)S(1)}, u32[]{:S(2)}, u32[]{:S(2)}) collective-permute-start(bf16[128,512]{1,0:T(8,128)(2,1)S(1)} %collective-permute-done.28.refs_0_), channel_id=1, source_target_pairs={{0,1},{1,0},{2,3},{3,2},{4,5},{5,4},{6,7},{7,6},{8,9},{9,8},{10,11... | collective-permute-start | bytes 393224 | tf_op jit(solution)/shard_map/ppermute | solution.py:45
  67.9 1.3 %collective-permute-start.31 = (bf16[128,512]{1,0:T(8,128)(2,1)S(1)}, bf16[128,512]{1,0:T(8,128)(2,1)S(1)}, u32[]{:S(2)}, u32[]{:S(2)}) collective-permute-start(bf16[128,512]{1,0:T(8,128)(2,1)S(1)} %collective-permute-done.29.refs_1_), channel_id=1, source_target_pairs={{0,1},{1,0},{2,3},{3,2},{4,5},{5,4},{6,7},{7,6},{8,9},{9,8},{10,11... | collective-permute-start | bytes 393224 | tf_op jit(solution)/shard_map/ppermute | solution.py:45
  69.9 1.4 %collective-permute-start.32 = (f32[128,128]{1,0:T(8,128)S(1)}, f32[128,128]{1,0:T(8,128)S(1)}, u32[]{:S(2)}, u32[]{:S(2)}) collective-permute-start(f32[128,128]{1,0:T(8,128)S(1)} %get-tuple-element.48), channel_id=1, source_target_pairs={{0,1},{1,0},{2,3},{3,2},{4,5},{5,4},{6,7},{7,6},{8,9},{9,8},{10,11... | collective-permute-start | bytes 196616 | tf_op jit(solution)/shard_map/ppermute | solution.py:45
  71.3 5.4 %collective-permute-start.33 = (f32[128,128]{1,0:T(8,128)S(1)}, f32[128,128]{1,0:T(8,128)S(1)}, u32[]{:S(2)}, u32[]{:S(2)}) collective-permute-start(f32[128,128]{1,0:T(8,128)S(1)} %add.93), channel_id=1, source_target_pairs={{0,6},{1,7},{2,4},{3,5},{4,2},{5,3},{6,0},{7,1},{8,14},{9,15},{10,... | collective-permute-start | bytes 196616 | tf_op jit(solution)/shard_map/ppermute | solution.py:45
  72.8 4.7 %collective-permute-start.34 = (f32[128,128]{1,0:T(8,128)S(1)}, f32[128,128]{1,0:T(8,128)S(1)}, u32[]{:S(2)}, u32[]{:S(2)}) collective-permute-start(f32[128,128]{1,0:T(8,128)S(1)} %add.93), channel_id=1, source_target_pairs={{0,2},{1,5},{2,0},{3,7},{4,6},{5,1},{6,4},{7,3},{8,10},{9,13},{10,... | collective-permute-start | bytes 196616 | tf_op jit(solution)/shard_map/ppermute | solution.py:45
  73.8 4.3 %collective-permute-start.35 = (f32[128,128]{1,0:T(8,128)S(1)}, f32[128,128]{1,0:T(8,128)S(1)}, u32[]{:S(2)}, u32[]{:S(2)}) collective-permute-start(f32[128,128]{1,0:T(8,128)S(1)} %add.93), channel_id=1, source_target_pairs={{0,4},{1,3},{2,6},{3,1},{4,0},{5,7},{6,2},{7,5},{8,12},{9,11},{10,... | collective-permute-start | bytes 196616 | tf_op jit(solution)/shard_map/ppermute | solution.py:45
  78.1 5.7 %collective-permute-start.36 = (f32[128,128]{1,0:T(8,128)S(1)}, f32[128,128]{1,0:T(8,128)S(1)}, u32[]{:S(2)}, u32[]{:S(2)}) collective-permute-start(f32[128,128]{1,0:T(8,128)S(1)} %add_add_fusion.1), channel_id=1, source_target_pairs={{0,16},{1,17},{2,18},{3,19},{4,20},{5,21},{6,22},{7,23},{8,24},{9,... | collective-permute-start | bytes 196616 | tf_op jit(solution)/shard_map/ppermute | solution.py:45
  80.8 6.7 %collective-permute-start.37 = (f32[128,128]{1,0:T(8,128)S(1)}, f32[128,128]{1,0:T(8,128)S(1)}, u32[]{:S(2)}, u32[]{:S(2)}) collective-permute-start(f32[128,128]{1,0:T(8,128)S(1)} %add_add_fusion.1), channel_id=1, source_target_pairs={{0,24},{1,25},{2,26},{3,27},{4,28},{5,29},{6,30},{7,31},{8,16},{9,... | collective-permute-start | bytes 196616 | tf_op jit(solution)/shard_map/ppermute | solution.py:45
  83.2 4.7 %collective-permute-start.38 = (f32[128,128]{1,0:T(8,128)S(1)}, f32[128,128]{1,0:T(8,128)S(1)}, u32[]{:S(2)}, u32[]{:S(2)}) collective-permute-start(f32[128,128]{1,0:T(8,128)S(1)} %add_add_fusion.1), channel_id=1, source_target_pairs={{0,8},{1,9},{2,10},{3,11},{4,12},{5,13},{6,14},{7,15},{8,0},{9,1},... | collective-permute-start | bytes 196616 | tf_op jit(solution)/shard_map/ppermute | solution.py:45
  87.9 1.3 %collective-permute-start.39 = (f32[128,128]{1,0:T(8,128)S(1)}, f32[128,128]{1,0:T(8,128)S(1)}, u32[]{:S(2)}, u32[]{:S(2)}) collective-permute-start(f32[128,128]{1,0:T(8,128)S(1)} %add_add_fusion.own_ref), channel_id=1, source_target_pairs={{0,1},{1,0},{2,3},{3,2},{4,5},{5,4},{6,7},{7,6},{8,9},{9,8},{10,11... | collective-permute-start | bytes 196616 | tf_op jit(solution)/shard_map/ppermute | solution.py:45

commit v7 on v6

--- a/solution.py
+++ b/solution.py
@@ -27,13 +27,9 @@
 
 
 def small_masks():
-    bits = later_bits(3)
-    groups = [[(6, 6), (2, 4), (4, 2)]]
-    while bits:
-        low, high = bits[0], sum(bits[1:2])
-        groups.append([(mask, mask) for mask in ((high, high | low, low) if high else (low,))])
-        bits = bits[2:]
-    return groups
+    plane = [place_masks(place) for place in (3, 2, 1)]
+    others = [(16, 16), (24, 20), (8, 4)]
+    return [plane, others] + [[(bit, bit)] for bit in later_bits(5)]
 
 
 def place_masks(place):

time: 94.6 us -> 94.3 us (level)
  no operation moved by 1% of the time
where the time goes in v7:
time: 94.3 us; the launch traced here: 94.1 us
  waiting for transfers between devices  43.5 us (46%)
  starting transfers between devices  37.2 us (39%)
  Pallas kernels  12 us (13%)
    ppermute x40, waiting for transfers between devices, swap(): lax.ppermute(value, 'rows', [(i, i ^ masks[i & 1]) for i in range(size)])  43.5 us
    ppermute x40, starting transfers between devices, swap(): lax.ppermute(value, 'rows', [(i, i ^ masks[i & 1]) for i in range(size)])  37.2 us
    pallas_call x15, Pallas kernels, call(): pl.pallas_call(kernel, in_specs=in_specs or [VMEM] * len(operands), out_s...  12 us
  transfers between devices with their start and end apart: 40, of which 23 were waited for; matrix products, arithmetic and copies ran while one was open for 0% of the time, Pallas kernels for 4%

profile of v7, /device:TPU:0, one launch (start us, length us, event | category | flops | bytes accessed | tf_op | source)
XLA Modules:
  0.0 94.1 jit_solution(2148793694490809439)
XLA Ops:
  0.6 2.0 %shard_map.50 = (bf16[128,512]{1,0:T(8,128)(2,1)S(1)}, bf16[128,512]{1,0:T(8,128)(2,1)S(1)}, bf16[128,512]{1,0:T(8,128)(2,1)S(1)}, bf16[128,512]{1,0:T(8,128)(2,...) custom-call(bf16[384,4096]{1,0:T(8,128)(2,1)} %basis_ref.1, ...), custom_call_target="tpu_custom_call" | custom-call | flops 201326592 | tf_op jit(solution)/shard_map/pallas_call | solution.py:45
  2.6 0.5 collective-permute-start.1
  3.2 0.4 collective-permute-start.5
  3.7 0.5 shard_map.51
  4.2 3.9 %collective-permute-start.2 = (bf16[128,512]{1,0:T(8,128)(2,1)S(1)}, bf16[128,512]{1,0:T(8,128)(2,1)S(1)}, u32[]{:S(2)}, u32[]{:S(2)}) collective-permute-start(bf16[128,512]{1,0:T(8,128)(2,1)S(1)} %add_convert_fusion.5), channel_id=1, source_target_pairs={{0,6},{1,11},{2,4},{3,9},{4,2},{5,15},{6,0},{7,13},{8,14},{9,3},{1... | collective-permute-start | bytes 393224 | tf_op jit(solution)/shard_map/ppermute | solution.py:41
  8.2 0.6 collective-permute-start.4
  8.9 4.1 %collective-permute-done.2 = bf16[128,512]{1,0:T(8,128)(2,1)S(1)} collective-permute-done((bf16[128,512]{1,0:T(8,128)(2,1)S(1)}, bf16[128,512]{1,0:T(8,128)(2,1)S(1)}, u32[]{:S(2)}, u32[]{:S(2)}) %collective-permute-start.2) | collective-permute-done | bytes 131104 | tf_op jit(solution)/shard_map/ppermute | solution.py:41
  13.0 1.7 %collective-permute-done.4 = bf16[128,512]{1,0:T(8,128)(2,1)S(1)} collective-permute-done((bf16[128,512]{1,0:T(8,128)(2,1)S(1)}, bf16[128,512]{1,0:T(8,128)(2,1)S(1)}, u32[]{:S(2)}, u32[]{:S(2)}) %collective-permute-start.4) | collective-permute-done | bytes 131104 | tf_op jit(solution)/shard_map/ppermute | solution.py:41
  14.8 1.8 %collective-permute-start.7 = (bf16[128,512]{1,0:T(8,128)(2,1)S(1)}, bf16[128,512]{1,0:T(8,128)(2,1)S(1)}, u32[]{:S(2)}, u32[]{:S(2)}) collective-permute-start(bf16[128,512]{1,0:T(8,128)(2,1)S(1)} %get-tuple-element.52), channel_id=1, source_target_pairs={{0,8},{1,17},{2,10},{3,19},{4,12},{5,21},{6,14},{7,23},{8,0},{9,25... | collective-permute-start | bytes 393224 | tf_op jit(solution)/shard_map/ppermute | solution.py:41
  16.6 3.4 %collective-permute-done.7 = bf16[128,512]{1,0:T(8,128)(2,1)S(1)} collective-permute-done((bf16[128,512]{1,0:T(8,128)(2,1)S(1)}, bf16[128,512]{1,0:T(8,128)(2,1)S(1)}, u32[]{:S(2)}, u32[]{:S(2)}) %collective-permute-start.7) | collective-permute-done | bytes 131104 | tf_op jit(solution)/shard_map/ppermute | solution.py:41
  20.1 3.0 %collective-permute-start.8 = (bf16[128,512]{1,0:T(8,128)(2,1)S(1)}, bf16[128,512]{1,0:T(8,128)(2,1)S(1)}, u32[]{:S(2)}, u32[]{:S(2)}) collective-permute-start(bf16[128,512]{1,0:T(8,128)(2,1)S(1)} %fusion), channel_id=1, source_target_pairs={{0,16},{1,5},{2,18},{3,7},{4,20},{5,1},{6,22},{7,3},{8,24},{9,13},... | collective-permute-start | bytes 393224 | tf_op jit(solution)/shard_map/ppermute | solution.py:41
  23.1 2.9 %collective-permute-done.8 = bf16[128,512]{1,0:T(8,128)(2,1)S(1)} collective-permute-done((bf16[128,512]{1,0:T(8,128)(2,1)S(1)}, bf16[128,512]{1,0:T(8,128)(2,1)S(1)}, u32[]{:S(2)}, u32[]{:S(2)}) %collective-permute-start.8) | collective-permute-done | bytes 131104 | tf_op jit(solution)/shard_map/ppermute | solution.py:41
  26.1 2.5 %collective-permute-start.9 = (bf16[128,512]{1,0:T(8,128)(2,1)S(1)}, bf16[128,512]{1,0:T(8,128)(2,1)S(1)}, u32[]{:S(2)}, u32[]{:S(2)}) collective-permute-start(bf16[128,512]{1,0:T(8,128)(2,1)S(1)} %multiply_convert_fusion.1.refs_0_), channel_id=1, source_target_pairs={{0,6},{1,11},{2,4},{3,9},{4,2},{5,15},{6,0},{7,13},{8,14},{9,3},{1... | collective-permute-start | bytes 393224 | tf_op jit(solution)/shard_map/ppermute | solution.py:41
  28.6 0.6 collective-permute-start.12
  29.1 0.5 collective-permute-start.13
  29.7 3.3 %collective-permute-done.9.refs_1_ = bf16[128,512]{1,0:T(8,128)(2,1)S(1)} collective-permute-done((bf16[128,512]{1,0:T(8,128)(2,1)S(1)}, bf16[128,512]{1,0:T(8,128)(2,1)S(1)}, u32[]{:S(2)}, u32[]{:S(2)}) %collective-permute-start.9) | collective-permute-done | bytes 131104 | tf_op jit(solution)/shard_map/ppermute | solution.py:41
  32.9 0.6 collective-permute-done.12.refs_0_
  33.5 0.8 collective-permute-done.13.refs_1_
  34.3 0.4 shard_map.52.rem_ref
  34.7 0.4 shard_map.53.rem_ref
  35.1 0.4 shard_map.54.rem_ref
  35.6 0.1 collective-permute-done.15.refs_1_
  35.7 0.4 shard_map.55
  36.1 0.2 shard_map.58
  36.3 0.5 collective-permute-start.17
  36.8 0.4 shard_map.57
  37.2 0.2 collective-permute-start.19
  37.4 0.4 collective-permute-start.21
  37.9 0.4 shard_map.56
  38.3 1.8 %collective-permute-start.18 = (bf16[128,512]{1,0:T(8,128)(2,1)S(1)}, bf16[128,512]{1,0:T(8,128)(2,1)S(1)}, u32[]{:S(2)}, u32[]{:S(2)}) collective-permute-start(bf16[128,512]{1,0:T(8,128)(2,1)S(1)} %add_convert_fusion.2), channel_id=1, source_target_pairs={{0,6},{1,11},{2,4},{3,9},{4,2},{5,15},{6,0},{7,13},{8,14},{9,3},{1... | collective-permute-start | bytes 393224 | tf_op jit(solution)/shard_map/ppermute | solution.py:41
  40.2 0.7 collective-permute-start.20
  41.0 1.1 %collective-permute-start.22 = (bf16[128,512]{1,0:T(8,128)(2,1)S(1)}, bf16[128,512]{1,0:T(8,128)(2,1)S(1)}, u32[]{:S(2)}, u32[]{:S(2)}) collective-permute-start(bf16[128,512]{1,0:T(8,128)(2,1)S(1)} %add_convert_fusion), channel_id=1, source_target_pairs={{0,4},{1,3},{2,6},{3,1},{4,0},{5,7},{6,2},{7,5},{8,12},{9,11},{10,... | collective-permute-start | bytes 393224 | tf_op jit(solution)/shard_map/ppermute | solution.py:41
  42.1 4.4 %collective-permute-done.18 = bf16[128,512]{1,0:T(8,128)(2,1)S(1)} collective-permute-done((bf16[128,512]{1,0:T(8,128)(2,1)S(1)}, bf16[128,512]{1,0:T(8,128)(2,1)S(1)}, u32[]{:S(2)}, u32[]{:S(2)}) %collective-permute-start.18) | collective-permute-done | bytes 131104 | tf_op jit(solution)/shard_map/ppermute | solution.py:41
  46.5 1.5 %collective-permute-done.20 = bf16[128,512]{1,0:T(8,128)(2,1)S(1)} collective-permute-done((bf16[128,512]{1,0:T(8,128)(2,1)S(1)}, bf16[128,512]{1,0:T(8,128)(2,1)S(1)}, u32[]{:S(2)}, u32[]{:S(2)}) %collective-permute-start.20) | collective-permute-done | bytes 131104 | tf_op jit(solution)/shard_map/ppermute | solution.py:41
  48.1 2.1 %collective-permute-start.23 = (bf16[128,512]{1,0:T(8,128)(2,1)S(1)}, bf16[128,512]{1,0:T(8,128)(2,1)S(1)}, u32[]{:S(2)}, u32[]{:S(2)}) collective-permute-start(bf16[128,512]{1,0:T(8,128)(2,1)S(1)} %get-tuple-element.50), channel_id=1, source_target_pairs={{0,8},{1,17},{2,10},{3,19},{4,12},{5,21},{6,14},{7,23},{8,0},{9,25... | collective-permute-start | bytes 393224 | tf_op jit(solution)/shard_map/ppermute | solution.py:41
  50.2 4.0 %collective-permute-done.23 = bf16[128,512]{1,0:T(8,128)(2,1)S(1)} collective-permute-done((bf16[128,512]{1,0:T(8,128)(2,1)S(1)}, bf16[128,512]{1,0:T(8,128)(2,1)S(1)}, u32[]{:S(2)}, u32[]{:S(2)}) %collective-permute-start.23) | collective-permute-done | bytes 131104 | tf_op jit(solution)/shard_map/ppermute | solution.py:41
  54.3 2.8 %collective-permute-start.24 = (bf16[128,512]{1,0:T(8,128)(2,1)S(1)}, bf16[128,512]{1,0:T(8,128)(2,1)S(1)}, u32[]{:S(2)}, u32[]{:S(2)}) collective-permute-start(bf16[128,512]{1,0:T(8,128)(2,1)S(1)} %fusion.1), channel_id=1, source_target_pairs={{0,16},{1,5},{2,18},{3,7},{4,20},{5,1},{6,22},{7,3},{8,24},{9,13},... | collective-permute-start | bytes 393224 | tf_op jit(solution)/shard_map/ppermute | solution.py:41
  57.1 3.2 %collective-permute-done.24 = bf16[128,512]{1,0:T(8,128)(2,1)S(1)} collective-permute-done((bf16[128,512]{1,0:T(8,128)(2,1)S(1)}, bf16[128,512]{1,0:T(8,128)(2,1)S(1)}, u32[]{:S(2)}, u32[]{:S(2)}) %collective-permute-start.24) | collective-permute-done | bytes 131104 | tf_op jit(solution)/shard_map/ppermute | solution.py:41
  60.3 1.4 %collective-permute-start.25 = (bf16[128,512]{1,0:T(8,128)(2,1)S(1)}, bf16[128,512]{1,0:T(8,128)(2,1)S(1)}, u32[]{:S(2)}, u32[]{:S(2)}) collective-permute-start(bf16[128,512]{1,0:T(8,128)(2,1)S(1)} %multiply_convert_fusion.refs_0_), channel_id=1, source_target_pairs={{0,6},{1,11},{2,4},{3,9},{4,2},{5,15},{6,0},{7,13},{8,14},{9,3},{1... | collective-permute-start | bytes 393224 | tf_op jit(solution)/shard_map/ppermute | solution.py:41
  61.6 1.3 %collective-permute-start.28 = (bf16[128,512]{1,0:T(8,128)(2,1)S(1)}, bf16[128,512]{1,0:T(8,128)(2,1)S(1)}, u32[]{:S(2)}, u32[]{:S(2)}) collective-permute-start(bf16[128,512]{1,0:T(8,128)(2,1)S(1)} %multiply_convert_fusion.refs_0_), channel_id=1, source_target_pairs={{0,2},{1,9},{2,0},{3,11},{4,6},{5,13},{6,4},{7,15},{8,10},{9,1},{1... | collective-permute-start | bytes 393224 | tf_op jit(solution)/shard_map/ppermute | solution.py:41
  62.9 0.9 collective-permute-start.29
  63.8 2.7 %collective-permute-done.25.refs_1_ = bf16[128,512]{1,0:T(8,128)(2,1)S(1)} collective-permute-done((bf16[128,512]{1,0:T(8,128)(2,1)S(1)}, bf16[128,512]{1,0:T(8,128)(2,1)S(1)}, u32[]{:S(2)}, u32[]{:S(2)}) %collective-permute-start.25) | collective-permute-done | bytes 131104 | tf_op jit(solution)/shard_map/ppermute | solution.py:41
  66.5 0.8 collective-permute-done.28.refs_0_
  67.3 0.6 collective-permute-done.29.refs_1_
  67.9 0.4 shard_map.59.rem_ref
  68.3 0.4 shard_map.60.rem_ref
  68.7 0.4 shard_map.61.rem_ref
  69.2 0.1 collective-permute-done.31.refs_1_
  69.3 0.4 shard_map.62.turned_ref
  69.7 0.3 shard_map.63
  69.9 0.5 collective-permute-start.32
  70.4 0.9 collective-permute-done.32
  71.3 1.5 %collective-permute-start.33 = (f32[128,128]{1,0:T(8,128)S(1)}, f32[128,128]{1,0:T(8,128)S(1)}, u32[]{:S(2)}, u32[]{:S(2)}) collective-permute-start(f32[128,128]{1,0:T(8,128)S(1)} %add.93), channel_id=1, source_target_pairs={{0,6},{1,11},{2,4},{3,9},{4,2},{5,15},{6,0},{7,13},{8,14},{9,3},{1... | collective-permute-start | bytes 196616 | tf_op jit(solution)/shard_map/ppermute | solution.py:41
  72.8 1.0 %collective-permute-start.34 = (f32[128,128]{1,0:T(8,128)S(1)}, f32[128,128]{1,0:T(8,128)S(1)}, u32[]{:S(2)}, u32[]{:S(2)}) collective-permute-start(f32[128,128]{1,0:T(8,128)S(1)} %add.93), channel_id=1, source_target_pairs={{0,2},{1,9},{2,0},{3,11},{4,6},{5,13},{6,4},{7,15},{8,10},{9,1},{1... | collective-permute-start | bytes 196616 | tf_op jit(solution)/shard_map/ppermute | solution.py:41
  73.8 1.1 %collective-permute-start.35 = (f32[128,128]{1,0:T(8,128)S(1)}, f32[128,128]{1,0:T(8,128)S(1)}, u32[]{:S(2)}, u32[]{:S(2)}) collective-permute-start(f32[128,128]{1,0:T(8,128)S(1)} %add.93), channel_id=1, source_target_pairs={{0,4},{1,3},{2,6},{3,1},{4,0},{5,7},{6,2},{7,5},{8,12},{9,11},{10,... | collective-permute-start | bytes 196616 | tf_op jit(solution)/shard_map/ppermute | solution.py:41
  74.9 2.4 %collective-permute-done.33 = f32[128,128]{1,0:T(8,128)S(1)} collective-permute-done((f32[128,128]{1,0:T(8,128)S(1)}, f32[128,128]{1,0:T(8,128)S(1)}, u32[]{:S(2)}, u32[]{:S(2)}) %collective-permute-start.33) | collective-permute-done | bytes 65568 | tf_op jit(solution)/shard_map/ppermute | solution.py:41
  77.3 0.7 collective-permute-done.34
  78.0 2.8 %collective-permute-start.36 = (f32[128,128]{1,0:T(8,128)S(1)}, f32[128,128]{1,0:T(8,128)S(1)}, u32[]{:S(2)}, u32[]{:S(2)}) collective-permute-start(f32[128,128]{1,0:T(8,128)S(1)} %add_add_fusion.1), channel_id=1, source_target_pairs={{0,16},{1,17},{2,18},{3,19},{4,20},{5,21},{6,22},{7,23},{8,24},{9,... | collective-permute-start | bytes 196616 | tf_op jit(solution)/shard_map/ppermute | solution.py:41
  80.8 2.4 %collective-permute-start.37 = (f32[128,128]{1,0:T(8,128)S(1)}, f32[128,128]{1,0:T(8,128)S(1)}, u32[]{:S(2)}, u32[]{:S(2)}) collective-permute-start(f32[128,128]{1,0:T(8,128)S(1)} %add_add_fusion.1), channel_id=1, source_target_pairs={{0,24},{1,21},{2,26},{3,23},{4,28},{5,17},{6,30},{7,19},{8,16},{9,... | collective-permute-start | bytes 196616 | tf_op jit(solution)/shard_map/ppermute | solution.py:41
  83.2 0.5 collective-permute-start.38
  83.7 3.4 %collective-permute-done.37 = f32[128,128]{1,0:T(8,128)S(1)} collective-permute-done((f32[128,128]{1,0:T(8,128)S(1)}, f32[128,128]{1,0:T(8,128)S(1)}, u32[]{:S(2)}, u32[]{:S(2)}) %collective-permute-start.37) | collective-permute-done | bytes 65568 | tf_op jit(solution)/shard_map/ppermute | solution.py:41
  87.1 0.5 collective-permute-done.38
  87.7 1.2 %collective-permute-done.39.other_ref = f32[128,128]{1,0:T(8,128)S(1)} collective-permute-done((f32[128,128]{1,0:T(8,128)S(1)}, f32[128,128]{1,0:T(8,128)S(1)}, u32[]{:S(2)}, u32[]{:S(2)}) %collective-permute-start.39) | collective-permute-done | bytes 65568 | tf_op jit(solution)/shard_map/ppermute | solution.py:41
  89.0 5.2 %shard_map.64 = (bf16[384,128]{1,0:T(8,128)(2,1)}, bf16[384,128]{1,0:T(8,128)(2,1)}) custom-call(f32[128,128]{1,0:T(8,128)S(1)} %add_add_fusion.own_ref, f32[128,128]{1,0:T(8,128)S(1)} %collective-permute-done.39.other_ref, bf16[384,128]{1,0:T(8,128)(2,1)S(1)} %get-tuple-element.49.rem_ref, bf16[384,128]{1,0:T(8,128)(2,1)S(1)} %get-tuple-element.46.user_ref), custom_call_target="tpu_custom_call" | custom-call | tf_op jit(solution)/shard_map/pallas_call | solution.py:45
  (46 shorter events, 1.1 us)
Async XLA Ops:
  2.6 1.6 %collective-permute-start.1 = (bf16[128,512]{1,0:T(8,128)(2,1)S(1)}, bf16[128,512]{1,0:T(8,128)(2,1)S(1)}, u32[]{:S(2)}, u32[]{:S(2)}) collective-permute-start(bf16[128,512]{1,0:T(8,128)(2,1)S(1)} %get-tuple-element.32), channel_id=1, source_target_pairs={{0,1},{1,0},{2,3},{3,2},{4,5},{5,4},{6,7},{7,6},{8,9},{9,8},{10,11... | collective-permute-start | bytes 393224 | tf_op jit(solution)/shard_map/ppermute | solution.py:41
  3.1 5.0 %collective-permute-start.3 = (bf16[128,512]{1,0:T(8,128)(2,1)S(1)}, bf16[128,512]{1,0:T(8,128)(2,1)S(1)}, u32[]{:S(2)}, u32[]{:S(2)}) collective-permute-start(bf16[128,512]{1,0:T(8,128)(2,1)S(1)} %get-tuple-element.34), channel_id=1, source_target_pairs={{0,1},{1,0},{2,3},{3,2},{4,5},{5,4},{6,7},{7,6},{8,9},{9,8},{10,11... | collective-permute-start | bytes 393224 | tf_op jit(solution)/shard_map/ppermute | solution.py:41
  3.2 5.6 %collective-permute-start.5 = (bf16[128,512]{1,0:T(8,128)(2,1)S(1)}, bf16[128,512]{1,0:T(8,128)(2,1)S(1)}, u32[]{:S(2)}, u32[]{:S(2)}) collective-permute-start(bf16[128,512]{1,0:T(8,128)(2,1)S(1)} %get-tuple-element.36), channel_id=1, source_target_pairs={{0,1},{1,0},{2,3},{3,2},{4,5},{5,4},{6,7},{7,6},{8,9},{9,8},{10,11... | collective-permute-start | bytes 393224 | tf_op jit(solution)/shard_map/ppermute | solution.py:41
  3.6 5.3 %collective-permute-start = (bf16[128,512]{1,0:T(8,128)(2,1)S(1)}, bf16[128,512]{1,0:T(8,128)(2,1)S(1)}, u32[]{:S(2)}, u32[]{:S(2)}) collective-permute-start(bf16[128,512]{1,0:T(8,128)(2,1)S(1)} %get-tuple-element.30), channel_id=1, source_target_pairs={{0,1},{1,0},{2,3},{3,2},{4,5},{5,4},{6,7},{7,6},{8,9},{9,8},{10,11... | collective-permute-start | bytes 393224 | tf_op jit(solution)/shard_map/ppermute | solution.py:41
  4.2 8.8 %collective-permute-start.2 = (bf16[128,512]{1,0:T(8,128)(2,1)S(1)}, bf16[128,512]{1,0:T(8,128)(2,1)S(1)}, u32[]{:S(2)}, u32[]{:S(2)}) collective-permute-start(bf16[128,512]{1,0:T(8,128)(2,1)S(1)} %add_convert_fusion.5), channel_id=1, source_target_pairs={{0,6},{1,11},{2,4},{3,9},{4,2},{5,15},{6,0},{7,13},{8,14},{9,3},{1... | collective-permute-start | bytes 393224 | tf_op jit(solution)/shard_map/ppermute | solution.py:41
  8.2 6.6 %collective-permute-start.4 = (bf16[128,512]{1,0:T(8,128)(2,1)S(1)}, bf16[128,512]{1,0:T(8,128)(2,1)S(1)}, u32[]{:S(2)}, u32[]{:S(2)}) collective-permute-start(bf16[128,512]{1,0:T(8,128)(2,1)S(1)} %add_convert_fusion.4), channel_id=1, source_target_pairs={{0,2},{1,9},{2,0},{3,11},{4,6},{5,13},{6,4},{7,15},{8,10},{9,1},{1... | collective-permute-start | bytes 393224 | tf_op jit(solution)/shard_map/ppermute | solution.py:41
  8.8 5.9 %collective-permute-start.6 = (bf16[128,512]{1,0:T(8,128)(2,1)S(1)}, bf16[128,512]{1,0:T(8,128)(2,1)S(1)}, u32[]{:S(2)}, u32[]{:S(2)}) collective-permute-start(bf16[128,512]{1,0:T(8,128)(2,1)S(1)} %add_convert_fusion.3), channel_id=1, source_target_pairs={{0,4},{1,3},{2,6},{3,1},{4,0},{5,7},{6,2},{7,5},{8,12},{9,11},{10,... | collective-permute-start | bytes 393224 | tf_op jit(solution)/shard_map/ppermute | solution.py:41
  14.8 5.2 %collective-permute-start.7 = (bf16[128,512]{1,0:T(8,128)(2,1)S(1)}, bf16[128,512]{1,0:T(8,128)(2,1)S(1)}, u32[]{:S(2)}, u32[]{:S(2)}) collective-permute-start(bf16[128,512]{1,0:T(8,128)(2,1)S(1)} %get-tuple-element.52), channel_id=1, source_target_pairs={{0,8},{1,17},{2,10},{3,19},{4,12},{5,21},{6,14},{7,23},{8,0},{9,25... | collective-permute-start | bytes 393224 | tf_op jit(solution)/shard_map/ppermute | solution.py:41
  20.1 6.0 %collective-permute-start.8 = (bf16[128,512]{1,0:T(8,128)(2,1)S(1)}, bf16[128,512]{1,0:T(8,128)(2,1)S(1)}, u32[]{:S(2)}, u32[]{:S(2)}) collective-permute-start(bf16[128,512]{1,0:T(8,128)(2,1)S(1)} %fusion), channel_id=1, source_target_pairs={{0,16},{1,5},{2,18},{3,7},{4,20},{5,1},{6,22},{7,3},{8,24},{9,13},... | collective-permute-start | bytes 393224 | tf_op jit(solution)/shard_map/ppermute | solution.py:41
  26.1 6.8 %collective-permute-start.9 = (bf16[128,512]{1,0:T(8,128)(2,1)S(1)}, bf16[128,512]{1,0:T(8,128)(2,1)S(1)}, u32[]{:S(2)}, u32[]{:S(2)}) collective-permute-start(bf16[128,512]{1,0:T(8,128)(2,1)S(1)} %multiply_convert_fusion.1.refs_0_), channel_id=1, source_target_pairs={{0,6},{1,11},{2,4},{3,9},{4,2},{5,15},{6,0},{7,13},{8,14},{9,3},{1... | collective-permute-start | bytes 393224 | tf_op jit(solution)/shard_map/ppermute | solution.py:41
  28.6 5.0 %collective-permute-start.12 = (bf16[128,512]{1,0:T(8,128)(2,1)S(1)}, bf16[128,512]{1,0:T(8,128)(2,1)S(1)}, u32[]{:S(2)}, u32[]{:S(2)}) collective-permute-start(bf16[128,512]{1,0:T(8,128)(2,1)S(1)} %multiply_convert_fusion.1.refs_0_), channel_id=1, source_target_pairs={{0,2},{1,9},{2,0},{3,11},{4,6},{5,13},{6,4},{7,15},{8,10},{9,1},{1... | collective-permute-start | bytes 393224 | tf_op jit(solution)/shard_map/ppermute | solution.py:41
  29.1 5.2 %collective-permute-start.13 = (bf16[128,512]{1,0:T(8,128)(2,1)S(1)}, bf16[128,512]{1,0:T(8,128)(2,1)S(1)}, u32[]{:S(2)}, u32[]{:S(2)}) collective-permute-start(bf16[128,512]{1,0:T(8,128)(2,1)S(1)} %multiply_convert_fusion.1.refs_0_), channel_id=1, source_target_pairs={{0,4},{1,3},{2,6},{3,1},{4,0},{5,7},{6,2},{7,5},{8,12},{9,11},{10,... | collective-permute-start | bytes 393224 | tf_op jit(solution)/shard_map/ppermute | solution.py:41
  29.7 5.1 %collective-permute-start.10 = (bf16[128,512]{1,0:T(8,128)(2,1)S(1)}, bf16[128,512]{1,0:T(8,128)(2,1)S(1)}, u32[]{:S(2)}, u32[]{:S(2)}) collective-permute-start(bf16[128,512]{1,0:T(8,128)(2,1)S(1)} %multiply_convert_fusion.1.refs_0_), channel_id=1, source_target_pairs={{0,1},{1,0},{2,3},{3,2},{4,5},{5,4},{6,7},{7,6},{8,9},{9,8},{10,11... | collective-permute-start | bytes 393224 | tf_op jit(solution)/shard_map/ppermute | solution.py:41
  32.9 1.8 %collective-permute-start.11 = (bf16[128,512]{1,0:T(8,128)(2,1)S(1)}, bf16[128,512]{1,0:T(8,128)(2,1)S(1)}, u32[]{:S(2)}, u32[]{:S(2)}) collective-permute-start(bf16[128,512]{1,0:T(8,128)(2,1)S(1)} %collective-permute-done.9.refs_1_), channel_id=1, source_target_pairs={{0,1},{1,0},{2,3},{3,2},{4,5},{5,4},{6,7},{7,6},{8,9},{9,8},{10,11... | collective-permute-start | bytes 393224 | tf_op jit(solution)/shard_map/ppermute | solution.py:41
  33.5 2.0 %collective-permute-start.14 = (bf16[128,512]{1,0:T(8,128)(2,1)S(1)}, bf16[128,512]{1,0:T(8,128)(2,1)S(1)}, u32[]{:S(2)}, u32[]{:S(2)}) collective-permute-start(bf16[128,512]{1,0:T(8,128)(2,1)S(1)} %collective-permute-done.12.refs_0_), channel_id=1, source_target_pairs={{0,1},{1,0},{2,3},{3,2},{4,5},{5,4},{6,7},{7,6},{8,9},{9,8},{10,11... | collective-permute-start | bytes 393224 | tf_op jit(solution)/shard_map/ppermute | solution.py:41
  34.3 1.3 %collective-permute-start.15 = (bf16[128,512]{1,0:T(8,128)(2,1)S(1)}, bf16[128,512]{1,0:T(8,128)(2,1)S(1)}, u32[]{:S(2)}, u32[]{:S(2)}) collective-permute-start(bf16[128,512]{1,0:T(8,128)(2,1)S(1)} %collective-permute-done.13.refs_1_), channel_id=1, source_target_pairs={{0,1},{1,0},{2,3},{3,2},{4,5},{5,4},{6,7},{7,6},{8,9},{9,8},{10,11... | collective-permute-start | bytes 393224 | tf_op jit(solution)/shard_map/ppermute | solution.py:41
  36.3 2.0 %collective-permute-start.17 = (bf16[128,512]{1,0:T(8,128)(2,1)S(1)}, bf16[128,512]{1,0:T(8,128)(2,1)S(1)}, u32[]{:S(2)}, u32[]{:S(2)}) collective-permute-start(bf16[128,512]{1,0:T(8,128)(2,1)S(1)} %shard_map.58), channel_id=1, source_target_pairs={{0,1},{1,0},{2,3},{3,2},{4,5},{5,4},{6,7},{7,6},{8,9},{9,8},{10,11... | collective-permute-start | bytes 393224 | tf_op jit(solution)/shard_map/ppermute | solution.py:41
  37.2 3.0 %collective-permute-start.19 = (bf16[128,512]{1,0:T(8,128)(2,1)S(1)}, bf16[128,512]{1,0:T(8,128)(2,1)S(1)}, u32[]{:S(2)}, u32[]{:S(2)}) collective-permute-start(bf16[128,512]{1,0:T(8,128)(2,1)S(1)} %get-tuple-element.43), channel_id=1, source_target_pairs={{0,1},{1,0},{2,3},{3,2},{4,5},{5,4},{6,7},{7,6},{8,9},{9,8},{10,11... | collective-permute-start | bytes 393224 | tf_op jit(solution)/shard_map/ppermute | solution.py:41
  37.4 3.6 %collective-permute-start.21 = (bf16[128,512]{1,0:T(8,128)(2,1)S(1)}, bf16[128,512]{1,0:T(8,128)(2,1)S(1)}, u32[]{:S(2)}, u32[]{:S(2)}) collective-permute-start(bf16[128,512]{1,0:T(8,128)(2,1)S(1)} %get-tuple-element.45), channel_id=1, source_target_pairs={{0,1},{1,0},{2,3},{3,2},{4,5},{5,4},{6,7},{7,6},{8,9},{9,8},{10,11... | collective-permute-start | bytes 393224 | tf_op jit(solution)/shard_map/ppermute | solution.py:41
  37.7 4.4 %collective-permute-start.16 = (bf16[128,512]{1,0:T(8,128)(2,1)S(1)}, bf16[128,512]{1,0:T(8,128)(2,1)S(1)}, u32[]{:S(2)}, u32[]{:S(2)}) collective-permute-start(bf16[128,512]{1,0:T(8,128)(2,1)S(1)} %get-tuple-element.40), channel_id=1, source_target_pairs={{0,1},{1,0},{2,3},{3,2},{4,5},{5,4},{6,7},{7,6},{8,9},{9,8},{10,11... | collective-permute-start | bytes 393224 | tf_op jit(solution)/shard_map/ppermute | solution.py:41
  38.3 8.2 %collective-permute-start.18 = (bf16[128,512]{1,0:T(8,128)(2,1)S(1)}, bf16[128,512]{1,0:T(8,128)(2,1)S(1)}, u32[]{:S(2)}, u32[]{:S(2)}) collective-permute-start(bf16[128,512]{1,0:T(8,128)(2,1)S(1)} %add_convert_fusion.2), channel_id=1, source_target_pairs={{0,6},{1,11},{2,4},{3,9},{4,2},{5,15},{6,0},{7,13},{8,14},{9,3},{1... | collective-permute-start | bytes 393224 | tf_op jit(solution)/shard_map/ppermute | solution.py:41
  40.2 7.8 %collective-permute-start.20 = (bf16[128,512]{1,0:T(8,128)(2,1)S(1)}, bf16[128,512]{1,0:T(8,128)(2,1)S(1)}, u32[]{:S(2)}, u32[]{:S(2)}) collective-permute-start(bf16[128,512]{1,0:T(8,128)(2,1)S(1)} %add_convert_fusion.1), channel_id=1, source_target_pairs={{0,2},{1,9},{2,0},{3,11},{4,6},{5,13},{6,4},{7,15},{8,10},{9,1},{1... | collective-permute-start | bytes 393224 | tf_op jit(solution)/shard_map/ppermute | solution.py:41
  41.0 7.0 %collective-permute-start.22 = (bf16[128,512]{1,0:T(8,128)(2,1)S(1)}, bf16[128,512]{1,0:T(8,128)(2,1)S(1)}, u32[]{:S(2)}, u32[]{:S(2)}) collective-permute-start(bf16[128,512]{1,0:T(8,128)(2,1)S(1)} %add_convert_fusion), channel_id=1, source_target_pairs={{0,4},{1,3},{2,6},{3,1},{4,0},{5,7},{6,2},{7,5},{8,12},{9,11},{10,... | collective-permute-start | bytes 393224 | tf_op jit(solution)/shard_map/ppermute | solution.py:41
  48.1 6.2 %collective-permute-start.23 = (bf16[128,512]{1,0:T(8,128)(2,1)S(1)}, bf16[128,512]{1,0:T(8,128)(2,1)S(1)}, u32[]{:S(2)}, u32[]{:S(2)}) collective-permute-start(bf16[128,512]{1,0:T(8,128)(2,1)S(1)} %get-tuple-element.50), channel_id=1, source_target_pairs={{0,8},{1,17},{2,10},{3,19},{4,12},{5,21},{6,14},{7,23},{8,0},{9,25... | collective-permute-start | bytes 393224 | tf_op jit(solution)/shard_map/ppermute | solution.py:41
  54.3 5.9 %collective-permute-start.24 = (bf16[128,512]{1,0:T(8,128)(2,1)S(1)}, bf16[128,512]{1,0:T(8,128)(2,1)S(1)}, u32[]{:S(2)}, u32[]{:S(2)}) collective-permute-start(bf16[128,512]{1,0:T(8,128)(2,1)S(1)} %fusion.1), channel_id=1, source_target_pairs={{0,16},{1,5},{2,18},{3,7},{4,20},{5,1},{6,22},{7,3},{8,24},{9,13},... | collective-permute-start | bytes 393224 | tf_op jit(solution)/shard_map/ppermute | solution.py:41
  60.3 6.2 %collective-permute-start.25 = (bf16[128,512]{1,0:T(8,128)(2,1)S(1)}, bf16[128,512]{1,0:T(8,128)(2,1)S(1)}, u32[]{:S(2)}, u32[]{:S(2)}) collective-permute-start(bf16[128,512]{1,0:T(8,128)(2,1)S(1)} %multiply_convert_fusion.refs_0_), channel_id=1, source_target_pairs={{0,6},{1,11},{2,4},{3,9},{4,2},{5,15},{6,0},{7,13},{8,14},{9,3},{1... | collective-permute-start | bytes 393224 | tf_op jit(solution)/shard_map/ppermute | solution.py:41
  61.6 5.6 %collective-permute-start.28 = (bf16[128,512]{1,0:T(8,128)(2,1)S(1)}, bf16[128,512]{1,0:T(8,128)(2,1)S(1)}, u32[]{:S(2)}, u32[]{:S(2)}) collective-permute-start(bf16[128,512]{1,0:T(8,128)(2,1)S(1)} %multiply_convert_fusion.refs_0_), channel_id=1, source_target_pairs={{0,2},{1,9},{2,0},{3,11},{4,6},{5,13},{6,4},{7,15},{8,10},{9,1},{1... | collective-permute-start | bytes 393224 | tf_op jit(solution)/shard_map/ppermute | solution.py:41
  62.9 5.0 %collective-permute-start.29 = (bf16[128,512]{1,0:T(8,128)(2,1)S(1)}, bf16[128,512]{1,0:T(8,128)(2,1)S(1)}, u32[]{:S(2)}, u32[]{:S(2)}) collective-permute-start(bf16[128,512]{1,0:T(8,128)(2,1)S(1)} %multiply_convert_fusion.refs_0_), channel_id=1, source_target_pairs={{0,4},{1,3},{2,6},{3,1},{4,0},{5,7},{6,2},{7,5},{8,12},{9,11},{10,... | collective-permute-start | bytes 393224 | tf_op jit(solution)/shard_map/ppermute | solution.py:41
  63.8 4.5 %collective-permute-start.26 = (bf16[128,512]{1,0:T(8,128)(2,1)S(1)}, bf16[128,512]{1,0:T(8,128)(2,1)S(1)}, u32[]{:S(2)}, u32[]{:S(2)}) collective-permute-start(bf16[128,512]{1,0:T(8,128)(2,1)S(1)} %multiply_convert_fusion.refs_0_), channel_id=1, source_target_pairs={{0,1},{1,0},{2,3},{3,2},{4,5},{5,4},{6,7},{7,6},{8,9},{9,8},{10,11... | collective-permute-start | bytes 393224 | tf_op jit(solution)/shard_map/ppermute | solution.py:41
  66.5 1.8 %collective-permute-start.27 = (bf16[128,512]{1,0:T(8,128)(2,1)S(1)}, bf16[128,512]{1,0:T(8,128)(2,1)S(1)}, u32[]{:S(2)}, u32[]{:S(2)}) collective-permute-start(bf16[128,512]{1,0:T(8,128)(2,1)S(1)} %collective-permute-done.25.refs_1_), channel_id=1, source_target_pairs={{0,1},{1,0},{2,3},{3,2},{4,5},{5,4},{6,7},{7,6},{8,9},{9,8},{10,11... | collective-permute-start | bytes 393224 | tf_op jit(solution)/shard_map/ppermute | solution.py:41
  67.3 1.9 %collective-permute-start.30 = (bf16[128,512]{1,0:T(8,128)(2,1)S(1)}, bf16[128,512]{1,0:T(8,128)(2,1)S(1)}, u32[]{:S(2)}, u32[]{:S(2)}) collective-permute-start(bf16[128,512]{1,0:T(8,128)(2,1)S(1)} %collective-permute-done.28.refs_0_), channel_id=1, source_target_pairs={{0,1},{1,0},{2,3},{3,2},{4,5},{5,4},{6,7},{7,6},{8,9},{9,8},{10,11... | collective-permute-start | bytes 393224 | tf_op jit(solution)/shard_map/ppermute | solution.py:41
  67.9 1.3 %collective-permute-start.31 = (bf16[128,512]{1,0:T(8,128)(2,1)S(1)}, bf16[128,512]{1,0:T(8,128)(2,1)S(1)}, u32[]{:S(2)}, u32[]{:S(2)}) collective-permute-start(bf16[128,512]{1,0:T(8,128)(2,1)S(1)} %collective-permute-done.29.refs_1_), channel_id=1, source_target_pairs={{0,1},{1,0},{2,3},{3,2},{4,5},{5,4},{6,7},{7,6},{8,9},{9,8},{10,11... | collective-permute-start | bytes 393224 | tf_op jit(solution)/shard_map/ppermute | solution.py:41
  69.9 1.4 %collective-permute-start.32 = (f32[128,128]{1,0:T(8,128)S(1)}, f32[128,128]{1,0:T(8,128)S(1)}, u32[]{:S(2)}, u32[]{:S(2)}) collective-permute-start(f32[128,128]{1,0:T(8,128)S(1)} %get-tuple-element.48), channel_id=1, source_target_pairs={{0,1},{1,0},{2,3},{3,2},{4,5},{5,4},{6,7},{7,6},{8,9},{9,8},{10,11... | collective-permute-start | bytes 196616 | tf_op jit(solution)/shard_map/ppermute | solution.py:41
  71.3 5.9 %collective-permute-start.33 = (f32[128,128]{1,0:T(8,128)S(1)}, f32[128,128]{1,0:T(8,128)S(1)}, u32[]{:S(2)}, u32[]{:S(2)}) collective-permute-start(f32[128,128]{1,0:T(8,128)S(1)} %add.93), channel_id=1, source_target_pairs={{0,6},{1,11},{2,4},{3,9},{4,2},{5,15},{6,0},{7,13},{8,14},{9,3},{1... | collective-permute-start | bytes 196616 | tf_op jit(solution)/shard_map/ppermute | solution.py:41
  72.8 5.2 %collective-permute-start.34 = (f32[128,128]{1,0:T(8,128)S(1)}, f32[128,128]{1,0:T(8,128)S(1)}, u32[]{:S(2)}, u32[]{:S(2)}) collective-permute-start(f32[128,128]{1,0:T(8,128)S(1)} %add.93), channel_id=1, source_target_pairs={{0,2},{1,9},{2,0},{3,11},{4,6},{5,13},{6,4},{7,15},{8,10},{9,1},{1... | collective-permute-start | bytes 196616 | tf_op jit(solution)/shard_map/ppermute | solution.py:41
  73.8 4.3 %collective-permute-start.35 = (f32[128,128]{1,0:T(8,128)S(1)}, f32[128,128]{1,0:T(8,128)S(1)}, u32[]{:S(2)}, u32[]{:S(2)}) collective-permute-start(f32[128,128]{1,0:T(8,128)S(1)} %add.93), channel_id=1, source_target_pairs={{0,4},{1,3},{2,6},{3,1},{4,0},{5,7},{6,2},{7,5},{8,12},{9,11},{10,... | collective-permute-start | bytes 196616 | tf_op jit(solution)/shard_map/ppermute | solution.py:41
  78.0 5.7 %collective-permute-start.36 = (f32[128,128]{1,0:T(8,128)S(1)}, f32[128,128]{1,0:T(8,128)S(1)}, u32[]{:S(2)}, u32[]{:S(2)}) collective-permute-start(f32[128,128]{1,0:T(8,128)S(1)} %add_add_fusion.1), channel_id=1, source_target_pairs={{0,16},{1,17},{2,18},{3,19},{4,20},{5,21},{6,22},{7,23},{8,24},{9,... | collective-permute-start | bytes 196616 | tf_op jit(solution)/shard_map/ppermute | solution.py:41
  80.8 6.3 %collective-permute-start.37 = (f32[128,128]{1,0:T(8,128)S(1)}, f32[128,128]{1,0:T(8,128)S(1)}, u32[]{:S(2)}, u32[]{:S(2)}) collective-permute-start(f32[128,128]{1,0:T(8,128)S(1)} %add_add_fusion.1), channel_id=1, source_target_pairs={{0,24},{1,21},{2,26},{3,23},{4,28},{5,17},{6,30},{7,19},{8,16},{9,... | collective-permute-start | bytes 196616 | tf_op jit(solution)/shard_map/ppermute | solution.py:41
  83.2 4.4 %collective-permute-start.38 = (f32[128,128]{1,0:T(8,128)S(1)}, f32[128,128]{1,0:T(8,128)S(1)}, u32[]{:S(2)}, u32[]{:S(2)}) collective-permute-start(f32[128,128]{1,0:T(8,128)S(1)} %add_add_fusion.1), channel_id=1, source_target_pairs={{0,8},{1,5},{2,10},{3,7},{4,12},{5,1},{6,14},{7,3},{8,0},{9,13},{1... | collective-permute-start | bytes 196616 | tf_op jit(solution)/shard_map/ppermute | solution.py:41
  87.7 1.3 %collective-permute-start.39 = (f32[128,128]{1,0:T(8,128)S(1)}, f32[128,128]{1,0:T(8,128)S(1)}, u32[]{:S(2)}, u32[]{:S(2)}) collective-permute-start(f32[128,128]{1,0:T(8,128)S(1)} %add_add_fusion.own_ref), channel_id=1, source_target_pairs={{0,1},{1,0},{2,3},{3,2},{4,5},{5,4},{6,7},{7,6},{8,9},{9,8},{10,11... | collective-permute-start | bytes 196616 | tf_op jit(solution)/shard_map/ppermute | solution.py:41

commit v8 on v7

--- a/solution.py
+++ b/solution.py
@@ -160,9 +160,8 @@
     for place in (3, 2, 1):
         coef[place] = swap(coef[0], place_masks(place))
     other = {place: swap(coef[place], CORE) for place in (0, 3, 2, 1)}
-    (rem,) = image_call(False, (0, 3), own_half, rem, [coef[0], coef[3]], [F32])
     (rem,) = image_call(True, (0, 3), other_half, rem, [other[0], other[3]], [F32])
-    (rem,) = image_call(False, (2, 1), own_half, rem, [coef[2], coef[1]], [F32])
+    (rem,) = image_call(False, (0, 3, 2, 1), own_half, rem, [coef[0], coef[3], coef[2], coef[1]], [F32])
     return image_call(True, (2, 1), other_half, rem, [other[2], other[1]], dtypes)
 
 

time: 94.3 us -> 94.2 us (level)
    pallas_call x15 -> x13, Pallas kernels: 12 us -> 11.7 us  [call(): pl.pallas_call(kernel, in_specs=in_specs or [VMEM] * len(operands), out_s...]
  transfers between devices with their start and end apart: 40 -> 40, of which waited for: 23 -> 23; matrix products, arithmetic and copies ran while one was open for 0% -> 0% of each run, Pallas kernels for 4% -> 3%
where the time goes in v8:
time: 94.2 us; the launch traced here: 94.1 us
  waiting for transfers between devices  44.1 us (47%)
  starting transfers between devices  36.9 us (39%)
  Pallas kernels  11.7 us (12%)
    ppermute x40, waiting for transfers between devices, swap(): lax.ppermute(value, 'rows', [(i, i ^ masks[i & 1]) for i in range(size)])  44.1 us
    ppermute x40, starting transfers between devices, swap(): lax.ppermute(value, 'rows', [(i, i ^ masks[i & 1]) for i in range(size)])  36.9 us
    pallas_call x13, Pallas kernels, call(): pl.pallas_call(kernel, in_specs=in_specs or [VMEM] * len(operands), out_s...  11.7 us
  transfers between devices with their start and end apart: 40, of which 23 were waited for; matrix products, arithmetic and copies ran while one was open for 0% of the time, Pallas kernels for 3%

profile of v8, /device:TPU:0, one launch (start us, length us, event | category | flops | bytes accessed | tf_op | source)
XLA Modules:
  0.0 94.1 jit_solution(7303649608979182082)
XLA Ops:
  0.6 2.0 %shard_map.50 = (bf16[128,512]{1,0:T(8,128)(2,1)S(1)}, bf16[128,512]{1,0:T(8,128)(2,1)S(1)}, bf16[128,512]{1,0:T(8,128)(2,1)S(1)}, bf16[128,512]{1,0:T(8,128)(2,...) custom-call(bf16[384,4096]{1,0:T(8,128)(2,1)} %basis_ref.1, ...), custom_call_target="tpu_custom_call" | custom-call | flops 201326592 | tf_op jit(solution)/shard_map/pallas_call | solution.py:45
  2.6 0.5 collective-permute-start.1
  3.2 0.4 collective-permute-start.5
  3.7 0.5 shard_map.51
  4.2 3.9 %collective-permute-start.2 = (bf16[128,512]{1,0:T(8,128)(2,1)S(1)}, bf16[128,512]{1,0:T(8,128)(2,1)S(1)}, u32[]{:S(2)}, u32[]{:S(2)}) collective-permute-start(bf16[128,512]{1,0:T(8,128)(2,1)S(1)} %add_convert_fusion.5), channel_id=1, source_target_pairs={{0,6},{1,11},{2,4},{3,9},{4,2},{5,15},{6,0},{7,13},{8,14},{9,3},{1... | collective-permute-start | bytes 393224 | tf_op jit(solution)/shard_map/ppermute | solution.py:41
  8.2 0.6 collective-permute-start.4
  8.9 4.1 %collective-permute-done.2 = bf16[128,512]{1,0:T(8,128)(2,1)S(1)} collective-permute-done((bf16[128,512]{1,0:T(8,128)(2,1)S(1)}, bf16[128,512]{1,0:T(8,128)(2,1)S(1)}, u32[]{:S(2)}, u32[]{:S(2)}) %collective-permute-start.2) | collective-permute-done | bytes 131104 | tf_op jit(solution)/shard_map/ppermute | solution.py:41
  13.0 1.7 %collective-permute-done.4 = bf16[128,512]{1,0:T(8,128)(2,1)S(1)} collective-permute-done((bf16[128,512]{1,0:T(8,128)(2,1)S(1)}, bf16[128,512]{1,0:T(8,128)(2,1)S(1)}, u32[]{:S(2)}, u32[]{:S(2)}) %collective-permute-start.4) | collective-permute-done | bytes 131104 | tf_op jit(solution)/shard_map/ppermute | solution.py:41
  14.8 1.8 %collective-permute-start.7 = (bf16[128,512]{1,0:T(8,128)(2,1)S(1)}, bf16[128,512]{1,0:T(8,128)(2,1)S(1)}, u32[]{:S(2)}, u32[]{:S(2)}) collective-permute-start(bf16[128,512]{1,0:T(8,128)(2,1)S(1)} %get-tuple-element.52), channel_id=1, source_target_pairs={{0,8},{1,17},{2,10},{3,19},{4,12},{5,21},{6,14},{7,23},{8,0},{9,25... | collective-permute-start | bytes 393224 | tf_op jit(solution)/shard_map/ppermute | solution.py:41
  16.6 3.4 %collective-permute-done.7 = bf16[128,512]{1,0:T(8,128)(2,1)S(1)} collective-permute-done((bf16[128,512]{1,0:T(8,128)(2,1)S(1)}, bf16[128,512]{1,0:T(8,128)(2,1)S(1)}, u32[]{:S(2)}, u32[]{:S(2)}) %collective-permute-start.7) | collective-permute-done | bytes 131104 | tf_op jit(solution)/shard_map/ppermute | solution.py:41
  20.1 3.0 %collective-permute-start.8 = (bf16[128,512]{1,0:T(8,128)(2,1)S(1)}, bf16[128,512]{1,0:T(8,128)(2,1)S(1)}, u32[]{:S(2)}, u32[]{:S(2)}) collective-permute-start(bf16[128,512]{1,0:T(8,128)(2,1)S(1)} %fusion), channel_id=1, source_target_pairs={{0,16},{1,5},{2,18},{3,7},{4,20},{5,1},{6,22},{7,3},{8,24},{9,13},... | collective-permute-start | bytes 393224 | tf_op jit(solution)/shard_map/ppermute | solution.py:41
  23.1 2.9 %collective-permute-done.8 = bf16[128,512]{1,0:T(8,128)(2,1)S(1)} collective-permute-done((bf16[128,512]{1,0:T(8,128)(2,1)S(1)}, bf16[128,512]{1,0:T(8,128)(2,1)S(1)}, u32[]{:S(2)}, u32[]{:S(2)}) %collective-permute-start.8) | collective-permute-done | bytes 131104 | tf_op jit(solution)/shard_map/ppermute | solution.py:41
  26.1 2.5 %collective-permute-start.10 = (bf16[128,512]{1,0:T(8,128)(2,1)S(1)}, bf16[128,512]{1,0:T(8,128)(2,1)S(1)}, u32[]{:S(2)}, u32[]{:S(2)}) collective-permute-start(bf16[128,512]{1,0:T(8,128)(2,1)S(1)} %multiply_convert_fusion.1.refs_0_), channel_id=1, source_target_pairs={{0,6},{1,11},{2,4},{3,9},{4,2},{5,15},{6,0},{7,13},{8,14},{9,3},{1... | collective-permute-start | bytes 393224 | tf_op jit(solution)/shard_map/ppermute | solution.py:41
  28.6 0.6 collective-permute-start.12
  29.1 0.5 collective-permute-start.13
  29.7 3.3 %collective-permute-done.10.refs_1_ = bf16[128,512]{1,0:T(8,128)(2,1)S(1)} collective-permute-done((bf16[128,512]{1,0:T(8,128)(2,1)S(1)}, bf16[128,512]{1,0:T(8,128)(2,1)S(1)}, u32[]{:S(2)}, u32[]{:S(2)}) %collective-permute-start.10) | collective-permute-done | bytes 131104 | tf_op jit(solution)/shard_map/ppermute | solution.py:41
  32.9 0.6 collective-permute-done.12.refs_2_
  33.5 0.8 collective-permute-done.13.refs_3_
  34.3 0.4 shard_map.52.rem_ref
  34.7 0.6 shard_map.53.rem_ref
  35.4 0.3 collective-permute-done.15.refs_1_
  35.7 0.4 shard_map.54
  36.1 0.2 shard_map.57
  36.3 0.3 collective-permute-start.17
  36.6 0.4 shard_map.56
  37.0 0.4 collective-permute-start.19
  37.4 0.2 collective-permute-start.21
  37.6 0.3 collective-permute-start.16
  37.9 0.4 shard_map.55
  38.3 1.6 %collective-permute-start.18 = (bf16[128,512]{1,0:T(8,128)(2,1)S(1)}, bf16[128,512]{1,0:T(8,128)(2,1)S(1)}, u32[]{:S(2)}, u32[]{:S(2)}) collective-permute-start(bf16[128,512]{1,0:T(8,128)(2,1)S(1)} %add_convert_fusion.2), channel_id=1, source_target_pairs={{0,6},{1,11},{2,4},{3,9},{4,2},{5,15},{6,0},{7,13},{8,14},{9,3},{1... | collective-permute-start | bytes 393224 | tf_op jit(solution)/shard_map/ppermute | solution.py:41
  40.0 0.8 collective-permute-start.20
  40.8 1.3 %collective-permute-start.22 = (bf16[128,512]{1,0:T(8,128)(2,1)S(1)}, bf16[128,512]{1,0:T(8,128)(2,1)S(1)}, u32[]{:S(2)}, u32[]{:S(2)}) collective-permute-start(bf16[128,512]{1,0:T(8,128)(2,1)S(1)} %add_convert_fusion), channel_id=1, source_target_pairs={{0,4},{1,3},{2,6},{3,1},{4,0},{5,7},{6,2},{7,5},{8,12},{9,11},{10,... | collective-permute-start | bytes 393224 | tf_op jit(solution)/shard_map/ppermute | solution.py:41
  42.1 4.7 %collective-permute-done.18 = bf16[128,512]{1,0:T(8,128)(2,1)S(1)} collective-permute-done((bf16[128,512]{1,0:T(8,128)(2,1)S(1)}, bf16[128,512]{1,0:T(8,128)(2,1)S(1)}, u32[]{:S(2)}, u32[]{:S(2)}) %collective-permute-start.18) | collective-permute-done | bytes 131104 | tf_op jit(solution)/shard_map/ppermute | solution.py:41
  46.8 1.0 %collective-permute-done.20 = bf16[128,512]{1,0:T(8,128)(2,1)S(1)} collective-permute-done((bf16[128,512]{1,0:T(8,128)(2,1)S(1)}, bf16[128,512]{1,0:T(8,128)(2,1)S(1)}, u32[]{:S(2)}, u32[]{:S(2)}) %collective-permute-start.20) | collective-permute-done | bytes 131104 | tf_op jit(solution)/shard_map/ppermute | solution.py:41
  47.9 2.2 %collective-permute-start.23 = (bf16[128,512]{1,0:T(8,128)(2,1)S(1)}, bf16[128,512]{1,0:T(8,128)(2,1)S(1)}, u32[]{:S(2)}, u32[]{:S(2)}) collective-permute-start(bf16[128,512]{1,0:T(8,128)(2,1)S(1)} %get-tuple-element.50), channel_id=1, source_target_pairs={{0,8},{1,17},{2,10},{3,19},{4,12},{5,21},{6,14},{7,23},{8,0},{9,25... | collective-permute-start | bytes 393224 | tf_op jit(solution)/shard_map/ppermute | solution.py:41
  50.1 4.2 %collective-permute-done.23 = bf16[128,512]{1,0:T(8,128)(2,1)S(1)} collective-permute-done((bf16[128,512]{1,0:T(8,128)(2,1)S(1)}, bf16[128,512]{1,0:T(8,128)(2,1)S(1)}, u32[]{:S(2)}, u32[]{:S(2)}) %collective-permute-start.23) | collective-permute-done | bytes 131104 | tf_op jit(solution)/shard_map/ppermute | solution.py:41
  54.4 2.6 %collective-permute-start.24 = (bf16[128,512]{1,0:T(8,128)(2,1)S(1)}, bf16[128,512]{1,0:T(8,128)(2,1)S(1)}, u32[]{:S(2)}, u32[]{:S(2)}) collective-permute-start(bf16[128,512]{1,0:T(8,128)(2,1)S(1)} %fusion.1), channel_id=1, source_target_pairs={{0,16},{1,5},{2,18},{3,7},{4,20},{5,1},{6,22},{7,3},{8,24},{9,13},... | collective-permute-start | bytes 393224 | tf_op jit(solution)/shard_map/ppermute | solution.py:41
  56.9 3.4 %collective-permute-done.24 = bf16[128,512]{1,0:T(8,128)(2,1)S(1)} collective-permute-done((bf16[128,512]{1,0:T(8,128)(2,1)S(1)}, bf16[128,512]{1,0:T(8,128)(2,1)S(1)}, u32[]{:S(2)}, u32[]{:S(2)}) %collective-permute-start.24) | collective-permute-done | bytes 131104 | tf_op jit(solution)/shard_map/ppermute | solution.py:41
  60.4 1.1 %collective-permute-start.26 = (bf16[128,512]{1,0:T(8,128)(2,1)S(1)}, bf16[128,512]{1,0:T(8,128)(2,1)S(1)}, u32[]{:S(2)}, u32[]{:S(2)}) collective-permute-start(bf16[128,512]{1,0:T(8,128)(2,1)S(1)} %multiply_convert_fusion.refs_0_), channel_id=1, source_target_pairs={{0,6},{1,11},{2,4},{3,9},{4,2},{5,15},{6,0},{7,13},{8,14},{9,3},{1... | collective-permute-start | bytes 393224 | tf_op jit(solution)/shard_map/ppermute | solution.py:41
  61.5 1.2 %collective-permute-start.28 = (bf16[128,512]{1,0:T(8,128)(2,1)S(1)}, bf16[128,512]{1,0:T(8,128)(2,1)S(1)}, u32[]{:S(2)}, u32[]{:S(2)}) collective-permute-start(bf16[128,512]{1,0:T(8,128)(2,1)S(1)} %multiply_convert_fusion.refs_0_), channel_id=1, source_target_pairs={{0,2},{1,9},{2,0},{3,11},{4,6},{5,13},{6,4},{7,15},{8,10},{9,1},{1... | collective-permute-start | bytes 393224 | tf_op jit(solution)/shard_map/ppermute | solution.py:41
  62.7 1.2 %collective-permute-start.29 = (bf16[128,512]{1,0:T(8,128)(2,1)S(1)}, bf16[128,512]{1,0:T(8,128)(2,1)S(1)}, u32[]{:S(2)}, u32[]{:S(2)}) collective-permute-start(bf16[128,512]{1,0:T(8,128)(2,1)S(1)} %multiply_convert_fusion.refs_0_), channel_id=1, source_target_pairs={{0,4},{1,3},{2,6},{3,1},{4,0},{5,7},{6,2},{7,5},{8,12},{9,11},{10,... | collective-permute-start | bytes 393224 | tf_op jit(solution)/shard_map/ppermute | solution.py:41
  63.9 2.4 %collective-permute-done.26.refs_1_ = bf16[128,512]{1,0:T(8,128)(2,1)S(1)} collective-permute-done((bf16[128,512]{1,0:T(8,128)(2,1)S(1)}, bf16[128,512]{1,0:T(8,128)(2,1)S(1)}, u32[]{:S(2)}, u32[]{:S(2)}) %collective-permute-start.26) | collective-permute-done | bytes 131104 | tf_op jit(solution)/shard_map/ppermute | solution.py:41
  66.3 1.1 %collective-permute-done.28.refs_2_ = bf16[128,512]{1,0:T(8,128)(2,1)S(1)} collective-permute-done((bf16[128,512]{1,0:T(8,128)(2,1)S(1)}, bf16[128,512]{1,0:T(8,128)(2,1)S(1)}, u32[]{:S(2)}, u32[]{:S(2)}) %collective-permute-start.28) | collective-permute-done | bytes 131104 | tf_op jit(solution)/shard_map/ppermute | solution.py:41
  67.4 0.3 collective-permute-done.29.refs_3_
  67.7 0.2 collective-permute-start.31
  67.9 0.4 shard_map.58.rem_ref
  68.3 0.6 shard_map.59.rem_ref
  69.1 0.4 shard_map.60.turned_ref
  69.5 0.3 shard_map.61
  69.7 0.3 collective-permute-start.32
  70.0 1.0 %collective-permute-done.32 = f32[128,128]{1,0:T(8,128)S(1)} collective-permute-done((f32[128,128]{1,0:T(8,128)S(1)}, f32[128,128]{1,0:T(8,128)S(1)}, u32[]{:S(2)}, u32[]{:S(2)}) %collective-permute-start.32) | collective-permute-done | bytes 65568 | tf_op jit(solution)/shard_map/ppermute | solution.py:41
  71.1 1.5 %collective-permute-start.33 = (f32[128,128]{1,0:T(8,128)S(1)}, f32[128,128]{1,0:T(8,128)S(1)}, u32[]{:S(2)}, u32[]{:S(2)}) collective-permute-start(f32[128,128]{1,0:T(8,128)S(1)} %add.93), channel_id=1, source_target_pairs={{0,6},{1,11},{2,4},{3,9},{4,2},{5,15},{6,0},{7,13},{8,14},{9,3},{1... | collective-permute-start | bytes 196616 | tf_op jit(solution)/shard_map/ppermute | solution.py:41
  72.6 1.2 %collective-permute-start.34 = (f32[128,128]{1,0:T(8,128)S(1)}, f32[128,128]{1,0:T(8,128)S(1)}, u32[]{:S(2)}, u32[]{:S(2)}) collective-permute-start(f32[128,128]{1,0:T(8,128)S(1)} %add.93), channel_id=1, source_target_pairs={{0,2},{1,9},{2,0},{3,11},{4,6},{5,13},{6,4},{7,15},{8,10},{9,1},{1... | collective-permute-start | bytes 196616 | tf_op jit(solution)/shard_map/ppermute | solution.py:41
  73.8 0.9 collective-permute-start.35
  74.6 2.3 %collective-permute-done.33 = f32[128,128]{1,0:T(8,128)S(1)} collective-permute-done((f32[128,128]{1,0:T(8,128)S(1)}, f32[128,128]{1,0:T(8,128)S(1)}, u32[]{:S(2)}, u32[]{:S(2)}) %collective-permute-start.33) | collective-permute-done | bytes 65568 | tf_op jit(solution)/shard_map/ppermute | solution.py:41
  77.0 0.7 collective-permute-done.34
  77.7 0.3 collective-permute-done.35
  78.0 2.6 %collective-permute-start.36 = (f32[128,128]{1,0:T(8,128)S(1)}, f32[128,128]{1,0:T(8,128)S(1)}, u32[]{:S(2)}, u32[]{:S(2)}) collective-permute-start(f32[128,128]{1,0:T(8,128)S(1)} %add_add_fusion.1), channel_id=1, source_target_pairs={{0,16},{1,17},{2,18},{3,19},{4,20},{5,21},{6,22},{7,23},{8,24},{9,... | collective-permute-start | bytes 196616 | tf_op jit(solution)/shard_map/ppermute | solution.py:41
  80.6 2.4 %collective-permute-start.37 = (f32[128,128]{1,0:T(8,128)S(1)}, f32[128,128]{1,0:T(8,128)S(1)}, u32[]{:S(2)}, u32[]{:S(2)}) collective-permute-start(f32[128,128]{1,0:T(8,128)S(1)} %add_add_fusion.1), channel_id=1, source_target_pairs={{0,24},{1,21},{2,26},{3,23},{4,28},{5,17},{6,30},{7,19},{8,16},{9,... | collective-permute-start | bytes 196616 | tf_op jit(solution)/shard_map/ppermute | solution.py:41
  83.0 0.5 collective-permute-start.38
  83.5 3.6 %collective-permute-done.37 = f32[128,128]{1,0:T(8,128)S(1)} collective-permute-done((f32[128,128]{1,0:T(8,128)S(1)}, f32[128,128]{1,0:T(8,128)S(1)}, u32[]{:S(2)}, u32[]{:S(2)}) %collective-permute-start.37) | collective-permute-done | bytes 65568 | tf_op jit(solution)/shard_map/ppermute | solution.py:41
  87.2 0.4 collective-permute-done.38
  87.7 1.2 %collective-permute-done.39.other_ref = f32[128,128]{1,0:T(8,128)S(1)} collective-permute-done((f32[128,128]{1,0:T(8,128)S(1)}, f32[128,128]{1,0:T(8,128)S(1)}, u32[]{:S(2)}, u32[]{:S(2)}) %collective-permute-start.39) | collective-permute-done | bytes 65568 | tf_op jit(solution)/shard_map/ppermute | solution.py:41
  88.9 5.2 %shard_map.62 = (bf16[384,128]{1,0:T(8,128)(2,1)}, bf16[384,128]{1,0:T(8,128)(2,1)}) custom-call(f32[128,128]{1,0:T(8,128)S(1)} %add_add_fusion.own_ref, f32[128,128]{1,0:T(8,128)S(1)} %collective-permute-done.39.other_ref, bf16[384,128]{1,0:T(8,128)(2,1)S(1)} %get-tuple-element.49.rem_ref, bf16[384,128]{1,0:T(8,128)(2,1)S(1)} %get-tuple-element.46.user_ref), custom_call_target="tpu_custom_call" | custom-call | tf_op jit(solution)/shard_map/pallas_call | solution.py:45
  (44 shorter events, 1.1 us)
Async XLA Ops:
  2.6 1.6 %collective-permute-start.1 = (bf16[128,512]{1,0:T(8,128)(2,1)S(1)}, bf16[128,512]{1,0:T(8,128)(2,1)S(1)}, u32[]{:S(2)}, u32[]{:S(2)}) collective-permute-start(bf16[128,512]{1,0:T(8,128)(2,1)S(1)} %get-tuple-element.32), channel_id=1, source_target_pairs={{0,1},{1,0},{2,3},{3,2},{4,5},{5,4},{6,7},{7,6},{8,9},{9,8},{10,11... | collective-permute-start | bytes 393224 | tf_op jit(solution)/shard_map/ppermute | solution.py:41
  3.1 5.0 %collective-permute-start.3 = (bf16[128,512]{1,0:T(8,128)(2,1)S(1)}, bf16[128,512]{1,0:T(8,128)(2,1)S(1)}, u32[]{:S(2)}, u32[]{:S(2)}) collective-permute-start(bf16[128,512]{1,0:T(8,128)(2,1)S(1)} %get-tuple-element.34), channel_id=1, source_target_pairs={{0,1},{1,0},{2,3},{3,2},{4,5},{5,4},{6,7},{7,6},{8,9},{9,8},{10,11... | collective-permute-start | bytes 393224 | tf_op jit(solution)/shard_map/ppermute | solution.py:41
  3.2 5.6 %collective-permute-start.5 = (bf16[128,512]{1,0:T(8,128)(2,1)S(1)}, bf16[128,512]{1,0:T(8,128)(2,1)S(1)}, u32[]{:S(2)}, u32[]{:S(2)}) collective-permute-start(bf16[128,512]{1,0:T(8,128)(2,1)S(1)} %get-tuple-element.36), channel_id=1, source_target_pairs={{0,1},{1,0},{2,3},{3,2},{4,5},{5,4},{6,7},{7,6},{8,9},{9,8},{10,11... | collective-permute-start | bytes 393224 | tf_op jit(solution)/shard_map/ppermute | solution.py:41
  3.6 5.3 %collective-permute-start = (bf16[128,512]{1,0:T(8,128)(2,1)S(1)}, bf16[128,512]{1,0:T(8,128)(2,1)S(1)}, u32[]{:S(2)}, u32[]{:S(2)}) collective-permute-start(bf16[128,512]{1,0:T(8,128)(2,1)S(1)} %get-tuple-element.30), channel_id=1, source_target_pairs={{0,1},{1,0},{2,3},{3,2},{4,5},{5,4},{6,7},{7,6},{8,9},{9,8},{10,11... | collective-permute-start | bytes 393224 | tf_op jit(solution)/shard_map/ppermute | solution.py:41
  4.2 8.8 %collective-permute-start.2 = (bf16[128,512]{1,0:T(8,128)(2,1)S(1)}, bf16[128,512]{1,0:T(8,128)(2,1)S(1)}, u32[]{:S(2)}, u32[]{:S(2)}) collective-permute-start(bf16[128,512]{1,0:T(8,128)(2,1)S(1)} %add_convert_fusion.5), channel_id=1, source_target_pairs={{0,6},{1,11},{2,4},{3,9},{4,2},{5,15},{6,0},{7,13},{8,14},{9,3},{1... | collective-permute-start | bytes 393224 | tf_op jit(solution)/shard_map/ppermute | solution.py:41
  8.2 6.6 %collective-permute-start.4 = (bf16[128,512]{1,0:T(8,128)(2,1)S(1)}, bf16[128,512]{1,0:T(8,128)(2,1)S(1)}, u32[]{:S(2)}, u32[]{:S(2)}) collective-permute-start(bf16[128,512]{1,0:T(8,128)(2,1)S(1)} %add_convert_fusion.4), channel_id=1, source_target_pairs={{0,2},{1,9},{2,0},{3,11},{4,6},{5,13},{6,4},{7,15},{8,10},{9,1},{1... | collective-permute-start | bytes 393224 | tf_op jit(solution)/shard_map/ppermute | solution.py:41
  8.8 5.9 %collective-permute-start.6 = (bf16[128,512]{1,0:T(8,128)(2,1)S(1)}, bf16[128,512]{1,0:T(8,128)(2,1)S(1)}, u32[]{:S(2)}, u32[]{:S(2)}) collective-permute-start(bf16[128,512]{1,0:T(8,128)(2,1)S(1)} %add_convert_fusion.3), channel_id=1, source_target_pairs={{0,4},{1,3},{2,6},{3,1},{4,0},{5,7},{6,2},{7,5},{8,12},{9,11},{10,... | collective-permute-start | bytes 393224 | tf_op jit(solution)/shard_map/ppermute | solution.py:41
  14.8 5.2 %collective-permute-start.7 = (bf16[128,512]{1,0:T(8,128)(2,1)S(1)}, bf16[128,512]{1,0:T(8,128)(2,1)S(1)}, u32[]{:S(2)}, u32[]{:S(2)}) collective-permute-start(bf16[128,512]{1,0:T(8,128)(2,1)S(1)} %get-tuple-element.52), channel_id=1, source_target_pairs={{0,8},{1,17},{2,10},{3,19},{4,12},{5,21},{6,14},{7,23},{8,0},{9,25... | collective-permute-start | bytes 393224 | tf_op jit(solution)/shard_map/ppermute | solution.py:41
  20.1 6.0 %collective-permute-start.8 = (bf16[128,512]{1,0:T(8,128)(2,1)S(1)}, bf16[128,512]{1,0:T(8,128)(2,1)S(1)}, u32[]{:S(2)}, u32[]{:S(2)}) collective-permute-start(bf16[128,512]{1,0:T(8,128)(2,1)S(1)} %fusion), channel_id=1, source_target_pairs={{0,16},{1,5},{2,18},{3,7},{4,20},{5,1},{6,22},{7,3},{8,24},{9,13},... | collective-permute-start | bytes 393224 | tf_op jit(solution)/shard_map/ppermute | solution.py:41
  26.1 6.8 %collective-permute-start.10 = (bf16[128,512]{1,0:T(8,128)(2,1)S(1)}, bf16[128,512]{1,0:T(8,128)(2,1)S(1)}, u32[]{:S(2)}, u32[]{:S(2)}) collective-permute-start(bf16[128,512]{1,0:T(8,128)(2,1)S(1)} %multiply_convert_fusion.1.refs_0_), channel_id=1, source_target_pairs={{0,6},{1,11},{2,4},{3,9},{4,2},{5,15},{6,0},{7,13},{8,14},{9,3},{1... | collective-permute-start | bytes 393224 | tf_op jit(solution)/shard_map/ppermute | solution.py:41
  28.6 5.0 %collective-permute-start.12 = (bf16[128,512]{1,0:T(8,128)(2,1)S(1)}, bf16[128,512]{1,0:T(8,128)(2,1)S(1)}, u32[]{:S(2)}, u32[]{:S(2)}) collective-permute-start(bf16[128,512]{1,0:T(8,128)(2,1)S(1)} %multiply_convert_fusion.1.refs_0_), channel_id=1, source_target_pairs={{0,2},{1,9},{2,0},{3,11},{4,6},{5,13},{6,4},{7,15},{8,10},{9,1},{1... | collective-permute-start | bytes 393224 | tf_op jit(solution)/shard_map/ppermute | solution.py:41
  29.1 5.2 %collective-permute-start.13 = (bf16[128,512]{1,0:T(8,128)(2,1)S(1)}, bf16[128,512]{1,0:T(8,128)(2,1)S(1)}, u32[]{:S(2)}, u32[]{:S(2)}) collective-permute-start(bf16[128,512]{1,0:T(8,128)(2,1)S(1)} %multiply_convert_fusion.1.refs_0_), channel_id=1, source_target_pairs={{0,4},{1,3},{2,6},{3,1},{4,0},{5,7},{6,2},{7,5},{8,12},{9,11},{10,... | collective-permute-start | bytes 393224 | tf_op jit(solution)/shard_map/ppermute | solution.py:41
  29.7 4.7 %collective-permute-start.9 = (bf16[128,512]{1,0:T(8,128)(2,1)S(1)}, bf16[128,512]{1,0:T(8,128)(2,1)S(1)}, u32[]{:S(2)}, u32[]{:S(2)}) collective-permute-start(bf16[128,512]{1,0:T(8,128)(2,1)S(1)} %multiply_convert_fusion.1.refs_0_), channel_id=1, source_target_pairs={{0,1},{1,0},{2,3},{3,2},{4,5},{5,4},{6,7},{7,6},{8,9},{9,8},{10,11... | collective-permute-start | bytes 393224 | tf_op jit(solution)/shard_map/ppermute | solution.py:41
  32.9 1.4 %collective-permute-start.11 = (bf16[128,512]{1,0:T(8,128)(2,1)S(1)}, bf16[128,512]{1,0:T(8,128)(2,1)S(1)}, u32[]{:S(2)}, u32[]{:S(2)}) collective-permute-start(bf16[128,512]{1,0:T(8,128)(2,1)S(1)} %collective-permute-done.10.refs_1_), channel_id=1, source_target_pairs={{0,1},{1,0},{2,3},{3,2},{4,5},{5,4},{6,7},{7,6},{8,9},{9,8},{10,11... | collective-permute-start | bytes 393224 | tf_op jit(solution)/shard_map/ppermute | solution.py:41
  33.5 1.9 %collective-permute-start.14 = (bf16[128,512]{1,0:T(8,128)(2,1)S(1)}, bf16[128,512]{1,0:T(8,128)(2,1)S(1)}, u32[]{:S(2)}, u32[]{:S(2)}) collective-permute-start(bf16[128,512]{1,0:T(8,128)(2,1)S(1)} %collective-permute-done.12.refs_2_), channel_id=1, source_target_pairs={{0,1},{1,0},{2,3},{3,2},{4,5},{5,4},{6,7},{7,6},{8,9},{9,8},{10,11... | collective-permute-start | bytes 393224 | tf_op jit(solution)/shard_map/ppermute | solution.py:41
  34.3 1.3 %collective-permute-start.15 = (bf16[128,512]{1,0:T(8,128)(2,1)S(1)}, bf16[128,512]{1,0:T(8,128)(2,1)S(1)}, u32[]{:S(2)}, u32[]{:S(2)}) collective-permute-start(bf16[128,512]{1,0:T(8,128)(2,1)S(1)} %collective-permute-done.13.refs_3_), channel_id=1, source_target_pairs={{0,1},{1,0},{2,3},{3,2},{4,5},{5,4},{6,7},{7,6},{8,9},{9,8},{10,11... | collective-permute-start | bytes 393224 | tf_op jit(solution)/shard_map/ppermute | solution.py:41
  36.3 2.0 %collective-permute-start.17 = (bf16[128,512]{1,0:T(8,128)(2,1)S(1)}, bf16[128,512]{1,0:T(8,128)(2,1)S(1)}, u32[]{:S(2)}, u32[]{:S(2)}) collective-permute-start(bf16[128,512]{1,0:T(8,128)(2,1)S(1)} %shard_map.57), channel_id=1, source_target_pairs={{0,1},{1,0},{2,3},{3,2},{4,5},{5,4},{6,7},{7,6},{8,9},{9,8},{10,11... | collective-permute-start | bytes 393224 | tf_op jit(solution)/shard_map/ppermute | solution.py:41
  37.0 3.0 %collective-permute-start.19 = (bf16[128,512]{1,0:T(8,128)(2,1)S(1)}, bf16[128,512]{1,0:T(8,128)(2,1)S(1)}, u32[]{:S(2)}, u32[]{:S(2)}) collective-permute-start(bf16[128,512]{1,0:T(8,128)(2,1)S(1)} %get-tuple-element.43), channel_id=1, source_target_pairs={{0,1},{1,0},{2,3},{3,2},{4,5},{5,4},{6,7},{7,6},{8,9},{9,8},{10,11... | collective-permute-start | bytes 393224 | tf_op jit(solution)/shard_map/ppermute | solution.py:41
  37.4 3.4 %collective-permute-start.21 = (bf16[128,512]{1,0:T(8,128)(2,1)S(1)}, bf16[128,512]{1,0:T(8,128)(2,1)S(1)}, u32[]{:S(2)}, u32[]{:S(2)}) collective-permute-start(bf16[128,512]{1,0:T(8,128)(2,1)S(1)} %get-tuple-element.45), channel_id=1, source_target_pairs={{0,1},{1,0},{2,3},{3,2},{4,5},{5,4},{6,7},{7,6},{8,9},{9,8},{10,11... | collective-permute-start | bytes 393224 | tf_op jit(solution)/shard_map/ppermute | solution.py:41
  37.6 4.5 %collective-permute-start.16 = (bf16[128,512]{1,0:T(8,128)(2,1)S(1)}, bf16[128,512]{1,0:T(8,128)(2,1)S(1)}, u32[]{:S(2)}, u32[]{:S(2)}) collective-permute-start(bf16[128,512]{1,0:T(8,128)(2,1)S(1)} %get-tuple-element.40), channel_id=1, source_target_pairs={{0,1},{1,0},{2,3},{3,2},{4,5},{5,4},{6,7},{7,6},{8,9},{9,8},{10,11... | collective-permute-start | bytes 393224 | tf_op jit(solution)/shard_map/ppermute | solution.py:41
  38.3 8.4 %collective-permute-start.18 = (bf16[128,512]{1,0:T(8,128)(2,1)S(1)}, bf16[128,512]{1,0:T(8,128)(2,1)S(1)}, u32[]{:S(2)}, u32[]{:S(2)}) collective-permute-start(bf16[128,512]{1,0:T(8,128)(2,1)S(1)} %add_convert_fusion.2), channel_id=1, source_target_pairs={{0,6},{1,11},{2,4},{3,9},{4,2},{5,15},{6,0},{7,13},{8,14},{9,3},{1... | collective-permute-start | bytes 393224 | tf_op jit(solution)/shard_map/ppermute | solution.py:41
  40.0 7.8 %collective-permute-start.20 = (bf16[128,512]{1,0:T(8,128)(2,1)S(1)}, bf16[128,512]{1,0:T(8,128)(2,1)S(1)}, u32[]{:S(2)}, u32[]{:S(2)}) collective-permute-start(bf16[128,512]{1,0:T(8,128)(2,1)S(1)} %add_convert_fusion.1), channel_id=1, source_target_pairs={{0,2},{1,9},{2,0},{3,11},{4,6},{5,13},{6,4},{7,15},{8,10},{9,1},{1... | collective-permute-start | bytes 393224 | tf_op jit(solution)/shard_map/ppermute | solution.py:41
  40.8 7.0 %collective-permute-start.22 = (bf16[128,512]{1,0:T(8,128)(2,1)S(1)}, bf16[128,512]{1,0:T(8,128)(2,1)S(1)}, u32[]{:S(2)}, u32[]{:S(2)}) collective-permute-start(bf16[128,512]{1,0:T(8,128)(2,1)S(1)} %add_convert_fusion), channel_id=1, source_target_pairs={{0,4},{1,3},{2,6},{3,1},{4,0},{5,7},{6,2},{7,5},{8,12},{9,11},{10,... | collective-permute-start | bytes 393224 | tf_op jit(solution)/shard_map/ppermute | solution.py:41
  47.9 6.4 %collective-permute-start.23 = (bf16[128,512]{1,0:T(8,128)(2,1)S(1)}, bf16[128,512]{1,0:T(8,128)(2,1)S(1)}, u32[]{:S(2)}, u32[]{:S(2)}) collective-permute-start(bf16[128,512]{1,0:T(8,128)(2,1)S(1)} %get-tuple-element.50), channel_id=1, source_target_pairs={{0,8},{1,17},{2,10},{3,19},{4,12},{5,21},{6,14},{7,23},{8,0},{9,25... | collective-permute-start | bytes 393224 | tf_op jit(solution)/shard_map/ppermute | solution.py:41
  54.4 5.9 %collective-permute-start.24 = (bf16[128,512]{1,0:T(8,128)(2,1)S(1)}, bf16[128,512]{1,0:T(8,128)(2,1)S(1)}, u32[]{:S(2)}, u32[]{:S(2)}) collective-permute-start(bf16[128,512]{1,0:T(8,128)(2,1)S(1)} %fusion.1), channel_id=1, source_target_pairs={{0,16},{1,5},{2,18},{3,7},{4,20},{5,1},{6,22},{7,3},{8,24},{9,13},... | collective-permute-start | bytes 393224 | tf_op jit(solution)/shard_map/ppermute | solution.py:41
  60.4 6.0 %collective-permute-start.26 = (bf16[128,512]{1,0:T(8,128)(2,1)S(1)}, bf16[128,512]{1,0:T(8,128)(2,1)S(1)}, u32[]{:S(2)}, u32[]{:S(2)}) collective-permute-start(bf16[128,512]{1,0:T(8,128)(2,1)S(1)} %multiply_convert_fusion.refs_0_), channel_id=1, source_target_pairs={{0,6},{1,11},{2,4},{3,9},{4,2},{5,15},{6,0},{7,13},{8,14},{9,3},{1... | collective-permute-start | bytes 393224 | tf_op jit(solution)/shard_map/ppermute | solution.py:41
  61.5 5.9 %collective-permute-start.28 = (bf16[128,512]{1,0:T(8,128)(2,1)S(1)}, bf16[128,512]{1,0:T(8,128)(2,1)S(1)}, u32[]{:S(2)}, u32[]{:S(2)}) collective-permute-start(bf16[128,512]{1,0:T(8,128)(2,1)S(1)} %multiply_convert_fusion.refs_0_), channel_id=1, source_target_pairs={{0,2},{1,9},{2,0},{3,11},{4,6},{5,13},{6,4},{7,15},{8,10},{9,1},{1... | collective-permute-start | bytes 393224 | tf_op jit(solution)/shard_map/ppermute | solution.py:41
  62.7 5.0 %collective-permute-start.29 = (bf16[128,512]{1,0:T(8,128)(2,1)S(1)}, bf16[128,512]{1,0:T(8,128)(2,1)S(1)}, u32[]{:S(2)}, u32[]{:S(2)}) collective-permute-start(bf16[128,512]{1,0:T(8,128)(2,1)S(1)} %multiply_convert_fusion.refs_0_), channel_id=1, source_target_pairs={{0,4},{1,3},{2,6},{3,1},{4,0},{5,7},{6,2},{7,5},{8,12},{9,11},{10,... | collective-permute-start | bytes 393224 | tf_op jit(solution)/shard_map/ppermute | solution.py:41
  63.9 4.0 %collective-permute-start.25 = (bf16[128,512]{1,0:T(8,128)(2,1)S(1)}, bf16[128,512]{1,0:T(8,128)(2,1)S(1)}, u32[]{:S(2)}, u32[]{:S(2)}) collective-permute-start(bf16[128,512]{1,0:T(8,128)(2,1)S(1)} %multiply_convert_fusion.refs_0_), channel_id=1, source_target_pairs={{0,1},{1,0},{2,3},{3,2},{4,5},{5,4},{6,7},{7,6},{8,9},{9,8},{10,11... | collective-permute-start | bytes 393224 | tf_op jit(solution)/shard_map/ppermute | solution.py:41
  66.3 1.6 %collective-permute-start.27 = (bf16[128,512]{1,0:T(8,128)(2,1)S(1)}, bf16[128,512]{1,0:T(8,128)(2,1)S(1)}, u32[]{:S(2)}, u32[]{:S(2)}) collective-permute-start(bf16[128,512]{1,0:T(8,128)(2,1)S(1)} %collective-permute-done.26.refs_1_), channel_id=1, source_target_pairs={{0,1},{1,0},{2,3},{3,2},{4,5},{5,4},{6,7},{7,6},{8,9},{9,8},{10,11... | collective-permute-start | bytes 393224 | tf_op jit(solution)/shard_map/ppermute | solution.py:41
  67.4 1.5 %collective-permute-start.30 = (bf16[128,512]{1,0:T(8,128)(2,1)S(1)}, bf16[128,512]{1,0:T(8,128)(2,1)S(1)}, u32[]{:S(2)}, u32[]{:S(2)}) collective-permute-start(bf16[128,512]{1,0:T(8,128)(2,1)S(1)} %collective-permute-done.28.refs_2_), channel_id=1, source_target_pairs={{0,1},{1,0},{2,3},{3,2},{4,5},{5,4},{6,7},{7,6},{8,9},{9,8},{10,11... | collective-permute-start | bytes 393224 | tf_op jit(solution)/shard_map/ppermute | solution.py:41
  67.7 1.3 %collective-permute-start.31 = (bf16[128,512]{1,0:T(8,128)(2,1)S(1)}, bf16[128,512]{1,0:T(8,128)(2,1)S(1)}, u32[]{:S(2)}, u32[]{:S(2)}) collective-permute-start(bf16[128,512]{1,0:T(8,128)(2,1)S(1)} %collective-permute-done.29.refs_3_), channel_id=1, source_target_pairs={{0,1},{1,0},{2,3},{3,2},{4,5},{5,4},{6,7},{7,6},{8,9},{9,8},{10,11... | collective-permute-start | bytes 393224 | tf_op jit(solution)/shard_map/ppermute | solution.py:41
  69.7 1.3 %collective-permute-start.32 = (f32[128,128]{1,0:T(8,128)S(1)}, f32[128,128]{1,0:T(8,128)S(1)}, u32[]{:S(2)}, u32[]{:S(2)}) collective-permute-start(f32[128,128]{1,0:T(8,128)S(1)} %get-tuple-element.48), channel_id=1, source_target_pairs={{0,1},{1,0},{2,3},{3,2},{4,5},{5,4},{6,7},{7,6},{8,9},{9,8},{10,11... | collective-permute-start | bytes 196616 | tf_op jit(solution)/shard_map/ppermute | solution.py:41
  71.1 5.9 %collective-permute-start.33 = (f32[128,128]{1,0:T(8,128)S(1)}, f32[128,128]{1,0:T(8,128)S(1)}, u32[]{:S(2)}, u32[]{:S(2)}) collective-permute-start(f32[128,128]{1,0:T(8,128)S(1)} %add.93), channel_id=1, source_target_pairs={{0,6},{1,11},{2,4},{3,9},{4,2},{5,15},{6,0},{7,13},{8,14},{9,3},{1... | collective-permute-start | bytes 196616 | tf_op jit(solution)/shard_map/ppermute | solution.py:41
  72.6 5.1 %collective-permute-start.34 = (f32[128,128]{1,0:T(8,128)S(1)}, f32[128,128]{1,0:T(8,128)S(1)}, u32[]{:S(2)}, u32[]{:S(2)}) collective-permute-start(f32[128,128]{1,0:T(8,128)S(1)} %add.93), channel_id=1, source_target_pairs={{0,2},{1,9},{2,0},{3,11},{4,6},{5,13},{6,4},{7,15},{8,10},{9,1},{1... | collective-permute-start | bytes 196616 | tf_op jit(solution)/shard_map/ppermute | solution.py:41
  73.8 4.3 %collective-permute-start.35 = (f32[128,128]{1,0:T(8,128)S(1)}, f32[128,128]{1,0:T(8,128)S(1)}, u32[]{:S(2)}, u32[]{:S(2)}) collective-permute-start(f32[128,128]{1,0:T(8,128)S(1)} %add.93), channel_id=1, source_target_pairs={{0,4},{1,3},{2,6},{3,1},{4,0},{5,7},{6,2},{7,5},{8,12},{9,11},{10,... | collective-permute-start | bytes 196616 | tf_op jit(solution)/shard_map/ppermute | solution.py:41
  78.0 5.5 %collective-permute-start.36 = (f32[128,128]{1,0:T(8,128)S(1)}, f32[128,128]{1,0:T(8,128)S(1)}, u32[]{:S(2)}, u32[]{:S(2)}) collective-permute-start(f32[128,128]{1,0:T(8,128)S(1)} %add_add_fusion.1), channel_id=1, source_target_pairs={{0,16},{1,17},{2,18},{3,19},{4,20},{5,21},{6,22},{7,23},{8,24},{9,... | collective-permute-start | bytes 196616 | tf_op jit(solution)/shard_map/ppermute | solution.py:41
  80.6 6.5 %collective-permute-start.37 = (f32[128,128]{1,0:T(8,128)S(1)}, f32[128,128]{1,0:T(8,128)S(1)}, u32[]{:S(2)}, u32[]{:S(2)}) collective-permute-start(f32[128,128]{1,0:T(8,128)S(1)} %add_add_fusion.1), channel_id=1, source_target_pairs={{0,24},{1,21},{2,26},{3,23},{4,28},{5,17},{6,30},{7,19},{8,16},{9,... | collective-permute-start | bytes 196616 | tf_op jit(solution)/shard_map/ppermute | solution.py:41
  83.0 4.5 %collective-permute-start.38 = (f32[128,128]{1,0:T(8,128)S(1)}, f32[128,128]{1,0:T(8,128)S(1)}, u32[]{:S(2)}, u32[]{:S(2)}) collective-permute-start(f32[128,128]{1,0:T(8,128)S(1)} %add_add_fusion.1), channel_id=1, source_target_pairs={{0,8},{1,5},{2,10},{3,7},{4,12},{5,1},{6,14},{7,3},{8,0},{9,13},{1... | collective-permute-start | bytes 196616 | tf_op jit(solution)/shard_map/ppermute | solution.py:41
  87.6 1.3 %collective-permute-start.39 = (f32[128,128]{1,0:T(8,128)S(1)}, f32[128,128]{1,0:T(8,128)S(1)}, u32[]{:S(2)}, u32[]{:S(2)}) collective-permute-start(f32[128,128]{1,0:T(8,128)S(1)} %add_add_fusion.own_ref), channel_id=1, source_target_pairs={{0,1},{1,0},{2,3},{3,2},{4,5},{5,4},{6,7},{7,6},{8,9},{9,8},{10,11... | collective-permute-start | bytes 196616 | tf_op jit(solution)/shard_map/ppermute | solution.py:41
